TPU v7x, 256 devices: a whole 4x4x8 slice. The times are simulated.
256 devices in a mesh: rep: 32 (over x_lo, z, core), tp: 8 (over y, x_hi).
Axes of the slice: x: 4 (x_hi: 2, x_lo: 2; x = x_hi * 2 + x_lo), y: 4, z: 8, core: 2. Of those that a mesh axis runs over, the one named last changes fastest.
Arguments:
- kv_cache: bfloat16 [512, 8, 256, 256], P('rep', 'tp'), may hold values from -160 to 160
- lengths: int32 [512], P('rep'), may hold values from 2 to 256, as said below
- departing: int32 [32, 13], P('rep'), may hold values from 0 to 15, as said below
- destination: int32 [32, 13], P('rep'), may hold values from 0 to 31, as said below
- queries: bfloat16 [2, 512, 64, 128], P(None, 'rep', 'tp'), may hold values from -160 to 160
- new_kv: bfloat16 [2, 512, 8, 256], P(None, 'rep', 'tp'), may hold values from -160 to 160
- codes: bfloat16 [2560, 128, 128], P(('tp', 'rep')), may hold values from -6 to 6
- scales: float32 [2560], P(('tp', 'rep')), may hold values from 0.02 to 0.25
- block_slot: int32 [2560], P(('tp', 'rep')), may hold values from 0 to 2559, as said below
Outputs:
- projected: bfloat16 [2, 512, 5120], P(None, 'rep', 'tp')
Inputs may be any that keep to these rules, and one draw needn't show every extreme that they name: `lengths`: every slot holds at least two positions, and some slot holds exactly 256. `departing`: each row names 13 different slots. `destination`: in each round every replica is named exactly once and never by itself; no row names a replica twice. `block_slot`: a permutation; the entries at positions of one tp index are exactly that index's consecutive range of 320 block numbers.
All inputs are finite; a program needn't handle non-finite values.
Results may differ from a plain program's by a relative error of at most 0.02.
Values may be sent and summed in bfloat16 or wider, within the bound.
No kernel may reach another device: no remote copies, remote signals or barrier semaphores. Data moves between devices by JAX's collectives and lax.ppermute only.
A program may use at most 64 MiB of HBM per device.

v0:
```python
import math

import jax
import jax.numpy as jnp
from jax import lax
from jax.sharding import PartitionSpec as P


def attend_cached(grouped, cache, lengths):
    width = grouped.shape[-1]
    scale_factor = 1.0 / math.sqrt(width)
    scores = (
        jnp.einsum(
            "nsgqd,ngpd->nsgqp", grouped, cache[..., :width], preferred_element_type=jnp.float32
        )
        * scale_factor
    )
    valid = (jnp.arange(cache.shape[2], dtype=jnp.int32)[None, :] < lengths[:, None])[
        :, None, None, None, :
    ]
    scores = jnp.where(valid, scores, -jnp.inf)
    top = jnp.max(scores, axis=-1)
    expo = jnp.where(valid, jnp.exp(scores - top[..., None]), 0.0)
    total = jnp.sum(expo, axis=-1)
    carried = jnp.einsum(
        "nsgqp,ngpd->nsgqd",
        expo.astype(jnp.bfloat16),
        cache[..., width:],
        preferred_element_type=jnp.float32,
    )
    return (top, total, carried)


def attend_fresh(top, total, carried, grouped, fresh):
    width = grouped.shape[-1]
    steps = grouped.shape[1]
    scale_factor = 1.0 / math.sqrt(width)
    extra = (
        jnp.einsum(
            "nsgqd,nugd->nsgqu", grouped, fresh[..., :width], preferred_element_type=jnp.float32
        )
        * scale_factor
    )
    allowed = (jnp.arange(steps)[None, :] <= jnp.arange(steps)[:, None])[None, :, None, None, :]
    extra = jnp.where(allowed, extra, -jnp.inf)
    peak = jnp.maximum(top, jnp.max(extra, axis=-1))
    factor = jnp.exp(top - peak)
    weights = jnp.where(allowed, jnp.exp(extra - peak[..., None]), 0.0)
    denom = total * factor + jnp.sum(weights, axis=-1)
    numer = carried * factor[..., None] + jnp.einsum(
        "nsgqu,nugd->nsgqd", weights, fresh[..., width:].astype(jnp.float32)
    )
    return (numer / denom[..., None]).astype(jnp.bfloat16)


def shards(kv_cache, lengths, departing, destination, queries, new_kv, codes, scales, block_slot):
    steps, slots, heads, width = queries.shape
    groups = kv_cache.shape[1]
    grouped = jnp.transpose(queries, (1, 0, 2, 3)).reshape(
        slots, steps, groups, heads // groups, width
    )
    fresh = jnp.transpose(new_kv, (1, 0, 2, 3))
    replicas = lax.axis_size("rep")
    leaving = departing[0]
    heading = destination[0]
    peers = jnp.arange(replicas, dtype=jnp.int32)
    chosen = heading[None, :] == peers[:, None]
    sending = jnp.any(chosen, axis=1)
    round_id = jnp.where(sending, jnp.argmax(chosen, axis=1), -1)
    picked = leaving[jnp.maximum(round_id, 0)]
    outgoing = jnp.where(
        sending[:, None, None, None], kv_cache[picked], jnp.zeros((), jnp.bfloat16)
    )
    meta = jnp.stack([jnp.where(sending, lengths[picked], 0), round_id], axis=1)
    arrived, arrived_meta = (
        lax.all_to_all(outgoing, "rep", split_axis=0, concat_axis=0, tiled=True),
        lax.all_to_all(meta, "rep", split_axis=0, concat_axis=0, tiled=True),
    )
    target = jnp.where(arrived_meta[:, 1] >= 0, leaving[jnp.maximum(arrived_meta[:, 1], 0)], slots)
    cache_now = kv_cache.at[target].set(arrived, mode="drop")
    lengths_now = lengths.at[target].set(arrived_meta[:, 0], mode="drop")
    top, total, carried = attend_cached(grouped, cache_now, lengths_now)
    attended = attend_fresh(top, total, carried, grouped, fresh)
    rows = jnp.transpose(attended.reshape(slots, steps, heads, width), (1, 0, 2, 3)).reshape(
        steps * slots, heads, width
    )
    group_blocks = codes.shape[0] * replicas
    columns = group_blocks // heads
    base = lax.axis_index("tp") * group_blocks
    initial = jnp.zeros((group_blocks, width, width), jnp.bfloat16)
    block_codes = lax.all_gather(codes, "rep", axis=0, tiled=True)
    block_scales = lax.all_gather(scales.astype(jnp.bfloat16), "rep", axis=0, tiled=True).astype(
        jnp.float32
    )
    block_ids = lax.all_gather(block_slot, "rep", axis=0, tiled=True)
    dequant = (block_codes.astype(jnp.float32) * block_scales[:, None, None]).astype(jnp.bfloat16)
    placed = initial.at[block_ids - base].set(dequant)
    matrix = placed.reshape(heads, columns, width, width)
    terms = jnp.einsum("nha,hcab->ncb", rows, matrix, preferred_element_type=jnp.float32).reshape(
        rows.shape[0], columns * width
    )
    summed = lax.psum_scatter(
        terms.astype(jnp.bfloat16), "tp", scatter_dimension=1, tiled=True
    ).astype(jnp.float32)
    return summed.astype(jnp.bfloat16).reshape(steps, slots, summed.shape[1])


def solution(mesh):
    placed = (
        P("rep", "tp", None, None),
        P("rep"),
        P("rep", None),
        P("rep", None),
        P(None, "rep", "tp", None),
        P(None, "rep", "tp", None),
        P(("tp", "rep"), None, None),
        P(("tp", "rep")),
        P(("tp", "rep")),
    )
    return jax.shard_map(
        shards, mesh=mesh, in_specs=placed, out_specs=P(None, "rep", "tp"), check_vma=False
    )
```

profile of v0, /device:TPU:8, one launch (start us, length us, event | category | flops | bytes accessed | tf_op | source)
XLA Modules:
  0.0 411.0 jit_solution(16971237327153373325)
XLA Ops:
  6.5 0.7 copy.63
  7.3 1.6 copy.62
  9.0 0.6 iota_reduce_fusion
  9.6 0.7 gather_fusion
  10.3 0.7 gather_fusion.1
  11.0 0.7 copy.28
  11.7 9.8 %all-to-all-start = ((s32[32,1,2]{2,1,0:T(1,128)}), s32[32,1,2]{2,1,0:T(1,128)S(1)}, u32[]{:S(2)}, u32[]{:S(2)}) async-start(s32[32,1,2]{2,1,0:T(1,128)} %copy.28), calls=%async_computation | async-start | bytes 32768 | tf_op jit(solution)/shard_map/all_to_all | solution.py:77
  21.5 2.8 gather_fusion.3
  24.3 4.5 %fusion.1 = bf16[32,1,256,256]{3,2,1,0:T(8,128)(2,1)} fusion(bf16[32,256,256]{2,1,0:T(8,128)(2,1)} %gather_fusion.3, pred[32]{0:T(512)(128)(4,1)S(1)} %fusion.23), kind=kLoop, calls=%fused_computation.11 | loop fusion | flops 2097152 | bytes 8388640 | tf_op jit(solution)/shard_map/jit(_where)/select_n | solution.py:71
  28.8 1.0 all-to-all-done
  29.9 7.6 %all-to-all-start.1 = ((bf16[32,1,256,256]{3,2,1,0:T(8,128)(2,1)}), bf16[32,1,256,256]{3,2,1,0:T(8,128)(2,1)}, u32[]{:S(2)}, u32[]{:S(2)}) async-start(bf16[32,1,256,256]{3,2,1,0:T(8,128)(2,1)} %fusion.1), calls=%async_computation.1 | async-start | bytes 8388608 | tf_op jit(solution)/shard_map/all_to_all | solution.py:76
  37.5 0.6 dynamic-slice
  38.8 0.2 dynamic-update-slice.1
  39.0 176.7 %all-reduce.1 = bf16[320]{0:T(512)(128)(2,1)S(1)} all-reduce(bf16[320]{0:T(512)(128)(2,1)S(1)} %dynamic-update-slice.1), channel_id=1, replica_groups=mesh['rep'=32,'tp'=8] {'rep'}, use_global_device_ids=true, to_apply=%add.1 | all-reduce | flops 320 | bytes 1280
  215.8 0.2 dynamic-update-slice
  216.0 12.0 %all-reduce = s32[320]{0:T(512)S(1)} all-reduce(s32[320]{0:T(512)S(1)} %dynamic-update-slice), channel_id=1, replica_groups=mesh['rep'=32,'tp'=8] {'rep'}, use_global_device_ids=true, to_apply=%add | all-reduce | flops 320 | bytes 2560
  228.0 0.4 fusion.31
  228.6 0.7 gather_fusion.2
  229.3 0.7 scatter_fusion.1
  230.0 6.3 %scatter_fusion = bf16[16,256,256]{2,1,0:T(8,128)(2,1)S(1)} fusion(bf16[16,256,256]{2,1,0:T(8,128)(2,1)S(1)} %bitcast.136, s32[32]{0:T(128)S(1)} %fusion.26, bf16[32,256,256]{2,1,0:T(8,128)(2,1)} %bitcast.14), kind=kCustom, calls=%fused_computation.4 | custom fusion | bytes 12583040 | tf_op jit(solution)/shard_map/scatter | solution.py:80
  236.3 0.5 fusion.30
  236.9 0.3 convolution_bitcast_fusion.2
  237.2 0.2 fusion.12
  237.5 0.3 fusion.9
  237.8 10.8 %multiply_convert_fusion = bf16[320,128,128]{2,1,0:T(8,128)(2,1)} fusion(bf16[320,128,128]{2,1,0:T(8,128)(2,1)} %all-gather.2.cloned.1.call-done, f32[320]{0:T(512)S(1)} %convert_element_type.32), kind=kLoop, calls=%fused_computation.7 | loop fusion | flops 15728640 | bytes 20972800 | tf_op jit(solution)/shard_map/convert_element_type | solution.py:96
  248.6 6.6 %broadcast_in_dim.96 = bf16[320,128,128]{2,1,0:T(8,128)(2,1)} broadcast(bf16[]{:T(256)} %constant.14.clone.1), dimensions={} | broadcast | bytes 10485762 | tf_op jit(solution)/shard_map/broadcast_in_dim | solution.py:90
  255.2 47.4 %scatter_fusion.2 = bf16[320,128,128]{2,1,0:T(8,128)(2,1)} fusion(bf16[320,128,128]{2,1,0:T(8,128)(2,1)} %broadcast_in_dim.96, s32[320]{0:T(512)S(1)} %compare_select_fusion, bf16[320,128,128]{2,1,0:T(8,128)(2,1)} %multiply_convert_fusion), kind=kCustom, calls=%fused_computation.6 | custom fusion | bytes 31458560 | tf_op jit(solution)/shard_map/scatter | solution.py:97
  302.7 13.7 %copy.35 = bf16[40,128,128,8]{2,1,0,3:T(8,128)(2,1)} copy(bf16[40,128,128,8]{1,2,0,3:T(8,128)(2,1)} %bitcast.134) | data formatting | bytes 20971520 | tf_op jit(solution)/shard_map/nha,hcab->ncb/dot_general | solution.py:99
  316.4 7.1 %fusion = bf16[32,5120]{1,0:T(8,128)(2,1)S(1)} fusion(bf16[5120,128,8]{1,0,2:T(8,128)(2,1)} %bitcast.139, bf16[32,8,128]{2,1,0:T(8,128)(2,1)S(1)} %bitcast.141), kind=kOutput, calls=%fused_computation.9 | convolution fusion | flops 335708160 | bytes 10878976 | tf_op jit(solution)/shard_map/nha,hcab->ncb/dot_general | solution.py:99
  323.5 1.4 copy.41
  325.0 77.6 %reduce-scatter.4.cloned.1.call-done = bf16[640,32]{1,0:T(8,128)(2,1)} async-done(((bf16[5120,32]{1,0:T(8,128)(2,1)}), bf16[640,32]{1,0:T(8,128)(2,1)}) %reduce-scatter.4.cloned.1.call-update) | async-done | bytes 40976
  402.5 1.6 copy.42
  (43 shorter events, 0.6 us)
Async XLA Ops:
  6.5 221.5 %copy-start = (bf16[2,16,8,128]{3,2,1,0:T(8,128)(2,1)S(1)}, bf16[2,16,8,128]{3,2,1,0:T(8,128)(2,1)}, u32[]{:S(2)}) copy-start(bf16[2,16,8,128]{3,2,1,0:T(8,128)(2,1)} %param.13) | copy-start | bytes 196612
  6.5 3.1 copy-start.1
  6.5 2.3 copy-start.3
  6.5 231.3 %all-gather.2.cloned.1.call-start = ((), (), s32[]{:S(2)}) async-start(), calls=%async_computation.3 | async-start | bytes 10813440 | tf_op jit(solution)/shard_map/all_gather | solution.py:91
  11.7 18.1 %all-to-all-start = ((s32[32,1,2]{2,1,0:T(1,128)}), s32[32,1,2]{2,1,0:T(1,128)S(1)}, u32[]{:S(2)}, u32[]{:S(2)}) async-start(s32[32,1,2]{2,1,0:T(1,128)} %copy.28), calls=%async_computation | async-start | bytes 32768 | tf_op jit(solution)/shard_map/all_to_all | solution.py:77
  28.8 8.7 %copy-start.4 = (f32[10]{0:T(128)S(1)}, f32[10]{0:T(128)}, u32[]{:S(2)}) copy-start(f32[10]{0:T(128)} %param.16) | copy-start | bytes 124
  28.8 8.7 %copy-start.6 = (u32[256]{0:T(256)S(1)}, u32[256]{0:T(256)}, u32[]{:S(2)}) copy-start(u32[256]{0:T(256)} %constant.46) | copy-start | bytes 3076
  28.8 186.9 %copy-start.2 = (bf16[2,16,1,256]{3,1,2,0:T(8,128)(2,1)S(1)}, bf16[2,16,1,256]{3,1,2,0:T(8,128)(2,1)}, u32[]{:S(2)}) copy-start(bf16[2,16,1,256]{3,1,2,0:T(8,128)(2,1)} %param.14) | copy-start | bytes 49156
  28.8 187.0 %copy-start.5 = (s32[10]{0:T(128)S(1)}, s32[10]{0:T(128)}, u32[]{:S(2)}) copy-start(s32[10]{0:T(128)} %param.17) | copy-start | bytes 124
  29.9 200.2 %all-to-all-start.1 = ((bf16[32,1,256,256]{3,2,1,0:T(8,128)(2,1)}), bf16[32,1,256,256]{3,2,1,0:T(8,128)(2,1)}, u32[]{:S(2)}, u32[]{:S(2)}) async-start(bf16[32,1,256,256]{3,2,1,0:T(8,128)(2,1)} %fusion.1), calls=%async_computation.1 | async-start | bytes 8388608 | tf_op jit(solution)/shard_map/all_to_all | solution.py:76
  37.4 365.1 %reduce-scatter.4.cloned.1.call-start = ((), (), s32[]{:S(2)}) async-start(), calls=%async_computation.4 | async-start | bytes 1474560
Sparse Core Ops, SparseCore 0:
  9.2 163.1 all-gather.1
  325.1 77.3 reduce-scatter.3
where the time goes:
time: 413 us; the launch traced here: 411 us
  blocking collectives  189 us (46%)
  local copies, waits for them, and re-layouts  86.9 us (21%)
  waiting for transfers between devices  78.6 us (19%)
  starting transfers between devices  17.4 us (4%)
  other arithmetic  16.5 us (4%)
  between operations  14.2 us (3%)
  matrix products  8.6 us (2%)
    unnamed x2, blocking collectives  189 us
    unnamed x3, waiting for transfers between devices  77.6 us
    scatter x1, local copies, waits for them, and re-layouts, shards(): placed = initial.at[block_ids - base].set(dequant)  47.4 us
    dot_general x1, local copies, waits for them, and re-layouts, shards(): jnp.einsum('nha,hcab->ncb', rows, matrix, preferred_element_type=jnp.floa...  13.7 us
    convert_element_type x1, other arithmetic, shards(): (block_codes.astype(jnp.float32) * block_scales[:, None, None]).astype(jn...  10.8 us
    all_to_all x1, starting transfers between devices, shards(): lax.all_to_all(meta, 'rep', split_axis=0, concat_axis=0, tiled=True)  9.78 us
  transfers between devices with their start and end apart: 4, of which 2 were waited for; matrix products, arithmetic and copies ran while one was open for 5% of the time, Pallas kernels for 0%

commit v1 on v0

v1 whole, which is shorter than its diff:
```python
import math

import jax
import jax.numpy as jnp
from jax import lax
from jax.experimental import pallas as pl
from jax.experimental.pallas import tpu as pltpu
from jax.sharding import Mesh, PartitionSpec as P

BF16, F32, I32 = jnp.bfloat16, jnp.float32, jnp.int32

XL, Z, CORE, TP = 2, 8, 2, 8
REP = XL * Z * CORE

HD = 128
SLOTS = 16
STEPS = 2
HEADS = 8
CTX = 256
MOVE = 13
STAY = SLOTS - MOVE
COLS = 40
OUT_COLS = COLS // TP
OWN = 10
ROWS = SLOTS * STEPS
PACK = STEPS * HEADS + 2 * STEPS

ROUND, HEAD, COL, SCALE, DEP, DEST = 0, 1, 11, 21, 32, 48

VMEM_LIMIT = 40 * 1024 * 1024


def smem():
    return pl.BlockSpec(memory_space=pltpu.SMEM)


def vmem():
    return pl.BlockSpec(memory_space=pltpu.VMEM)


def call(body, out_shape, in_specs, scratch=(), **kw):
    single = not isinstance(out_shape, (list, tuple))
    return pl.pallas_call(
        body,
        out_shape=out_shape,
        in_specs=in_specs,
        out_specs=vmem() if single else [vmem()] * len(out_shape),
        scratch_shapes=list(scratch),
        compiler_params=pltpu.CompilerParams(vmem_limit_bytes=VMEM_LIMIT),
        **kw,
    )


def notice_body(place, dep, dest, ids, scales, queries, fresh, notice, packs):
    row = lax.broadcasted_iota(I32, (REP, HD), 0)
    lane = lax.broadcasted_iota(I32, (REP, HD), 1)
    base = place[0]
    out = jnp.full((REP, HD), -1.0, F32)
    for k in range(MOVE):
        out = jnp.where((lane == ROUND) & (row == dest[0, k]), float(k), out)
        out = jnp.where(lane == DEP + k, dep[0, k].astype(F32), out)
        out = jnp.where(lane == DEST + k, dest[0, k].astype(F32), out)
    for n in range(OWN):
        place_n = ids[n] - base
        head = lax.div(place_n, COLS)
        out = jnp.where(lane == HEAD + n, head.astype(F32), out)
        out = jnp.where(lane == COL + n, (place_n - head * COLS).astype(F32), out)
        out = jnp.where(lane == SCALE + n, scales[n], out)
    notice[:, 0, :] = out
    for s in range(SLOTS):
        packs[s] = jnp.concatenate(
            [queries[t, s] for t in range(STEPS)]
            + [fresh[t, s, :, j * HD : (j + 1) * HD] for t in range(STEPS) for j in range(2)],
            axis=0,
        )


def pull_body(notices, dep, packs, out):
    def one(peer, carry):
        turn = notices[peer, 0, ROUND].astype(I32)
        slot = dep[0, jnp.maximum(turn, 0)]
        out[peer] = packs[slot]
        return carry

    lax.fori_loop(0, REP, one, 0, unroll=4)


def attend_body(lengths, dep, dest, pulled, packs, cache, out, work, scores, held):
    scale = 1.0 / math.sqrt(HD)
    per = STEPS * HEADS
    for s in range(SLOTS):
        held[s] = packs[s]

    def fetch(k, c):
        held[dep[0, k]] = pulled[dest[0, k]]
        return c

    lax.fori_loop(0, MOVE, fetch, 0, unroll=True)
    for s in range(SLOTS):
        q = held[s][:per]
        sc = lax.dot_general(
            q, cache[s, 0, :, :HD], (((1,), (1,)), ((), ())), preferred_element_type=F32
        )
        pos = lax.broadcasted_iota(I32, (per, CTX), 1)
        scores[s] = jnp.where(pos < lengths[s], sc * scale, -jnp.inf)
    step = lax.broadcasted_iota(I32, (per, 1), 0) // HEADS
    for s in range(SLOTS):
        sc = scores[s]
        top = jnp.max(sc, axis=1, keepdims=True)
        expo = jnp.exp(sc - top)
        total = jnp.sum(expo, axis=1, keepdims=True)
        carried = jnp.dot(expo.astype(BF16), cache[s, 0, :, HD:], preferred_element_type=F32)
        pack = held[s].astype(F32)
        q = pack[:per]
        peak = top
        extra = []
        for u in range(STEPS):
            f = jnp.sum(q * pack[per + 2 * u : per + 2 * u + 1], axis=1, keepdims=True) * scale
            f = jnp.where(step >= u, f, -jnp.inf)
            extra.append(f)
            peak = jnp.maximum(peak, f)
        factor = jnp.exp(top - peak)
        denom = total * factor
        numer = carried * factor
        for u in range(STEPS):
            w = jnp.exp(extra[u] - peak)
            denom = denom + w
            numer = numer + w * pack[per + 2 * u + 1 : per + 2 * u + 2]
        work[pl.ds(s * per, per), :] = numer / denom
    for h in range(HEADS):
        for t in range(STEPS):
            out[h, t * SLOTS : (t + 1) * SLOTS, :] = work[
                pl.ds(t * HEADS + h, SLOTS, stride=per), :
            ].astype(BF16)


def project_body(place, notices, mine, other, *rest):
    arrays, out, rows, total = rest[:-3], rest[-3], rest[-2], rest[-1]
    xl, z, core = place[1], place[2], place[3]
    rows[:, :ROWS, :] = mine[...]
    rows[:, ROWS:, :] = other[...]
    total[...] = jnp.zeros_like(total)
    away = 1 - 2 * core

    def run(blocks, first, z_src, core_src):
        src = (xl * Z + z_src) * CORE + core_src
        for lo in range(0, OWN, 5):
            products = []
            for n in range(lo, lo + 5):
                h = notices[src, 0, HEAD + n].astype(I32)
                products.append(
                    jnp.dot(rows[h], blocks[first + n], preferred_element_type=F32)
                    * notices[src, 0, SCALE + n]
                )
            for n in range(lo, lo + 5):
                c = notices[src, 0, COL + n].astype(I32)
                total[c] += products[n - lo]

    run(arrays[0], 0, z, core)
    run(arrays[1], 0, z, 1 - core)
    for step in range(1, Z // 2):
        from_z = lax.rem(z - away * step + Z, Z)
        sib_z = lax.rem(z + away * step + Z, Z)
        a, b = arrays[2 * step], arrays[2 * step + 1]
        run(a, 0, from_z, core)
        run(a, OWN, from_z, 1 - core)
        run(b, 0, sib_z, 1 - core)
        run(b, OWN, sib_z, core)
    far = lax.rem(z + Z // 2, Z)
    run(arrays[Z], 0, far, core)
    run(arrays[Z + 1], 0, far, 1 - core)
    out[...] = total[...].astype(BF16)


def sum_body(place, notices, parts, send, stay, keep, total):
    rep, pair = place[4], place[5]
    for c in range(OUT_COLS):
        acc = parts[0, c].astype(F32)
        for t in range(1, TP):
            acc = acc + parts[t, c].astype(F32)
        total[:, c * HD : (c + 1) * HD] = acc.astype(BF16)
    row = lax.broadcasted_iota(I32, (REP * 8, 1), 0)
    goal, part = lax.div(row, 8), lax.rem(row, 8)
    side, step = lax.div(part, STEPS), lax.rem(part, STEPS)
    want = jnp.full((REP * 8, 1), -1, I32)
    for s, owner in ((0, rep), (1, pair)):
        for k in range(MOVE):
            slot = notices[owner, 0, DEP + k].astype(I32)
            dest = notices[owner, 0, DEST + k].astype(I32)
            want = jnp.where((goal == dest) & (side == s), slot, want)
    want = jnp.where(want >= 0, side * ROWS + step * SLOTS + want, -1)
    col = lax.broadcasted_iota(I32, (REP * 8, XL * ROWS), 1)
    pick = jnp.where(col == want, 1.0, 0.0).astype(BF16)
    packed = jnp.dot(pick, total[...], preferred_element_type=F32)
    send[...] = packed.reshape(REP, 8, OUT_COLS * HD)[:, : 2 * STEPS, :].astype(BF16)
    keep[...] = total[:ROWS, :]
    stay[...] = total[ROWS:, :]


def finish_body(place, notices, dep, moved, keep, stay, out, arrived):
    arrived[:, : 2 * STEPS, :] = moved[...].astype(F32)
    arrived[:, 2 * STEPS :, :] = jnp.zeros_like(arrived[:, 2 * STEPS :, :])
    rows = arrived[...].reshape(REP * 8, OUT_COLS * HD).astype(BF16)
    lane = lax.broadcasted_iota(I32, (1, REP * 8), 1)
    peer, part = lax.div(lane, 8), lax.rem(lane, 8)
    side, step = lax.div(part, STEPS), lax.rem(part, STEPS)
    peer = lax.rem(peer + side * (REP // XL), REP)
    slot = jnp.full((1, REP * 8), -1, I32)
    for p in range(REP):
        turn = notices[p, 0, ROUND].astype(I32)
        mine = jnp.where(turn >= 0, dep[0, jnp.maximum(turn, 0)], -1)
        slot = jnp.where(peer == p, mine, slot)
    slot = jnp.where((slot >= 0) & (part < 2 * STEPS), slot + step * SLOTS, -1)
    row = lax.broadcasted_iota(I32, (ROWS, REP * 8), 0)
    pick = jnp.where(row == slot, 1.0, 0.0).astype(BF16)
    came = jnp.dot(pick, rows, preferred_element_type=F32)
    here = lax.rem(lax.broadcasted_iota(I32, (ROWS, 1), 0), SLOTS)
    left = jnp.zeros((ROWS, 1), jnp.bool_)
    for k in range(MOVE):
        left = left | (here == dep[0, k])
    both = keep[...].astype(F32) + stay[...].astype(F32)
    result = jnp.where(left, came, both).astype(BF16)
    for t in range(STEPS):
        out[t] = result[t * SLOTS : (t + 1) * SLOTS]


def shards(kv_cache, lengths, departing, destination, queries, new_kv, codes, scales, block_slot):
    rep_axes, tp_axes = ("xl", "z", "core"), ("y", "xh")
    xl, z, core = (lax.axis_index(a) for a in rep_axes)
    rep = lax.axis_index(rep_axes)
    base = lax.axis_index(tp_axes) * (HEADS * COLS)
    place = jnp.stack([base, xl, z, core, rep, (rep + REP // XL) % REP]).astype(I32)

    def exchange(x, axes):
        return lax.all_to_all(x, axes, split_axis=0, concat_axis=0, tiled=True)

    def swap(x, axis):
        return lax.ppermute(x, axis, [(0, 1), (1, 0)])

    ring = [
        (i * CORE + c, ((i + (1 - 2 * c)) % Z) * CORE + c) for i in range(Z) for c in range(CORE)
    ]

    sib = swap(codes, "core")
    notice, packs = call(
        notice_body,
        [
            jax.ShapeDtypeStruct((REP, 1, HD), F32),
            jax.ShapeDtypeStruct((SLOTS, PACK, HD), BF16),
        ],
        [smem()] * 5 + [vmem()] * 2,
    )(place, departing, destination, block_slot, scales, queries, new_kv)
    pair = jnp.concatenate([codes, sib], axis=0)

    one = lax.ppermute(pair, ("z", "core"), ring)
    notices = exchange(notice, rep_axes)

    one, notices = lax.optimization_barrier((one, notices))
    two = lax.ppermute(one, ("z", "core"), ring)
    one_sib = swap(one, "core")
    to_pull = call(
        pull_body,
        jax.ShapeDtypeStruct((REP, PACK, HD), BF16),
        [smem(), smem(), vmem()],
    )(notices, departing, packs)
    pulled = exchange(to_pull, rep_axes)

    two, pulled = lax.optimization_barrier((two, pulled))
    three = lax.ppermute(two, ("z", "core"), ring)
    two_sib = swap(two, "core")
    mine = call(
        attend_body,
        jax.ShapeDtypeStruct((HEADS, ROWS, HD), BF16),
        [smem()] * 3 + [vmem()] * 3,
        [
            pltpu.VMEM((SLOTS * STEPS * HEADS, HD), F32),
            pltpu.VMEM((SLOTS, STEPS * HEADS, CTX), F32),
            pltpu.VMEM((SLOTS, PACK, HD), BF16),
        ],
    )(lengths, departing, destination, pulled, packs, kv_cache)
    three, mine = lax.optimization_barrier((three, mine))
    four = lax.ppermute(three[:OWN], ("z", "core"), ring)
    three_sib = swap(three, "core")
    other = swap(mine, "xl")
    four_sib = swap(four, "core")
    arrays = [codes, sib, one, one_sib, two, two_sib, three, three_sib, four, four_sib]
    parts = call(
        project_body,
        jax.ShapeDtypeStruct((COLS, XL * ROWS, HD), BF16),
        [smem()] * 2 + [vmem()] * (2 + len(arrays)),
        [
            pltpu.VMEM((HEADS, XL * ROWS, HD), BF16),
            pltpu.VMEM((COLS, XL * ROWS, HD), F32),
        ],
    )(place, notices, mine, other, *arrays)
    parts = exchange(parts, tp_axes).reshape(TP, OUT_COLS, XL * ROWS, HD)
    send, stay, keep = call(
        sum_body,
        [
            jax.ShapeDtypeStruct((REP, 2 * STEPS, OUT_COLS * HD), BF16),
            jax.ShapeDtypeStruct((ROWS, OUT_COLS * HD), BF16),
            jax.ShapeDtypeStruct((ROWS, OUT_COLS * HD), BF16),
        ],
        [smem()] * 2 + [vmem()],
        [pltpu.VMEM((XL * ROWS, OUT_COLS * HD), BF16)],
    )(place, notices, parts)
    stay = swap(stay, "xl")
    moved = exchange(send, rep_axes)
    return call(
        finish_body,
        jax.ShapeDtypeStruct((STEPS, SLOTS, OUT_COLS * HD), BF16),
        [smem()] * 3 + [vmem()] * 3,
        [pltpu.VMEM((REP, 8, OUT_COLS * HD), F32)],
    )(place, notices, departing, moved, keep, stay)


def solution(mesh):
    rep, tp = ("xl", "z", "core"), ("y", "xh")
    parts = Mesh(mesh.devices.reshape(XL, Z, CORE, 4, 2), rep + tp)
    placed = (
        P(rep, tp, None, None),
        P(rep),
        P(rep, None),
        P(rep, None),
        P(None, rep, tp, None),
        P(None, rep, tp, None),
        P(tp + rep, None, None),
        P(tp + rep),
        P(tp + rep),
    )
    return jax.shard_map(
        shards, mesh=parts, in_specs=placed, out_specs=P(None, rep, tp), check_vma=False
    )
```

time: 413 us -> 111 us (0.27)
  blocking collectives: 189 us -> 51.1 us
  local copies, waits for them, and re-layouts: 86.9 us -> 4.98 us
  waiting for transfers between devices: 78.6 us -> 31.7 us
  other arithmetic: 16.5 us -> 1.9 us
  between operations: 14.2 us -> 0.11 us
  Pallas kernels: 0 us -> 9.17 us
  matrix products: 8.6 us -> 0 us
  starting transfers between devices: 17.4 us -> 10.5 us
    unnamed x2 -> x0, blocking collectives: 189 us -> none
    unnamed x3 -> x0, waiting for transfers between devices: 77.6 us -> none
    scatter x3 -> x0, local copies, waits for them, and re-layouts: 54.4 us -> none  [the longest x1 47.4 us: shards(): placed = initial.at[block_ids - base].set(dequant)]
    all_to_all x0 -> x3, blocking collectives: none -> 51.1 us  [exchange(): return lax.all_to_all(x, axes, split_axis=0, concat_axis=0, tiled=True)]
    ppermute x0 -> x11, waiting for transfers between devices: none -> 24.7 us  [the longest x1 8.57 us: shards(): three = lax.ppermute(two, ('z', 'core'), ring)]
    dot_general x1 -> x0, local copies, waits for them, and re-layouts: 13.7 us -> none  [shards(): jnp.einsum('nha,hcab->ncb', rows, matrix, preferred_element_type=jnp.floa...]
    all_to_all x2 -> x1, starting transfers between devices: 17.4 us -> 3.86 us  [exchange(): return lax.all_to_all(x, axes, split_axis=0, concat_axis=0, tiled=True)]
    convert_element_type x3 -> x0, other arithmetic: 10.8 us -> none  [the longest x1 10.8 us: shards(): (block_codes.astype(jnp.float32) * block_scales[:, None, None]).astype(jn...]
  transfers between devices with their start and end apart: 4 -> 12, of which waited for: 2 -> 6; matrix products, arithmetic and copies ran while one was open for 5% -> 1% of each run, Pallas kernels for 0% -> 3%
where the time goes in v1:
time: 111 us; the launch traced here: 109 us
  blocking collectives  51.1 us (46%)
  waiting for transfers between devices  31.7 us (29%)
  starting transfers between devices  10.5 us (9%)
  Pallas kernels  9.17 us (8%)
  local copies, waits for them, and re-layouts  4.98 us (4%)
  other arithmetic  1.9 us (2%)
    all_to_all x3, blocking collectives, exchange(): return lax.all_to_all(x, axes, split_axis=0, concat_axis=0, tiled=True)  51.1 us
    ppermute x1, waiting for transfers between devices, shards(): three = lax.ppermute(two, ('z', 'core'), ring)  8.57 us
    ppermute x1, waiting for transfers between devices, shards(): four = lax.ppermute(three[:OWN], ('z', 'core'), ring)  8.17 us
    ppermute x7, waiting for transfers between devices, swap(): return lax.ppermute(x, axis, [(0, 1), (1, 0)])  7.94 us
    all_to_all x1, waiting for transfers between devices, exchange(): return lax.all_to_all(x, axes, split_axis=0, concat_axis=0, tiled=True)  6.99 us
    unnamed x19, local copies, waits for them, and re-layouts  4.87 us
    all_to_all x1, starting transfers between devices, exchange(): return lax.all_to_all(x, axes, split_axis=0, concat_axis=0, tiled=True)  3.86 us
    ppermute x7, starting transfers between devices, swap(): return lax.ppermute(x, axis, [(0, 1), (1, 0)])  3.16 us
  transfers between devices with their start and end apart: 12, of which 6 were waited for; matrix products, arithmetic and copies ran while one was open for 1% of the time, Pallas kernels for 3%

profile of v1, /device:TPU:8, one launch (start us, length us, event | category | flops | bytes accessed | tf_op | source)
XLA Modules:
  0.0 109.4 jit_solution(4252252772283928203)
XLA Ops:
  0.0 1.8 %collective-permute-done.rest_1_ = bf16[10,128,128]{2,1,0:T(8,128)(2,1)S(1)} collective-permute-done((bf16[10,128,128]{2,1,0:T(8,128)(2,1)}, bf16[10,128,128]{2,1,0:T(8,128)(2,1)S(1)}, u32[]{:S(2)}, u32[]{:S(2)}) %collective-permute-start) | collective-permute-done | bytes 327712 | tf_op jit(solution)/shard_map/ppermute | solution.py:238
  1.8 1.9 %pad_maximum_fusion = bf16[20,128,128]{2,1,0:T(8,128)(2,1)} fusion(bf16[10,128,128]{2,1,0:T(8,128)(2,1)S(1)} %collective-permute-done.rest_1_, bf16[10,128,128]{2,1,0:T(8,128)(2,1)} %rest_0_.1), kind=kLoop, calls=%fused_computation | loop fusion | flops 327680 | bytes 1310720 | tf_op jit(solution)/shard_map/concatenate | solution.py:253
  3.7 1.9 %collective-permute-start.1 = (bf16[20,128,128]{2,1,0:T(8,128)(2,1)}, bf16[20,128,128]{2,1,0:T(8,128)(2,1)S(1)}, u32[]{:S(2)}, u32[]{:S(2)}) collective-permute-start(bf16[20,128,128]{2,1,0:T(8,128)(2,1)} %pad_maximum_fusion), channel_id=1, source_target_pairs={{0,16},{8,120},{16,32},{24,8},{32,48},{40,24},{48,64},{56,40},{64,... | collective-permute-start | bytes 1966088 | tf_op jit(solution)/shard_map/ppermute | solution.py:255
  5.7 0.7 copy.10.fresh
  6.4 0.1 stack.27.place
  6.5 0.8 copy-done.2
  7.4 0.7 copy-done.3
  8.0 0.7 copy-done.5
  8.7 0.7 copy-done.6
  9.3 0.7 copy-done.7
  10.0 0.7 shard_map.91
  10.7 17.1 %all_to_all.20.notices = f32[32,1,128]{2,1,0:T(1,128)S(1)} all-to-all(f32[32,1,128]{2,1,0:T(1,128)S(1)} %get-tuple-element.16), channel_id=1, replica_groups=mesh['xl'=2,'z'=8,'core'=2,'y'=4,'xh'=2] {'xl','z','core'}, dimensions={0} | all-to-all | bytes 32768 | tf_op jit(solution)/shard_map/all_to_all | solution.py:235
  27.8 0.6 collective-permute-start.2
  28.4 1.0 shard_map.92
  29.3 15.8 %all_to_all.21.pulled = bf16[32,20,128]{2,1,0:T(8,128)(2,1)S(1)} all-to-all(bf16[32,20,128]{2,1,0:T(8,128)(2,1)S(1)} %shard_map.92), channel_id=1, replica_groups=mesh['xl'=2,'z'=8,'core'=2,'y'=4,'xh'=2] {'xl','z','core'}, dimensions={0} | all-to-all | bytes 327680 | tf_op jit(solution)/shard_map/all_to_all | solution.py:235
  45.1 0.9 collective-permute-start.3
  46.0 0.5 collective-permute-start.6
  46.5 0.7 copy-done.8
  47.1 1.2 %shard_map.93.mine = bf16[8,32,128]{2,1,0:T(8,128)(2,1)S(1)} custom-call(s32[16]{0:T(128)S(1)} %copy-done.8, s32[1,13]{1,0:T(1,128)S(1)} %copy-done.3, s32[1,13]{1,0:T(1,128)S(1)} %copy-done.5, bf16[32,20,128]{2,1,0:T(8,128)(2,1)S(1)} %all_to_all.21.pulled, bf16[16,20,128]{2,1,0:T(8,128)(2,1)S(1)} %get-tuple-element.19.packs, ...), custom_call_target="tpu_custom_call" | custom-call | tf_op jit(solution)/shard_map/pallas_call | solution.py:271
  48.3 8.6 %collective-permute-done.3.rest_6_ = bf16[20,128,128]{2,1,0:T(8,128)(2,1)S(1)} collective-permute-done((bf16[20,128,128]{2,1,0:T(8,128)(2,1)S(1)}, bf16[20,128,128]{2,1,0:T(8,128)(2,1)S(1)}, u32[]{:S(2)}, u32[]{:S(2)}) %collective-permute-start.3) | collective-permute-done | bytes 655392 | tf_op jit(solution)/shard_map/ppermute | solution.py:269
  57.0 0.1 collective-permute-start.7
  57.1 8.2 %collective-permute-done.8.rest_8_ = bf16[10,128,128]{2,1,0:T(8,128)(2,1)S(1)} collective-permute-done((bf16[10,128,128]{2,1,0:T(8,128)(2,1)S(1)}, bf16[10,128,128]{2,1,0:T(8,128)(2,1)S(1)}, u32[]{:S(2)}, u32[]{:S(2)}) %collective-permute-start.8) | collective-permute-done | bytes 327712 | tf_op jit(solution)/shard_map/ppermute | solution.py:282
  65.3 0.7 collective-permute-start.4
  66.0 3.8 %collective-permute-done.4.other = bf16[8,32,128]{2,1,0:T(8,128)(2,1)S(1)} collective-permute-done((bf16[8,32,128]{2,1,0:T(8,128)(2,1)S(1)}, bf16[8,32,128]{2,1,0:T(8,128)(2,1)S(1)}, u32[]{:S(2)}, u32[]{:S(2)}) %collective-permute-start.4) | collective-permute-done | bytes 65568 | tf_op jit(solution)/shard_map/ppermute | solution.py:238
  69.8 2.5 %shard_map.94 = bf16[40,64,128]{2,1,0:T(8,128)(2,1)S(1)} custom-call(s32[6]{0:T(128)S(1)} %stack.27.place, f32[32,1,128]{2,1,0:T(1,128)S(1)} %all_to_all.20.notices, bf16[8,32,128]{2,1,0:T(8,128)(2,1)S(1)} %shard_map.93.mine, bf16[8,32,128]{2,1,0:T(8,128)(2,1)S(1)} %collective-permute-done.4.other, bf16[10,128,128]{2,1,0:T(8,128)(2,1)S(1)} %copy-done.1, ...), custom_call_target="tpu_custom_call" | custom-call | tf_op jit(solution)/shard_map/pallas_call | solution.py:287
  72.3 18.2 %all_to_all.22 = bf16[40,64,128]{2,1,0:T(8,128)(2,1)S(1)} all-to-all(bf16[40,64,128]{2,1,0:T(8,128)(2,1)S(1)} %shard_map.94), channel_id=1, replica_groups=mesh['xl'=2,'z'=8,'core'=2,'y'=4,'xh'=2] {'y','xh'}, dimensions={0} | all-to-all | bytes 1310720 | tf_op jit(solution)/shard_map/all_to_all | solution.py:235
  90.5 2.1 %shard_map.95 = (bf16[32,4,640]{2,1,0:T(4,128)(2,1)}, bf16[32,640]{1,0:T(8,128)(2,1)S(1)}, bf16[32,640]{1,0:T(8,128)(2,1)S(1)}) custom-call(s32[6]{0:T(128)S(1)} %stack.27.place, f32[32,1,128]{2,1,0:T(1,128)S(1)} %all_to_all.20.notices, bf16[8,5,64,128]{3,2,1,0:T(8,128)(2,1)S(1)} %bitcast.7), custom_call_target="tpu_custom_call" | custom-call | tf_op jit(solution)/shard_map/pallas_call | solution.py:297
  92.7 3.9 %all-to-all-start.3 = ((bf16[32,4,640]{2,1,0:T(4,128)(2,1)}), bf16[32,4,640]{2,1,0:T(4,128)(2,1)S(1)}, u32[]{:S(2)}, u32[]{:S(2)}) async-start(bf16[32,4,640]{2,1,0:T(4,128)(2,1)} %get-tuple-element.24), calls=%async_computation.3 | async-start | bytes 327680 | tf_op jit(solution)/shard_map/all_to_all | solution.py:235
  96.5 1.9 %collective-permute-start.10 = (bf16[32,640]{1,0:T(8,128)(2,1)S(1)}, bf16[32,640]{1,0:T(8,128)(2,1)S(1)}, u32[]{:S(2)}, u32[]{:S(2)}) collective-permute-start(bf16[32,640]{1,0:T(8,128)(2,1)S(1)} %get-tuple-element.26), channel_id=1, source_target_pairs={{0,128},{128,0},{1,129},{129,1},{2,130},{130,2},{3,131},{131,3},{4... | collective-permute-start | bytes 122888 | tf_op jit(solution)/shard_map/ppermute | solution.py:238
  98.4 2.3 %collective-permute-done.10.stay = bf16[32,640]{1,0:T(8,128)(2,1)S(1)} collective-permute-done((bf16[32,640]{1,0:T(8,128)(2,1)S(1)}, bf16[32,640]{1,0:T(8,128)(2,1)S(1)}, u32[]{:S(2)}, u32[]{:S(2)}) %collective-permute-start.10) | collective-permute-done | bytes 40992 | tf_op jit(solution)/shard_map/ppermute | solution.py:238
  100.7 7.0 %all-to-all-done.3.moved = bf16[32,4,640]{2,1,0:T(4,128)(2,1)S(1)} async-done(((bf16[32,4,640]{2,1,0:T(4,128)(2,1)}), bf16[32,4,640]{2,1,0:T(4,128)(2,1)S(1)}, u32[]{:S(2)}, u32[]{:S(2)}) %all-to-all-start.3) | async-done | bytes 163872 | tf_op jit(solution)/shard_map/all_to_all | solution.py:235
  107.7 1.7 %shard_map.96 = bf16[2,16,640]{2,1,0:T(8,128)(2,1)} custom-call(s32[6]{0:T(128)S(1)} %stack.27.place, f32[32,1,128]{2,1,0:T(1,128)S(1)} %all_to_all.20.notices, s32[1,13]{1,0:T(1,128)S(1)} %copy-done.4, bf16[32,4,640]{2,1,0:T(4,128)(2,1)S(1)} %all-to-all-done.3.moved, bf16[32,640]{1,0:T(8,128)(2,1)S(1)} %get-tuple-element.25.keep, ...), custom_call_target="tpu_custom_call" | custom-call | tf_op jit(solution)/shard_map/pallas_call | solution.py:309
  (23 shorter events, 0.2 us)
Async XLA Ops:
  0.0 46.5 %copy-start = (bf16[16,1,256,256]{3,2,1,0:T(8,128)(2,1)S(1)}, bf16[16,1,256,256]{3,2,1,0:T(8,128)(2,1)}, u32[]{:S(2)}) copy-start(bf16[16,1,256,256]{3,2,1,0:T(8,128)(2,1)} %cache.1) | copy-start | bytes 6291460
  0.0 1.8 %collective-permute-start = (bf16[10,128,128]{2,1,0:T(8,128)(2,1)}, bf16[10,128,128]{2,1,0:T(8,128)(2,1)S(1)}, u32[]{:S(2)}, u32[]{:S(2)}) collective-permute-start(bf16[10,128,128]{2,1,0:T(8,128)(2,1)} %rest_0_.1), channel_id=1, source_target_pairs={{0,8},{8,0},{1,9},{9,1},{2,10},{10,2},{3,11},{11,3},{4,12},{12,4},... | collective-permute-start | bytes 983048 | tf_op jit(solution)/shard_map/ppermute | solution.py:238
  3.7 66.1 %copy-start.1 = (bf16[10,128,128]{2,1,0:T(8,128)(2,1)S(1)}, bf16[10,128,128]{2,1,0:T(8,128)(2,1)}, u32[]{:S(2)}) copy-start(bf16[10,128,128]{2,1,0:T(8,128)(2,1)} %rest_0_.1) | copy-start | bytes 983044
  3.7 24.0 %collective-permute-start.1 = (bf16[20,128,128]{2,1,0:T(8,128)(2,1)}, bf16[20,128,128]{2,1,0:T(8,128)(2,1)S(1)}, u32[]{:S(2)}, u32[]{:S(2)}) collective-permute-start(bf16[20,128,128]{2,1,0:T(8,128)(2,1)} %pad_maximum_fusion), channel_id=1, source_target_pairs={{0,16},{8,120},{16,32},{24,8},{32,48},{40,24},{48,64},{56,40},{64,... | collective-permute-start | bytes 1966088 | tf_op jit(solution)/shard_map/ppermute | solution.py:255
  6.5 0.8 copy-start.2
  7.4 0.7 copy-start.3
  8.0 0.7 copy-start.5
  8.7 0.7 copy-start.6
  9.3 0.7 copy-start.7
  27.8 17.3 %collective-permute-start.2 = (bf16[20,128,128]{2,1,0:T(8,128)(2,1)S(1)}, bf16[20,128,128]{2,1,0:T(8,128)(2,1)S(1)}, u32[]{:S(2)}, u32[]{:S(2)}) collective-permute-start(bf16[20,128,128]{2,1,0:T(8,128)(2,1)S(1)} %collective-permute-done.1.rest_2_), channel_id=1, source_target_pairs={{0,16},{8,120},{16,32},{24,8},{32,48},{40,24},{48,64},{56,40},{64,... | collective-permute-start | bytes 1966088 | tf_op jit(solution)/shard_map/ppermute | solution.py:259
  45.1 11.8 %collective-permute-start.3 = (bf16[20,128,128]{2,1,0:T(8,128)(2,1)S(1)}, bf16[20,128,128]{2,1,0:T(8,128)(2,1)S(1)}, u32[]{:S(2)}, u32[]{:S(2)}) collective-permute-start(bf16[20,128,128]{2,1,0:T(8,128)(2,1)S(1)} %collective-permute-done.2.rest_4_), channel_id=1, source_target_pairs={{0,16},{8,120},{16,32},{24,8},{32,48},{40,24},{48,64},{56,40},{64,... | collective-permute-start | bytes 1966088 | tf_op jit(solution)/shard_map/ppermute | solution.py:269
  46.0 20.0 %collective-permute-start.5 = (bf16[20,128,128]{2,1,0:T(8,128)(2,1)S(1)}, bf16[20,128,128]{2,1,0:T(8,128)(2,1)S(1)}, u32[]{:S(2)}, u32[]{:S(2)}) collective-permute-start(bf16[20,128,128]{2,1,0:T(8,128)(2,1)S(1)} %collective-permute-done.1.rest_2_), channel_id=1, source_target_pairs={{0,8},{8,0},{1,9},{9,1},{2,10},{10,2},{3,11},{11,3},{4,12},{12,4},... | collective-permute-start | bytes 1966088 | tf_op jit(solution)/shard_map/ppermute | solution.py:238
  46.0 20.0 %collective-permute-start.6 = (bf16[20,128,128]{2,1,0:T(8,128)(2,1)S(1)}, bf16[20,128,128]{2,1,0:T(8,128)(2,1)S(1)}, u32[]{:S(2)}, u32[]{:S(2)}) collective-permute-start(bf16[20,128,128]{2,1,0:T(8,128)(2,1)S(1)} %collective-permute-done.2.rest_4_), channel_id=1, source_target_pairs={{0,8},{8,0},{1,9},{9,1},{2,10},{10,2},{3,11},{11,3},{4,12},{12,4},... | collective-permute-start | bytes 1966088 | tf_op jit(solution)/shard_map/ppermute | solution.py:238
  46.5 0.7 copy-start.8
  56.9 8.4 %collective-permute-start.8 = (bf16[10,128,128]{2,1,0:T(8,128)(2,1)S(1)}, bf16[10,128,128]{2,1,0:T(8,128)(2,1)S(1)}, u32[]{:S(2)}, u32[]{:S(2)}) collective-permute-start(bf16[10,128,128]{2,1,0:T(8,128)(2,1)S(1)} %slice.3), channel_id=1, source_target_pairs={{0,16},{8,120},{16,32},{24,8},{32,48},{40,24},{48,64},{56,40},{64,... | collective-permute-start | bytes 983048 | tf_op jit(solution)/shard_map/ppermute | solution.py:282
  57.0 12.8 %collective-permute-start.7 = (bf16[20,128,128]{2,1,0:T(8,128)(2,1)S(1)}, bf16[20,128,128]{2,1,0:T(8,128)(2,1)S(1)}, u32[]{:S(2)}, u32[]{:S(2)}) collective-permute-start(bf16[20,128,128]{2,1,0:T(8,128)(2,1)S(1)} %collective-permute-done.3.rest_6_), channel_id=1, source_target_pairs={{0,8},{8,0},{1,9},{9,1},{2,10},{10,2},{3,11},{11,3},{4,12},{12,4},... | collective-permute-start | bytes 1966088 | tf_op jit(solution)/shard_map/ppermute | solution.py:238
  65.3 4.5 %collective-permute-start.9 = (bf16[10,128,128]{2,1,0:T(8,128)(2,1)S(1)}, bf16[10,128,128]{2,1,0:T(8,128)(2,1)S(1)}, u32[]{:S(2)}, u32[]{:S(2)}) collective-permute-start(bf16[10,128,128]{2,1,0:T(8,128)(2,1)S(1)} %collective-permute-done.8.rest_8_), channel_id=1, source_target_pairs={{0,8},{8,0},{1,9},{9,1},{2,10},{10,2},{3,11},{11,3},{4,12},{12,4},... | collective-permute-start | bytes 983048 | tf_op jit(solution)/shard_map/ppermute | solution.py:238
  65.3 4.5 %collective-permute-start.4 = (bf16[8,32,128]{2,1,0:T(8,128)(2,1)S(1)}, bf16[8,32,128]{2,1,0:T(8,128)(2,1)S(1)}, u32[]{:S(2)}, u32[]{:S(2)}) collective-permute-start(bf16[8,32,128]{2,1,0:T(8,128)(2,1)S(1)} %shard_map.93.mine), channel_id=1, source_target_pairs={{0,128},{128,0},{1,129},{129,1},{2,130},{130,2},{3,131},{131,3},{4... | collective-permute-start | bytes 196616 | tf_op jit(solution)/shard_map/ppermute | solution.py:238
  72.3 35.4 %copy-start.4 = (s32[1,13]{1,0:T(1,128)S(1)}, s32[1,13]{1,0:T(1,128)}, u32[]{:S(2)}) copy-start(s32[1,13]{1,0:T(1,128)} %dep.7) | copy-start | bytes 160
  92.7 15.0 %all-to-all-start.3 = ((bf16[32,4,640]{2,1,0:T(4,128)(2,1)}), bf16[32,4,640]{2,1,0:T(4,128)(2,1)S(1)}, u32[]{:S(2)}, u32[]{:S(2)}) async-start(bf16[32,4,640]{2,1,0:T(4,128)(2,1)} %get-tuple-element.24), calls=%async_computation.3 | async-start | bytes 327680 | tf_op jit(solution)/shard_map/all_to_all | solution.py:235
  96.5 4.1 %collective-permute-start.10 = (bf16[32,640]{1,0:T(8,128)(2,1)S(1)}, bf16[32,640]{1,0:T(8,128)(2,1)S(1)}, u32[]{:S(2)}, u32[]{:S(2)}) collective-permute-start(bf16[32,640]{1,0:T(8,128)(2,1)S(1)} %get-tuple-element.26), channel_id=1, source_target_pairs={{0,128},{128,0},{1,129},{129,1},{2,130},{130,2},{3,131},{131,3},{4... | collective-permute-start | bytes 122888 | tf_op jit(solution)/shard_map/ppermute | solution.py:238

commit v2 on v1

v2 whole, which is shorter than its diff:
```python
import math

import jax
import jax.numpy as jnp
from jax import lax
from jax.experimental import pallas as pl
from jax.experimental.pallas import tpu as pltpu
from jax.sharding import Mesh, PartitionSpec as P

BF16, F32, I32 = jnp.bfloat16, jnp.float32, jnp.int32

XL, Z, CORE, TP = 2, 8, 2, 8
REP = XL * Z * CORE

HD = 128
SLOTS = 16
STEPS = 2
HEADS = 8
CTX = 256
MOVE = 13
STAY = SLOTS - MOVE
COLS = 40
OUT_COLS = COLS // TP
OWN = 10
ROWS = SLOTS * STEPS
PACK = STEPS * HEADS + 2 * STEPS

ROUND, PAIR_ROUND, ME, HEAD, COL, SCALE, DEP, DEST, LEN = 0, 1, 2, 3, 13, 23, 33, 46, 59

VMEM_LIMIT = 40 * 1024 * 1024


def smem():
    return pl.BlockSpec(memory_space=pltpu.SMEM)


def vmem():
    return pl.BlockSpec(memory_space=pltpu.VMEM)


def hbm():
    return pl.BlockSpec(memory_space=pltpu.HBM)


def call(body, out_shape, in_specs, scratch=(), **kw):
    single = not isinstance(out_shape, (list, tuple))
    return pl.pallas_call(
        body,
        out_shape=out_shape,
        in_specs=in_specs,
        out_specs=vmem() if single else [vmem()] * len(out_shape),
        scratch_shapes=list(scratch),
        compiler_params=pltpu.CompilerParams(vmem_limit_bytes=VMEM_LIMIT),
        **kw,
    )


def copy_in(pairs, sems):
    copies = [pltpu.make_async_copy(a, b, sems.at[i]) for i, (a, b) in enumerate(pairs)]
    for c in copies:
        c.start()
    for c in copies:
        c.wait()


def notice_body(place, *refs):
    given, (notice, packs), held, sems = refs[:7], refs[7:9], refs[9:16], refs[16]
    copy_in(zip(given, held), sems)
    dep, dest, lengths, ids, scales, queries, fresh = held
    row = lax.broadcasted_iota(I32, (REP, HD), 0)
    lane = lax.broadcasted_iota(I32, (REP, HD), 1)
    base = place[0]
    pair_row = lax.rem(row + REP // XL, REP)
    out = jnp.where(lane == ME, row, -1).astype(F32)
    for k in range(MOVE):
        out = jnp.where((lane == ROUND) & (row == dest[0, k]), float(k), out)
        out = jnp.where((lane == PAIR_ROUND) & (pair_row == dest[0, k]), float(k), out)
        out = jnp.where(lane == DEP + k, dep[0, k].astype(F32), out)
        out = jnp.where(lane == DEST + k, dest[0, k].astype(F32), out)
    for n in range(OWN):
        place_n = ids[n] - base
        head = lax.div(place_n, COLS)
        out = jnp.where(lane == HEAD + n, head.astype(F32), out)
        out = jnp.where(lane == COL + n, (place_n - head * COLS).astype(F32), out)
        out = jnp.where(lane == SCALE + n, scales[n], out)
    for s in range(SLOTS):
        out = jnp.where(lane == LEN + s, lengths[s].astype(F32), out)
    notice[:, 0, :] = out
    for s in range(SLOTS):
        packs[s] = jnp.concatenate(
            [queries[t, s] for t in range(STEPS)]
            + [fresh[t, s : s + 1, j * HD : (j + 1) * HD] for t in range(STEPS) for j in range(2)],
            axis=0,
        )


def join_body(first, second, out, sems):
    copy_in([(first, out.at[:OWN]), (second, out.at[OWN:])], sems)


def at(notices, rep, lane):
    return notices[rep, 0, lane].astype(I32)


def pull_body(notices, packs, out):
    me = at(notices, 0, ME)

    def one(peer, carry):
        turn = at(notices, peer, ROUND)
        out[peer] = packs[at(notices, me, DEP + jnp.maximum(turn, 0))]
        return carry

    lax.fori_loop(0, REP, one, 0, unroll=4)


def attend_body(notices, pulled, packs, cache, send, out, scores, held):
    scale = 1.0 / math.sqrt(HD)
    per = STEPS * HEADS
    me = at(notices, 0, ME)
    for s in range(SLOTS):
        held[s] = packs[s]
    for k in range(MOVE):
        held[at(notices, me, DEP + k)] = pulled[at(notices, me, DEST + k)]
    pos = lax.broadcasted_iota(I32, (per, CTX), 1)
    for s in range(SLOTS):
        q = held[s][:per]
        sc = lax.dot_general(
            q, cache[s, 0, :, :HD], (((1,), (1,)), ((), ())), preferred_element_type=F32
        )
        scores[s] = jnp.where(pos < at(notices, me, LEN + s), sc * scale, -jnp.inf)
    step = lax.broadcasted_iota(I32, (per, 1), 0) // HEADS
    for s in range(SLOTS):
        sc = scores[s]
        top = jnp.max(sc, axis=1, keepdims=True)
        expo = jnp.exp(sc - top)
        total = jnp.sum(expo, axis=1, keepdims=True)
        carried = jnp.dot(expo.astype(BF16), cache[s, 0, :, HD:], preferred_element_type=F32)
        pack = held[s].astype(F32)
        q = pack[:per]
        peak = top
        extra = []
        for u in range(STEPS):
            f = jnp.sum(q * pack[per + 2 * u : per + 2 * u + 1], axis=1, keepdims=True) * scale
            f = jnp.where(step >= u, f, -jnp.inf)
            extra.append(f)
            peak = jnp.maximum(peak, f)
        factor = jnp.exp(top - peak)
        denom = total * factor
        numer = carried * factor
        for u in range(STEPS):
            w = jnp.exp(extra[u] - peak)
            denom = denom + w
            numer = numer + w * pack[per + 2 * u + 1 : per + 2 * u + 2]
        out[s] = (numer / denom).astype(BF16)
    for k in range(MOVE):
        goal = at(notices, me, DEST + k)
        rows = out[at(notices, me, DEP + k)]
        send[goal, :per, :] = rows
        send[lax.rem(goal + REP // XL, REP), per:, :] = rows


def project_body(notices, came, mine, other, *rest):
    arrays, out, slots, rows, total = rest[:-4], rest[-4], rest[-3], rest[-2], rest[-1]
    per = STEPS * HEADS
    me = at(notices, 0, ME)
    pair = lax.rem(me + REP // XL, REP)
    xl, z, core = lax.div(me, Z * CORE), lax.rem(lax.div(me, CORE), Z), lax.rem(me, CORE)
    first, second = xl * SLOTS, (1 - xl) * SLOTS
    for s in range(SLOTS):
        slots[pl.ds(pl.multiple_of((first + s) * per, per), per), :] = mine[s].astype(F32)
        slots[pl.ds(pl.multiple_of((second + s) * per, per), per), :] = other[s].astype(F32)

    def place_rows(peer, carry):
        for lane, owner, start, lo in ((ROUND, me, first, 0), (PAIR_ROUND, pair, second, per)):
            turn = at(notices, peer, lane)
            slot = start + at(notices, owner, DEP + jnp.maximum(turn, 0))
            goal = jnp.where(turn >= 0, slot, XL * SLOTS)
            slots[pl.ds(pl.multiple_of(goal * per, per), per), :] = came[
                peer, lo : lo + per, :
            ].astype(F32)
        return carry

    lax.fori_loop(0, REP, place_rows, 0, unroll=4)
    for h in range(HEADS):
        for side in range(XL):
            for t in range(STEPS):
                lo = side * ROWS + t * SLOTS
                rows[h, lo : lo + SLOTS, :] = slots[
                    pl.ds(side * SLOTS * per + t * HEADS + h, SLOTS, stride=per), :
                ].astype(BF16)
    total[...] = jnp.zeros_like(total)
    away = 1 - 2 * core

    def run(blocks, first, z_src, core_src):
        src = (xl * Z + z_src) * CORE + core_src
        for lo in range(0, OWN, 5):
            products = []
            for n in range(lo, lo + 5):
                products.append(
                    jnp.dot(
                        rows[at(notices, src, HEAD + n)],
                        blocks[first + n],
                        preferred_element_type=F32,
                    )
                    * notices[src, 0, SCALE + n]
                )
            for n in range(lo, lo + 5):
                total[at(notices, src, COL + n)] += products[n - lo]

    run(arrays[0], 0, z, core)
    run(arrays[0], OWN, z, 1 - core)
    for step in range(1, Z // 2):
        from_z = lax.rem(z - away * step + Z, Z)
        sib_z = lax.rem(z + away * step + Z, Z)
        a, b = arrays[2 * step - 1], arrays[2 * step]
        run(a, 0, from_z, core)
        run(a, OWN, from_z, 1 - core)
        run(b, 0, sib_z, 1 - core)
        run(b, OWN, sib_z, core)
    far = lax.rem(z + Z // 2, Z)
    run(arrays[Z - 1], 0, far, core)
    run(arrays[Z], 0, far, 1 - core)
    out[:COLS] = total[:, :ROWS, :].astype(BF16)
    out[COLS:] = total[:, ROWS:, :].astype(BF16)


def sum_body(parts, out):
    for c in range(OUT_COLS):
        acc = parts[0, c].astype(F32)
        for t in range(1, XL * TP):
            acc = acc + parts[t, c].astype(F32)
        acc = acc.astype(BF16)
        for t in range(STEPS):
            out[t, :, c * HD : (c + 1) * HD] = acc[t * SLOTS : (t + 1) * SLOTS, :]


def shards(kv_cache, lengths, departing, destination, queries, new_kv, codes, scales, block_slot):
    rep_axes, tp_axes = ("xl", "z", "core"), ("y", "xh")
    base = lax.axis_index(tp_axes) * (HEADS * COLS)
    per = STEPS * HEADS

    def in_hbm(x):
        return pltpu.with_memory_space_constraint(x, pltpu.HBM)

    def exchange(x, axes):
        return lax.all_to_all(x, axes, split_axis=0, concat_axis=0, tiled=True)

    def swap(x, axis):
        return lax.ppermute(x, axis, [(0, 1), (1, 0)])

    def around(x, hops):
        pairs = [
            (i * CORE + c, ((i + hops * (1 - 2 * c)) % Z) * CORE + c)
            for i in range(Z)
            for c in range(CORE)
        ]
        return lax.ppermute(x, ("z", "core"), pairs)

    sib = swap(codes, "core")
    given = [
        departing,
        destination,
        lengths,
        block_slot,
        scales,
        queries,
        new_kv.reshape(STEPS, SLOTS, 2 * HD),
    ]
    notice, packs = call(
        notice_body,
        [
            jax.ShapeDtypeStruct((REP, 1, HD), F32),
            jax.ShapeDtypeStruct((SLOTS, PACK, HD), BF16),
        ],
        [smem()] + [hbm()] * len(given),
        [pltpu.SMEM(a.shape, a.dtype) for a in given[:5]]
        + [pltpu.VMEM(a.shape, a.dtype) for a in given[5:]]
        + [pltpu.SemaphoreType.DMA((len(given),))],
    )(base.astype(I32)[None], *(in_hbm(a) for a in given))
    own = call(
        join_body,
        jax.ShapeDtypeStruct((CORE * OWN, HD, HD), BF16),
        [pl.BlockSpec(memory_space=pl.ANY)] * 2,
        [pltpu.SemaphoreType.DMA((2,))],
    )(in_hbm(codes), sib)

    one = around(own, 1)
    notices = exchange(notice, rep_axes)
    one, notices = lax.optimization_barrier((one, notices))

    two = around(one, 1)
    one_sib = swap(one, "core")
    to_pull = call(
        pull_body, jax.ShapeDtypeStruct((REP, PACK, HD), BF16), [smem(), vmem()]
    )(notices, packs)
    pulled = exchange(to_pull, rep_axes)
    two, pulled = lax.optimization_barrier((two, pulled))

    four = around(two[:OWN], 2)
    three = around(two, 1)
    two_sib = swap(two, "core")
    send, mine = call(
        attend_body,
        [
            jax.ShapeDtypeStruct((REP, 2 * per, HD), BF16),
            jax.ShapeDtypeStruct((SLOTS, per, HD), BF16),
        ],
        [smem()] + [vmem()] * 3,
        [pltpu.VMEM((SLOTS, per, CTX), F32), pltpu.VMEM((SLOTS, PACK, HD), BF16)],
    )(notices, pulled, packs, kv_cache)
    other = swap(mine, "xl")
    came = exchange(send, rep_axes)
    three, four, came, other = lax.optimization_barrier((three, four, came, other))
    arrays = [own, one, one_sib, two, two_sib, three, swap(three, "core"), four, swap(four, "core")]
    parts = call(
        project_body,
        jax.ShapeDtypeStruct((XL * COLS, ROWS, HD), BF16),
        [smem()] + [vmem()] * (3 + len(arrays)),
        [
            pltpu.VMEM(((XL * SLOTS + 1) * per, HD), F32),
            pltpu.VMEM((HEADS, XL * ROWS, HD), BF16),
            pltpu.VMEM((COLS, XL * ROWS, HD), F32),
        ],
    )(notices, came, mine, other, *arrays)
    parts = exchange(parts, ("xl",) + tp_axes).reshape(XL * TP, OUT_COLS, ROWS, HD)
    return call(
        sum_body, jax.ShapeDtypeStruct((STEPS, SLOTS, OUT_COLS * HD), BF16), [vmem()]
    )(parts)


def solution(mesh):
    rep, tp = ("xl", "z", "core"), ("y", "xh")
    parts = Mesh(mesh.devices.reshape(XL, Z, CORE, 4, 2), rep + tp)
    placed = (
        P(rep, tp, None, None),
        P(rep),
        P(rep, None),
        P(rep, None),
        P(None, rep, tp, None),
        P(None, rep, tp, None),
        P(tp + rep, None, None),
        P(tp + rep),
        P(tp + rep),
    )
    return jax.shard_map(
        shards, mesh=parts, in_specs=placed, out_specs=P(None, rep, tp), check_vma=False
    )
```

time: 111 us -> 91.5 us (0.82)
  waiting for transfers between devices: 31.7 us -> 16 us
  local copies, waits for them, and re-layouts: 4.98 us -> 0.72 us
  starting transfers between devices: 10.5 us -> 13.2 us
  other arithmetic: 1.9 us -> 0 us
    ppermute x4, waiting for transfers between devices: 16.7 us -> 8.56 us  [around(): return lax.ppermute(x, ('z', 'core'), pairs)]
    all_to_all x1, waiting for transfers between devices: 6.99 us -> 0.01 us  [exchange(): return lax.all_to_all(x, axes, split_axis=0, concat_axis=0, tiled=True)]
    unnamed x19 -> x4, local copies, waits for them, and re-layouts: 4.87 us -> 0.7 us
    ppermute x4, starting transfers between devices: 3.47 us -> 6.23 us  [around(): return lax.ppermute(x, ('z', 'core'), pairs)]
    concatenate x1 -> x0, other arithmetic: 1.9 us -> none  [shards(): pair = jnp.concatenate([codes, sib], axis=0)]
    ppermute x7 -> x6, waiting for transfers between devices: 7.94 us -> 7.45 us  [swap(): return lax.ppermute(x, axis, [(0, 1), (1, 0)])]
    ppermute x7 -> x6, starting transfers between devices: 3.16 us -> 2.84 us  [swap(): return lax.ppermute(x, axis, [(0, 1), (1, 0)])]
  transfers between devices with their start and end apart: 12 -> 11, of which waited for: 6 -> 4; matrix products, arithmetic and copies ran while one was open for 1% -> 0% of each run, Pallas kernels for 3% -> 4%
where the time goes in v2:
time: 91.5 us; the launch traced here: 90.5 us
  blocking collectives  51.6 us (56%)
  waiting for transfers between devices  16 us (17%)
  starting transfers between devices  13.2 us (14%)
  Pallas kernels  8.83 us (10%)
    all_to_all x3, blocking collectives, exchange(): return lax.all_to_all(x, axes, split_axis=0, concat_axis=0, tiled=True)  51.6 us
    ppermute x4, waiting for transfers between devices, around(): return lax.ppermute(x, ('z', 'core'), pairs)  8.56 us
    ppermute x6, waiting for transfers between devices, swap(): return lax.ppermute(x, axis, [(0, 1), (1, 0)])  7.45 us
    ppermute x4, starting transfers between devices, around(): return lax.ppermute(x, ('z', 'core'), pairs)  6.23 us
    all_to_all x1, starting transfers between devices, exchange(): return lax.all_to_all(x, axes, split_axis=0, concat_axis=0, tiled=True)  4.15 us
    pallas_call x1, Pallas kernels, shards(): call(project_body, jax.ShapeDtypeStruct((XL * COLS, ROWS, HD), BF16), [sm...  3.48 us
    ppermute x6, starting transfers between devices, swap(): return lax.ppermute(x, axis, [(0, 1), (1, 0)])  2.84 us
  transfers between devices with their start and end apart: 11, of which 4 were waited for; matrix products, arithmetic and copies ran while one was open for 0% of the time, Pallas kernels for 4%

profile of v2, /device:TPU:8, one launch (start us, length us, event | category | flops | bytes accessed | tf_op | source)
XLA Modules:
  0.0 90.5 jit_solution(16986284242975420141)
XLA Ops:
  0.0 0.0 collective-permute-start
  0.0 1.8 %collective-permute-done.second = bf16[10,128,128]{2,1,0:T(8,128)(2,1)S(1)} collective-permute-done((bf16[10,128,128]{2,1,0:T(8,128)(2,1)}, bf16[10,128,128]{2,1,0:T(8,128)(2,1)S(1)}, u32[]{:S(2)}, u32[]{:S(2)}) %collective-permute-start) | collective-permute-done | bytes 327712 | tf_op jit(solution)/shard_map/ppermute | solution.py:249
  1.8 1.0 %shard_map.91.rest_0_ = bf16[20,128,128]{2,1,0:T(8,128)(2,1)S(1)} custom-call(bf16[10,128,128]{2,1,0:T(8,128)(2,1)} %first.1, bf16[10,128,128]{2,1,0:T(8,128)(2,1)S(1)} %collective-permute-done.second), custom_call_target="tpu_custom_call" | custom-call | tf_op jit(solution)/shard_map/pallas_call | solution.py:280
  2.8 2.0 %collective-permute-start.1 = (bf16[20,128,128]{2,1,0:T(8,128)(2,1)S(1)}, bf16[20,128,128]{2,1,0:T(8,128)(2,1)}, u32[]{:S(2)}, u32[]{:S(2)}) collective-permute-start(bf16[20,128,128]{2,1,0:T(8,128)(2,1)S(1)} %shard_map.91.rest_0_), channel_id=1, source_target_pairs={{0,16},{8,120},{16,32},{24,8},{32,48},{40,24},{48,64},{56,40},{64,... | collective-permute-start | bytes 1966088 | tf_op jit(solution)/shard_map/ppermute | solution.py:257
  4.8 1.1 %shard_map.92 = (f32[32,1,128]{2,1,0:T(1,128)S(1)}, bf16[16,20,128]{2,1,0:T(8,128)(2,1)S(1)}) custom-call(s32[1]{0:T(128)} %bitcast.place, s32[1,13]{1,0:T(1,128)} %refs_0_.1, s32[1,13]{1,0:T(1,128)} %refs_1_.1, s32[16]{0:T(128)} %refs_2_.1, s32[10]{0:T(128)} %refs_3_.1, f32[10]{0:T(128)} %refs_4_.1, bf16[2,16,8,128]{3,2,1,0:T(8,128)(2,1)} %refs_5_.1, ...), custom_call_target="tpu_custom_call" | custom-call | tf_op jit(solution)/shard_map/pallas_call | solution.py:269
  5.9 17.1 %all_to_all.20.notices = f32[32,1,128]{2,1,0:T(1,128)S(1)} all-to-all(f32[32,1,128]{2,1,0:T(1,128)S(1)} %get-tuple-element.17), channel_id=1, replica_groups=mesh['xl'=2,'z'=8,'core'=2,'y'=4,'xh'=2] {'xl','z','core'}, dimensions={0} | all-to-all | bytes 32768 | tf_op jit(solution)/shard_map/all_to_all | solution.py:246
  23.0 0.0 collective-permute-done.1.rest_1_
  23.0 0.6 collective-permute-start.2
  23.6 1.1 %shard_map.93 = bf16[32,20,128]{2,1,0:T(8,128)(2,1)S(1)} custom-call(f32[32,1,128]{2,1,0:T(1,128)S(1)} %all_to_all.20.notices, bf16[16,20,128]{2,1,0:T(8,128)(2,1)S(1)} %get-tuple-element.20.packs), custom_call_target="tpu_custom_call" | custom-call | tf_op jit(solution)/shard_map/pallas_call | solution.py:293
  24.7 15.8 %all_to_all.21.pulled = bf16[32,20,128]{2,1,0:T(8,128)(2,1)S(1)} all-to-all(bf16[32,20,128]{2,1,0:T(8,128)(2,1)S(1)} %shard_map.93), channel_id=1, replica_groups=mesh['xl'=2,'z'=8,'core'=2,'y'=4,'xh'=2] {'xl','z','core'}, dimensions={0} | all-to-all | bytes 327680 | tf_op jit(solution)/shard_map/all_to_all | solution.py:246
  40.5 0.0 collective-permute-done.2.rest_3_
  40.5 0.9 collective-permute-start.3
  41.3 1.5 %shard_map.94 = (bf16[32,32,128]{2,1,0:T(8,128)(2,1)S(1)}, bf16[16,16,128]{2,1,0:T(8,128)(2,1)S(1)}) custom-call(f32[32,1,128]{2,1,0:T(1,128)S(1)} %all_to_all.20.notices, bf16[32,20,128]{2,1,0:T(8,128)(2,1)S(1)} %all_to_all.21.pulled, bf16[16,20,128]{2,1,0:T(8,128)(2,1)S(1)} %get-tuple-element.20.packs, bf16[16,1,256,256]{3,2,1,0:T(8,128)(2,1)S(1)} %copy-done), custom_call_target="tpu_custom_call" | custom-call | tf_op jit(solution)/shard_map/pallas_call | solution.py:302
  42.8 0.7 copy-done.1
  43.5 4.2 %all-to-all-start.2 = ((bf16[32,32,128]{2,1,0:T(8,128)(2,1)}), bf16[32,32,128]{2,1,0:T(8,128)(2,1)S(1)}, u32[]{:S(2)}, u32[]{:S(2)}) async-start(bf16[32,32,128]{2,1,0:T(8,128)(2,1)} %copy-done.1), calls=%async_computation.2 | async-start | bytes 524288 | tf_op jit(solution)/shard_map/all_to_all | solution.py:246
  47.7 2.8 %collective-permute-start.4 = (bf16[10,128,128]{2,1,0:T(8,128)(2,1)S(1)}, bf16[10,128,128]{2,1,0:T(8,128)(2,1)S(1)}, u32[]{:S(2)}, u32[]{:S(2)}) collective-permute-start(bf16[10,128,128]{2,1,0:T(8,128)(2,1)S(1)} %slice.3), channel_id=1, source_target_pairs={{0,32},{8,104},{16,48},{24,120},{32,64},{40,8},{48,80},{56,24},{64... | collective-permute-start | bytes 983048 | tf_op jit(solution)/shard_map/ppermute | solution.py:257
  50.5 1.5 %collective-permute-start.5 = (bf16[16,16,128]{2,1,0:T(8,128)(2,1)S(1)}, bf16[16,16,128]{2,1,0:T(8,128)(2,1)S(1)}, u32[]{:S(2)}, u32[]{:S(2)}) collective-permute-start(bf16[16,16,128]{2,1,0:T(8,128)(2,1)S(1)} %get-tuple-element.24.mine), channel_id=1, source_target_pairs={{0,128},{128,0},{1,129},{129,1},{2,130},{130,2},{3,131},{131,3},{4... | collective-permute-start | bytes 196616 | tf_op jit(solution)/shard_map/ppermute | solution.py:249
  52.0 0.9 collective-permute-start.6
  52.8 0.0 collective-permute-start.7
  52.8 3.6 %collective-permute-done.5.other = bf16[16,16,128]{2,1,0:T(8,128)(2,1)S(1)} collective-permute-done((bf16[16,16,128]{2,1,0:T(8,128)(2,1)S(1)}, bf16[16,16,128]{2,1,0:T(8,128)(2,1)S(1)}, u32[]{:S(2)}, u32[]{:S(2)}) %collective-permute-start.5) | collective-permute-done | bytes 65568 | tf_op jit(solution)/shard_map/ppermute | solution.py:249
  56.4 8.6 %collective-permute-done.4.rest_7_ = bf16[10,128,128]{2,1,0:T(8,128)(2,1)S(1)} collective-permute-done((bf16[10,128,128]{2,1,0:T(8,128)(2,1)S(1)}, bf16[10,128,128]{2,1,0:T(8,128)(2,1)S(1)}, u32[]{:S(2)}, u32[]{:S(2)}) %collective-permute-start.4) | collective-permute-done | bytes 327712 | tf_op jit(solution)/shard_map/ppermute | solution.py:257
  64.9 0.0 all-to-all-done.2.came
  64.9 0.0 collective-permute-done.3.rest_5_
  64.9 0.0 collective-permute-start.8
  65.0 0.5 collective-permute-start.9
  65.5 0.0 collective-permute-done.6.rest_2_
  65.5 0.0 collective-permute-done.7.rest_4_
  65.5 2.0 %collective-permute-done.9.rest_8_ = bf16[10,128,128]{2,1,0:T(8,128)(2,1)S(1)} collective-permute-done((bf16[10,128,128]{2,1,0:T(8,128)(2,1)S(1)}, bf16[10,128,128]{2,1,0:T(8,128)(2,1)S(1)}, u32[]{:S(2)}, u32[]{:S(2)}) %collective-permute-start.9) | collective-permute-done | bytes 327712 | tf_op jit(solution)/shard_map/ppermute | solution.py:249
  67.5 0.0 collective-permute-done.8.rest_6_
  67.5 3.5 %shard_map.95 = bf16[80,32,128]{2,1,0:T(8,128)(2,1)S(1)} custom-call(f32[32,1,128]{2,1,0:T(1,128)S(1)} %all_to_all.20.notices, bf16[32,32,128]{2,1,0:T(8,128)(2,1)S(1)} %all-to-all-done.2.came, bf16[16,16,128]{2,1,0:T(8,128)(2,1)S(1)} %get-tuple-element.24.mine, bf16[16,16,128]{2,1,0:T(8,128)(2,1)S(1)} %collective-permute-done.5.other, ...), custom_call_target="tpu_custom_call" | custom-call | tf_op jit(solution)/shard_map/pallas_call | solution.py:315
  71.0 18.7 %all_to_all.22 = bf16[80,32,128]{2,1,0:T(8,128)(2,1)S(1)} all-to-all(bf16[80,32,128]{2,1,0:T(8,128)(2,1)S(1)} %shard_map.95), channel_id=1, replica_groups=mesh['xl'=2,'z'=8,'core'=2,'y'=4,'xh'=2] {'xl','y','xh'}, dimensions={0} | all-to-all | bytes 1310720 | tf_op jit(solution)/shard_map/all_to_all | solution.py:246
  89.8 0.7 shard_map.96
  (4 shorter events, 0.0 us)
Async XLA Ops:
  0.0 41.3 %copy-start = (bf16[16,1,256,256]{3,2,1,0:T(8,128)(2,1)S(1)}, bf16[16,1,256,256]{3,2,1,0:T(8,128)(2,1)}, u32[]{:S(2)}) copy-start(bf16[16,1,256,256]{3,2,1,0:T(8,128)(2,1)} %cache.1) | copy-start | bytes 6291460
  0.0 1.8 %collective-permute-start = (bf16[10,128,128]{2,1,0:T(8,128)(2,1)}, bf16[10,128,128]{2,1,0:T(8,128)(2,1)S(1)}, u32[]{:S(2)}, u32[]{:S(2)}) collective-permute-start(bf16[10,128,128]{2,1,0:T(8,128)(2,1)} %first.1), channel_id=1, source_target_pairs={{0,8},{8,0},{1,9},{9,1},{2,10},{10,2},{3,11},{11,3},{4,12},{12,4},... | collective-permute-start | bytes 983048 | tf_op jit(solution)/shard_map/ppermute | solution.py:249
  2.8 20.2 %collective-permute-start.1 = (bf16[20,128,128]{2,1,0:T(8,128)(2,1)S(1)}, bf16[20,128,128]{2,1,0:T(8,128)(2,1)}, u32[]{:S(2)}, u32[]{:S(2)}) collective-permute-start(bf16[20,128,128]{2,1,0:T(8,128)(2,1)S(1)} %shard_map.91.rest_0_), channel_id=1, source_target_pairs={{0,16},{8,120},{16,32},{24,8},{32,48},{40,24},{48,64},{56,40},{64,... | collective-permute-start | bytes 1966088 | tf_op jit(solution)/shard_map/ppermute | solution.py:257
  23.0 17.4 %collective-permute-start.2 = (bf16[20,128,128]{2,1,0:T(8,128)(2,1)}, bf16[20,128,128]{2,1,0:T(8,128)(2,1)S(1)}, u32[]{:S(2)}, u32[]{:S(2)}) collective-permute-start(bf16[20,128,128]{2,1,0:T(8,128)(2,1)} %collective-permute-done.1.rest_1_), channel_id=1, source_target_pairs={{0,16},{8,120},{16,32},{24,8},{32,48},{40,24},{48,64},{56,40},{64,... | collective-permute-start | bytes 1966088 | tf_op jit(solution)/shard_map/ppermute | solution.py:257
  40.5 24.5 %collective-permute-start.3 = (bf16[20,128,128]{2,1,0:T(8,128)(2,1)S(1)}, bf16[20,128,128]{2,1,0:T(8,128)(2,1)}, u32[]{:S(2)}, u32[]{:S(2)}) collective-permute-start(bf16[20,128,128]{2,1,0:T(8,128)(2,1)S(1)} %collective-permute-done.2.rest_3_), channel_id=1, source_target_pairs={{0,16},{8,120},{16,32},{24,8},{32,48},{40,24},{48,64},{56,40},{64,... | collective-permute-start | bytes 1966088 | tf_op jit(solution)/shard_map/ppermute | solution.py:257
  42.8 0.7 copy-start.1
  43.5 21.4 %all-to-all-start.2 = ((bf16[32,32,128]{2,1,0:T(8,128)(2,1)}), bf16[32,32,128]{2,1,0:T(8,128)(2,1)S(1)}, u32[]{:S(2)}, u32[]{:S(2)}) async-start(bf16[32,32,128]{2,1,0:T(8,128)(2,1)} %copy-done.1), calls=%async_computation.2 | async-start | bytes 524288 | tf_op jit(solution)/shard_map/all_to_all | solution.py:246
  47.7 17.2 %collective-permute-start.4 = (bf16[10,128,128]{2,1,0:T(8,128)(2,1)S(1)}, bf16[10,128,128]{2,1,0:T(8,128)(2,1)S(1)}, u32[]{:S(2)}, u32[]{:S(2)}) collective-permute-start(bf16[10,128,128]{2,1,0:T(8,128)(2,1)S(1)} %slice.3), channel_id=1, source_target_pairs={{0,32},{8,104},{16,48},{24,120},{32,64},{40,8},{48,80},{56,24},{64... | collective-permute-start | bytes 983048 | tf_op jit(solution)/shard_map/ppermute | solution.py:257
  50.5 5.9 %collective-permute-start.5 = (bf16[16,16,128]{2,1,0:T(8,128)(2,1)S(1)}, bf16[16,16,128]{2,1,0:T(8,128)(2,1)S(1)}, u32[]{:S(2)}, u32[]{:S(2)}) collective-permute-start(bf16[16,16,128]{2,1,0:T(8,128)(2,1)S(1)} %get-tuple-element.24.mine), channel_id=1, source_target_pairs={{0,128},{128,0},{1,129},{129,1},{2,130},{130,2},{3,131},{131,3},{4... | collective-permute-start | bytes 196616 | tf_op jit(solution)/shard_map/ppermute | solution.py:249
  52.0 13.5 %collective-permute-start.6 = (bf16[20,128,128]{2,1,0:T(8,128)(2,1)}, bf16[20,128,128]{2,1,0:T(8,128)(2,1)S(1)}, u32[]{:S(2)}, u32[]{:S(2)}) collective-permute-start(bf16[20,128,128]{2,1,0:T(8,128)(2,1)} %collective-permute-done.1.rest_1_), channel_id=1, source_target_pairs={{0,8},{8,0},{1,9},{9,1},{2,10},{10,2},{3,11},{11,3},{4,12},{12,4},... | collective-permute-start | bytes 1966088 | tf_op jit(solution)/shard_map/ppermute | solution.py:249
  52.8 12.6 %collective-permute-start.7 = (bf16[20,128,128]{2,1,0:T(8,128)(2,1)S(1)}, bf16[20,128,128]{2,1,0:T(8,128)(2,1)S(1)}, u32[]{:S(2)}, u32[]{:S(2)}) collective-permute-start(bf16[20,128,128]{2,1,0:T(8,128)(2,1)S(1)} %collective-permute-done.2.rest_3_), channel_id=1, source_target_pairs={{0,8},{8,0},{1,9},{9,1},{2,10},{10,2},{3,11},{11,3},{4,12},{12,4},... | collective-permute-start | bytes 1966088 | tf_op jit(solution)/shard_map/ppermute | solution.py:249
  64.9 2.6 %collective-permute-start.8 = (bf16[20,128,128]{2,1,0:T(8,128)(2,1)}, bf16[20,128,128]{2,1,0:T(8,128)(2,1)S(1)}, u32[]{:S(2)}, u32[]{:S(2)}) collective-permute-start(bf16[20,128,128]{2,1,0:T(8,128)(2,1)} %collective-permute-done.3.rest_5_), channel_id=1, source_target_pairs={{0,8},{8,0},{1,9},{9,1},{2,10},{10,2},{3,11},{11,3},{4,12},{12,4},... | collective-permute-start | bytes 1966088 | tf_op jit(solution)/shard_map/ppermute | solution.py:249
  65.0 2.6 %collective-permute-start.9 = (bf16[10,128,128]{2,1,0:T(8,128)(2,1)S(1)}, bf16[10,128,128]{2,1,0:T(8,128)(2,1)S(1)}, u32[]{:S(2)}, u32[]{:S(2)}) collective-permute-start(bf16[10,128,128]{2,1,0:T(8,128)(2,1)S(1)} %collective-permute-done.4.rest_7_), channel_id=1, source_target_pairs={{0,8},{8,0},{1,9},{9,1},{2,10},{10,2},{3,11},{11,3},{4,12},{12,4},... | collective-permute-start | bytes 983048 | tf_op jit(solution)/shard_map/ppermute | solution.py:249

commit v3 on v2

--- a/solution.py
+++ b/solution.py
@@ -189,7 +189,6 @@
                     pl.ds(side * SLOTS * per + t * HEADS + h, SLOTS, stride=per), :
                 ].astype(BF16)
     total[...] = jnp.zeros_like(total)
-    away = 1 - 2 * core
 
     def run(blocks, first, z_src, core_src):
         src = (xl * Z + z_src) * CORE + core_src
@@ -207,19 +206,22 @@
             for n in range(lo, lo + 5):
                 total[at(notices, src, COL + n)] += products[n - lo]
 
-    run(arrays[0], 0, z, core)
-    run(arrays[0], OWN, z, 1 - core)
-    for step in range(1, Z // 2):
-        from_z = lax.rem(z - away * step + Z, Z)
-        sib_z = lax.rem(z + away * step + Z, Z)
-        a, b = arrays[2 * step - 1], arrays[2 * step]
-        run(a, 0, from_z, core)
-        run(a, OWN, from_z, 1 - core)
-        run(b, 0, sib_z, 1 - core)
-        run(b, OWN, sib_z, core)
-    far = lax.rem(z + Z // 2, Z)
-    run(arrays[Z - 1], 0, far, core)
-    run(arrays[Z], 0, far, 1 - core)
+    own, one, one_sib, two_a, two_a_sib, mid, mid_sib, last, last_sib = arrays
+    run(own, 0, z, core)
+    run(own, OWN, z, 1 - core)
+    for line, a, b, c, d in (
+        (core, one, two_a, mid, last),
+        (1 - core, one_sib, two_a_sib, mid_sib, last_sib),
+    ):
+        away = 1 - 2 * line
+        far = [lax.rem(z - away * step + Z, Z) for step in range(Z // 2 + 1)]
+        run(a, 0, far[1], line)
+        run(a, OWN, far[1], 1 - line)
+        run(b, 0, far[2], line)
+        run(c, 0, far[2], 1 - line)
+        run(c, OWN, far[3], line)
+        run(d, 0, far[3], 1 - line)
+        run(d, OWN, far[4], line)
     out[:COLS] = total[:, :ROWS, :].astype(BF16)
     out[COLS:] = total[:, ROWS:, :].astype(BF16)
 
@@ -256,6 +258,7 @@
         ]
         return lax.ppermute(x, ("z", "core"), pairs)
 
+    two_a = around(codes, 2)
     sib = swap(codes, "core")
     given = [
         departing,
@@ -277,28 +280,29 @@
         + [pltpu.VMEM(a.shape, a.dtype) for a in given[5:]]
         + [pltpu.SemaphoreType.DMA((len(given),))],
     )(base.astype(I32)[None], *(in_hbm(a) for a in given))
-    own = call(
+    sib, notice = lax.optimization_barrier((sib, notice))
+    join = call(
         join_body,
         jax.ShapeDtypeStruct((CORE * OWN, HD, HD), BF16),
         [pl.BlockSpec(memory_space=pl.ANY)] * 2,
         [pltpu.SemaphoreType.DMA((2,))],
-    )(in_hbm(codes), sib)
+    )
+    own = join(in_hbm(codes), sib)
 
     one = around(own, 1)
     notices = exchange(notice, rep_axes)
-    one, notices = lax.optimization_barrier((one, notices))
-
-    two = around(one, 1)
-    one_sib = swap(one, "core")
+    one, two_a, notices = lax.optimization_barrier((one, two_a, notices))
+
+    mid = around(join(one[OWN:], two_a), 1)
+    one_sib, two_a_sib = swap(one, "core"), swap(two_a, "core")
     to_pull = call(
         pull_body, jax.ShapeDtypeStruct((REP, PACK, HD), BF16), [smem(), vmem()]
     )(notices, packs)
     pulled = exchange(to_pull, rep_axes)
-    two, pulled = lax.optimization_barrier((two, pulled))
-
-    four = around(two[:OWN], 2)
-    three = around(two, 1)
-    two_sib = swap(two, "core")
+    mid, pulled = lax.optimization_barrier((mid, pulled))
+
+    last = around(mid, 1)
+    mid_sib = swap(mid, "core")
     send, mine = call(
         attend_body,
         [
@@ -310,8 +314,8 @@
     )(notices, pulled, packs, kv_cache)
     other = swap(mine, "xl")
     came = exchange(send, rep_axes)
-    three, four, came, other = lax.optimization_barrier((three, four, came, other))
-    arrays = [own, one, one_sib, two, two_sib, three, swap(three, "core"), four, swap(four, "core")]
+    last, came, other = lax.optimization_barrier((last, came, other))
+    arrays = [own, one, one_sib, two_a, two_a_sib, mid, mid_sib, last, swap(last, "core")]
     parts = call(
         project_body,
         jax.ShapeDtypeStruct((XL * COLS, ROWS, HD), BF16),

time: 91.5 us -> 96.2 us (1.051)
  blocking collectives: 51.6 us -> 36.5 us
  waiting for transfers between devices: 16 us -> 25.3 us
  starting transfers between devices: 13.2 us -> 20.2 us
  Pallas kernels: 8.83 us -> 10.8 us
  local copies, waits for them, and re-layouts: 0.72 us -> 2.16 us
    all_to_all x3 -> x2, blocking collectives: 51.6 us -> 36.5 us  [exchange(): return lax.all_to_all(x, axes, split_axis=0, concat_axis=0, tiled=True)]
    all_to_all x1 -> x2, waiting for transfers between devices: 0.01 us -> 12.6 us  [exchange(): return lax.all_to_all(x, axes, split_axis=0, concat_axis=0, tiled=True)]
    all_to_all x1 -> x2, starting transfers between devices: 4.15 us -> 11.3 us  [exchange(): return lax.all_to_all(x, axes, split_axis=0, concat_axis=0, tiled=True)]
    ppermute x6, waiting for transfers between devices: 7.45 us -> 4.72 us  [swap(): return lax.ppermute(x, axis, [(0, 1), (1, 0)])]
    unnamed x4 -> x8, local copies, waits for them, and re-layouts: 0.7 us -> 2.14 us
    pallas_call x1 -> x2, Pallas kernels: 0.99 us -> 2.09 us  [the longest x1 1.09 us: shards(): mid = around(join(one[OWN:], two_a), 1)]
  transfers between devices with their start and end apart: 11 -> 12, of which waited for: 4 -> 5; matrix products, arithmetic and copies ran while one was open for 0% -> 0% of each run, Pallas kernels for 4% -> 5%
where the time goes in v3:
time: 96.2 us; the launch traced here: 95.1 us
  blocking collectives  36.5 us (38%)
  waiting for transfers between devices  25.3 us (26%)
  starting transfers between devices  20.2 us (21%)
  Pallas kernels  10.8 us (11%)
  local copies, waits for them, and re-layouts  2.16 us (2%)
    all_to_all x2, blocking collectives, exchange(): return lax.all_to_all(x, axes, split_axis=0, concat_axis=0, tiled=True)  36.5 us
    all_to_all x2, waiting for transfers between devices, exchange(): return lax.all_to_all(x, axes, split_axis=0, concat_axis=0, tiled=True)  12.6 us
    all_to_all x2, starting transfers between devices, exchange(): return lax.all_to_all(x, axes, split_axis=0, concat_axis=0, tiled=True)  11.3 us
    ppermute x4, waiting for transfers between devices, around(): return lax.ppermute(x, ('z', 'core'), pairs)  7.91 us
    ppermute x4, starting transfers between devices, around(): return lax.ppermute(x, ('z', 'core'), pairs)  6.06 us
    ppermute x6, waiting for transfers between devices, swap(): return lax.ppermute(x, axis, [(0, 1), (1, 0)])  4.72 us
    pallas_call x1, Pallas kernels, shards(): call(project_body, jax.ShapeDtypeStruct((XL * COLS, ROWS, HD), BF16), [sm...  3.58 us
    ppermute x6, starting transfers between devices, swap(): return lax.ppermute(x, axis, [(0, 1), (1, 0)])  2.91 us
  transfers between devices with their start and end apart: 12, of which 5 were waited for; matrix products, arithmetic and copies ran while one was open for 0% of the time, Pallas kernels for 5%

profile of v3, /device:TPU:8, one launch (start us, length us, event | category | flops | bytes accessed | tf_op | source)
XLA Modules:
  0.0 95.1 jit_solution(9154462746536782186)
XLA Ops:
  0.0 0.0 collective-permute-start
  0.0 1.8 %shard_map.91 = (f32[32,1,128]{2,1,0:T(1,128)}, bf16[16,20,128]{2,1,0:T(8,128)(2,1)S(1)}) custom-call(s32[1]{0:T(128)} %bitcast.place, s32[1,13]{1,0:T(1,128)} %refs_0_.1, s32[1,13]{1,0:T(1,128)} %refs_1_.1, s32[16]{0:T(128)} %refs_2_.1, s32[10]{0:T(128)} %refs_3_.1, f32[10]{0:T(128)} %refs_4_.1, bf16[2,16,8,128]{3,2,1,0:T(8,128)(2,1)} %refs_5_.1, ...), custom_call_target="tpu_custom_call" | custom-call | tf_op jit(solution)/shard_map/pallas_call | solution.py:272
  1.9 0.0 collective-permute-done.second
  1.9 1.0 %shard_map.92.rest_0_ = bf16[20,128,128]{2,1,0:T(8,128)(2,1)S(1)} custom-call(bf16[10,128,128]{2,1,0:T(8,128)(2,1)} %first.1, bf16[10,128,128]{2,1,0:T(8,128)(2,1)S(1)} %collective-permute-done.second), custom_call_target="tpu_custom_call" | custom-call | tf_op jit(solution)/shard_map/pallas_call | solution.py:290
  2.9 2.0 %collective-permute-start.1 = (bf16[20,128,128]{2,1,0:T(8,128)(2,1)S(1)}, bf16[20,128,128]{2,1,0:T(8,128)(2,1)S(1)}, u32[]{:S(2)}, u32[]{:S(2)}) collective-permute-start(bf16[20,128,128]{2,1,0:T(8,128)(2,1)S(1)} %shard_map.92.rest_0_), channel_id=1, source_target_pairs={{0,16},{8,120},{16,32},{24,8},{32,48},{40,24},{48,64},{56,40},{64,... | collective-permute-start | bytes 1966088 | tf_op jit(solution)/shard_map/ppermute | solution.py:259
  4.9 3.3 %collective-permute-start.2 = (bf16[10,128,128]{2,1,0:T(8,128)(2,1)}, bf16[10,128,128]{2,1,0:T(8,128)(2,1)}, u32[]{:S(2)}, u32[]{:S(2)}) collective-permute-start(bf16[10,128,128]{2,1,0:T(8,128)(2,1)} %first.1), channel_id=1, source_target_pairs={{0,32},{8,104},{16,48},{24,120},{32,64},{40,8},{48,80},{56,24},{64... | collective-permute-start | bytes 983048 | tf_op jit(solution)/shard_map/ppermute | solution.py:259
  8.1 7.1 %all-to-all-start = ((f32[32,1,128]{2,1,0:T(1,128)}), f32[32,1,128]{2,1,0:T(1,128)S(1)}, u32[]{:S(2)}, u32[]{:S(2)}) async-start(f32[32,1,128]{2,1,0:T(1,128)} %get-tuple-element.21), calls=%async_computation | async-start | bytes 32768 | tf_op jit(solution)/shard_map/all_to_all | solution.py:248
  15.2 7.9 %collective-permute-done.2.second.rest_3_ = bf16[10,128,128]{2,1,0:T(8,128)(2,1)} collective-permute-done((bf16[10,128,128]{2,1,0:T(8,128)(2,1)}, bf16[10,128,128]{2,1,0:T(8,128)(2,1)}, u32[]{:S(2)}, u32[]{:S(2)}) %collective-permute-start.2) | collective-permute-done | bytes 327712 | tf_op jit(solution)/shard_map/ppermute | solution.py:259
  23.1 4.3 %all-to-all-done.notices = f32[32,1,128]{2,1,0:T(1,128)S(1)} async-done(((f32[32,1,128]{2,1,0:T(1,128)}), f32[32,1,128]{2,1,0:T(1,128)S(1)}, u32[]{:S(2)}, u32[]{:S(2)}) %all-to-all-start) | async-done | bytes 16416 | tf_op jit(solution)/shard_map/all_to_all | solution.py:248
  27.4 0.0 collective-permute-done.1.rest_1_
  27.5 1.1 %shard_map.93 = bf16[20,128,128]{2,1,0:T(8,128)(2,1)S(1)} custom-call(bf16[10,128,128]{2,1,0:T(8,128)(2,1)S(1)} %slice.3.first, bf16[10,128,128]{2,1,0:T(8,128)(2,1)} %collective-permute-done.2.second.rest_3_), custom_call_target="tpu_custom_call" | custom-call | tf_op jit(solution)/shard_map/pallas_call | solution.py:296
  28.6 0.1 collective-permute-start.3
  28.7 1.1 %shard_map.94 = bf16[32,20,128]{2,1,0:T(8,128)(2,1)S(1)} custom-call(f32[32,1,128]{2,1,0:T(1,128)S(1)} %all-to-all-done.notices, bf16[16,20,128]{2,1,0:T(8,128)(2,1)S(1)} %get-tuple-element.25.packs), custom_call_target="tpu_custom_call" | custom-call | tf_op jit(solution)/shard_map/pallas_call | solution.py:298
  29.7 17.6 %all_to_all.20.pulled = bf16[32,20,128]{2,1,0:T(8,128)(2,1)S(1)} all-to-all(bf16[32,20,128]{2,1,0:T(8,128)(2,1)S(1)} %shard_map.94), channel_id=1, replica_groups=mesh['xl'=2,'z'=8,'core'=2,'y'=4,'xh'=2] {'xl','z','core'}, dimensions={0} | all-to-all | bytes 327680 | tf_op jit(solution)/shard_map/all_to_all | solution.py:248
  47.3 0.7 collective-permute-start.4
  48.0 1.5 %shard_map.95 = (bf16[32,32,128]{2,1,0:T(8,128)(2,1)S(1)}, bf16[16,16,128]{2,1,0:T(8,128)(2,1)S(1)}) custom-call(f32[32,1,128]{2,1,0:T(1,128)S(1)} %all-to-all-done.notices, bf16[32,20,128]{2,1,0:T(8,128)(2,1)S(1)} %all_to_all.20.pulled, bf16[16,20,128]{2,1,0:T(8,128)(2,1)S(1)} %get-tuple-element.25.packs, bf16[16,1,256,256]{3,2,1,0:T(8,128)(2,1)S(1)} %copy-done), custom_call_target="tpu_custom_call" | custom-call | tf_op jit(solution)/shard_map/pallas_call | solution.py:306
  49.5 0.7 copy-done.1
  50.2 0.6 copy-done.2
  50.8 4.2 %all-to-all-start.2 = ((bf16[32,32,128]{2,1,0:T(8,128)(2,1)}), bf16[32,32,128]{2,1,0:T(8,128)(2,1)S(1)}, u32[]{:S(2)}, u32[]{:S(2)}) async-start(bf16[32,32,128]{2,1,0:T(8,128)(2,1)} %copy-done.1), calls=%async_computation.2 | async-start | bytes 524288 | tf_op jit(solution)/shard_map/all_to_all | solution.py:248
  55.0 1.9 %collective-permute-start.5 = (bf16[16,16,128]{2,1,0:T(8,128)(2,1)}, bf16[16,16,128]{2,1,0:T(8,128)(2,1)S(1)}, u32[]{:S(2)}, u32[]{:S(2)}) collective-permute-start(bf16[16,16,128]{2,1,0:T(8,128)(2,1)} %copy-done.2), channel_id=1, source_target_pairs={{0,128},{128,0},{1,129},{129,1},{2,130},{130,2},{3,131},{131,3},{4... | collective-permute-start | bytes 196616 | tf_op jit(solution)/shard_map/ppermute | solution.py:251
  56.9 0.5 collective-permute-start.8
  57.4 2.4 %collective-permute-done.5.other = bf16[16,16,128]{2,1,0:T(8,128)(2,1)S(1)} collective-permute-done((bf16[16,16,128]{2,1,0:T(8,128)(2,1)}, bf16[16,16,128]{2,1,0:T(8,128)(2,1)S(1)}, u32[]{:S(2)}, u32[]{:S(2)}) %collective-permute-start.5) | collective-permute-done | bytes 65568 | tf_op jit(solution)/shard_map/ppermute | solution.py:251
  59.9 8.3 %all-to-all-done.2.came = bf16[32,32,128]{2,1,0:T(8,128)(2,1)S(1)} async-done(((bf16[32,32,128]{2,1,0:T(8,128)(2,1)}), bf16[32,32,128]{2,1,0:T(8,128)(2,1)S(1)}, u32[]{:S(2)}, u32[]{:S(2)}) %all-to-all-start.2) | async-done | bytes 262176 | tf_op jit(solution)/shard_map/all_to_all | solution.py:248
  68.2 0.0 collective-permute-done.4.rest_7_
  68.2 0.0 collective-permute-start.9
  68.2 0.5 collective-permute-start.7
  68.7 2.3 %collective-permute-done.7.rest_4_ = bf16[10,128,128]{2,1,0:T(8,128)(2,1)S(1)} collective-permute-done((bf16[10,128,128]{2,1,0:T(8,128)(2,1)}, bf16[10,128,128]{2,1,0:T(8,128)(2,1)S(1)}, u32[]{:S(2)}, u32[]{:S(2)}) %collective-permute-start.7) | collective-permute-done | bytes 327712 | tf_op jit(solution)/shard_map/ppermute | solution.py:251
  71.0 0.0 collective-permute-done.9.rest_8_
  71.0 0.8 copy-done.3
  71.8 3.6 %shard_map.96 = bf16[80,32,128]{2,1,0:T(8,128)(2,1)S(1)} custom-call(f32[32,1,128]{2,1,0:T(1,128)S(1)} %all-to-all-done.notices, bf16[32,32,128]{2,1,0:T(8,128)(2,1)S(1)} %all-to-all-done.2.came, bf16[16,16,128]{2,1,0:T(8,128)(2,1)S(1)} %copy-done.3, bf16[16,16,128]{2,1,0:T(8,128)(2,1)S(1)} %collective-permute-done.5.other, ...), custom_call_target="tpu_custom_call" | custom-call | tf_op jit(solution)/shard_map/pallas_call | solution.py:319
  75.4 18.9 %all_to_all.21 = bf16[80,32,128]{2,1,0:T(8,128)(2,1)S(1)} all-to-all(bf16[80,32,128]{2,1,0:T(8,128)(2,1)S(1)} %shard_map.96), channel_id=1, replica_groups=mesh['xl'=2,'z'=8,'core'=2,'y'=4,'xh'=2] {'xl','y','xh'}, dimensions={0} | all-to-all | bytes 1310720 | tf_op jit(solution)/shard_map/all_to_all | solution.py:248
  94.3 0.7 shard_map.97
  (10 shorter events, 0.0 us)
Async XLA Ops:
  0.0 48.0 %copy-start = (bf16[16,1,256,256]{3,2,1,0:T(8,128)(2,1)S(1)}, bf16[16,1,256,256]{3,2,1,0:T(8,128)(2,1)}, u32[]{:S(2)}) copy-start(bf16[16,1,256,256]{3,2,1,0:T(8,128)(2,1)} %cache.1) | copy-start | bytes 6291460
  0.0 1.9 %collective-permute-start = (bf16[10,128,128]{2,1,0:T(8,128)(2,1)}, bf16[10,128,128]{2,1,0:T(8,128)(2,1)S(1)}, u32[]{:S(2)}, u32[]{:S(2)}) collective-permute-start(bf16[10,128,128]{2,1,0:T(8,128)(2,1)} %first.1), channel_id=1, source_target_pairs={{0,8},{8,0},{1,9},{9,1},{2,10},{10,2},{3,11},{11,3},{4,12},{12,4},... | collective-permute-start | bytes 983048 | tf_op jit(solution)/shard_map/ppermute | solution.py:251
  2.9 24.6 %collective-permute-start.1 = (bf16[20,128,128]{2,1,0:T(8,128)(2,1)S(1)}, bf16[20,128,128]{2,1,0:T(8,128)(2,1)S(1)}, u32[]{:S(2)}, u32[]{:S(2)}) collective-permute-start(bf16[20,128,128]{2,1,0:T(8,128)(2,1)S(1)} %shard_map.92.rest_0_), channel_id=1, source_target_pairs={{0,16},{8,120},{16,32},{24,8},{32,48},{40,24},{48,64},{56,40},{64,... | collective-permute-start | bytes 1966088 | tf_op jit(solution)/shard_map/ppermute | solution.py:259
  4.9 18.3 %collective-permute-start.2 = (bf16[10,128,128]{2,1,0:T(8,128)(2,1)}, bf16[10,128,128]{2,1,0:T(8,128)(2,1)}, u32[]{:S(2)}, u32[]{:S(2)}) collective-permute-start(bf16[10,128,128]{2,1,0:T(8,128)(2,1)} %first.1), channel_id=1, source_target_pairs={{0,32},{8,104},{16,48},{24,120},{32,64},{40,8},{48,80},{56,24},{64... | collective-permute-start | bytes 983048 | tf_op jit(solution)/shard_map/ppermute | solution.py:259
  8.1 19.3 %all-to-all-start = ((f32[32,1,128]{2,1,0:T(1,128)}), f32[32,1,128]{2,1,0:T(1,128)S(1)}, u32[]{:S(2)}, u32[]{:S(2)}) async-start(f32[32,1,128]{2,1,0:T(1,128)} %get-tuple-element.21), calls=%async_computation | async-start | bytes 32768 | tf_op jit(solution)/shard_map/all_to_all | solution.py:248
  28.6 18.7 %collective-permute-start.3 = (bf16[20,128,128]{2,1,0:T(8,128)(2,1)S(1)}, bf16[20,128,128]{2,1,0:T(8,128)(2,1)}, u32[]{:S(2)}, u32[]{:S(2)}) collective-permute-start(bf16[20,128,128]{2,1,0:T(8,128)(2,1)S(1)} %shard_map.93), channel_id=1, source_target_pairs={{0,16},{8,120},{16,32},{24,8},{32,48},{40,24},{48,64},{56,40},{64,... | collective-permute-start | bytes 1966088 | tf_op jit(solution)/shard_map/ppermute | solution.py:259
  47.3 20.9 %collective-permute-start.4 = (bf16[20,128,128]{2,1,0:T(8,128)(2,1)}, bf16[20,128,128]{2,1,0:T(8,128)(2,1)}, u32[]{:S(2)}, u32[]{:S(2)}) collective-permute-start(bf16[20,128,128]{2,1,0:T(8,128)(2,1)} %collective-permute-done.3.rest_5_), channel_id=1, source_target_pairs={{0,16},{8,120},{16,32},{24,8},{32,48},{40,24},{48,64},{56,40},{64,... | collective-permute-start | bytes 1966088 | tf_op jit(solution)/shard_map/ppermute | solution.py:259
  49.5 0.7 copy-start.1
  50.2 0.6 copy-start.2
  50.8 17.4 %all-to-all-start.2 = ((bf16[32,32,128]{2,1,0:T(8,128)(2,1)}), bf16[32,32,128]{2,1,0:T(8,128)(2,1)S(1)}, u32[]{:S(2)}, u32[]{:S(2)}) async-start(bf16[32,32,128]{2,1,0:T(8,128)(2,1)} %copy-done.1), calls=%async_computation.2 | async-start | bytes 524288 | tf_op jit(solution)/shard_map/all_to_all | solution.py:248
  55.0 4.8 %collective-permute-start.5 = (bf16[16,16,128]{2,1,0:T(8,128)(2,1)}, bf16[16,16,128]{2,1,0:T(8,128)(2,1)S(1)}, u32[]{:S(2)}, u32[]{:S(2)}) collective-permute-start(bf16[16,16,128]{2,1,0:T(8,128)(2,1)} %copy-done.2), channel_id=1, source_target_pairs={{0,128},{128,0},{1,129},{129,1},{2,130},{130,2},{3,131},{131,3},{4... | collective-permute-start | bytes 196616 | tf_op jit(solution)/shard_map/ppermute | solution.py:251
  56.9 14.1 %collective-permute-start.6 = (bf16[20,128,128]{2,1,0:T(8,128)(2,1)S(1)}, bf16[20,128,128]{2,1,0:T(8,128)(2,1)S(1)}, u32[]{:S(2)}, u32[]{:S(2)}) collective-permute-start(bf16[20,128,128]{2,1,0:T(8,128)(2,1)S(1)} %collective-permute-done.1.rest_1_), channel_id=1, source_target_pairs={{0,8},{8,0},{1,9},{9,1},{2,10},{10,2},{3,11},{11,3},{4,12},{12,4},... | collective-permute-start | bytes 1966088 | tf_op jit(solution)/shard_map/ppermute | solution.py:251
  56.9 14.1 %collective-permute-start.8 = (bf16[20,128,128]{2,1,0:T(8,128)(2,1)}, bf16[20,128,128]{2,1,0:T(8,128)(2,1)S(1)}, u32[]{:S(2)}, u32[]{:S(2)}) collective-permute-start(bf16[20,128,128]{2,1,0:T(8,128)(2,1)} %collective-permute-done.3.rest_5_), channel_id=1, source_target_pairs={{0,8},{8,0},{1,9},{9,1},{2,10},{10,2},{3,11},{11,3},{4,12},{12,4},... | collective-permute-start | bytes 1966088 | tf_op jit(solution)/shard_map/ppermute | solution.py:251
  68.2 2.8 %collective-permute-start.9 = (bf16[20,128,128]{2,1,0:T(8,128)(2,1)}, bf16[20,128,128]{2,1,0:T(8,128)(2,1)S(1)}, u32[]{:S(2)}, u32[]{:S(2)}) collective-permute-start(bf16[20,128,128]{2,1,0:T(8,128)(2,1)} %collective-permute-done.4.rest_7_), channel_id=1, source_target_pairs={{0,8},{8,0},{1,9},{9,1},{2,10},{10,2},{3,11},{11,3},{4,12},{12,4},... | collective-permute-start | bytes 1966088 | tf_op jit(solution)/shard_map/ppermute | solution.py:251
  68.2 2.8 %collective-permute-start.7 = (bf16[10,128,128]{2,1,0:T(8,128)(2,1)}, bf16[10,128,128]{2,1,0:T(8,128)(2,1)S(1)}, u32[]{:S(2)}, u32[]{:S(2)}) collective-permute-start(bf16[10,128,128]{2,1,0:T(8,128)(2,1)} %collective-permute-done.2.second.rest_3_), channel_id=1, source_target_pairs={{0,8},{8,0},{1,9},{9,1},{2,10},{10,2},{3,11},{11,3},{4,12},{12,4},... | collective-permute-start | bytes 983048 | tf_op jit(solution)/shard_map/ppermute | solution.py:251
  71.0 0.8 copy-start.3

commit v4 on v3

--- a/solution.py
+++ b/solution.py
@@ -95,7 +95,8 @@
 
 
 def join_body(first, second, out, sems):
-    copy_in([(first, out.at[:OWN]), (second, out.at[OWN:])], sems)
+    n = first.shape[0]
+    copy_in([(first.at[n - OWN :], out.at[:OWN]), (second.at[:OWN], out.at[OWN:])], sems)
 
 
 def at(notices, rep, lane):
@@ -206,20 +207,20 @@
             for n in range(lo, lo + 5):
                 total[at(notices, src, COL + n)] += products[n - lo]
 
-    own, one, one_sib, two_a, two_a_sib, mid, mid_sib, last, last_sib = arrays
+    own, one, one_sib, two, two_sib, three, three_sib, last, last_sib = arrays
     run(own, 0, z, core)
     run(own, OWN, z, 1 - core)
     for line, a, b, c, d in (
-        (core, one, two_a, mid, last),
-        (1 - core, one_sib, two_a_sib, mid_sib, last_sib),
+        (core, one, two, three, last),
+        (1 - core, one_sib, two_sib, three_sib, last_sib),
     ):
         away = 1 - 2 * line
         far = [lax.rem(z - away * step + Z, Z) for step in range(Z // 2 + 1)]
         run(a, 0, far[1], line)
         run(a, OWN, far[1], 1 - line)
         run(b, 0, far[2], line)
-        run(c, 0, far[2], 1 - line)
-        run(c, OWN, far[3], line)
+        run(b, OWN, far[2], 1 - line)
+        run(c, 0, far[3], line)
         run(d, 0, far[3], 1 - line)
         run(d, OWN, far[4], line)
     out[:COLS] = total[:, :ROWS, :].astype(BF16)
@@ -258,7 +259,6 @@
         ]
         return lax.ppermute(x, ("z", "core"), pairs)
 
-    two_a = around(codes, 2)
     sib = swap(codes, "core")
     given = [
         departing,
@@ -291,18 +291,18 @@
 
     one = around(own, 1)
     notices = exchange(notice, rep_axes)
-    one, two_a, notices = lax.optimization_barrier((one, two_a, notices))
-
-    mid = around(join(one[OWN:], two_a), 1)
-    one_sib, two_a_sib = swap(one, "core"), swap(two_a, "core")
+    one, notices = lax.optimization_barrier((one, notices))
+
+    two, three = around(one, 1), around(one[:OWN], 2)
+    one_sib = swap(one, "core")
     to_pull = call(
         pull_body, jax.ShapeDtypeStruct((REP, PACK, HD), BF16), [smem(), vmem()]
     )(notices, packs)
     pulled = exchange(to_pull, rep_axes)
-    mid, pulled = lax.optimization_barrier((mid, pulled))
-
-    last = around(mid, 1)
-    mid_sib = swap(mid, "core")
+    two, three, pulled = lax.optimization_barrier((two, three, pulled))
+
+    last = around(join(two, three), 1)
+    two_sib, three_sib = swap(two, "core"), swap(three, "core")
     send, mine = call(
         attend_body,
         [
@@ -315,7 +315,7 @@
     other = swap(mine, "xl")
     came = exchange(send, rep_axes)
     last, came, other = lax.optimization_barrier((last, came, other))
-    arrays = [own, one, one_sib, two_a, two_a_sib, mid, mid_sib, last, swap(last, "core")]
+    arrays = [own, one, one_sib, two, two_sib, three, three_sib, last, swap(last, "core")]
     parts = call(
         project_body,
         jax.ShapeDtypeStruct((XL * COLS, ROWS, HD), BF16),

time: 96.2 us -> 94 us (0.977)
  blocking collectives: 36.5 us -> 56.3 us
  waiting for transfers between devices: 25.3 us -> 13.6 us
  starting transfers between devices: 20.2 us -> 12.2 us
  local copies, waits for them, and re-layouts: 2.16 us -> 0.03 us
    all_to_all x2 -> x3, blocking collectives: 36.5 us -> 56.3 us  [exchange(): return lax.all_to_all(x, axes, split_axis=0, concat_axis=0, tiled=True)]
    ppermute x4, waiting for transfers between devices: 7.91 us -> 0.01 us  [around(): return lax.ppermute(x, ('z', 'core'), pairs)]
    all_to_all x2 -> x1, starting transfers between devices: 11.3 us -> 4.8 us  [exchange(): return lax.all_to_all(x, axes, split_axis=0, concat_axis=0, tiled=True)]
    all_to_all x2 -> x1, waiting for transfers between devices: 12.6 us -> 8.41 us  [exchange(): return lax.all_to_all(x, axes, split_axis=0, concat_axis=0, tiled=True)]
    unnamed x8 -> x2, local copies, waits for them, and re-layouts: 2.14 us -> 0.01 us
    ppermute x4, starting transfers between devices: 6.06 us -> 4.54 us  [around(): return lax.ppermute(x, ('z', 'core'), pairs)]
  transfers between devices with their start and end apart: 12 -> 11, of which waited for: 5 -> 4; matrix products, arithmetic and copies ran while one was open for 0% -> 0% of each run, Pallas kernels for 5% -> 5%
where the time goes in v4:
time: 94 us; the launch traced here: 93 us
  blocking collectives  56.3 us (60%)
  waiting for transfers between devices  13.6 us (14%)
  starting transfers between devices  12.2 us (13%)
  Pallas kernels  10.8 us (11%)
    all_to_all x3, blocking collectives, exchange(): return lax.all_to_all(x, axes, split_axis=0, concat_axis=0, tiled=True)  56.3 us
    all_to_all x1, waiting for transfers between devices, exchange(): return lax.all_to_all(x, axes, split_axis=0, concat_axis=0, tiled=True)  8.41 us
    ppermute x6, waiting for transfers between devices, swap(): return lax.ppermute(x, axis, [(0, 1), (1, 0)])  5.16 us
    all_to_all x1, starting transfers between devices, exchange(): return lax.all_to_all(x, axes, split_axis=0, concat_axis=0, tiled=True)  4.8 us
    ppermute x4, starting transfers between devices, around(): return lax.ppermute(x, ('z', 'core'), pairs)  4.54 us
    pallas_call x1, Pallas kernels, shards(): call(project_body, jax.ShapeDtypeStruct((XL * COLS, ROWS, HD), BF16), [sm...  3.48 us
    ppermute x6, starting transfers between devices, swap(): return lax.ppermute(x, axis, [(0, 1), (1, 0)])  2.91 us
    pallas_call x1, Pallas kernels, shards(): call(attend_body, [jax.ShapeDtypeStruct((REP, 2 * per, HD), BF16), jax.Sh...  2.19 us
  transfers between devices with their start and end apart: 11, of which 4 were waited for; matrix products, arithmetic and copies ran while one was open for 0% of the time, Pallas kernels for 5%

profile of v4, /device:TPU:8, one launch (start us, length us, event | category | flops | bytes accessed | tf_op | source)
XLA Modules:
  0.0 93.0 jit_solution(17189510404565613878)
XLA Ops:
  0.0 0.0 collective-permute-start
  0.0 1.1 %shard_map.91 = (f32[32,1,128]{2,1,0:T(1,128)S(1)}, bf16[16,20,128]{2,1,0:T(8,128)(2,1)S(1)}) custom-call(s32[1]{0:T(128)} %bitcast.place, s32[1,13]{1,0:T(1,128)} %refs_0_.1, s32[1,13]{1,0:T(1,128)} %refs_1_.1, s32[16]{0:T(128)} %refs_2_.1, s32[10]{0:T(128)} %refs_3_.1, f32[10]{0:T(128)} %refs_4_.1, bf16[2,16,8,128]{3,2,1,0:T(8,128)(2,1)} %refs_5_.1, ...), custom_call_target="tpu_custom_call" | custom-call | tf_op jit(solution)/shard_map/pallas_call | solution.py:272
  1.1 0.7 collective-permute-done.second
  1.8 1.1 %shard_map.92.rest_0_ = bf16[20,128,128]{2,1,0:T(8,128)(2,1)S(1)} custom-call(bf16[10,128,128]{2,1,0:T(8,128)(2,1)} %first.1, bf16[10,128,128]{2,1,0:T(8,128)(2,1)S(1)} %collective-permute-done.second), custom_call_target="tpu_custom_call" | custom-call | tf_op jit(solution)/shard_map/pallas_call | solution.py:290
  3.0 2.0 %collective-permute-start.1 = (bf16[20,128,128]{2,1,0:T(8,128)(2,1)S(1)}, bf16[20,128,128]{2,1,0:T(8,128)(2,1)S(1)}, u32[]{:S(2)}, u32[]{:S(2)}) collective-permute-start(bf16[20,128,128]{2,1,0:T(8,128)(2,1)S(1)} %shard_map.92.rest_0_), channel_id=1, source_target_pairs={{0,16},{8,120},{16,32},{24,8},{32,48},{40,24},{48,64},{56,40},{64,... | collective-permute-start | bytes 1966088 | tf_op jit(solution)/shard_map/ppermute | solution.py:260
  5.0 17.0 %all_to_all.20.notices = f32[32,1,128]{2,1,0:T(1,128)S(1)} all-to-all(f32[32,1,128]{2,1,0:T(1,128)S(1)} %get-tuple-element.21), channel_id=1, replica_groups=mesh['xl'=2,'z'=8,'core'=2,'y'=4,'xh'=2] {'xl','z','core'}, dimensions={0} | all-to-all | bytes 32768 | tf_op jit(solution)/shard_map/all_to_all | solution.py:249
  22.0 0.0 collective-permute-done.1.rest_1_
  22.0 0.6 collective-permute-start.2
  22.7 0.6 collective-permute-start.3
  23.3 1.1 %shard_map.93 = bf16[32,20,128]{2,1,0:T(8,128)(2,1)S(1)} custom-call(f32[32,1,128]{2,1,0:T(1,128)S(1)} %all_to_all.20.notices, bf16[16,20,128]{2,1,0:T(8,128)(2,1)S(1)} %get-tuple-element.24.packs), custom_call_target="tpu_custom_call" | custom-call | tf_op jit(solution)/shard_map/pallas_call | solution.py:298
  24.4 20.5 %all_to_all.21.pulled = bf16[32,20,128]{2,1,0:T(8,128)(2,1)S(1)} all-to-all(bf16[32,20,128]{2,1,0:T(8,128)(2,1)S(1)} %shard_map.93), channel_id=1, replica_groups=mesh['xl'=2,'z'=8,'core'=2,'y'=4,'xh'=2] {'xl','z','core'}, dimensions={0} | all-to-all | bytes 327680 | tf_op jit(solution)/shard_map/all_to_all | solution.py:249
  44.9 0.0 collective-permute-done.3.second.rest_5_
  44.9 0.0 collective-permute-done.2.first.rest_3_
  44.9 1.1 %shard_map.94 = bf16[20,128,128]{2,1,0:T(8,128)(2,1)} custom-call(bf16[20,128,128]{2,1,0:T(8,128)(2,1)S(1)} %collective-permute-done.2.first.rest_3_, bf16[10,128,128]{2,1,0:T(8,128)(2,1)S(1)} %collective-permute-done.3.second.rest_5_), custom_call_target="tpu_custom_call" | custom-call | tf_op jit(solution)/shard_map/pallas_call | solution.py:304
  46.0 1.3 %collective-permute-start.4 = (bf16[20,128,128]{2,1,0:T(8,128)(2,1)}, bf16[20,128,128]{2,1,0:T(8,128)(2,1)S(1)}, u32[]{:S(2)}, u32[]{:S(2)}) collective-permute-start(bf16[20,128,128]{2,1,0:T(8,128)(2,1)} %shard_map.94), channel_id=1, source_target_pairs={{0,16},{8,120},{16,32},{24,8},{32,48},{40,24},{48,64},{56,40},{64,... | collective-permute-start | bytes 1966088 | tf_op jit(solution)/shard_map/ppermute | solution.py:260
  47.3 2.2 %shard_map.95 = (bf16[32,32,128]{2,1,0:T(8,128)(2,1)}, bf16[16,16,128]{2,1,0:T(8,128)(2,1)S(1)}) custom-call(f32[32,1,128]{2,1,0:T(1,128)S(1)} %all_to_all.20.notices, bf16[32,20,128]{2,1,0:T(8,128)(2,1)S(1)} %all_to_all.21.pulled, bf16[16,20,128]{2,1,0:T(8,128)(2,1)S(1)} %get-tuple-element.24.packs, bf16[16,1,256,256]{3,2,1,0:T(8,128)(2,1)S(1)} %copy-done), custom_call_target="tpu_custom_call" | custom-call | tf_op jit(solution)/shard_map/pallas_call | solution.py:306
  49.5 4.8 %all-to-all-start.2 = ((bf16[32,32,128]{2,1,0:T(8,128)(2,1)}), bf16[32,32,128]{2,1,0:T(8,128)(2,1)S(1)}, u32[]{:S(2)}, u32[]{:S(2)}) async-start(bf16[32,32,128]{2,1,0:T(8,128)(2,1)} %get-tuple-element.28), calls=%async_computation.2 | async-start | bytes 524288 | tf_op jit(solution)/shard_map/all_to_all | solution.py:249
  54.3 1.9 %collective-permute-start.5 = (bf16[16,16,128]{2,1,0:T(8,128)(2,1)S(1)}, bf16[16,16,128]{2,1,0:T(8,128)(2,1)S(1)}, u32[]{:S(2)}, u32[]{:S(2)}) collective-permute-start(bf16[16,16,128]{2,1,0:T(8,128)(2,1)S(1)} %get-tuple-element.29.mine), channel_id=1, source_target_pairs={{0,128},{128,0},{1,129},{129,1},{2,130},{130,2},{3,131},{131,3},{4... | collective-permute-start | bytes 196616 | tf_op jit(solution)/shard_map/ppermute | solution.py:252
  56.2 0.0 collective-permute-start.6
  56.2 0.5 collective-permute-start.7
  56.7 2.4 %collective-permute-done.5.other = bf16[16,16,128]{2,1,0:T(8,128)(2,1)S(1)} collective-permute-done((bf16[16,16,128]{2,1,0:T(8,128)(2,1)S(1)}, bf16[16,16,128]{2,1,0:T(8,128)(2,1)S(1)}, u32[]{:S(2)}, u32[]{:S(2)}) %collective-permute-start.5) | collective-permute-done | bytes 65568 | tf_op jit(solution)/shard_map/ppermute | solution.py:252
  59.0 8.4 %all-to-all-done.2.came = bf16[32,32,128]{2,1,0:T(8,128)(2,1)S(1)} async-done(((bf16[32,32,128]{2,1,0:T(8,128)(2,1)}), bf16[32,32,128]{2,1,0:T(8,128)(2,1)S(1)}, u32[]{:S(2)}, u32[]{:S(2)}) %all-to-all-start.2) | async-done | bytes 262176 | tf_op jit(solution)/shard_map/all_to_all | solution.py:249
  67.4 0.0 collective-permute-done.4.rest_7_
  67.4 0.0 collective-permute-start.9
  67.4 0.5 collective-permute-start.8
  67.9 0.0 collective-permute-done.6.rest_2_
  68.0 2.1 %collective-permute-done.8.rest_6_ = bf16[10,128,128]{2,1,0:T(8,128)(2,1)S(1)} collective-permute-done((bf16[10,128,128]{2,1,0:T(8,128)(2,1)S(1)}, bf16[10,128,128]{2,1,0:T(8,128)(2,1)S(1)}, u32[]{:S(2)}, u32[]{:S(2)}) %collective-permute-start.8) | collective-permute-done | bytes 327712 | tf_op jit(solution)/shard_map/ppermute | solution.py:252
  70.0 0.0 collective-permute-done.7.rest_4_
  70.0 0.0 collective-permute-done.9.rest_8_
  70.0 3.5 %shard_map.96 = bf16[80,32,128]{2,1,0:T(8,128)(2,1)S(1)} custom-call(f32[32,1,128]{2,1,0:T(1,128)S(1)} %all_to_all.20.notices, bf16[32,32,128]{2,1,0:T(8,128)(2,1)S(1)} %all-to-all-done.2.came, bf16[16,16,128]{2,1,0:T(8,128)(2,1)S(1)} %get-tuple-element.29.mine, bf16[16,16,128]{2,1,0:T(8,128)(2,1)S(1)} %collective-permute-done.5.other, ...), custom_call_target="tpu_custom_call" | custom-call | tf_op jit(solution)/shard_map/pallas_call | solution.py:319
  73.5 18.7 %all_to_all.22 = bf16[80,32,128]{2,1,0:T(8,128)(2,1)S(1)} all-to-all(bf16[80,32,128]{2,1,0:T(8,128)(2,1)S(1)} %shard_map.96), channel_id=1, replica_groups=mesh['xl'=2,'z'=8,'core'=2,'y'=4,'xh'=2] {'xl','y','xh'}, dimensions={0} | all-to-all | bytes 1310720 | tf_op jit(solution)/shard_map/all_to_all | solution.py:249
  92.2 0.7 shard_map.97
  (3 shorter events, 0.0 us)
Async XLA Ops:
  0.0 1.8 %collective-permute-start = (bf16[10,128,128]{2,1,0:T(8,128)(2,1)}, bf16[10,128,128]{2,1,0:T(8,128)(2,1)S(1)}, u32[]{:S(2)}, u32[]{:S(2)}) collective-permute-start(bf16[10,128,128]{2,1,0:T(8,128)(2,1)} %first.1), channel_id=1, source_target_pairs={{0,8},{8,0},{1,9},{9,1},{2,10},{10,2},{3,11},{11,3},{4,12},{12,4},... | collective-permute-start | bytes 983048 | tf_op jit(solution)/shard_map/ppermute | solution.py:252
  1.8 45.4 %copy-start = (bf16[16,1,256,256]{3,2,1,0:T(8,128)(2,1)S(1)}, bf16[16,1,256,256]{3,2,1,0:T(8,128)(2,1)}, u32[]{:S(2)}) copy-start(bf16[16,1,256,256]{3,2,1,0:T(8,128)(2,1)} %cache.1) | copy-start | bytes 6291460
  3.0 19.0 %collective-permute-start.1 = (bf16[20,128,128]{2,1,0:T(8,128)(2,1)S(1)}, bf16[20,128,128]{2,1,0:T(8,128)(2,1)S(1)}, u32[]{:S(2)}, u32[]{:S(2)}) collective-permute-start(bf16[20,128,128]{2,1,0:T(8,128)(2,1)S(1)} %shard_map.92.rest_0_), channel_id=1, source_target_pairs={{0,16},{8,120},{16,32},{24,8},{32,48},{40,24},{48,64},{56,40},{64,... | collective-permute-start | bytes 1966088 | tf_op jit(solution)/shard_map/ppermute | solution.py:260
  22.0 22.9 %collective-permute-start.2 = (bf16[20,128,128]{2,1,0:T(8,128)(2,1)S(1)}, bf16[20,128,128]{2,1,0:T(8,128)(2,1)S(1)}, u32[]{:S(2)}, u32[]{:S(2)}) collective-permute-start(bf16[20,128,128]{2,1,0:T(8,128)(2,1)S(1)} %collective-permute-done.1.rest_1_), channel_id=1, source_target_pairs={{0,16},{8,120},{16,32},{24,8},{32,48},{40,24},{48,64},{56,40},{64,... | collective-permute-start | bytes 1966088 | tf_op jit(solution)/shard_map/ppermute | solution.py:260
  22.7 22.2 %collective-permute-start.3 = (bf16[10,128,128]{2,1,0:T(8,128)(2,1)S(1)}, bf16[10,128,128]{2,1,0:T(8,128)(2,1)S(1)}, u32[]{:S(2)}, u32[]{:S(2)}) collective-permute-start(bf16[10,128,128]{2,1,0:T(8,128)(2,1)S(1)} %slice.3), channel_id=1, source_target_pairs={{0,32},{8,104},{16,48},{24,120},{32,64},{40,8},{48,80},{56,24},{64... | collective-permute-start | bytes 983048 | tf_op jit(solution)/shard_map/ppermute | solution.py:260
  46.0 21.4 %collective-permute-start.4 = (bf16[20,128,128]{2,1,0:T(8,128)(2,1)}, bf16[20,128,128]{2,1,0:T(8,128)(2,1)S(1)}, u32[]{:S(2)}, u32[]{:S(2)}) collective-permute-start(bf16[20,128,128]{2,1,0:T(8,128)(2,1)} %shard_map.94), channel_id=1, source_target_pairs={{0,16},{8,120},{16,32},{24,8},{32,48},{40,24},{48,64},{56,40},{64,... | collective-permute-start | bytes 1966088 | tf_op jit(solution)/shard_map/ppermute | solution.py:260
  49.5 18.0 %all-to-all-start.2 = ((bf16[32,32,128]{2,1,0:T(8,128)(2,1)}), bf16[32,32,128]{2,1,0:T(8,128)(2,1)S(1)}, u32[]{:S(2)}, u32[]{:S(2)}) async-start(bf16[32,32,128]{2,1,0:T(8,128)(2,1)} %get-tuple-element.28), calls=%async_computation.2 | async-start | bytes 524288 | tf_op jit(solution)/shard_map/all_to_all | solution.py:249
  54.3 4.8 %collective-permute-start.5 = (bf16[16,16,128]{2,1,0:T(8,128)(2,1)S(1)}, bf16[16,16,128]{2,1,0:T(8,128)(2,1)S(1)}, u32[]{:S(2)}, u32[]{:S(2)}) collective-permute-start(bf16[16,16,128]{2,1,0:T(8,128)(2,1)S(1)} %get-tuple-element.29.mine), channel_id=1, source_target_pairs={{0,128},{128,0},{1,129},{129,1},{2,130},{130,2},{3,131},{131,3},{4... | collective-permute-start | bytes 196616 | tf_op jit(solution)/shard_map/ppermute | solution.py:252
  56.2 11.8 %collective-permute-start.6 = (bf16[20,128,128]{2,1,0:T(8,128)(2,1)S(1)}, bf16[20,128,128]{2,1,0:T(8,128)(2,1)}, u32[]{:S(2)}, u32[]{:S(2)}) collective-permute-start(bf16[20,128,128]{2,1,0:T(8,128)(2,1)S(1)} %collective-permute-done.1.rest_1_), channel_id=1, source_target_pairs={{0,8},{8,0},{1,9},{9,1},{2,10},{10,2},{3,11},{11,3},{4,12},{12,4},... | collective-permute-start | bytes 1966088 | tf_op jit(solution)/shard_map/ppermute | solution.py:252
  56.2 13.8 %collective-permute-start.7 = (bf16[20,128,128]{2,1,0:T(8,128)(2,1)S(1)}, bf16[20,128,128]{2,1,0:T(8,128)(2,1)}, u32[]{:S(2)}, u32[]{:S(2)}) collective-permute-start(bf16[20,128,128]{2,1,0:T(8,128)(2,1)S(1)} %collective-permute-done.2.first.rest_3_), channel_id=1, source_target_pairs={{0,8},{8,0},{1,9},{9,1},{2,10},{10,2},{3,11},{11,3},{4,12},{12,4},... | collective-permute-start | bytes 1966088 | tf_op jit(solution)/shard_map/ppermute | solution.py:252
  67.4 2.6 %collective-permute-start.9 = (bf16[20,128,128]{2,1,0:T(8,128)(2,1)S(1)}, bf16[20,128,128]{2,1,0:T(8,128)(2,1)S(1)}, u32[]{:S(2)}, u32[]{:S(2)}) collective-permute-start(bf16[20,128,128]{2,1,0:T(8,128)(2,1)S(1)} %collective-permute-done.4.rest_7_), channel_id=1, source_target_pairs={{0,8},{8,0},{1,9},{9,1},{2,10},{10,2},{3,11},{11,3},{4,12},{12,4},... | collective-permute-start | bytes 1966088 | tf_op jit(solution)/shard_map/ppermute | solution.py:252
  67.4 2.6 %collective-permute-start.8 = (bf16[10,128,128]{2,1,0:T(8,128)(2,1)S(1)}, bf16[10,128,128]{2,1,0:T(8,128)(2,1)S(1)}, u32[]{:S(2)}, u32[]{:S(2)}) collective-permute-start(bf16[10,128,128]{2,1,0:T(8,128)(2,1)S(1)} %collective-permute-done.3.second.rest_5_), channel_id=1, source_target_pairs={{0,8},{8,0},{1,9},{9,1},{2,10},{10,2},{3,11},{11,3},{4,12},{12,4},... | collective-permute-start | bytes 983048 | tf_op jit(solution)/shard_map/ppermute | solution.py:252

commit v5 on v2

--- a/solution.py
+++ b/solution.py
@@ -92,10 +92,6 @@
             + [fresh[t, s : s + 1, j * HD : (j + 1) * HD] for t in range(STEPS) for j in range(2)],
             axis=0,
         )
-
-
-def join_body(first, second, out, sems):
-    copy_in([(first, out.at[:OWN]), (second, out.at[OWN:])], sems)
 
 
 def at(notices, rep, lane):
@@ -189,7 +185,6 @@
                     pl.ds(side * SLOTS * per + t * HEADS + h, SLOTS, stride=per), :
                 ].astype(BF16)
     total[...] = jnp.zeros_like(total)
-    away = 1 - 2 * core
 
     def run(blocks, first, z_src, core_src):
         src = (xl * Z + z_src) * CORE + core_src
@@ -207,19 +202,17 @@
             for n in range(lo, lo + 5):
                 total[at(notices, src, COL + n)] += products[n - lo]
 
-    run(arrays[0], 0, z, core)
-    run(arrays[0], OWN, z, 1 - core)
-    for step in range(1, Z // 2):
-        from_z = lax.rem(z - away * step + Z, Z)
-        sib_z = lax.rem(z + away * step + Z, Z)
-        a, b = arrays[2 * step - 1], arrays[2 * step]
-        run(a, 0, from_z, core)
-        run(a, OWN, from_z, 1 - core)
-        run(b, 0, sib_z, 1 - core)
-        run(b, OWN, sib_z, core)
-    far = lax.rem(z + Z // 2, Z)
-    run(arrays[Z - 1], 0, far, core)
-    run(arrays[Z], 0, far, 1 - core)
+    half = Z // 2
+    for line, same, cross in (
+        (core, arrays[: half + 1], arrays[half + 1 : Z + 1]),
+        (1 - core, (None, *arrays[Z + 1 : Z + half + 1]), (None, *arrays[Z + half + 1 :])),
+    ):
+        for step in range(half + 1):
+            far = lax.rem(z - (1 - 2 * line) * step + Z, Z)
+            if same[step] is not None:
+                run(same[step], 0, far, line)
+            if step < half and cross[step] is not None:
+                run(cross[step], 0, far, 1 - line)
     out[:COLS] = total[:, :ROWS, :].astype(BF16)
     out[COLS:] = total[:, ROWS:, :].astype(BF16)
 
@@ -277,28 +270,17 @@
         + [pltpu.VMEM(a.shape, a.dtype) for a in given[5:]]
         + [pltpu.SemaphoreType.DMA((len(given),))],
     )(base.astype(I32)[None], *(in_hbm(a) for a in given))
-    own = call(
-        join_body,
-        jax.ShapeDtypeStruct((CORE * OWN, HD, HD), BF16),
-        [pl.BlockSpec(memory_space=pl.ANY)] * 2,
-        [pltpu.SemaphoreType.DMA((2,))],
-    )(in_hbm(codes), sib)
-
-    one = around(own, 1)
+    near, near_x = around(codes, 1), around(sib, 1)
     notices = exchange(notice, rep_axes)
-    one, notices = lax.optimization_barrier((one, notices))
-
-    two = around(one, 1)
-    one_sib = swap(one, "core")
+    near, notices = lax.optimization_barrier((near, notices))
+    two, two_x = around(near, 1), around(near_x, 1)
+    near_sib, near_x_sib = swap(near, "core"), swap(near_x, "core")
     to_pull = call(
         pull_body, jax.ShapeDtypeStruct((REP, PACK, HD), BF16), [smem(), vmem()]
     )(notices, packs)
     pulled = exchange(to_pull, rep_axes)
-    two, pulled = lax.optimization_barrier((two, pulled))
-
-    four = around(two[:OWN], 2)
-    three = around(two, 1)
-    two_sib = swap(two, "core")
+    three, three_x = around(two, 1), around(two_x, 1)
+    two_sib, two_x_sib = swap(two, "core"), swap(two_x, "core")
     send, mine = call(
         attend_body,
         [
@@ -310,8 +292,11 @@
     )(notices, pulled, packs, kv_cache)
     other = swap(mine, "xl")
     came = exchange(send, rep_axes)
-    three, four, came, other = lax.optimization_barrier((three, four, came, other))
-    arrays = [own, one, one_sib, two, two_sib, three, swap(three, "core"), four, swap(four, "core")]
+    four = around(three, 1)
+    three_sib, three_x_sib = swap(three, "core"), swap(three_x, "core")
+    four_sib = around(three_x, 1)
+    arrays = [codes, near, two, three, four, sib, near_x, two_x, three_x]
+    arrays += [near_sib, two_sib, three_sib, four_sib, near_x_sib, two_x_sib, three_x_sib]
     parts = call(
         project_body,
         jax.ShapeDtypeStruct((XL * COLS, ROWS, HD), BF16),

time: 91.5 us -> 89.8 us (0.981)
  blocking collectives: 51.6 us -> 34.2 us
  starting transfers between devices: 13.2 us -> 24.2 us
  waiting for transfers between devices: 16 us -> 19 us
    all_to_all x3 -> x2, blocking collectives: 51.6 us -> 34.2 us  [exchange(): return lax.all_to_all(x, axes, split_axis=0, concat_axis=0, tiled=True)]
    all_to_all x1 -> x2, waiting for transfers between devices: 0.01 us -> 11.8 us  [exchange(): return lax.all_to_all(x, axes, split_axis=0, concat_axis=0, tiled=True)]
    all_to_all x1 -> x2, starting transfers between devices: 4.15 us -> 9.1 us  [exchange(): return lax.all_to_all(x, axes, split_axis=0, concat_axis=0, tiled=True)]
    ppermute x6 -> x8, waiting for transfers between devices: 7.45 us -> 2.87 us  [swap(): return lax.ppermute(x, axis, [(0, 1), (1, 0)])]
    ppermute x4 -> x8, waiting for transfers between devices: 8.56 us -> 4.32 us  [around(): return lax.ppermute(x, ('z', 'core'), pairs)]
    ppermute x4 -> x8, starting transfers between devices: 6.23 us -> 10.2 us  [around(): return lax.ppermute(x, ('z', 'core'), pairs)]
    ppermute x6 -> x8, starting transfers between devices: 2.84 us -> 4.89 us  [swap(): return lax.ppermute(x, axis, [(0, 1), (1, 0)])]
    pallas_call x1 -> x0, Pallas kernels: 0.99 us -> none  [shards(): call(join_body, jax.ShapeDtypeStruct((CORE * OWN, HD, HD), BF16), [pl.Blo...]
  transfers between devices with their start and end apart: 11 -> 18, of which waited for: 4 -> 6; matrix products, arithmetic and copies ran while one was open for 0% -> 0% of each run, Pallas kernels for 4% -> 6%
where the time goes in v5:
time: 89.8 us; the launch traced here: 88.5 us
  blocking collectives  34.2 us (38%)
  starting transfers between devices  24.2 us (27%)
  waiting for transfers between devices  19 us (21%)
  Pallas kernels  9.52 us (11%)
  local copies, waits for them, and re-layouts  1.59 us (2%)
    all_to_all x2, blocking collectives, exchange(): return lax.all_to_all(x, axes, split_axis=0, concat_axis=0, tiled=True)  34.2 us
    all_to_all x2, waiting for transfers between devices, exchange(): return lax.all_to_all(x, axes, split_axis=0, concat_axis=0, tiled=True)  11.8 us
    ppermute x8, starting transfers between devices, around(): return lax.ppermute(x, ('z', 'core'), pairs)  10.2 us
    all_to_all x2, starting transfers between devices, exchange(): return lax.all_to_all(x, axes, split_axis=0, concat_axis=0, tiled=True)  9.1 us
    ppermute x8, starting transfers between devices, swap(): return lax.ppermute(x, axis, [(0, 1), (1, 0)])  4.89 us
    ppermute x8, waiting for transfers between devices, around(): return lax.ppermute(x, ('z', 'core'), pairs)  4.32 us
    pallas_call x1, Pallas kernels, shards(): call(project_body, jax.ShapeDtypeStruct((XL * COLS, ROWS, HD), BF16), [sm...  3.77 us
    ppermute x8, waiting for transfers between devices, swap(): return lax.ppermute(x, axis, [(0, 1), (1, 0)])  2.87 us
  transfers between devices with their start and end apart: 18, of which 6 were waited for; matrix products, arithmetic and copies ran while one was open for 0% of the time, Pallas kernels for 6%

profile of v5, /device:TPU:8, one launch (start us, length us, event | category | flops | bytes accessed | tf_op | source)
XLA Modules:
  0.0 88.5 jit_solution(16076228394915180314)
XLA Ops:
  0.0 2.0 %collective-permute-start = (bf16[10,128,128]{2,1,0:T(8,128)(2,1)}, bf16[10,128,128]{2,1,0:T(8,128)(2,1)S(1)}, u32[]{:S(2)}, u32[]{:S(2)}) collective-permute-start(bf16[10,128,128]{2,1,0:T(8,128)(2,1)} %rest_0_.1), channel_id=1, source_target_pairs={{0,16},{8,120},{16,32},{24,8},{32,48},{40,24},{48,64},{56,40},{64,... | collective-permute-start | bytes 983048 | tf_op jit(solution)/shard_map/ppermute | solution.py:250
  2.0 0.0 collective-permute-done.5.rest_5_
  2.0 1.9 %collective-permute-start.6 = (bf16[10,128,128]{2,1,0:T(8,128)(2,1)S(1)}, bf16[10,128,128]{2,1,0:T(8,128)(2,1)S(1)}, u32[]{:S(2)}, u32[]{:S(2)}) collective-permute-start(bf16[10,128,128]{2,1,0:T(8,128)(2,1)S(1)} %collective-permute-done.5.rest_5_), channel_id=1, source_target_pairs={{0,16},{8,120},{16,32},{24,8},{32,48},{40,24},{48,64},{56,40},{64,... | collective-permute-start | bytes 983048 | tf_op jit(solution)/shard_map/ppermute | solution.py:250
  3.9 1.1 %shard_map.91 = (f32[32,1,128]{2,1,0:T(1,128)S(1)}, bf16[16,20,128]{2,1,0:T(8,128)(2,1)S(1)}) custom-call(s32[1]{0:T(128)} %bitcast.place, s32[1,13]{1,0:T(1,128)} %refs_0_.1, s32[1,13]{1,0:T(1,128)} %refs_1_.1, s32[16]{0:T(128)} %refs_2_.1, s32[10]{0:T(128)} %refs_3_.1, f32[10]{0:T(128)} %refs_4_.1, bf16[2,16,8,128]{3,2,1,0:T(8,128)(2,1)} %refs_5_.1, ...), custom_call_target="tpu_custom_call" | custom-call | tf_op jit(solution)/shard_map/pallas_call | solution.py:262
  5.0 16.9 %all_to_all.20.notices = f32[32,1,128]{2,1,0:T(1,128)S(1)} all-to-all(f32[32,1,128]{2,1,0:T(1,128)S(1)} %get-tuple-element.11), channel_id=1, replica_groups=mesh['xl'=2,'z'=8,'core'=2,'y'=4,'xh'=2] {'xl','z','core'}, dimensions={0} | all-to-all | bytes 32768 | tf_op jit(solution)/shard_map/all_to_all | solution.py:239
  21.9 0.6 collective-permute-start.2
  22.5 0.0 collective-permute-done.6.rest_6_
  22.5 0.5 collective-permute-start.7
  23.1 1.8 %shard_map.92 = bf16[32,20,128]{2,1,0:T(8,128)(2,1)} custom-call(f32[32,1,128]{2,1,0:T(1,128)S(1)} %all_to_all.20.notices, bf16[16,20,128]{2,1,0:T(8,128)(2,1)S(1)} %get-tuple-element.13.packs), custom_call_target="tpu_custom_call" | custom-call | tf_op jit(solution)/shard_map/pallas_call | solution.py:278
  24.8 5.2 %all-to-all-start.1 = ((bf16[32,20,128]{2,1,0:T(8,128)(2,1)}), bf16[32,20,128]{2,1,0:T(8,128)(2,1)S(1)}, u32[]{:S(2)}, u32[]{:S(2)}) async-start(bf16[32,20,128]{2,1,0:T(8,128)(2,1)} %shard_map.92), calls=%async_computation.1 | async-start | bytes 393216 | tf_op jit(solution)/shard_map/all_to_all | solution.py:239
  30.1 0.4 collective-permute-start.9
  30.4 1.7 %collective-permute-start.3 = (bf16[10,128,128]{2,1,0:T(8,128)(2,1)S(1)}, bf16[10,128,128]{2,1,0:T(8,128)(2,1)S(1)}, u32[]{:S(2)}, u32[]{:S(2)}) collective-permute-start(bf16[10,128,128]{2,1,0:T(8,128)(2,1)S(1)} %collective-permute-done.2.rest_2_), channel_id=1, source_target_pairs={{0,16},{8,120},{16,32},{24,8},{32,48},{40,24},{48,64},{56,40},{64,... | collective-permute-start | bytes 983048 | tf_op jit(solution)/shard_map/ppermute | solution.py:250
  32.1 1.3 %collective-permute-start.10 = (bf16[10,128,128]{2,1,0:T(8,128)(2,1)S(1)}, bf16[10,128,128]{2,1,0:T(8,128)(2,1)S(1)}, u32[]{:S(2)}, u32[]{:S(2)}) collective-permute-start(bf16[10,128,128]{2,1,0:T(8,128)(2,1)S(1)} %collective-permute-done.2.rest_2_), channel_id=1, source_target_pairs={{0,8},{8,0},{1,9},{9,1},{2,10},{10,2},{3,11},{11,3},{4,12},{12,4},... | collective-permute-start | bytes 983048 | tf_op jit(solution)/shard_map/ppermute | solution.py:242
  33.4 0.3 collective-permute-done.7.rest_7_
  33.7 0.0 collective-permute-start.8
  33.7 0.9 collective-permute-start.13
  34.6 7.4 %all-to-all-done.1.pulled = bf16[32,20,128]{2,1,0:T(8,128)(2,1)S(1)} async-done(((bf16[32,20,128]{2,1,0:T(8,128)(2,1)}), bf16[32,20,128]{2,1,0:T(8,128)(2,1)S(1)}, u32[]{:S(2)}, u32[]{:S(2)}) %all-to-all-start.1) | async-done | bytes 163872 | tf_op jit(solution)/shard_map/all_to_all | solution.py:239
  42.0 1.6 %copy-done = bf16[16,1,256,256]{3,2,1,0:T(8,128)(2,1)S(1)} copy-done((bf16[16,1,256,256]{3,2,1,0:T(8,128)(2,1)S(1)}, bf16[16,1,256,256]{3,2,1,0:T(8,128)(2,1)}, u32[]{:S(2)}) %copy-start) | copy-done | bytes 2097176
  43.6 2.2 %shard_map.93 = (bf16[32,32,128]{2,1,0:T(8,128)(2,1)}, bf16[16,16,128]{2,1,0:T(8,128)(2,1)S(1)}) custom-call(f32[32,1,128]{2,1,0:T(1,128)S(1)} %all_to_all.20.notices, bf16[32,20,128]{2,1,0:T(8,128)(2,1)S(1)} %all-to-all-done.1.pulled, bf16[16,20,128]{2,1,0:T(8,128)(2,1)S(1)} %get-tuple-element.13.packs, bf16[16,1,256,256]{3,2,1,0:T(8,128)(2,1)S(1)} %copy-done), custom_call_target="tpu_custom_call" | custom-call | tf_op jit(solution)/shard_map/pallas_call | solution.py:284
  45.8 3.9 %all-to-all-start.2 = ((bf16[32,32,128]{2,1,0:T(8,128)(2,1)}), bf16[32,32,128]{2,1,0:T(8,128)(2,1)S(1)}, u32[]{:S(2)}, u32[]{:S(2)}) async-start(bf16[32,32,128]{2,1,0:T(8,128)(2,1)} %get-tuple-element.14), calls=%async_computation.2 | async-start | bytes 524288 | tf_op jit(solution)/shard_map/all_to_all | solution.py:239
  49.6 1.9 %collective-permute-start.1 = (bf16[16,16,128]{2,1,0:T(8,128)(2,1)S(1)}, bf16[16,16,128]{2,1,0:T(8,128)(2,1)S(1)}, u32[]{:S(2)}, u32[]{:S(2)}) collective-permute-start(bf16[16,16,128]{2,1,0:T(8,128)(2,1)S(1)} %get-tuple-element.15.mine), channel_id=1, source_target_pairs={{0,128},{128,0},{1,129},{129,1},{2,130},{130,2},{3,131},{131,3},{4... | collective-permute-start | bytes 196616 | tf_op jit(solution)/shard_map/ppermute | solution.py:242
  51.5 2.9 %collective-permute-done.1.other = bf16[16,16,128]{2,1,0:T(8,128)(2,1)S(1)} collective-permute-done((bf16[16,16,128]{2,1,0:T(8,128)(2,1)S(1)}, bf16[16,16,128]{2,1,0:T(8,128)(2,1)S(1)}, u32[]{:S(2)}, u32[]{:S(2)}) %collective-permute-start.1) | collective-permute-done | bytes 65568 | tf_op jit(solution)/shard_map/ppermute | solution.py:242
  54.4 1.9 %collective-permute-start.4 = (bf16[10,128,128]{2,1,0:T(8,128)(2,1)S(1)}, bf16[10,128,128]{2,1,0:T(8,128)(2,1)}, u32[]{:S(2)}, u32[]{:S(2)}) collective-permute-start(bf16[10,128,128]{2,1,0:T(8,128)(2,1)S(1)} %collective-permute-done.3.rest_3_), channel_id=1, source_target_pairs={{0,16},{8,120},{16,32},{24,8},{32,48},{40,24},{48,64},{56,40},{64,... | collective-permute-start | bytes 983048 | tf_op jit(solution)/shard_map/ppermute | solution.py:250
  56.3 0.4 collective-permute-start.14
  56.7 0.1 collective-permute-start.15
  56.8 1.6 %collective-permute-start.12 = (bf16[10,128,128]{2,1,0:T(8,128)(2,1)}, bf16[10,128,128]{2,1,0:T(8,128)(2,1)}, u32[]{:S(2)}, u32[]{:S(2)}) collective-permute-start(bf16[10,128,128]{2,1,0:T(8,128)(2,1)} %collective-permute-done.8.rest_8_), channel_id=1, source_target_pairs={{0,16},{8,120},{16,32},{24,8},{32,48},{40,24},{48,64},{56,40},{64,... | collective-permute-start | bytes 983048 | tf_op jit(solution)/shard_map/ppermute | solution.py:250
  58.4 4.4 %all-to-all-done.2.came = bf16[32,32,128]{2,1,0:T(8,128)(2,1)S(1)} async-done(((bf16[32,32,128]{2,1,0:T(8,128)(2,1)}), bf16[32,32,128]{2,1,0:T(8,128)(2,1)S(1)}, u32[]{:S(2)}, u32[]{:S(2)}) %all-to-all-start.2) | async-done | bytes 262176 | tf_op jit(solution)/shard_map/all_to_all | solution.py:239
  62.8 0.5 collective-permute-done.4.rest_4_
  63.3 3.5 %collective-permute-done.12.rest_12_ = bf16[10,128,128]{2,1,0:T(8,128)(2,1)} collective-permute-done((bf16[10,128,128]{2,1,0:T(8,128)(2,1)}, bf16[10,128,128]{2,1,0:T(8,128)(2,1)}, u32[]{:S(2)}, u32[]{:S(2)}) %collective-permute-start.12) | collective-permute-done | bytes 327712 | tf_op jit(solution)/shard_map/ppermute | solution.py:250
  66.8 3.8 %shard_map.94 = bf16[80,32,128]{2,1,0:T(8,128)(2,1)S(1)} custom-call(f32[32,1,128]{2,1,0:T(1,128)S(1)} %all_to_all.20.notices, bf16[32,32,128]{2,1,0:T(8,128)(2,1)S(1)} %all-to-all-done.2.came, bf16[16,16,128]{2,1,0:T(8,128)(2,1)S(1)} %get-tuple-element.15.mine, bf16[16,16,128]{2,1,0:T(8,128)(2,1)S(1)} %collective-permute-done.1.other, ...), custom_call_target="tpu_custom_call" | custom-call | tf_op jit(solution)/shard_map/pallas_call | solution.py:300
  70.6 17.2 %all_to_all.21 = bf16[80,32,128]{2,1,0:T(8,128)(2,1)S(1)} all-to-all(bf16[80,32,128]{2,1,0:T(8,128)(2,1)S(1)} %shard_map.94), channel_id=1, replica_groups=mesh['xl'=2,'z'=8,'core'=2,'y'=4,'xh'=2] {'xl','y','xh'}, dimensions={0} | all-to-all | bytes 1310720 | tf_op jit(solution)/shard_map/all_to_all | solution.py:239
  87.8 0.7 shard_map.95
  (15 shorter events, 0.0 us)
Async XLA Ops:
  0.0 66.8 %copy-start.1 = (bf16[10,128,128]{2,1,0:T(8,128)(2,1)S(1)}, bf16[10,128,128]{2,1,0:T(8,128)(2,1)}, u32[]{:S(2)}) copy-start(bf16[10,128,128]{2,1,0:T(8,128)(2,1)} %rest_0_.1) | copy-start | bytes 983044
  0.0 2.0 %collective-permute-start.5 = (bf16[10,128,128]{2,1,0:T(8,128)(2,1)}, bf16[10,128,128]{2,1,0:T(8,128)(2,1)S(1)}, u32[]{:S(2)}, u32[]{:S(2)}) collective-permute-start(bf16[10,128,128]{2,1,0:T(8,128)(2,1)} %rest_0_.1), channel_id=1, source_target_pairs={{0,8},{8,0},{1,9},{9,1},{2,10},{10,2},{3,11},{11,3},{4,12},{12,4},... | collective-permute-start | bytes 983048 | tf_op jit(solution)/shard_map/ppermute | solution.py:242
  0.0 21.9 %collective-permute-start = (bf16[10,128,128]{2,1,0:T(8,128)(2,1)}, bf16[10,128,128]{2,1,0:T(8,128)(2,1)S(1)}, u32[]{:S(2)}, u32[]{:S(2)}) collective-permute-start(bf16[10,128,128]{2,1,0:T(8,128)(2,1)} %rest_0_.1), channel_id=1, source_target_pairs={{0,16},{8,120},{16,32},{24,8},{32,48},{40,24},{48,64},{56,40},{64,... | collective-permute-start | bytes 983048 | tf_op jit(solution)/shard_map/ppermute | solution.py:250
  2.0 20.5 %collective-permute-start.6 = (bf16[10,128,128]{2,1,0:T(8,128)(2,1)S(1)}, bf16[10,128,128]{2,1,0:T(8,128)(2,1)S(1)}, u32[]{:S(2)}, u32[]{:S(2)}) collective-permute-start(bf16[10,128,128]{2,1,0:T(8,128)(2,1)S(1)} %collective-permute-done.5.rest_5_), channel_id=1, source_target_pairs={{0,16},{8,120},{16,32},{24,8},{32,48},{40,24},{48,64},{56,40},{64,... | collective-permute-start | bytes 983048 | tf_op jit(solution)/shard_map/ppermute | solution.py:250
  21.9 8.5 %collective-permute-start.2 = (bf16[10,128,128]{2,1,0:T(8,128)(2,1)S(1)}, bf16[10,128,128]{2,1,0:T(8,128)(2,1)S(1)}, u32[]{:S(2)}, u32[]{:S(2)}) collective-permute-start(bf16[10,128,128]{2,1,0:T(8,128)(2,1)S(1)} %collective-permute-done.rest_1_), channel_id=1, source_target_pairs={{0,16},{8,120},{16,32},{24,8},{32,48},{40,24},{48,64},{56,40},{64,... | collective-permute-start | bytes 983048 | tf_op jit(solution)/shard_map/ppermute | solution.py:250
  22.5 11.2 %collective-permute-start.7 = (bf16[10,128,128]{2,1,0:T(8,128)(2,1)S(1)}, bf16[10,128,128]{2,1,0:T(8,128)(2,1)S(1)}, u32[]{:S(2)}, u32[]{:S(2)}) collective-permute-start(bf16[10,128,128]{2,1,0:T(8,128)(2,1)S(1)} %collective-permute-done.6.rest_6_), channel_id=1, source_target_pairs={{0,16},{8,120},{16,32},{24,8},{32,48},{40,24},{48,64},{56,40},{64,... | collective-permute-start | bytes 983048 | tf_op jit(solution)/shard_map/ppermute | solution.py:250
  24.8 17.1 %all-to-all-start.1 = ((bf16[32,20,128]{2,1,0:T(8,128)(2,1)}), bf16[32,20,128]{2,1,0:T(8,128)(2,1)S(1)}, u32[]{:S(2)}, u32[]{:S(2)}) async-start(bf16[32,20,128]{2,1,0:T(8,128)(2,1)} %shard_map.92), calls=%async_computation.1 | async-start | bytes 393216 | tf_op jit(solution)/shard_map/all_to_all | solution.py:239
  30.1 19.5 %collective-permute-start.9 = (bf16[10,128,128]{2,1,0:T(8,128)(2,1)S(1)}, bf16[10,128,128]{2,1,0:T(8,128)(2,1)S(1)}, u32[]{:S(2)}, u32[]{:S(2)}) collective-permute-start(bf16[10,128,128]{2,1,0:T(8,128)(2,1)S(1)} %collective-permute-done.rest_1_), channel_id=1, source_target_pairs={{0,8},{8,0},{1,9},{9,1},{2,10},{10,2},{3,11},{11,3},{4,12},{12,4},... | collective-permute-start | bytes 983048 | tf_op jit(solution)/shard_map/ppermute | solution.py:242
  30.4 21.1 %collective-permute-start.3 = (bf16[10,128,128]{2,1,0:T(8,128)(2,1)S(1)}, bf16[10,128,128]{2,1,0:T(8,128)(2,1)S(1)}, u32[]{:S(2)}, u32[]{:S(2)}) collective-permute-start(bf16[10,128,128]{2,1,0:T(8,128)(2,1)S(1)} %collective-permute-done.2.rest_2_), channel_id=1, source_target_pairs={{0,16},{8,120},{16,32},{24,8},{32,48},{40,24},{48,64},{56,40},{64,... | collective-permute-start | bytes 983048 | tf_op jit(solution)/shard_map/ppermute | solution.py:250
  32.1 24.2 %collective-permute-start.10 = (bf16[10,128,128]{2,1,0:T(8,128)(2,1)S(1)}, bf16[10,128,128]{2,1,0:T(8,128)(2,1)S(1)}, u32[]{:S(2)}, u32[]{:S(2)}) collective-permute-start(bf16[10,128,128]{2,1,0:T(8,128)(2,1)S(1)} %collective-permute-done.2.rest_2_), channel_id=1, source_target_pairs={{0,8},{8,0},{1,9},{9,1},{2,10},{10,2},{3,11},{11,3},{4,12},{12,4},... | collective-permute-start | bytes 983048 | tf_op jit(solution)/shard_map/ppermute | solution.py:242
  33.7 22.9 %collective-permute-start.8 = (bf16[10,128,128]{2,1,0:T(8,128)(2,1)S(1)}, bf16[10,128,128]{2,1,0:T(8,128)(2,1)}, u32[]{:S(2)}, u32[]{:S(2)}) collective-permute-start(bf16[10,128,128]{2,1,0:T(8,128)(2,1)S(1)} %collective-permute-done.7.rest_7_), channel_id=1, source_target_pairs={{0,16},{8,120},{16,32},{24,8},{32,48},{40,24},{48,64},{56,40},{64,... | collective-permute-start | bytes 983048 | tf_op jit(solution)/shard_map/ppermute | solution.py:250
  33.7 23.1 %collective-permute-start.13 = (bf16[10,128,128]{2,1,0:T(8,128)(2,1)S(1)}, bf16[10,128,128]{2,1,0:T(8,128)(2,1)}, u32[]{:S(2)}, u32[]{:S(2)}) collective-permute-start(bf16[10,128,128]{2,1,0:T(8,128)(2,1)S(1)} %collective-permute-done.6.rest_6_), channel_id=1, source_target_pairs={{0,8},{8,0},{1,9},{9,1},{2,10},{10,2},{3,11},{11,3},{4,12},{12,4},... | collective-permute-start | bytes 983048 | tf_op jit(solution)/shard_map/ppermute | solution.py:242
  42.0 1.6 %copy-start = (bf16[16,1,256,256]{3,2,1,0:T(8,128)(2,1)S(1)}, bf16[16,1,256,256]{3,2,1,0:T(8,128)(2,1)}, u32[]{:S(2)}) copy-start(bf16[16,1,256,256]{3,2,1,0:T(8,128)(2,1)} %cache.1) | copy-start | bytes 6291460
  45.8 17.1 %all-to-all-start.2 = ((bf16[32,32,128]{2,1,0:T(8,128)(2,1)}), bf16[32,32,128]{2,1,0:T(8,128)(2,1)S(1)}, u32[]{:S(2)}, u32[]{:S(2)}) async-start(bf16[32,32,128]{2,1,0:T(8,128)(2,1)} %get-tuple-element.14), calls=%async_computation.2 | async-start | bytes 524288 | tf_op jit(solution)/shard_map/all_to_all | solution.py:239
  49.6 4.7 %collective-permute-start.1 = (bf16[16,16,128]{2,1,0:T(8,128)(2,1)S(1)}, bf16[16,16,128]{2,1,0:T(8,128)(2,1)S(1)}, u32[]{:S(2)}, u32[]{:S(2)}) collective-permute-start(bf16[16,16,128]{2,1,0:T(8,128)(2,1)S(1)} %get-tuple-element.15.mine), channel_id=1, source_target_pairs={{0,128},{128,0},{1,129},{129,1},{2,130},{130,2},{3,131},{131,3},{4... | collective-permute-start | bytes 196616 | tf_op jit(solution)/shard_map/ppermute | solution.py:242
  51.5 11.3 %collective-permute-start.11 = (bf16[10,128,128]{2,1,0:T(8,128)(2,1)S(1)}, bf16[10,128,128]{2,1,0:T(8,128)(2,1)}, u32[]{:S(2)}, u32[]{:S(2)}) collective-permute-start(bf16[10,128,128]{2,1,0:T(8,128)(2,1)S(1)} %collective-permute-done.3.rest_3_), channel_id=1, source_target_pairs={{0,8},{8,0},{1,9},{9,1},{2,10},{10,2},{3,11},{11,3},{4,12},{12,4},... | collective-permute-start | bytes 983048 | tf_op jit(solution)/shard_map/ppermute | solution.py:242
  54.4 8.9 %collective-permute-start.4 = (bf16[10,128,128]{2,1,0:T(8,128)(2,1)S(1)}, bf16[10,128,128]{2,1,0:T(8,128)(2,1)}, u32[]{:S(2)}, u32[]{:S(2)}) collective-permute-start(bf16[10,128,128]{2,1,0:T(8,128)(2,1)S(1)} %collective-permute-done.3.rest_3_), channel_id=1, source_target_pairs={{0,16},{8,120},{16,32},{24,8},{32,48},{40,24},{48,64},{56,40},{64,... | collective-permute-start | bytes 983048 | tf_op jit(solution)/shard_map/ppermute | solution.py:250
  56.3 7.0 %collective-permute-start.14 = (bf16[10,128,128]{2,1,0:T(8,128)(2,1)S(1)}, bf16[10,128,128]{2,1,0:T(8,128)(2,1)}, u32[]{:S(2)}, u32[]{:S(2)}) collective-permute-start(bf16[10,128,128]{2,1,0:T(8,128)(2,1)S(1)} %collective-permute-done.7.rest_7_), channel_id=1, source_target_pairs={{0,8},{8,0},{1,9},{9,1},{2,10},{10,2},{3,11},{11,3},{4,12},{12,4},... | collective-permute-start | bytes 983048 | tf_op jit(solution)/shard_map/ppermute | solution.py:242
  56.7 6.6 %collective-permute-start.15 = (bf16[10,128,128]{2,1,0:T(8,128)(2,1)}, bf16[10,128,128]{2,1,0:T(8,128)(2,1)}, u32[]{:S(2)}, u32[]{:S(2)}) collective-permute-start(bf16[10,128,128]{2,1,0:T(8,128)(2,1)} %collective-permute-done.8.rest_8_), channel_id=1, source_target_pairs={{0,8},{8,0},{1,9},{9,1},{2,10},{10,2},{3,11},{11,3},{4,12},{12,4},... | collective-permute-start | bytes 983048 | tf_op jit(solution)/shard_map/ppermute | solution.py:242
  56.8 10.0 %collective-permute-start.12 = (bf16[10,128,128]{2,1,0:T(8,128)(2,1)}, bf16[10,128,128]{2,1,0:T(8,128)(2,1)}, u32[]{:S(2)}, u32[]{:S(2)}) collective-permute-start(bf16[10,128,128]{2,1,0:T(8,128)(2,1)} %collective-permute-done.8.rest_8_), channel_id=1, source_target_pairs={{0,16},{8,120},{16,32},{24,8},{32,48},{40,24},{48,64},{56,40},{64,... | collective-permute-start | bytes 983048 | tf_op jit(solution)/shard_map/ppermute | solution.py:250

commit v6 on v5

--- a/solution.py
+++ b/solution.py
@@ -27,7 +27,7 @@
 
 ROUND, PAIR_ROUND, ME, HEAD, COL, SCALE, DEP, DEST, LEN = 0, 1, 2, 3, 13, 23, 33, 46, 59
 
-VMEM_LIMIT = 40 * 1024 * 1024
+VMEM_LIMIT = 16 * 1024 * 1024
 
 
 def smem():
@@ -109,45 +109,86 @@
     lax.fori_loop(0, REP, one, 0, unroll=4)
 
 
-def attend_body(notices, pulled, packs, cache, send, out, scores, held):
-    scale = 1.0 / math.sqrt(HD)
-    per = STEPS * HEADS
+def score(pack, keys, length):
+    per = STEPS * HEADS
+    sc = lax.dot_general(
+        pack[:per], keys, (((1,), (1,)), ((), ())), preferred_element_type=F32
+    )
+    pos = lax.broadcasted_iota(I32, (per, CTX), 1)
+    return jnp.where(pos < length, sc * (1.0 / math.sqrt(HD)), -jnp.inf)
+
+
+def blend(pack, sc, values):
+    per = STEPS * HEADS
+    step = lax.broadcasted_iota(I32, (per, 1), 0) // HEADS
+    top = jnp.max(sc, axis=1, keepdims=True)
+    expo = jnp.exp(sc - top)
+    total = jnp.sum(expo, axis=1, keepdims=True)
+    carried = jnp.dot(expo.astype(BF16), values, preferred_element_type=F32)
+    pack = pack.astype(F32)
+    q = pack[:per]
+    peak = top
+    extra = []
+    for u in range(STEPS):
+        f = jnp.sum(q * pack[per + 2 * u : per + 2 * u + 1], axis=1, keepdims=True)
+        f = jnp.where(step >= u, f * (1.0 / math.sqrt(HD)), -jnp.inf)
+        extra.append(f)
+        peak = jnp.maximum(peak, f)
+    factor = jnp.exp(top - peak)
+    denom = total * factor
+    numer = carried * factor
+    for u in range(STEPS):
+        w = jnp.exp(extra[u] - peak)
+        denom = denom + w
+        numer = numer + w * pack[per + 2 * u + 1 : per + 2 * u + 2]
+    return (numer / denom).astype(BF16)
+
+
+def stay_body(dep, lengths, packs, cache, out, held, leaves, sems):
+    for s in range(SLOTS):
+        leaves[s] = 0
+    for k in range(MOVE):
+        leaves[dep[0, k]] = 1
+
+    def copy(s):
+        return pltpu.make_async_copy(cache.at[s], held.at[s], sems.at[s])
+
+    def start(s, carry):
+        @pl.when(leaves[s] == 0)
+        def _():
+            copy(s).start()
+
+        return carry
+
+    def one(s, carry):
+        @pl.when(leaves[s] == 0)
+        def _():
+            copy(s).wait()
+            pack = packs[s]
+            sc = score(pack, held[s, 0, :, :HD], lengths[s])
+            out[s] = blend(pack, sc, held[s, 0, :, HD:])
+
+        return carry
+
+    lax.fori_loop(0, SLOTS, start, 0)
+    lax.fori_loop(0, SLOTS, one, 0)
+
+
+def attend_body(notices, pulled, packs, cache, send, out, scores, held, near, sems):
+    per = STEPS * HEADS
+    copies = [pltpu.make_async_copy(cache.at[s], near.at[s], sems.at[s]) for s in range(SLOTS)]
+    for c in copies:
+        c.start()
     me = at(notices, 0, ME)
     for s in range(SLOTS):
         held[s] = packs[s]
     for k in range(MOVE):
         held[at(notices, me, DEP + k)] = pulled[at(notices, me, DEST + k)]
-    pos = lax.broadcasted_iota(I32, (per, CTX), 1)
-    for s in range(SLOTS):
-        q = held[s][:per]
-        sc = lax.dot_general(
-            q, cache[s, 0, :, :HD], (((1,), (1,)), ((), ())), preferred_element_type=F32
-        )
-        scores[s] = jnp.where(pos < at(notices, me, LEN + s), sc * scale, -jnp.inf)
-    step = lax.broadcasted_iota(I32, (per, 1), 0) // HEADS
-    for s in range(SLOTS):
-        sc = scores[s]
-        top = jnp.max(sc, axis=1, keepdims=True)
-        expo = jnp.exp(sc - top)
-        total = jnp.sum(expo, axis=1, keepdims=True)
-        carried = jnp.dot(expo.astype(BF16), cache[s, 0, :, HD:], preferred_element_type=F32)
-        pack = held[s].astype(F32)
-        q = pack[:per]
-        peak = top
-        extra = []
-        for u in range(STEPS):
-            f = jnp.sum(q * pack[per + 2 * u : per + 2 * u + 1], axis=1, keepdims=True) * scale
-            f = jnp.where(step >= u, f, -jnp.inf)
-            extra.append(f)
-            peak = jnp.maximum(peak, f)
-        factor = jnp.exp(top - peak)
-        denom = total * factor
-        numer = carried * factor
-        for u in range(STEPS):
-            w = jnp.exp(extra[u] - peak)
-            denom = denom + w
-            numer = numer + w * pack[per + 2 * u + 1 : per + 2 * u + 2]
-        out[s] = (numer / denom).astype(BF16)
+    for s in range(SLOTS):
+        copies[s].wait()
+        scores[s] = score(held[s], near[s, 0, :, :HD], at(notices, me, LEN + s))
+    for s in range(SLOTS):
+        out[s] = blend(held[s], scores[s], near[s, 0, :, HD:])
     for k in range(MOVE):
         goal = at(notices, me, DEST + k)
         rows = out[at(notices, me, DEP + k)]
@@ -270,11 +311,24 @@
         + [pltpu.VMEM(a.shape, a.dtype) for a in given[5:]]
         + [pltpu.SemaphoreType.DMA((len(given),))],
     )(base.astype(I32)[None], *(in_hbm(a) for a in given))
+    cache = in_hbm(kv_cache)
+    sib, notice = lax.optimization_barrier((sib, notice))
     near, near_x = around(codes, 1), around(sib, 1)
     notices = exchange(notice, rep_axes)
     near, notices = lax.optimization_barrier((near, notices))
     two, two_x = around(near, 1), around(near_x, 1)
     near_sib, near_x_sib = swap(near, "core"), swap(near_x, "core")
+    stays = call(
+        stay_body,
+        jax.ShapeDtypeStruct((SLOTS, per, HD), BF16),
+        [smem()] * 2 + [vmem(), hbm()],
+        [
+            pltpu.VMEM(kv_cache.shape, BF16),
+            pltpu.SMEM((SLOTS,), I32),
+            pltpu.SemaphoreType.DMA((SLOTS,)),
+        ],
+    )(departing, lengths, packs, cache)
+    other = swap(stays, "xl")
     to_pull = call(
         pull_body, jax.ShapeDtypeStruct((REP, PACK, HD), BF16), [smem(), vmem()]
     )(notices, packs)
@@ -287,10 +341,14 @@
             jax.ShapeDtypeStruct((REP, 2 * per, HD), BF16),
             jax.ShapeDtypeStruct((SLOTS, per, HD), BF16),
         ],
-        [smem()] + [vmem()] * 3,
-        [pltpu.VMEM((SLOTS, per, CTX), F32), pltpu.VMEM((SLOTS, PACK, HD), BF16)],
-    )(notices, pulled, packs, kv_cache)
-    other = swap(mine, "xl")
+        [smem()] + [vmem()] * 2 + [hbm()],
+        [
+            pltpu.VMEM((SLOTS, per, CTX), F32),
+            pltpu.VMEM((SLOTS, PACK, HD), BF16),
+            pltpu.VMEM(kv_cache.shape, BF16),
+            pltpu.SemaphoreType.DMA((SLOTS,)),
+        ],
+    )(notices, pulled, packs, cache)
     came = exchange(send, rep_axes)
     four = around(three, 1)
     three_sib, three_x_sib = swap(three, "core"), swap(three_x, "core")

time: 89.8 us -> 91.9 us (1.023)
  blocking collectives: 34.2 us -> 17.6 us
  starting transfers between devices: 24.2 us -> 33 us
  Pallas kernels: 9.52 us -> 15.9 us
  waiting for transfers between devices: 19 us -> 23.2 us
    all_to_all x2 -> x1, blocking collectives: 34.2 us -> 17.6 us  [exchange(): return lax.all_to_all(x, axes, split_axis=0, concat_axis=0, tiled=True)]
    all_to_all x2 -> x3, starting transfers between devices: 9.1 us -> 18.2 us  [exchange(): return lax.all_to_all(x, axes, split_axis=0, concat_axis=0, tiled=True)]
    all_to_all x2 -> x3, waiting for transfers between devices: 11.8 us -> 19.3 us  [exchange(): return lax.all_to_all(x, axes, split_axis=0, concat_axis=0, tiled=True)]
    pallas_call x1, Pallas kernels: 2.19 us -> 5.23 us  [shards(): call(attend_body, [jax.ShapeDtypeStruct((REP, 2 * per, HD), BF16), jax.Sh...]
    pallas_call x0 -> x1, Pallas kernels: none -> 2.76 us  [shards(): call(stay_body, jax.ShapeDtypeStruct((SLOTS, per, HD), BF16), [smem()] *...]
    ppermute x8, waiting for transfers between devices: 2.87 us -> 0.28 us  [swap(): return lax.ppermute(x, axis, [(0, 1), (1, 0)])]
    ppermute x8, starting transfers between devices: 10.2 us -> 8.75 us  [around(): return lax.ppermute(x, ('z', 'core'), pairs)]
    ppermute x8, starting transfers between devices: 4.89 us -> 6.01 us  [swap(): return lax.ppermute(x, axis, [(0, 1), (1, 0)])]
  transfers between devices with their start and end apart: 18 -> 19, of which waited for: 6 -> 6; matrix products, arithmetic and copies ran while one was open for 0% -> 0% of each run, Pallas kernels for 6% -> 13%
where the time goes in v6:
time: 91.9 us; the launch traced here: 91.2 us
  starting transfers between devices  33 us (36%)
  waiting for transfers between devices  23.2 us (25%)
  blocking collectives  17.6 us (19%)
  Pallas kernels  15.9 us (17%)
  local copies, waits for them, and re-layouts  1.31 us (1%)
    all_to_all x3, waiting for transfers between devices, exchange(): return lax.all_to_all(x, axes, split_axis=0, concat_axis=0, tiled=True)  19.3 us
    all_to_all x3, starting transfers between devices, exchange(): return lax.all_to_all(x, axes, split_axis=0, concat_axis=0, tiled=True)  18.2 us
    all_to_all x1, blocking collectives, exchange(): return lax.all_to_all(x, axes, split_axis=0, concat_axis=0, tiled=True)  17.6 us
    ppermute x8, starting transfers between devices, around(): return lax.ppermute(x, ('z', 'core'), pairs)  8.75 us
    ppermute x8, starting transfers between devices, swap(): return lax.ppermute(x, axis, [(0, 1), (1, 0)])  6.01 us
    pallas_call x1, Pallas kernels, shards(): call(attend_body, [jax.ShapeDtypeStruct((REP, 2 * per, HD), BF16), jax.Sh...  5.23 us
    pallas_call x1, Pallas kernels, shards(): call(project_body, jax.ShapeDtypeStruct((XL * COLS, ROWS, HD), BF16), [sm...  3.77 us
    ppermute x8, waiting for transfers between devices, around(): return lax.ppermute(x, ('z', 'core'), pairs)  3.64 us
  transfers between devices with their start and end apart: 19, of which 6 were waited for; matrix products, arithmetic and copies ran while one was open for 0% of the time, Pallas kernels for 13%

profile of v6, /device:TPU:8, one launch (start us, length us, event | category | flops | bytes accessed | tf_op | source)
XLA Modules:
  0.0 91.2 jit_solution(17033166349186598688)
XLA Ops:
  0.0 1.9 %collective-permute-start = (bf16[10,128,128]{2,1,0:T(8,128)(2,1)}, bf16[10,128,128]{2,1,0:T(8,128)(2,1)S(1)}, u32[]{:S(2)}, u32[]{:S(2)}) collective-permute-start(bf16[10,128,128]{2,1,0:T(8,128)(2,1)} %rest_0_.1), channel_id=1, source_target_pairs={{0,16},{8,120},{16,32},{24,8},{32,48},{40,24},{48,64},{56,40},{64,... | collective-permute-start | bytes 983048 | tf_op jit(solution)/shard_map/ppermute | solution.py:291
  1.9 1.7 %shard_map.91 = (f32[32,1,128]{2,1,0:T(1,128)}, bf16[16,20,128]{2,1,0:T(8,128)(2,1)S(1)}) custom-call(s32[1]{0:T(128)} %bitcast.place, s32[1,13]{1,0:T(1,128)} %dep.1, s32[1,13]{1,0:T(1,128)} %refs_1_.1, s32[16]{0:T(128)} %lengths.1, s32[10]{0:T(128)} %refs_3_.1, f32[10]{0:T(128)} %refs_4_.1, bf16[2,16,8,128]{3,2,1,0:T(8,128)(2,1)} %refs_5_.1, ...), custom_call_target="tpu_custom_call" | custom-call | tf_op jit(solution)/shard_map/pallas_call | solution.py:303
  3.6 2.0 %collective-permute-start.6 = (bf16[10,128,128]{2,1,0:T(8,128)(2,1)S(1)}, bf16[10,128,128]{2,1,0:T(8,128)(2,1)S(1)}, u32[]{:S(2)}, u32[]{:S(2)}) collective-permute-start(bf16[10,128,128]{2,1,0:T(8,128)(2,1)S(1)} %collective-permute-done.1.rest_5_), channel_id=1, source_target_pairs={{0,16},{8,120},{16,32},{24,8},{32,48},{40,24},{48,64},{56,40},{64,... | collective-permute-start | bytes 983048 | tf_op jit(solution)/shard_map/ppermute | solution.py:291
  5.6 8.0 %all-to-all-start = ((f32[32,1,128]{2,1,0:T(1,128)}), f32[32,1,128]{2,1,0:T(1,128)S(1)}, u32[]{:S(2)}, u32[]{:S(2)}) async-start(f32[32,1,128]{2,1,0:T(1,128)} %get-tuple-element.14), calls=%async_computation | async-start | bytes 32768 | tf_op jit(solution)/shard_map/all_to_all | solution.py:280
  13.6 8.3 %all-to-all-done.notices = f32[32,1,128]{2,1,0:T(1,128)S(1)} async-done(((f32[32,1,128]{2,1,0:T(1,128)}), f32[32,1,128]{2,1,0:T(1,128)S(1)}, u32[]{:S(2)}, u32[]{:S(2)}) %all-to-all-start) | async-done | bytes 16416 | tf_op jit(solution)/shard_map/all_to_all | solution.py:280
  21.9 0.6 collective-permute-start.3
  22.5 0.5 collective-permute-start.7
  23.1 1.8 %shard_map.92 = bf16[32,20,128]{2,1,0:T(8,128)(2,1)} custom-call(f32[32,1,128]{2,1,0:T(1,128)S(1)} %all-to-all-done.notices, bf16[16,20,128]{2,1,0:T(8,128)(2,1)S(1)} %get-tuple-element.16.packs), custom_call_target="tpu_custom_call" | custom-call | tf_op jit(solution)/shard_map/pallas_call | solution.py:332
  24.8 5.2 %all-to-all-start.1 = ((bf16[32,20,128]{2,1,0:T(8,128)(2,1)}), bf16[32,20,128]{2,1,0:T(8,128)(2,1)S(1)}, u32[]{:S(2)}, u32[]{:S(2)}) async-start(bf16[32,20,128]{2,1,0:T(8,128)(2,1)} %shard_map.92), calls=%async_computation.1 | async-start | bytes 393216 | tf_op jit(solution)/shard_map/all_to_all | solution.py:280
  30.1 0.0 copy-start.1
  30.1 0.6 copy-done.1
  30.7 0.7 copy-done.2
  31.4 2.8 %shard_map.94 = bf16[16,16,128]{2,1,0:T(8,128)(2,1)S(1)} custom-call(s32[1,13]{1,0:T(1,128)S(1)} %copy-done.1, s32[16]{0:T(128)S(1)} %copy-done.2, bf16[16,20,128]{2,1,0:T(8,128)(2,1)S(1)} %get-tuple-element.16.packs, bf16[16,1,256,256]{3,2,1,0:T(8,128)(2,1)} %cache.3), custom_call_target="tpu_custom_call" | custom-call | tf_op jit(solution)/shard_map/pallas_call | solution.py:321
  34.2 1.9 %collective-permute-start.2 = (bf16[16,16,128]{2,1,0:T(8,128)(2,1)S(1)}, bf16[16,16,128]{2,1,0:T(8,128)(2,1)S(1)}, u32[]{:S(2)}, u32[]{:S(2)}) collective-permute-start(bf16[16,16,128]{2,1,0:T(8,128)(2,1)S(1)} %shard_map.94), channel_id=1, source_target_pairs={{0,128},{128,0},{1,129},{129,1},{2,130},{130,2},{3,131},{131,3},{4... | collective-permute-start | bytes 196616 | tf_op jit(solution)/shard_map/ppermute | solution.py:283
  36.1 1.5 %collective-permute-start.4 = (bf16[10,128,128]{2,1,0:T(8,128)(2,1)S(1)}, bf16[10,128,128]{2,1,0:T(8,128)(2,1)S(1)}, u32[]{:S(2)}, u32[]{:S(2)}) collective-permute-start(bf16[10,128,128]{2,1,0:T(8,128)(2,1)S(1)} %collective-permute-done.3.rest_2_), channel_id=1, source_target_pairs={{0,16},{8,120},{16,32},{24,8},{32,48},{40,24},{48,64},{56,40},{64,... | collective-permute-start | bytes 983048 | tf_op jit(solution)/shard_map/ppermute | solution.py:291
  37.5 1.5 %collective-permute-start.13 = (bf16[10,128,128]{2,1,0:T(8,128)(2,1)S(1)}, bf16[10,128,128]{2,1,0:T(8,128)(2,1)S(1)}, u32[]{:S(2)}, u32[]{:S(2)}) collective-permute-start(bf16[10,128,128]{2,1,0:T(8,128)(2,1)S(1)} %collective-permute-done.6.rest_6_), channel_id=1, source_target_pairs={{0,8},{8,0},{1,9},{9,1},{2,10},{10,2},{3,11},{11,3},{4,12},{12,4},... | collective-permute-start | bytes 983048 | tf_op jit(solution)/shard_map/ppermute | solution.py:283
  39.0 0.3 collective-permute-done.2.other
  39.3 0.9 collective-permute-start.10
  40.2 1.7 %all-to-all-done.1.pulled = bf16[32,20,128]{2,1,0:T(8,128)(2,1)S(1)} async-done(((bf16[32,20,128]{2,1,0:T(8,128)(2,1)}), bf16[32,20,128]{2,1,0:T(8,128)(2,1)S(1)}, u32[]{:S(2)}, u32[]{:S(2)}) %all-to-all-start.1) | async-done | bytes 163872 | tf_op jit(solution)/shard_map/all_to_all | solution.py:280
  42.0 5.2 %shard_map.93 = (bf16[32,32,128]{2,1,0:T(8,128)(2,1)}, bf16[16,16,128]{2,1,0:T(8,128)(2,1)S(1)}) custom-call(f32[32,1,128]{2,1,0:T(1,128)S(1)} %all-to-all-done.notices, bf16[32,20,128]{2,1,0:T(8,128)(2,1)S(1)} %all-to-all-done.1.pulled, bf16[16,20,128]{2,1,0:T(8,128)(2,1)S(1)} %get-tuple-element.16.packs, bf16[16,1,256,256]{3,2,1,0:T(8,128)(2,1)} %cache.3), custom_call_target="tpu_custom_call" | custom-call | tf_op jit(solution)/shard_map/pallas_call | solution.py:338
  47.2 5.0 %all-to-all-start.2 = ((bf16[32,32,128]{2,1,0:T(8,128)(2,1)}), bf16[32,32,128]{2,1,0:T(8,128)(2,1)S(1)}, u32[]{:S(2)}, u32[]{:S(2)}) async-start(bf16[32,32,128]{2,1,0:T(8,128)(2,1)} %get-tuple-element.17), calls=%async_computation.2 | async-start | bytes 524288 | tf_op jit(solution)/shard_map/all_to_all | solution.py:280
  52.2 0.4 collective-permute-start.14
  52.6 0.2 collective-permute-start.11
  52.8 1.8 %collective-permute-start.5 = (bf16[10,128,128]{2,1,0:T(8,128)(2,1)S(1)}, bf16[10,128,128]{2,1,0:T(8,128)(2,1)}, u32[]{:S(2)}, u32[]{:S(2)}) collective-permute-start(bf16[10,128,128]{2,1,0:T(8,128)(2,1)S(1)} %collective-permute-done.4.rest_3_), channel_id=1, source_target_pairs={{0,16},{8,120},{16,32},{24,8},{32,48},{40,24},{48,64},{56,40},{64,... | collective-permute-start | bytes 983048 | tf_op jit(solution)/shard_map/ppermute | solution.py:291
  54.6 1.1 %collective-permute-start.15 = (bf16[10,128,128]{2,1,0:T(8,128)(2,1)}, bf16[10,128,128]{2,1,0:T(8,128)(2,1)}, u32[]{:S(2)}, u32[]{:S(2)}) collective-permute-start(bf16[10,128,128]{2,1,0:T(8,128)(2,1)} %collective-permute-done.8.rest_8_), channel_id=1, source_target_pairs={{0,8},{8,0},{1,9},{9,1},{2,10},{10,2},{3,11},{11,3},{4,12},{12,4},... | collective-permute-start | bytes 983048 | tf_op jit(solution)/shard_map/ppermute | solution.py:283
  55.7 0.5 collective-permute-start.12
  56.2 9.2 %all-to-all-done.2.came = bf16[32,32,128]{2,1,0:T(8,128)(2,1)S(1)} async-done(((bf16[32,32,128]{2,1,0:T(8,128)(2,1)}), bf16[32,32,128]{2,1,0:T(8,128)(2,1)S(1)}, u32[]{:S(2)}, u32[]{:S(2)}) %all-to-all-start.2) | async-done | bytes 262176 | tf_op jit(solution)/shard_map/all_to_all | solution.py:280
  65.4 0.1 collective-permute-done.5.rest_4_
  65.6 3.5 %collective-permute-done.12.rest_12_ = bf16[10,128,128]{2,1,0:T(8,128)(2,1)} collective-permute-done((bf16[10,128,128]{2,1,0:T(8,128)(2,1)}, bf16[10,128,128]{2,1,0:T(8,128)(2,1)}, u32[]{:S(2)}, u32[]{:S(2)}) %collective-permute-start.12) | collective-permute-done | bytes 327712 | tf_op jit(solution)/shard_map/ppermute | solution.py:291
  69.1 3.8 %shard_map.95 = bf16[80,32,128]{2,1,0:T(8,128)(2,1)S(1)} custom-call(f32[32,1,128]{2,1,0:T(1,128)S(1)} %all-to-all-done.notices, bf16[32,32,128]{2,1,0:T(8,128)(2,1)S(1)} %all-to-all-done.2.came, bf16[16,16,128]{2,1,0:T(8,128)(2,1)S(1)} %get-tuple-element.18.mine, bf16[16,16,128]{2,1,0:T(8,128)(2,1)S(1)} %collective-permute-done.2.other, ...), custom_call_target="tpu_custom_call" | custom-call | tf_op jit(solution)/shard_map/pallas_call | solution.py:358
  72.8 17.6 %all_to_all.20 = bf16[80,32,128]{2,1,0:T(8,128)(2,1)S(1)} all-to-all(bf16[80,32,128]{2,1,0:T(8,128)(2,1)S(1)} %shard_map.95), channel_id=1, replica_groups=mesh['xl'=2,'z'=8,'core'=2,'y'=4,'xh'=2] {'xl','y','xh'}, dimensions={0} | all-to-all | bytes 1310720 | tf_op jit(solution)/shard_map/all_to_all | solution.py:280
  90.5 0.7 shard_map.96
  (19 shorter events, 0.0 us)
Async XLA Ops:
  0.0 3.6 %collective-permute-start.1 = (bf16[10,128,128]{2,1,0:T(8,128)(2,1)}, bf16[10,128,128]{2,1,0:T(8,128)(2,1)S(1)}, u32[]{:S(2)}, u32[]{:S(2)}) collective-permute-start(bf16[10,128,128]{2,1,0:T(8,128)(2,1)} %rest_0_.1), channel_id=1, source_target_pairs={{0,8},{8,0},{1,9},{9,1},{2,10},{10,2},{3,11},{11,3},{4,12},{12,4},... | collective-permute-start | bytes 983048 | tf_op jit(solution)/shard_map/ppermute | solution.py:283
  0.0 13.6 %collective-permute-start = (bf16[10,128,128]{2,1,0:T(8,128)(2,1)}, bf16[10,128,128]{2,1,0:T(8,128)(2,1)S(1)}, u32[]{:S(2)}, u32[]{:S(2)}) collective-permute-start(bf16[10,128,128]{2,1,0:T(8,128)(2,1)} %rest_0_.1), channel_id=1, source_target_pairs={{0,16},{8,120},{16,32},{24,8},{32,48},{40,24},{48,64},{56,40},{64,... | collective-permute-start | bytes 983048 | tf_op jit(solution)/shard_map/ppermute | solution.py:291
  3.6 18.9 %collective-permute-start.6 = (bf16[10,128,128]{2,1,0:T(8,128)(2,1)S(1)}, bf16[10,128,128]{2,1,0:T(8,128)(2,1)S(1)}, u32[]{:S(2)}, u32[]{:S(2)}) collective-permute-start(bf16[10,128,128]{2,1,0:T(8,128)(2,1)S(1)} %collective-permute-done.1.rest_5_), channel_id=1, source_target_pairs={{0,16},{8,120},{16,32},{24,8},{32,48},{40,24},{48,64},{56,40},{64,... | collective-permute-start | bytes 983048 | tf_op jit(solution)/shard_map/ppermute | solution.py:291
  5.6 16.3 %all-to-all-start = ((f32[32,1,128]{2,1,0:T(1,128)}), f32[32,1,128]{2,1,0:T(1,128)S(1)}, u32[]{:S(2)}, u32[]{:S(2)}) async-start(f32[32,1,128]{2,1,0:T(1,128)} %get-tuple-element.14), calls=%async_computation | async-start | bytes 32768 | tf_op jit(solution)/shard_map/all_to_all | solution.py:280
  21.9 14.1 %collective-permute-start.3 = (bf16[10,128,128]{2,1,0:T(8,128)(2,1)S(1)}, bf16[10,128,128]{2,1,0:T(8,128)(2,1)S(1)}, u32[]{:S(2)}, u32[]{:S(2)}) collective-permute-start(bf16[10,128,128]{2,1,0:T(8,128)(2,1)S(1)} %collective-permute-done.rest_1_), channel_id=1, source_target_pairs={{0,16},{8,120},{16,32},{24,8},{32,48},{40,24},{48,64},{56,40},{64,... | collective-permute-start | bytes 983048 | tf_op jit(solution)/shard_map/ppermute | solution.py:291
  22.5 16.5 %collective-permute-start.7 = (bf16[10,128,128]{2,1,0:T(8,128)(2,1)S(1)}, bf16[10,128,128]{2,1,0:T(8,128)(2,1)S(1)}, u32[]{:S(2)}, u32[]{:S(2)}) collective-permute-start(bf16[10,128,128]{2,1,0:T(8,128)(2,1)S(1)} %collective-permute-done.6.rest_6_), channel_id=1, source_target_pairs={{0,16},{8,120},{16,32},{24,8},{32,48},{40,24},{48,64},{56,40},{64,... | collective-permute-start | bytes 983048 | tf_op jit(solution)/shard_map/ppermute | solution.py:291
  24.8 17.1 %all-to-all-start.1 = ((bf16[32,20,128]{2,1,0:T(8,128)(2,1)}), bf16[32,20,128]{2,1,0:T(8,128)(2,1)S(1)}, u32[]{:S(2)}, u32[]{:S(2)}) async-start(bf16[32,20,128]{2,1,0:T(8,128)(2,1)} %shard_map.92), calls=%async_computation.1 | async-start | bytes 393216 | tf_op jit(solution)/shard_map/all_to_all | solution.py:280
  30.1 0.7 copy-start.1
  30.7 0.7 copy-start.2
  31.4 37.7 %copy-start = (bf16[10,128,128]{2,1,0:T(8,128)(2,1)S(1)}, bf16[10,128,128]{2,1,0:T(8,128)(2,1)}, u32[]{:S(2)}) copy-start(bf16[10,128,128]{2,1,0:T(8,128)(2,1)} %rest_0_.1) | copy-start | bytes 983044
  34.2 5.1 %collective-permute-start.2 = (bf16[16,16,128]{2,1,0:T(8,128)(2,1)S(1)}, bf16[16,16,128]{2,1,0:T(8,128)(2,1)S(1)}, u32[]{:S(2)}, u32[]{:S(2)}) collective-permute-start(bf16[16,16,128]{2,1,0:T(8,128)(2,1)S(1)} %shard_map.94), channel_id=1, source_target_pairs={{0,128},{128,0},{1,129},{129,1},{2,130},{130,2},{3,131},{131,3},{4... | collective-permute-start | bytes 196616 | tf_op jit(solution)/shard_map/ppermute | solution.py:283
  36.1 16.2 %collective-permute-start.9 = (bf16[10,128,128]{2,1,0:T(8,128)(2,1)S(1)}, bf16[10,128,128]{2,1,0:T(8,128)(2,1)S(1)}, u32[]{:S(2)}, u32[]{:S(2)}) collective-permute-start(bf16[10,128,128]{2,1,0:T(8,128)(2,1)S(1)} %collective-permute-done.rest_1_), channel_id=1, source_target_pairs={{0,8},{8,0},{1,9},{9,1},{2,10},{10,2},{3,11},{11,3},{4,12},{12,4},... | collective-permute-start | bytes 983048 | tf_op jit(solution)/shard_map/ppermute | solution.py:283
  36.1 16.5 %collective-permute-start.4 = (bf16[10,128,128]{2,1,0:T(8,128)(2,1)S(1)}, bf16[10,128,128]{2,1,0:T(8,128)(2,1)S(1)}, u32[]{:S(2)}, u32[]{:S(2)}) collective-permute-start(bf16[10,128,128]{2,1,0:T(8,128)(2,1)S(1)} %collective-permute-done.3.rest_2_), channel_id=1, source_target_pairs={{0,16},{8,120},{16,32},{24,8},{32,48},{40,24},{48,64},{56,40},{64,... | collective-permute-start | bytes 983048 | tf_op jit(solution)/shard_map/ppermute | solution.py:291
  37.5 15.3 %collective-permute-start.13 = (bf16[10,128,128]{2,1,0:T(8,128)(2,1)S(1)}, bf16[10,128,128]{2,1,0:T(8,128)(2,1)S(1)}, u32[]{:S(2)}, u32[]{:S(2)}) collective-permute-start(bf16[10,128,128]{2,1,0:T(8,128)(2,1)S(1)} %collective-permute-done.6.rest_6_), channel_id=1, source_target_pairs={{0,8},{8,0},{1,9},{9,1},{2,10},{10,2},{3,11},{11,3},{4,12},{12,4},... | collective-permute-start | bytes 983048 | tf_op jit(solution)/shard_map/ppermute | solution.py:283
  39.0 15.6 %collective-permute-start.8 = (bf16[10,128,128]{2,1,0:T(8,128)(2,1)S(1)}, bf16[10,128,128]{2,1,0:T(8,128)(2,1)}, u32[]{:S(2)}, u32[]{:S(2)}) collective-permute-start(bf16[10,128,128]{2,1,0:T(8,128)(2,1)S(1)} %collective-permute-done.7.rest_7_), channel_id=1, source_target_pairs={{0,16},{8,120},{16,32},{24,8},{32,48},{40,24},{48,64},{56,40},{64,... | collective-permute-start | bytes 983048 | tf_op jit(solution)/shard_map/ppermute | solution.py:291
  39.3 16.4 %collective-permute-start.10 = (bf16[10,128,128]{2,1,0:T(8,128)(2,1)S(1)}, bf16[10,128,128]{2,1,0:T(8,128)(2,1)}, u32[]{:S(2)}, u32[]{:S(2)}) collective-permute-start(bf16[10,128,128]{2,1,0:T(8,128)(2,1)S(1)} %collective-permute-done.3.rest_2_), channel_id=1, source_target_pairs={{0,8},{8,0},{1,9},{9,1},{2,10},{10,2},{3,11},{11,3},{4,12},{12,4},... | collective-permute-start | bytes 983048 | tf_op jit(solution)/shard_map/ppermute | solution.py:283
  47.2 18.2 %all-to-all-start.2 = ((bf16[32,32,128]{2,1,0:T(8,128)(2,1)}), bf16[32,32,128]{2,1,0:T(8,128)(2,1)S(1)}, u32[]{:S(2)}, u32[]{:S(2)}) async-start(bf16[32,32,128]{2,1,0:T(8,128)(2,1)} %get-tuple-element.17), calls=%async_computation.2 | async-start | bytes 524288 | tf_op jit(solution)/shard_map/all_to_all | solution.py:280
  52.2 13.2 %collective-permute-start.14 = (bf16[10,128,128]{2,1,0:T(8,128)(2,1)S(1)}, bf16[10,128,128]{2,1,0:T(8,128)(2,1)}, u32[]{:S(2)}, u32[]{:S(2)}) collective-permute-start(bf16[10,128,128]{2,1,0:T(8,128)(2,1)S(1)} %collective-permute-done.7.rest_7_), channel_id=1, source_target_pairs={{0,8},{8,0},{1,9},{9,1},{2,10},{10,2},{3,11},{11,3},{4,12},{12,4},... | collective-permute-start | bytes 983048 | tf_op jit(solution)/shard_map/ppermute | solution.py:283
  52.6 12.8 %collective-permute-start.11 = (bf16[10,128,128]{2,1,0:T(8,128)(2,1)S(1)}, bf16[10,128,128]{2,1,0:T(8,128)(2,1)}, u32[]{:S(2)}, u32[]{:S(2)}) collective-permute-start(bf16[10,128,128]{2,1,0:T(8,128)(2,1)S(1)} %collective-permute-done.4.rest_3_), channel_id=1, source_target_pairs={{0,8},{8,0},{1,9},{9,1},{2,10},{10,2},{3,11},{11,3},{4,12},{12,4},... | collective-permute-start | bytes 983048 | tf_op jit(solution)/shard_map/ppermute | solution.py:283
  52.8 12.7 %collective-permute-start.5 = (bf16[10,128,128]{2,1,0:T(8,128)(2,1)S(1)}, bf16[10,128,128]{2,1,0:T(8,128)(2,1)}, u32[]{:S(2)}, u32[]{:S(2)}) collective-permute-start(bf16[10,128,128]{2,1,0:T(8,128)(2,1)S(1)} %collective-permute-done.4.rest_3_), channel_id=1, source_target_pairs={{0,16},{8,120},{16,32},{24,8},{32,48},{40,24},{48,64},{56,40},{64,... | collective-permute-start | bytes 983048 | tf_op jit(solution)/shard_map/ppermute | solution.py:291
  54.6 10.9 %collective-permute-start.15 = (bf16[10,128,128]{2,1,0:T(8,128)(2,1)}, bf16[10,128,128]{2,1,0:T(8,128)(2,1)}, u32[]{:S(2)}, u32[]{:S(2)}) collective-permute-start(bf16[10,128,128]{2,1,0:T(8,128)(2,1)} %collective-permute-done.8.rest_8_), channel_id=1, source_target_pairs={{0,8},{8,0},{1,9},{9,1},{2,10},{10,2},{3,11},{11,3},{4,12},{12,4},... | collective-permute-start | bytes 983048 | tf_op jit(solution)/shard_map/ppermute | solution.py:283
  55.7 13.3 %collective-permute-start.12 = (bf16[10,128,128]{2,1,0:T(8,128)(2,1)}, bf16[10,128,128]{2,1,0:T(8,128)(2,1)}, u32[]{:S(2)}, u32[]{:S(2)}) collective-permute-start(bf16[10,128,128]{2,1,0:T(8,128)(2,1)} %collective-permute-done.8.rest_8_), channel_id=1, source_target_pairs={{0,16},{8,120},{16,32},{24,8},{32,48},{40,24},{48,64},{56,40},{64,... | collective-permute-start | bytes 983048 | tf_op jit(solution)/shard_map/ppermute | solution.py:291

commit v7 on v6

--- a/solution.py
+++ b/solution.py
@@ -144,7 +144,8 @@
     return (numer / denom).astype(BF16)
 
 
-def stay_body(dep, lengths, packs, cache, out, held, leaves, sems):
+def stay_body(dep_in, lengths_in, packs, cache, out, dep, lengths, held, leaves, sems):
+    copy_in([(dep_in, dep), (lengths_in, lengths)], sems.at[SLOTS:])
     for s in range(SLOTS):
         leaves[s] = 0
     for k in range(MOVE):
@@ -174,21 +175,17 @@
     lax.fori_loop(0, SLOTS, one, 0)
 
 
-def attend_body(notices, pulled, packs, cache, send, out, scores, held, near, sems):
-    per = STEPS * HEADS
-    copies = [pltpu.make_async_copy(cache.at[s], near.at[s], sems.at[s]) for s in range(SLOTS)]
-    for c in copies:
-        c.start()
+def attend_body(notices, pulled, packs, cache, send, out, scores, held):
+    per = STEPS * HEADS
     me = at(notices, 0, ME)
     for s in range(SLOTS):
         held[s] = packs[s]
     for k in range(MOVE):
         held[at(notices, me, DEP + k)] = pulled[at(notices, me, DEST + k)]
     for s in range(SLOTS):
-        copies[s].wait()
-        scores[s] = score(held[s], near[s, 0, :, :HD], at(notices, me, LEN + s))
-    for s in range(SLOTS):
-        out[s] = blend(held[s], scores[s], near[s, 0, :, HD:])
+        scores[s] = score(held[s], cache[s, 0, :, :HD], at(notices, me, LEN + s))
+    for s in range(SLOTS):
+        out[s] = blend(held[s], scores[s], cache[s, 0, :, HD:])
     for k in range(MOVE):
         goal = at(notices, me, DEST + k)
         rows = out[at(notices, me, DEP + k)]
@@ -315,19 +312,22 @@
     sib, notice = lax.optimization_barrier((sib, notice))
     near, near_x = around(codes, 1), around(sib, 1)
     notices = exchange(notice, rep_axes)
-    near, notices = lax.optimization_barrier((near, notices))
-    two, two_x = around(near, 1), around(near_x, 1)
-    near_sib, near_x_sib = swap(near, "core"), swap(near_x, "core")
     stays = call(
         stay_body,
         jax.ShapeDtypeStruct((SLOTS, per, HD), BF16),
-        [smem()] * 2 + [vmem(), hbm()],
+        [hbm()] * 2 + [vmem(), hbm()],
         [
+            pltpu.SMEM(departing.shape, I32),
+            pltpu.SMEM(lengths.shape, I32),
             pltpu.VMEM(kv_cache.shape, BF16),
             pltpu.SMEM((SLOTS,), I32),
-            pltpu.SemaphoreType.DMA((SLOTS,)),
+            pltpu.SemaphoreType.DMA((SLOTS + 2,)),
         ],
-    )(departing, lengths, packs, cache)
+    )(in_hbm(departing), in_hbm(lengths), packs, cache)
+    near, stays = lax.optimization_barrier((near, stays))
+    near_x, notices = lax.optimization_barrier((near_x, notices))
+    two, two_x = around(near, 1), around(near_x, 1)
+    near_sib, near_x_sib = swap(near, "core"), swap(near_x, "core")
     other = swap(stays, "xl")
     to_pull = call(
         pull_body, jax.ShapeDtypeStruct((REP, PACK, HD), BF16), [smem(), vmem()]
@@ -341,14 +341,9 @@
             jax.ShapeDtypeStruct((REP, 2 * per, HD), BF16),
             jax.ShapeDtypeStruct((SLOTS, per, HD), BF16),
         ],
-        [smem()] + [vmem()] * 2 + [hbm()],
-        [
-            pltpu.VMEM((SLOTS, per, CTX), F32),
-            pltpu.VMEM((SLOTS, PACK, HD), BF16),
-            pltpu.VMEM(kv_cache.shape, BF16),
-            pltpu.SemaphoreType.DMA((SLOTS,)),
-        ],
-    )(notices, pulled, packs, cache)
+        [smem()] + [vmem()] * 3,
+        [pltpu.VMEM((SLOTS, per, CTX), F32), pltpu.VMEM((SLOTS, PACK, HD), BF16)],
+    )(notices, pulled, packs, kv_cache)
     came = exchange(send, rep_axes)
     four = around(three, 1)
     three_sib, three_x_sib = swap(three, "core"), swap(three_x, "core")

time: 91.9 us -> 86.3 us (0.939)
  Pallas kernels: 15.9 us -> 12.4 us
  waiting for transfers between devices: 23.2 us -> 22.2 us
    all_to_all x3, waiting for transfers between devices: 19.3 us -> 9.36 us  [exchange(): return lax.all_to_all(x, axes, split_axis=0, concat_axis=0, tiled=True)]
    ppermute x8, waiting for transfers between devices: 3.64 us -> 12.8 us  [around(): return lax.ppermute(x, ('z', 'core'), pairs)]
    pallas_call x1, Pallas kernels: 5.23 us -> 1.48 us  [shards(): call(attend_body, [jax.ShapeDtypeStruct((REP, 2 * per, HD), BF16), jax.Sh...]
    all_to_all x3, starting transfers between devices: 18.2 us -> 16.2 us  [exchange(): return lax.all_to_all(x, axes, split_axis=0, concat_axis=0, tiled=True)]
    ppermute x8, starting transfers between devices: 8.75 us -> 10 us  [around(): return lax.ppermute(x, ('z', 'core'), pairs)]
  transfers between devices with their start and end apart: 19 -> 19, of which waited for: 6 -> 4; matrix products, arithmetic and copies ran while one was open for 0% -> 0% of each run, Pallas kernels for 13% -> 9%
where the time goes in v7:
time: 86.3 us; the launch traced here: 85.6 us
  starting transfers between devices  32.5 us (38%)
  waiting for transfers between devices  22.2 us (26%)
  blocking collectives  17.6 us (20%)
  Pallas kernels  12.4 us (14%)
    all_to_all x1, blocking collectives, exchange(): return lax.all_to_all(x, axes, split_axis=0, concat_axis=0, tiled=True)  17.6 us
    all_to_all x3, starting transfers between devices, exchange(): return lax.all_to_all(x, axes, split_axis=0, concat_axis=0, tiled=True)  16.2 us
    ppermute x8, waiting for transfers between devices, around(): return lax.ppermute(x, ('z', 'core'), pairs)  12.8 us
    ppermute x8, starting transfers between devices, around(): return lax.ppermute(x, ('z', 'core'), pairs)  10 us
    all_to_all x3, waiting for transfers between devices, exchange(): return lax.all_to_all(x, axes, split_axis=0, concat_axis=0, tiled=True)  9.36 us
    ppermute x8, starting transfers between devices, swap(): return lax.ppermute(x, axis, [(0, 1), (1, 0)])  6.33 us
    pallas_call x1, Pallas kernels, shards(): call(project_body, jax.ShapeDtypeStruct((XL * COLS, ROWS, HD), BF16), [sm...  3.86 us
    pallas_call x1, Pallas kernels, shards(): call(stay_body, jax.ShapeDtypeStruct((SLOTS, per, HD), BF16), [hbm()] * 2...  2.91 us
  transfers between devices with their start and end apart: 19, of which 4 were waited for; matrix products, arithmetic and copies ran while one was open for 0% of the time, Pallas kernels for 9%

profile of v7, /device:TPU:8, one launch (start us, length us, event | category | flops | bytes accessed | tf_op | source)
XLA Modules:
  0.0 85.6 jit_solution(8043300922105061415)
XLA Ops:
  0.0 2.0 %collective-permute-start.2 = (bf16[10,128,128]{2,1,0:T(8,128)(2,1)}, bf16[10,128,128]{2,1,0:T(8,128)(2,1)S(1)}, u32[]{:S(2)}, u32[]{:S(2)}) collective-permute-start(bf16[10,128,128]{2,1,0:T(8,128)(2,1)} %rest_0_.1), channel_id=1, source_target_pairs={{0,16},{8,120},{16,32},{24,8},{32,48},{40,24},{48,64},{56,40},{64,... | collective-permute-start | bytes 983048 | tf_op jit(solution)/shard_map/ppermute | solution.py:288
  2.0 1.7 %shard_map.91 = (f32[32,1,128]{2,1,0:T(1,128)}, bf16[16,20,128]{2,1,0:T(8,128)(2,1)S(1)}) custom-call(s32[1]{0:T(128)} %bitcast.place, s32[1,13]{1,0:T(1,128)} %dep_in.1, s32[1,13]{1,0:T(1,128)} %refs_1_.1, s32[16]{0:T(128)} %lengths_in.1, s32[10]{0:T(128)} %refs_3_.1, f32[10]{0:T(128)} %refs_4_.1, bf16[2,16,8,128]{3,2,1,0:T(8,128)(2,1)} %refs_5_.1, ...), custom_call_target="tpu_custom_call" | custom-call | tf_op jit(solution)/shard_map/pallas_call | solution.py:300
  3.7 0.0 collective-permute-done.rest_5_
  3.7 2.0 %collective-permute-start.1 = (bf16[10,128,128]{2,1,0:T(8,128)(2,1)S(1)}, bf16[10,128,128]{2,1,0:T(8,128)(2,1)}, u32[]{:S(2)}, u32[]{:S(2)}) collective-permute-start(bf16[10,128,128]{2,1,0:T(8,128)(2,1)S(1)} %collective-permute-done.rest_5_), channel_id=1, source_target_pairs={{0,16},{8,120},{16,32},{24,8},{32,48},{40,24},{48,64},{56,40},{64,... | collective-permute-start | bytes 983048 | tf_op jit(solution)/shard_map/ppermute | solution.py:288
  5.7 8.0 %all-to-all-start = ((f32[32,1,128]{2,1,0:T(1,128)}), f32[32,1,128]{2,1,0:T(1,128)S(1)}, u32[]{:S(2)}, u32[]{:S(2)}) async-start(f32[32,1,128]{2,1,0:T(1,128)} %get-tuple-element.17), calls=%async_computation | async-start | bytes 32768 | tf_op jit(solution)/shard_map/all_to_all | solution.py:277
  13.7 2.9 %shard_map.94 = bf16[16,16,128]{2,1,0:T(8,128)(2,1)S(1)} custom-call(s32[1,13]{1,0:T(1,128)} %dep_in.1, s32[16]{0:T(128)} %lengths_in.1, bf16[16,20,128]{2,1,0:T(8,128)(2,1)S(1)} %get-tuple-element.19.packs, bf16[16,1,256,256]{3,2,1,0:T(8,128)(2,1)} %cache.3), custom_call_target="tpu_custom_call" | custom-call | tf_op jit(solution)/shard_map/pallas_call | solution.py:315
  16.6 0.0 copy-start.1
  16.6 1.9 %collective-permute-start.4 = (bf16[10,128,128]{2,1,0:T(8,128)(2,1)S(1)}, bf16[10,128,128]{2,1,0:T(8,128)(2,1)}, u32[]{:S(2)}, u32[]{:S(2)}) collective-permute-start(bf16[10,128,128]{2,1,0:T(8,128)(2,1)S(1)} %collective-permute-done.2.rest_1_), channel_id=1, source_target_pairs={{0,16},{8,120},{16,32},{24,8},{32,48},{40,24},{48,64},{56,40},{64,... | collective-permute-start | bytes 983048 | tf_op jit(solution)/shard_map/ppermute | solution.py:288
  18.5 3.5 %all-to-all-done.notices = f32[32,1,128]{2,1,0:T(1,128)S(1)} async-done(((f32[32,1,128]{2,1,0:T(1,128)}), f32[32,1,128]{2,1,0:T(1,128)S(1)}, u32[]{:S(2)}, u32[]{:S(2)}) %all-to-all-start) | async-done | bytes 16416 | tf_op jit(solution)/shard_map/all_to_all | solution.py:277
  22.0 0.0 collective-permute-done.1.rest_6_
  22.0 0.6 collective-permute-start.7
  22.6 1.8 %shard_map.92 = bf16[32,20,128]{2,1,0:T(8,128)(2,1)} custom-call(f32[32,1,128]{2,1,0:T(1,128)S(1)} %all-to-all-done.notices, bf16[16,20,128]{2,1,0:T(8,128)(2,1)S(1)} %get-tuple-element.19.packs), custom_call_target="tpu_custom_call" | custom-call | tf_op jit(solution)/shard_map/pallas_call | solution.py:332
  24.4 4.3 %all-to-all-start.1 = ((bf16[32,20,128]{2,1,0:T(8,128)(2,1)}), bf16[32,20,128]{2,1,0:T(8,128)(2,1)S(1)}, u32[]{:S(2)}, u32[]{:S(2)}) async-start(bf16[32,20,128]{2,1,0:T(8,128)(2,1)} %shard_map.92), calls=%async_computation.1 | async-start | bytes 393216 | tf_op jit(solution)/shard_map/all_to_all | solution.py:277
  28.7 1.9 %collective-permute-start.3 = (bf16[16,16,128]{2,1,0:T(8,128)(2,1)S(1)}, bf16[16,16,128]{2,1,0:T(8,128)(2,1)S(1)}, u32[]{:S(2)}, u32[]{:S(2)}) collective-permute-start(bf16[16,16,128]{2,1,0:T(8,128)(2,1)S(1)} %shard_map.94), channel_id=1, source_target_pairs={{0,128},{128,0},{1,129},{129,1},{2,130},{130,2},{3,131},{131,3},{4... | collective-permute-start | bytes 196616 | tf_op jit(solution)/shard_map/ppermute | solution.py:280
  30.6 1.5 %collective-permute-start.5 = (bf16[10,128,128]{2,1,0:T(8,128)(2,1)}, bf16[10,128,128]{2,1,0:T(8,128)(2,1)}, u32[]{:S(2)}, u32[]{:S(2)}) collective-permute-start(bf16[10,128,128]{2,1,0:T(8,128)(2,1)} %collective-permute-done.4.rest_2_), channel_id=1, source_target_pairs={{0,16},{8,120},{16,32},{24,8},{32,48},{40,24},{48,64},{56,40},{64,... | collective-permute-start | bytes 983048 | tf_op jit(solution)/shard_map/ppermute | solution.py:288
  32.1 1.5 %collective-permute-start.13 = (bf16[10,128,128]{2,1,0:T(8,128)(2,1)}, bf16[10,128,128]{2,1,0:T(8,128)(2,1)}, u32[]{:S(2)}, u32[]{:S(2)}) collective-permute-start(bf16[10,128,128]{2,1,0:T(8,128)(2,1)} %collective-permute-done.1.rest_6_), channel_id=1, source_target_pairs={{0,8},{8,0},{1,9},{9,1},{2,10},{10,2},{3,11},{11,3},{4,12},{12,4},... | collective-permute-start | bytes 983048 | tf_op jit(solution)/shard_map/ppermute | solution.py:280
  33.6 1.2 %collective-permute-start.10 = (bf16[10,128,128]{2,1,0:T(8,128)(2,1)}, bf16[10,128,128]{2,1,0:T(8,128)(2,1)}, u32[]{:S(2)}, u32[]{:S(2)}) collective-permute-start(bf16[10,128,128]{2,1,0:T(8,128)(2,1)} %collective-permute-done.4.rest_2_), channel_id=1, source_target_pairs={{0,8},{8,0},{1,9},{9,1},{2,10},{10,2},{3,11},{11,3},{4,12},{12,4},... | collective-permute-start | bytes 983048 | tf_op jit(solution)/shard_map/ppermute | solution.py:280
  34.7 5.8 %all-to-all-done.1.pulled = bf16[32,20,128]{2,1,0:T(8,128)(2,1)S(1)} async-done(((bf16[32,20,128]{2,1,0:T(8,128)(2,1)}), bf16[32,20,128]{2,1,0:T(8,128)(2,1)S(1)}, u32[]{:S(2)}, u32[]{:S(2)}) %all-to-all-start.1) | async-done | bytes 163872 | tf_op jit(solution)/shard_map/all_to_all | solution.py:277
  40.6 1.5 %shard_map.93 = (bf16[32,32,128]{2,1,0:T(8,128)(2,1)S(1)}, bf16[16,16,128]{2,1,0:T(8,128)(2,1)S(1)}) custom-call(f32[32,1,128]{2,1,0:T(1,128)S(1)} %all-to-all-done.notices, bf16[32,20,128]{2,1,0:T(8,128)(2,1)S(1)} %all-to-all-done.1.pulled, bf16[16,20,128]{2,1,0:T(8,128)(2,1)S(1)} %get-tuple-element.19.packs, bf16[16,1,256,256]{3,2,1,0:T(8,128)(2,1)S(1)} %copy-done), custom_call_target="tpu_custom_call" | custom-call | tf_op jit(solution)/shard_map/pallas_call | solution.py:338
  42.1 0.7 copy-done.2
  42.8 3.9 %all-to-all-start.2 = ((bf16[32,32,128]{2,1,0:T(8,128)(2,1)}), bf16[32,32,128]{2,1,0:T(8,128)(2,1)S(1)}, u32[]{:S(2)}, u32[]{:S(2)}) async-start(bf16[32,32,128]{2,1,0:T(8,128)(2,1)} %copy-done.2), calls=%async_computation.2 | async-start | bytes 524288 | tf_op jit(solution)/shard_map/all_to_all | solution.py:277
  46.7 0.2 collective-permute-start.14
  46.9 0.3 collective-permute-start.11
  47.3 1.7 %collective-permute-start.6 = (bf16[10,128,128]{2,1,0:T(8,128)(2,1)}, bf16[10,128,128]{2,1,0:T(8,128)(2,1)S(1)}, u32[]{:S(2)}, u32[]{:S(2)}) collective-permute-start(bf16[10,128,128]{2,1,0:T(8,128)(2,1)} %collective-permute-done.5.rest_3_), channel_id=1, source_target_pairs={{0,16},{8,120},{16,32},{24,8},{32,48},{40,24},{48,64},{56,40},{64,... | collective-permute-start | bytes 983048 | tf_op jit(solution)/shard_map/ppermute | solution.py:288
  49.0 1.2 %collective-permute-start.15 = (bf16[10,128,128]{2,1,0:T(8,128)(2,1)}, bf16[10,128,128]{2,1,0:T(8,128)(2,1)S(1)}, u32[]{:S(2)}, u32[]{:S(2)}) collective-permute-start(bf16[10,128,128]{2,1,0:T(8,128)(2,1)} %collective-permute-done.8.rest_8_), channel_id=1, source_target_pairs={{0,8},{8,0},{1,9},{9,1},{2,10},{10,2},{3,11},{11,3},{4,12},{12,4},... | collective-permute-start | bytes 983048 | tf_op jit(solution)/shard_map/ppermute | solution.py:280
  50.1 0.4 collective-permute-start.12
  50.5 9.3 %collective-permute-done.6.rest_4_ = bf16[10,128,128]{2,1,0:T(8,128)(2,1)S(1)} collective-permute-done((bf16[10,128,128]{2,1,0:T(8,128)(2,1)}, bf16[10,128,128]{2,1,0:T(8,128)(2,1)S(1)}, u32[]{:S(2)}, u32[]{:S(2)}) %collective-permute-start.6) | collective-permute-done | bytes 327712 | tf_op jit(solution)/shard_map/ppermute | solution.py:288
  59.9 0.0 all-to-all-done.2.came
  59.9 3.5 %collective-permute-done.12.rest_12_ = bf16[10,128,128]{2,1,0:T(8,128)(2,1)S(1)} collective-permute-done((bf16[10,128,128]{2,1,0:T(8,128)(2,1)}, bf16[10,128,128]{2,1,0:T(8,128)(2,1)S(1)}, u32[]{:S(2)}, u32[]{:S(2)}) %collective-permute-start.12) | collective-permute-done | bytes 327712 | tf_op jit(solution)/shard_map/ppermute | solution.py:288
  63.4 3.9 %shard_map.95 = bf16[80,32,128]{2,1,0:T(8,128)(2,1)S(1)} custom-call(f32[32,1,128]{2,1,0:T(1,128)S(1)} %all-to-all-done.notices, bf16[32,32,128]{2,1,0:T(8,128)(2,1)S(1)} %all-to-all-done.2.came, bf16[16,16,128]{2,1,0:T(8,128)(2,1)S(1)} %get-tuple-element.21.mine, bf16[16,16,128]{2,1,0:T(8,128)(2,1)S(1)} %collective-permute-done.3.other, ...), custom_call_target="tpu_custom_call" | custom-call | tf_op jit(solution)/shard_map/pallas_call | solution.py:353
  67.2 17.6 %all_to_all.20 = bf16[80,32,128]{2,1,0:T(8,128)(2,1)S(1)} all-to-all(bf16[80,32,128]{2,1,0:T(8,128)(2,1)S(1)} %shard_map.95), channel_id=1, replica_groups=mesh['xl'=2,'z'=8,'core'=2,'y'=4,'xh'=2] {'xl','y','xh'}, dimensions={0} | all-to-all | bytes 1310720 | tf_op jit(solution)/shard_map/all_to_all | solution.py:277
  84.9 0.7 shard_map.96
  (19 shorter events, 0.0 us)
Async XLA Ops:
  0.0 40.6 %copy-start = (bf16[16,1,256,256]{3,2,1,0:T(8,128)(2,1)S(1)}, bf16[16,1,256,256]{3,2,1,0:T(8,128)(2,1)}, u32[]{:S(2)}) copy-start(bf16[16,1,256,256]{3,2,1,0:T(8,128)(2,1)} %cache.3) | copy-start | bytes 6291460
  0.0 3.7 %collective-permute-start = (bf16[10,128,128]{2,1,0:T(8,128)(2,1)}, bf16[10,128,128]{2,1,0:T(8,128)(2,1)S(1)}, u32[]{:S(2)}, u32[]{:S(2)}) collective-permute-start(bf16[10,128,128]{2,1,0:T(8,128)(2,1)} %rest_0_.1), channel_id=1, source_target_pairs={{0,8},{8,0},{1,9},{9,1},{2,10},{10,2},{3,11},{11,3},{4,12},{12,4},... | collective-permute-start | bytes 983048 | tf_op jit(solution)/shard_map/ppermute | solution.py:280
  0.0 16.6 %collective-permute-start.2 = (bf16[10,128,128]{2,1,0:T(8,128)(2,1)}, bf16[10,128,128]{2,1,0:T(8,128)(2,1)S(1)}, u32[]{:S(2)}, u32[]{:S(2)}) collective-permute-start(bf16[10,128,128]{2,1,0:T(8,128)(2,1)} %rest_0_.1), channel_id=1, source_target_pairs={{0,16},{8,120},{16,32},{24,8},{32,48},{40,24},{48,64},{56,40},{64,... | collective-permute-start | bytes 983048 | tf_op jit(solution)/shard_map/ppermute | solution.py:288
  3.7 18.3 %collective-permute-start.1 = (bf16[10,128,128]{2,1,0:T(8,128)(2,1)S(1)}, bf16[10,128,128]{2,1,0:T(8,128)(2,1)}, u32[]{:S(2)}, u32[]{:S(2)}) collective-permute-start(bf16[10,128,128]{2,1,0:T(8,128)(2,1)S(1)} %collective-permute-done.rest_5_), channel_id=1, source_target_pairs={{0,16},{8,120},{16,32},{24,8},{32,48},{40,24},{48,64},{56,40},{64,... | collective-permute-start | bytes 983048 | tf_op jit(solution)/shard_map/ppermute | solution.py:288
  5.7 16.3 %all-to-all-start = ((f32[32,1,128]{2,1,0:T(1,128)}), f32[32,1,128]{2,1,0:T(1,128)S(1)}, u32[]{:S(2)}, u32[]{:S(2)}) async-start(f32[32,1,128]{2,1,0:T(1,128)} %get-tuple-element.17), calls=%async_computation | async-start | bytes 32768 | tf_op jit(solution)/shard_map/all_to_all | solution.py:277
  16.6 46.8 %copy-start.1 = (bf16[10,128,128]{2,1,0:T(8,128)(2,1)S(1)}, bf16[10,128,128]{2,1,0:T(8,128)(2,1)}, u32[]{:S(2)}) copy-start(bf16[10,128,128]{2,1,0:T(8,128)(2,1)} %rest_0_.1) | copy-start | bytes 983044
  16.6 13.9 %collective-permute-start.4 = (bf16[10,128,128]{2,1,0:T(8,128)(2,1)S(1)}, bf16[10,128,128]{2,1,0:T(8,128)(2,1)}, u32[]{:S(2)}, u32[]{:S(2)}) collective-permute-start(bf16[10,128,128]{2,1,0:T(8,128)(2,1)S(1)} %collective-permute-done.2.rest_1_), channel_id=1, source_target_pairs={{0,16},{8,120},{16,32},{24,8},{32,48},{40,24},{48,64},{56,40},{64,... | collective-permute-start | bytes 983048 | tf_op jit(solution)/shard_map/ppermute | solution.py:288
  22.0 11.5 %collective-permute-start.7 = (bf16[10,128,128]{2,1,0:T(8,128)(2,1)}, bf16[10,128,128]{2,1,0:T(8,128)(2,1)}, u32[]{:S(2)}, u32[]{:S(2)}) collective-permute-start(bf16[10,128,128]{2,1,0:T(8,128)(2,1)} %collective-permute-done.1.rest_6_), channel_id=1, source_target_pairs={{0,16},{8,120},{16,32},{24,8},{32,48},{40,24},{48,64},{56,40},{64,... | collective-permute-start | bytes 983048 | tf_op jit(solution)/shard_map/ppermute | solution.py:288
  24.4 16.2 %all-to-all-start.1 = ((bf16[32,20,128]{2,1,0:T(8,128)(2,1)}), bf16[32,20,128]{2,1,0:T(8,128)(2,1)S(1)}, u32[]{:S(2)}, u32[]{:S(2)}) async-start(bf16[32,20,128]{2,1,0:T(8,128)(2,1)} %shard_map.92), calls=%async_computation.1 | async-start | bytes 393216 | tf_op jit(solution)/shard_map/all_to_all | solution.py:277
  28.7 4.9 %collective-permute-start.3 = (bf16[16,16,128]{2,1,0:T(8,128)(2,1)S(1)}, bf16[16,16,128]{2,1,0:T(8,128)(2,1)S(1)}, u32[]{:S(2)}, u32[]{:S(2)}) collective-permute-start(bf16[16,16,128]{2,1,0:T(8,128)(2,1)S(1)} %shard_map.94), channel_id=1, source_target_pairs={{0,128},{128,0},{1,129},{129,1},{2,130},{130,2},{3,131},{131,3},{4... | collective-permute-start | bytes 196616 | tf_op jit(solution)/shard_map/ppermute | solution.py:280
  30.6 16.1 %collective-permute-start.9 = (bf16[10,128,128]{2,1,0:T(8,128)(2,1)S(1)}, bf16[10,128,128]{2,1,0:T(8,128)(2,1)}, u32[]{:S(2)}, u32[]{:S(2)}) collective-permute-start(bf16[10,128,128]{2,1,0:T(8,128)(2,1)S(1)} %collective-permute-done.2.rest_1_), channel_id=1, source_target_pairs={{0,8},{8,0},{1,9},{9,1},{2,10},{10,2},{3,11},{11,3},{4,12},{12,4},... | collective-permute-start | bytes 983048 | tf_op jit(solution)/shard_map/ppermute | solution.py:280
  30.6 16.3 %collective-permute-start.5 = (bf16[10,128,128]{2,1,0:T(8,128)(2,1)}, bf16[10,128,128]{2,1,0:T(8,128)(2,1)}, u32[]{:S(2)}, u32[]{:S(2)}) collective-permute-start(bf16[10,128,128]{2,1,0:T(8,128)(2,1)} %collective-permute-done.4.rest_2_), channel_id=1, source_target_pairs={{0,16},{8,120},{16,32},{24,8},{32,48},{40,24},{48,64},{56,40},{64,... | collective-permute-start | bytes 983048 | tf_op jit(solution)/shard_map/ppermute | solution.py:288
  32.1 15.2 %collective-permute-start.13 = (bf16[10,128,128]{2,1,0:T(8,128)(2,1)}, bf16[10,128,128]{2,1,0:T(8,128)(2,1)}, u32[]{:S(2)}, u32[]{:S(2)}) collective-permute-start(bf16[10,128,128]{2,1,0:T(8,128)(2,1)} %collective-permute-done.1.rest_6_), channel_id=1, source_target_pairs={{0,8},{8,0},{1,9},{9,1},{2,10},{10,2},{3,11},{11,3},{4,12},{12,4},... | collective-permute-start | bytes 983048 | tf_op jit(solution)/shard_map/ppermute | solution.py:280
  33.6 15.4 %collective-permute-start.8 = (bf16[10,128,128]{2,1,0:T(8,128)(2,1)}, bf16[10,128,128]{2,1,0:T(8,128)(2,1)}, u32[]{:S(2)}, u32[]{:S(2)}) collective-permute-start(bf16[10,128,128]{2,1,0:T(8,128)(2,1)} %collective-permute-done.7.rest_7_), channel_id=1, source_target_pairs={{0,16},{8,120},{16,32},{24,8},{32,48},{40,24},{48,64},{56,40},{64,... | collective-permute-start | bytes 983048 | tf_op jit(solution)/shard_map/ppermute | solution.py:288
  33.6 16.5 %collective-permute-start.10 = (bf16[10,128,128]{2,1,0:T(8,128)(2,1)}, bf16[10,128,128]{2,1,0:T(8,128)(2,1)}, u32[]{:S(2)}, u32[]{:S(2)}) collective-permute-start(bf16[10,128,128]{2,1,0:T(8,128)(2,1)} %collective-permute-done.4.rest_2_), channel_id=1, source_target_pairs={{0,8},{8,0},{1,9},{9,1},{2,10},{10,2},{3,11},{11,3},{4,12},{12,4},... | collective-permute-start | bytes 983048 | tf_op jit(solution)/shard_map/ppermute | solution.py:280
  42.1 0.7 copy-start.2
  42.8 17.1 %all-to-all-start.2 = ((bf16[32,32,128]{2,1,0:T(8,128)(2,1)}), bf16[32,32,128]{2,1,0:T(8,128)(2,1)S(1)}, u32[]{:S(2)}, u32[]{:S(2)}) async-start(bf16[32,32,128]{2,1,0:T(8,128)(2,1)} %copy-done.2), calls=%async_computation.2 | async-start | bytes 524288 | tf_op jit(solution)/shard_map/all_to_all | solution.py:277
  46.7 3.9 %collective-permute-start.14 = (bf16[10,128,128]{2,1,0:T(8,128)(2,1)}, bf16[10,128,128]{2,1,0:T(8,128)(2,1)S(1)}, u32[]{:S(2)}, u32[]{:S(2)}) collective-permute-start(bf16[10,128,128]{2,1,0:T(8,128)(2,1)} %collective-permute-done.7.rest_7_), channel_id=1, source_target_pairs={{0,8},{8,0},{1,9},{9,1},{2,10},{10,2},{3,11},{11,3},{4,12},{12,4},... | collective-permute-start | bytes 983048 | tf_op jit(solution)/shard_map/ppermute | solution.py:280
  46.9 3.6 %collective-permute-start.11 = (bf16[10,128,128]{2,1,0:T(8,128)(2,1)}, bf16[10,128,128]{2,1,0:T(8,128)(2,1)S(1)}, u32[]{:S(2)}, u32[]{:S(2)}) collective-permute-start(bf16[10,128,128]{2,1,0:T(8,128)(2,1)} %collective-permute-done.5.rest_3_), channel_id=1, source_target_pairs={{0,8},{8,0},{1,9},{9,1},{2,10},{10,2},{3,11},{11,3},{4,12},{12,4},... | collective-permute-start | bytes 983048 | tf_op jit(solution)/shard_map/ppermute | solution.py:280
  47.3 12.6 %collective-permute-start.6 = (bf16[10,128,128]{2,1,0:T(8,128)(2,1)}, bf16[10,128,128]{2,1,0:T(8,128)(2,1)S(1)}, u32[]{:S(2)}, u32[]{:S(2)}) collective-permute-start(bf16[10,128,128]{2,1,0:T(8,128)(2,1)} %collective-permute-done.5.rest_3_), channel_id=1, source_target_pairs={{0,16},{8,120},{16,32},{24,8},{32,48},{40,24},{48,64},{56,40},{64,... | collective-permute-start | bytes 983048 | tf_op jit(solution)/shard_map/ppermute | solution.py:288
  49.0 10.9 %collective-permute-start.15 = (bf16[10,128,128]{2,1,0:T(8,128)(2,1)}, bf16[10,128,128]{2,1,0:T(8,128)(2,1)S(1)}, u32[]{:S(2)}, u32[]{:S(2)}) collective-permute-start(bf16[10,128,128]{2,1,0:T(8,128)(2,1)} %collective-permute-done.8.rest_8_), channel_id=1, source_target_pairs={{0,8},{8,0},{1,9},{9,1},{2,10},{10,2},{3,11},{11,3},{4,12},{12,4},... | collective-permute-start | bytes 983048 | tf_op jit(solution)/shard_map/ppermute | solution.py:280
  50.1 13.2 %collective-permute-start.12 = (bf16[10,128,128]{2,1,0:T(8,128)(2,1)}, bf16[10,128,128]{2,1,0:T(8,128)(2,1)S(1)}, u32[]{:S(2)}, u32[]{:S(2)}) collective-permute-start(bf16[10,128,128]{2,1,0:T(8,128)(2,1)} %collective-permute-done.8.rest_8_), channel_id=1, source_target_pairs={{0,16},{8,120},{16,32},{24,8},{32,48},{40,24},{48,64},{56,40},{64,... | collective-permute-start | bytes 983048 | tf_op jit(solution)/shard_map/ppermute | solution.py:288

commit v8 on v7

--- a/solution.py
+++ b/solution.py
@@ -42,13 +42,17 @@
     return pl.BlockSpec(memory_space=pltpu.HBM)
 
 
+def spec(shape):
+    return vmem() if isinstance(shape, jax.ShapeDtypeStruct) else hbm()
+
+
 def call(body, out_shape, in_specs, scratch=(), **kw):
     single = not isinstance(out_shape, (list, tuple))
     return pl.pallas_call(
         body,
         out_shape=out_shape,
         in_specs=in_specs,
-        out_specs=vmem() if single else [vmem()] * len(out_shape),
+        out_specs=spec(out_shape) if single else [spec(o) for o in out_shape],
         scratch_shapes=list(scratch),
         compiler_params=pltpu.CompilerParams(vmem_limit_bytes=VMEM_LIMIT),
         **kw,
@@ -98,15 +102,23 @@
     return notices[rep, 0, lane].astype(I32)
 
 
-def pull_body(notices, packs, out):
+def pull_body(notices, packs, out, sems):
     me = at(notices, 0, ME)
 
-    def one(peer, carry):
-        turn = at(notices, peer, ROUND)
-        out[peer] = packs[at(notices, me, DEP + jnp.maximum(turn, 0))]
+    def copy(peer):
+        slot = at(notices, me, DEP + jnp.maximum(at(notices, peer, ROUND), 0))
+        return pltpu.make_async_copy(packs.at[slot], out.at[peer], sems.at[peer])
+
+    def start(peer, carry):
+        copy(peer).start()
         return carry
 
-    lax.fori_loop(0, REP, one, 0, unroll=4)
+    def wait(peer, carry):
+        pltpu.make_async_copy(packs.at[0], out.at[peer], sems.at[peer]).wait()
+        return carry
+
+    lax.fori_loop(0, REP, start, 0, unroll=8)
+    lax.fori_loop(0, REP, wait, 0, unroll=8)
 
 
 def score(pack, keys, length):
@@ -175,7 +187,7 @@
     lax.fori_loop(0, SLOTS, one, 0)
 
 
-def attend_body(notices, pulled, packs, cache, send, out, scores, held):
+def attend_body(notices, pulled, packs, cache, send, out, scores, held, sems):
     per = STEPS * HEADS
     me = at(notices, 0, ME)
     for s in range(SLOTS):
@@ -186,19 +198,42 @@
         scores[s] = score(held[s], cache[s, 0, :, :HD], at(notices, me, LEN + s))
     for s in range(SLOTS):
         out[s] = blend(held[s], scores[s], cache[s, 0, :, HD:])
+    copies = []
     for k in range(MOVE):
         goal = at(notices, me, DEST + k)
-        rows = out[at(notices, me, DEP + k)]
-        send[goal, :per, :] = rows
-        send[lax.rem(goal + REP // XL, REP), per:, :] = rows
+        rows = out.at[at(notices, me, DEP + k)]
+        for side, to in enumerate((goal, lax.rem(goal + REP // XL, REP))):
+            where = send.at[to, side * per : (side + 1) * per, :]
+            copies.append(pltpu.make_async_copy(rows, where, sems.at[k, side]))
+            copies[-1].start()
+    for c in copies:
+        c.wait()
+
+
+def add_blocks(notices, rows, total, blocks, line, step, origin):
+    me = at(notices, 0, ME)
+    xl, z = lax.div(me, Z * CORE), lax.rem(lax.div(me, CORE), Z)
+    far = lax.rem(z - (1 - 2 * line) * step + Z, Z)
+    src = (xl * Z + far) * CORE + origin
+    for lo in range(0, OWN, 5):
+        products = []
+        for n in range(lo, lo + 5):
+            products.append(
+                jnp.dot(
+                    rows[at(notices, src, HEAD + n)], blocks[n], preferred_element_type=F32
+                )
+                * notices[src, 0, SCALE + n]
+            )
+        for n in range(lo, lo + 5):
+            total[at(notices, src, COL + n)] += products[n - lo]
 
 
 def project_body(notices, came, mine, other, *rest):
-    arrays, out, slots, rows, total = rest[:-4], rest[-4], rest[-3], rest[-2], rest[-1]
+    arrays, rows, total, slots = rest[:-3], rest[-3], rest[-2], rest[-1]
     per = STEPS * HEADS
     me = at(notices, 0, ME)
     pair = lax.rem(me + REP // XL, REP)
-    xl, z, core = lax.div(me, Z * CORE), lax.rem(lax.div(me, CORE), Z), lax.rem(me, CORE)
+    xl, core = lax.div(me, Z * CORE), lax.rem(me, CORE)
     first, second = xl * SLOTS, (1 - xl) * SLOTS
     for s in range(SLOTS):
         slots[pl.ds(pl.multiple_of((first + s) * per, per), per), :] = mine[s].astype(F32)
@@ -223,34 +258,21 @@
                     pl.ds(side * SLOTS * per + t * HEADS + h, SLOTS, stride=per), :
                 ].astype(BF16)
     total[...] = jnp.zeros_like(total)
-
-    def run(blocks, first, z_src, core_src):
-        src = (xl * Z + z_src) * CORE + core_src
-        for lo in range(0, OWN, 5):
-            products = []
-            for n in range(lo, lo + 5):
-                products.append(
-                    jnp.dot(
-                        rows[at(notices, src, HEAD + n)],
-                        blocks[first + n],
-                        preferred_element_type=F32,
-                    )
-                    * notices[src, 0, SCALE + n]
-                )
-            for n in range(lo, lo + 5):
-                total[at(notices, src, COL + n)] += products[n - lo]
-
     half = Z // 2
-    for line, same, cross in (
-        (core, arrays[: half + 1], arrays[half + 1 : Z + 1]),
-        (1 - core, (None, *arrays[Z + 1 : Z + half + 1]), (None, *arrays[Z + half + 1 :])),
-    ):
-        for step in range(half + 1):
-            far = lax.rem(z - (1 - 2 * line) * step + Z, Z)
-            if same[step] is not None:
-                run(same[step], 0, far, line)
-            if step < half and cross[step] is not None:
-                run(cross[step], 0, far, 1 - line)
+    steps = [(0, core, core), (0, core, 1 - core)]
+    steps += [(i, core, core) for i in range(1, half)]
+    steps += [(i, core, 1 - core) for i in range(1, half)]
+    steps += [(i, 1 - core, 1 - core) for i in range(1, half)]
+    steps += [(i, 1 - core, core) for i in range(1, half)]
+    for blocks, (step, line, origin) in zip(arrays, steps):
+        add_blocks(notices, rows, total, blocks, line, step, origin)
+
+
+def last_body(notices, rows, so_far, four, four_x, out, total):
+    core = lax.rem(at(notices, 0, ME), CORE)
+    total[...] = so_far[...]
+    add_blocks(notices, rows, total, four, core, Z // 2, core)
+    add_blocks(notices, rows, total, four_x, core, Z // 2, 1 - core)
     out[:COLS] = total[:, :ROWS, :].astype(BF16)
     out[COLS:] = total[:, ROWS:, :].astype(BF16)
 
@@ -327,39 +349,49 @@
     near, stays = lax.optimization_barrier((near, stays))
     near_x, notices = lax.optimization_barrier((near_x, notices))
     two, two_x = around(near, 1), around(near_x, 1)
-    near_sib, near_x_sib = swap(near, "core"), swap(near_x, "core")
     other = swap(stays, "xl")
     to_pull = call(
-        pull_body, jax.ShapeDtypeStruct((REP, PACK, HD), BF16), [smem(), vmem()]
+        pull_body,
+        pltpu.HBM((REP, PACK, HD), BF16),
+        [smem(), vmem()],
+        [pltpu.SemaphoreType.DMA((REP,))],
     )(notices, packs)
     pulled = exchange(to_pull, rep_axes)
     three, three_x = around(two, 1), around(two_x, 1)
-    two_sib, two_x_sib = swap(two, "core"), swap(two_x, "core")
     send, mine = call(
         attend_body,
         [
-            jax.ShapeDtypeStruct((REP, 2 * per, HD), BF16),
+            pltpu.HBM((REP, 2 * per, HD), BF16),
             jax.ShapeDtypeStruct((SLOTS, per, HD), BF16),
         ],
         [smem()] + [vmem()] * 3,
-        [pltpu.VMEM((SLOTS, per, CTX), F32), pltpu.VMEM((SLOTS, PACK, HD), BF16)],
+        [
+            pltpu.VMEM((SLOTS, per, CTX), F32),
+            pltpu.VMEM((SLOTS, PACK, HD), BF16),
+            pltpu.SemaphoreType.DMA((MOVE, 2)),
+        ],
     )(notices, pulled, packs, kv_cache)
     came = exchange(send, rep_axes)
-    four = around(three, 1)
-    three_sib, three_x_sib = swap(three, "core"), swap(three_x, "core")
-    four_sib = around(three_x, 1)
-    arrays = [codes, near, two, three, four, sib, near_x, two_x, three_x]
-    arrays += [near_sib, two_sib, three_sib, four_sib, near_x_sib, two_x_sib, three_x_sib]
+    four, four_x = around(three, 1), around(three_x, 1)
+    rows, total = call(
+        project_body,
+        [
+            jax.ShapeDtypeStruct((HEADS, XL * ROWS, HD), BF16),
+            jax.ShapeDtypeStruct((COLS, XL * ROWS, HD), F32),
+        ],
+        [smem()] + [vmem()] * 17,
+        [pltpu.VMEM(((XL * SLOTS + 1) * per, HD), F32)],
+    )(
+        *(notices, came, mine, other),
+        *(codes, sib, near, two, three, near_x, two_x, three_x),
+        *(swap(x, "core") for x in (near, two, three, near_x, two_x, three_x)),
+    )
     parts = call(
-        project_body,
+        last_body,
         jax.ShapeDtypeStruct((XL * COLS, ROWS, HD), BF16),
-        [smem()] + [vmem()] * (3 + len(arrays)),
-        [
-            pltpu.VMEM(((XL * SLOTS + 1) * per, HD), F32),
-            pltpu.VMEM((HEADS, XL * ROWS, HD), BF16),
-            pltpu.VMEM((COLS, XL * ROWS, HD), F32),
-        ],
-    )(notices, came, mine, other, *arrays)
+        [smem()] + [vmem()] * 4,
+        [pltpu.VMEM((COLS, XL * ROWS, HD), F32)],
+    )(notices, rows, total, four, four_x)
     parts = exchange(parts, ("xl",) + tp_axes).reshape(XL * TP, OUT_COLS, ROWS, HD)
     return call(
         sum_body, jax.ShapeDtypeStruct((STEPS, SLOTS, OUT_COLS * HD), BF16), [vmem()]

time: 86.3 us -> 84 us (0.973)
  waiting for transfers between devices: 22.2 us -> 18.6 us
  Pallas kernels: 12.4 us -> 14.5 us
    ppermute x8, waiting for transfers between devices: 12.8 us -> 0.02 us  [around(): return lax.ppermute(x, ('z', 'core'), pairs)]
    all_to_all x3, waiting for transfers between devices: 9.36 us -> 18.5 us  [exchange(): return lax.all_to_all(x, axes, split_axis=0, concat_axis=0, tiled=True)]
    ppermute x8, starting transfers between devices: 10 us -> 12.6 us  [around(): return lax.ppermute(x, ('z', 'core'), pairs)]
    ppermute x8, starting transfers between devices: 6.33 us -> 3.86 us  [swap(): return lax.ppermute(x, axis, [(0, 1), (1, 0)])]
    pallas_call x3 -> x4, Pallas kernels: 7.1 us -> 9.12 us  [the longest x1 3.61 us: shards(): call(project_body, [jax.ShapeDtypeStruct((HEADS, XL * ROWS, HD), BF16), j...]
  transfers between devices with their start and end apart: 19 -> 19, of which waited for: 4 -> 3; matrix products, arithmetic and copies ran while one was open for 0% -> 0% of each run, Pallas kernels for 9% -> 15%
where the time goes in v8:
time: 84 us; the launch traced here: 83.5 us
  starting transfers between devices  32.7 us (39%)
  waiting for transfers between devices  18.6 us (22%)
  blocking collectives  17.7 us (21%)
  Pallas kernels  14.5 us (17%)
    all_to_all x3, waiting for transfers between devices, exchange(): return lax.all_to_all(x, axes, split_axis=0, concat_axis=0, tiled=True)  18.5 us
    all_to_all x1, blocking collectives, exchange(): return lax.all_to_all(x, axes, split_axis=0, concat_axis=0, tiled=True)  17.7 us
    all_to_all x3, starting transfers between devices, exchange(): return lax.all_to_all(x, axes, split_axis=0, concat_axis=0, tiled=True)  16.2 us
    ppermute x8, starting transfers between devices, around(): return lax.ppermute(x, ('z', 'core'), pairs)  12.6 us
    ppermute x8, starting transfers between devices, swap(): return lax.ppermute(x, axis, [(0, 1), (1, 0)])  3.86 us
    pallas_call x1, Pallas kernels, shards(): call(project_body, [jax.ShapeDtypeStruct((HEADS, XL * ROWS, HD), BF16), j...  3.61 us
    pallas_call x1, Pallas kernels, shards(): call(stay_body, jax.ShapeDtypeStruct((SLOTS, per, HD), BF16), [hbm()] * 2...  2.93 us
    pallas_call x1, Pallas kernels, shards(): call(attend_body, [pltpu.HBM((REP, 2 * per, HD), BF16), jax.ShapeDtypeStr...  2.39 us
  transfers between devices with their start and end apart: 19, of which 3 were waited for; matrix products, arithmetic and copies ran while one was open for 0% of the time, Pallas kernels for 15%

profile of v8, /device:TPU:8, one launch (start us, length us, event | category | flops | bytes accessed | tf_op | source)
XLA Modules:
  0.0 83.5 jit_solution(7256354197945192099)
XLA Ops:
  0.0 0.0 collective-permute-start
  0.0 2.0 %collective-permute-start.2 = (bf16[10,128,128]{2,1,0:T(8,128)(2,1)}, bf16[10,128,128]{2,1,0:T(8,128)(2,1)S(1)}, u32[]{:S(2)}, u32[]{:S(2)}) collective-permute-start(bf16[10,128,128]{2,1,0:T(8,128)(2,1)} %rest_0_.1), channel_id=1, source_target_pairs={{0,16},{8,120},{16,32},{24,8},{32,48},{40,24},{48,64},{56,40},{64,... | collective-permute-start | bytes 983048 | tf_op jit(solution)/shard_map/ppermute | solution.py:310
  2.0 1.7 %shard_map.91 = (f32[32,1,128]{2,1,0:T(1,128)}, bf16[16,20,128]{2,1,0:T(8,128)(2,1)S(1)}) custom-call(s32[1]{0:T(128)} %bitcast.place, s32[1,13]{1,0:T(1,128)} %dep_in.1, s32[1,13]{1,0:T(1,128)} %refs_1_.1, s32[16]{0:T(128)} %lengths_in.1, s32[10]{0:T(128)} %refs_3_.1, f32[10]{0:T(128)} %refs_4_.1, bf16[2,16,8,128]{3,2,1,0:T(8,128)(2,1)} %refs_5_.1, ...), custom_call_target="tpu_custom_call" | custom-call | tf_op jit(solution)/shard_map/pallas_call | solution.py:322
  3.7 2.0 %collective-permute-start.1 = (bf16[10,128,128]{2,1,0:T(8,128)(2,1)S(1)}, bf16[10,128,128]{2,1,0:T(8,128)(2,1)}, u32[]{:S(2)}, u32[]{:S(2)}) collective-permute-start(bf16[10,128,128]{2,1,0:T(8,128)(2,1)S(1)} %collective-permute-done.rest_1_), channel_id=1, source_target_pairs={{0,16},{8,120},{16,32},{24,8},{32,48},{40,24},{48,64},{56,40},{64,... | collective-permute-start | bytes 983048 | tf_op jit(solution)/shard_map/ppermute | solution.py:310
  5.7 8.0 %all-to-all-start = ((f32[32,1,128]{2,1,0:T(1,128)}), f32[32,1,128]{2,1,0:T(1,128)S(1)}, u32[]{:S(2)}, u32[]{:S(2)}) async-start(f32[32,1,128]{2,1,0:T(1,128)} %get-tuple-element.19), calls=%async_computation | async-start | bytes 32768 | tf_op jit(solution)/shard_map/all_to_all | solution.py:299
  13.7 2.9 %shard_map.94 = bf16[16,16,128]{2,1,0:T(8,128)(2,1)S(1)} custom-call(s32[1,13]{1,0:T(1,128)} %dep_in.1, s32[16]{0:T(128)} %lengths_in.1, bf16[16,20,128]{2,1,0:T(8,128)(2,1)S(1)} %get-tuple-element.21.packs, bf16[16,1,256,256]{3,2,1,0:T(8,128)(2,1)} %cache.3), custom_call_target="tpu_custom_call" | custom-call | tf_op jit(solution)/shard_map/pallas_call | solution.py:337
  16.6 0.0 copy-start.1
  16.7 1.8 %collective-permute-start.4 = (bf16[10,128,128]{2,1,0:T(8,128)(2,1)S(1)}, bf16[10,128,128]{2,1,0:T(8,128)(2,1)}, u32[]{:S(2)}, u32[]{:S(2)}) collective-permute-start(bf16[10,128,128]{2,1,0:T(8,128)(2,1)S(1)} %collective-permute-done.2.rest_2_), channel_id=1, source_target_pairs={{0,16},{8,120},{16,32},{24,8},{32,48},{40,24},{48,64},{56,40},{64,... | collective-permute-start | bytes 983048 | tf_op jit(solution)/shard_map/ppermute | solution.py:310
  18.5 3.5 %all-to-all-done.notices = f32[32,1,128]{2,1,0:T(1,128)S(1)} async-done(((f32[32,1,128]{2,1,0:T(1,128)}), f32[32,1,128]{2,1,0:T(1,128)S(1)}, u32[]{:S(2)}, u32[]{:S(2)}) %all-to-all-start) | async-done | bytes 16416 | tf_op jit(solution)/shard_map/all_to_all | solution.py:299
  22.0 0.6 collective-permute-start.6
  22.6 1.9 %shard_map.92 = bf16[32,20,128]{2,1,0:T(8,128)(2,1)} custom-call(f32[32,1,128]{2,1,0:T(1,128)S(1)} %all-to-all-done.notices, bf16[16,20,128]{2,1,0:T(8,128)(2,1)S(1)} %get-tuple-element.21.packs), custom_call_target="tpu_custom_call" | custom-call | tf_op jit(solution)/shard_map/pallas_call | solution.py:353
  24.6 4.3 %all-to-all-start.1 = ((bf16[32,20,128]{2,1,0:T(8,128)(2,1)}), bf16[32,20,128]{2,1,0:T(8,128)(2,1)S(1)}, u32[]{:S(2)}, u32[]{:S(2)}) async-start(bf16[32,20,128]{2,1,0:T(8,128)(2,1)} %shard_map.92), calls=%async_computation.1 | async-start | bytes 393216 | tf_op jit(solution)/shard_map/all_to_all | solution.py:299
  28.9 1.9 %collective-permute-start.3 = (bf16[16,16,128]{2,1,0:T(8,128)(2,1)S(1)}, bf16[16,16,128]{2,1,0:T(8,128)(2,1)S(1)}, u32[]{:S(2)}, u32[]{:S(2)}) collective-permute-start(bf16[16,16,128]{2,1,0:T(8,128)(2,1)S(1)} %shard_map.94), channel_id=1, source_target_pairs={{0,128},{128,0},{1,129},{129,1},{2,130},{130,2},{3,131},{131,3},{4... | collective-permute-start | bytes 196616 | tf_op jit(solution)/shard_map/ppermute | solution.py:302
  30.8 0.0 collective-permute-start.8
  30.8 0.0 collective-permute-done.4.rest_3_
  30.8 1.5 %collective-permute-start.5 = (bf16[10,128,128]{2,1,0:T(8,128)(2,1)}, bf16[10,128,128]{2,1,0:T(8,128)(2,1)}, u32[]{:S(2)}, u32[]{:S(2)}) collective-permute-start(bf16[10,128,128]{2,1,0:T(8,128)(2,1)} %collective-permute-done.4.rest_3_), channel_id=1, source_target_pairs={{0,16},{8,120},{16,32},{24,8},{32,48},{40,24},{48,64},{56,40},{64,... | collective-permute-start | bytes 983048 | tf_op jit(solution)/shard_map/ppermute | solution.py:310
  32.3 1.5 %collective-permute-start.7 = (bf16[10,128,128]{2,1,0:T(8,128)(2,1)}, bf16[10,128,128]{2,1,0:T(8,128)(2,1)}, u32[]{:S(2)}, u32[]{:S(2)}) collective-permute-start(bf16[10,128,128]{2,1,0:T(8,128)(2,1)} %collective-permute-done.6.rest_6_), channel_id=1, source_target_pairs={{0,16},{8,120},{16,32},{24,8},{32,48},{40,24},{48,64},{56,40},{64,... | collective-permute-start | bytes 983048 | tf_op jit(solution)/shard_map/ppermute | solution.py:310
  33.7 1.2 %collective-permute-start.11 = (bf16[10,128,128]{2,1,0:T(8,128)(2,1)}, bf16[10,128,128]{2,1,0:T(8,128)(2,1)}, u32[]{:S(2)}, u32[]{:S(2)}) collective-permute-start(bf16[10,128,128]{2,1,0:T(8,128)(2,1)} %collective-permute-done.1.rest_5_), channel_id=1, source_target_pairs={{0,8},{8,0},{1,9},{9,1},{2,10},{10,2},{3,11},{11,3},{4,12},{12,4},... | collective-permute-start | bytes 983048 | tf_op jit(solution)/shard_map/ppermute | solution.py:302
  34.9 0.0 collective-permute-start.9
  35.0 5.8 %all-to-all-done.1.pulled = bf16[32,20,128]{2,1,0:T(8,128)(2,1)S(1)} async-done(((bf16[32,20,128]{2,1,0:T(8,128)(2,1)}), bf16[32,20,128]{2,1,0:T(8,128)(2,1)S(1)}, u32[]{:S(2)}, u32[]{:S(2)}) %all-to-all-start.1) | async-done | bytes 163872 | tf_op jit(solution)/shard_map/all_to_all | solution.py:299
  40.8 2.4 %shard_map.93 = (bf16[32,32,128]{2,1,0:T(8,128)(2,1)}, bf16[16,16,128]{2,1,0:T(8,128)(2,1)S(1)}) custom-call(f32[32,1,128]{2,1,0:T(1,128)S(1)} %all-to-all-done.notices, bf16[32,20,128]{2,1,0:T(8,128)(2,1)S(1)} %all-to-all-done.1.pulled, bf16[16,20,128]{2,1,0:T(8,128)(2,1)S(1)} %get-tuple-element.21.packs, bf16[16,1,256,256]{3,2,1,0:T(8,128)(2,1)S(1)} %copy-done), custom_call_target="tpu_custom_call" | custom-call | tf_op jit(solution)/shard_map/pallas_call | solution.py:361
  43.2 3.9 %all-to-all-start.2 = ((bf16[32,32,128]{2,1,0:T(8,128)(2,1)}), bf16[32,32,128]{2,1,0:T(8,128)(2,1)S(1)}, u32[]{:S(2)}, u32[]{:S(2)}) async-start(bf16[32,32,128]{2,1,0:T(8,128)(2,1)} %get-tuple-element.22), calls=%async_computation.2 | async-start | bytes 524288 | tf_op jit(solution)/shard_map/all_to_all | solution.py:299
  47.1 0.2 collective-permute-start.12
  47.3 0.3 collective-permute-start.10
  47.7 0.2 collective-permute-start.13
  47.9 1.8 %collective-permute-start.14 = (bf16[10,128,128]{2,1,0:T(8,128)(2,1)}, bf16[10,128,128]{2,1,0:T(8,128)(2,1)S(1)}, u32[]{:S(2)}, u32[]{:S(2)}) collective-permute-start(bf16[10,128,128]{2,1,0:T(8,128)(2,1)} %collective-permute-done.5.rest_4_), channel_id=1, source_target_pairs={{0,16},{8,120},{16,32},{24,8},{32,48},{40,24},{48,64},{56,40},{64,... | collective-permute-start | bytes 983048 | tf_op jit(solution)/shard_map/ppermute | solution.py:310
  49.6 1.5 %collective-permute-start.15 = (bf16[10,128,128]{2,1,0:T(8,128)(2,1)}, bf16[10,128,128]{2,1,0:T(8,128)(2,1)S(1)}, u32[]{:S(2)}, u32[]{:S(2)}) collective-permute-start(bf16[10,128,128]{2,1,0:T(8,128)(2,1)} %collective-permute-done.7.rest_7_), channel_id=1, source_target_pairs={{0,16},{8,120},{16,32},{24,8},{32,48},{40,24},{48,64},{56,40},{64,... | collective-permute-start | bytes 983048 | tf_op jit(solution)/shard_map/ppermute | solution.py:310
  51.1 9.2 %all-to-all-done.2.came = bf16[32,32,128]{2,1,0:T(8,128)(2,1)S(1)} async-done(((bf16[32,32,128]{2,1,0:T(8,128)(2,1)}), bf16[32,32,128]{2,1,0:T(8,128)(2,1)S(1)}, u32[]{:S(2)}, u32[]{:S(2)}) %all-to-all-start.2) | async-done | bytes 262176 | tf_op jit(solution)/shard_map/all_to_all | solution.py:299
  60.3 3.6 %shard_map.95 = (bf16[8,64,128]{2,1,0:T(8,128)(2,1)S(1)}, f32[40,64,128]{2,1,0:T(8,128)S(1)}) custom-call(f32[32,1,128]{2,1,0:T(1,128)S(1)} %all-to-all-done.notices, bf16[32,32,128]{2,1,0:T(8,128)(2,1)S(1)} %all-to-all-done.2.came, bf16[16,16,128]{2,1,0:T(8,128)(2,1)S(1)} %get-tuple-element.23.mine, bf16[16,16,128]{2,1,0:T(8,128)(2,1)S(1)} %collective-permute-done.3.other, ...), custom_call_target="tpu_custom_call" | custom-call | tf_op jit(solution)/shard_map/pallas_call | solution.py:376
  63.9 1.2 %shard_map.96 = bf16[80,32,128]{2,1,0:T(8,128)(2,1)S(1)} custom-call(f32[32,1,128]{2,1,0:T(1,128)S(1)} %all-to-all-done.notices, bf16[8,64,128]{2,1,0:T(8,128)(2,1)S(1)} %get-tuple-element.27.rows, f32[40,64,128]{2,1,0:T(8,128)S(1)} %get-tuple-element.28.so_far, bf16[10,128,128]{2,1,0:T(8,128)(2,1)S(1)} %collective-permute-done.14.four, ...), custom_call_target="tpu_custom_call" | custom-call | tf_op jit(solution)/shard_map/pallas_call | solution.py:389
  65.1 17.7 %all_to_all.20 = bf16[80,32,128]{2,1,0:T(8,128)(2,1)S(1)} all-to-all(bf16[80,32,128]{2,1,0:T(8,128)(2,1)S(1)} %shard_map.96), channel_id=1, replica_groups=mesh['xl'=2,'z'=8,'core'=2,'y'=4,'xh'=2] {'xl','y','xh'}, dimensions={0} | all-to-all | bytes 1310720 | tf_op jit(solution)/shard_map/all_to_all | solution.py:299
  82.8 0.7 shard_map.97
  (18 shorter events, 0.0 us)
Async XLA Ops:
  0.0 40.8 %copy-start = (bf16[16,1,256,256]{3,2,1,0:T(8,128)(2,1)S(1)}, bf16[16,1,256,256]{3,2,1,0:T(8,128)(2,1)}, u32[]{:S(2)}) copy-start(bf16[16,1,256,256]{3,2,1,0:T(8,128)(2,1)} %cache.3) | copy-start | bytes 6291460
  0.0 3.7 %collective-permute-start = (bf16[10,128,128]{2,1,0:T(8,128)(2,1)}, bf16[10,128,128]{2,1,0:T(8,128)(2,1)S(1)}, u32[]{:S(2)}, u32[]{:S(2)}) collective-permute-start(bf16[10,128,128]{2,1,0:T(8,128)(2,1)} %rest_0_.1), channel_id=1, source_target_pairs={{0,8},{8,0},{1,9},{9,1},{2,10},{10,2},{3,11},{11,3},{4,12},{12,4},... | collective-permute-start | bytes 983048 | tf_op jit(solution)/shard_map/ppermute | solution.py:302
  0.0 16.6 %collective-permute-start.2 = (bf16[10,128,128]{2,1,0:T(8,128)(2,1)}, bf16[10,128,128]{2,1,0:T(8,128)(2,1)S(1)}, u32[]{:S(2)}, u32[]{:S(2)}) collective-permute-start(bf16[10,128,128]{2,1,0:T(8,128)(2,1)} %rest_0_.1), channel_id=1, source_target_pairs={{0,16},{8,120},{16,32},{24,8},{32,48},{40,24},{48,64},{56,40},{64,... | collective-permute-start | bytes 983048 | tf_op jit(solution)/shard_map/ppermute | solution.py:310
  3.7 18.3 %collective-permute-start.1 = (bf16[10,128,128]{2,1,0:T(8,128)(2,1)S(1)}, bf16[10,128,128]{2,1,0:T(8,128)(2,1)}, u32[]{:S(2)}, u32[]{:S(2)}) collective-permute-start(bf16[10,128,128]{2,1,0:T(8,128)(2,1)S(1)} %collective-permute-done.rest_1_), channel_id=1, source_target_pairs={{0,16},{8,120},{16,32},{24,8},{32,48},{40,24},{48,64},{56,40},{64,... | collective-permute-start | bytes 983048 | tf_op jit(solution)/shard_map/ppermute | solution.py:310
  5.7 16.3 %all-to-all-start = ((f32[32,1,128]{2,1,0:T(1,128)}), f32[32,1,128]{2,1,0:T(1,128)S(1)}, u32[]{:S(2)}, u32[]{:S(2)}) async-start(f32[32,1,128]{2,1,0:T(1,128)} %get-tuple-element.19), calls=%async_computation | async-start | bytes 32768 | tf_op jit(solution)/shard_map/all_to_all | solution.py:299
  16.6 43.7 %copy-start.1 = (bf16[10,128,128]{2,1,0:T(8,128)(2,1)S(1)}, bf16[10,128,128]{2,1,0:T(8,128)(2,1)}, u32[]{:S(2)}) copy-start(bf16[10,128,128]{2,1,0:T(8,128)(2,1)} %rest_0_.1) | copy-start | bytes 983044
  16.7 14.1 %collective-permute-start.4 = (bf16[10,128,128]{2,1,0:T(8,128)(2,1)S(1)}, bf16[10,128,128]{2,1,0:T(8,128)(2,1)}, u32[]{:S(2)}, u32[]{:S(2)}) collective-permute-start(bf16[10,128,128]{2,1,0:T(8,128)(2,1)S(1)} %collective-permute-done.2.rest_2_), channel_id=1, source_target_pairs={{0,16},{8,120},{16,32},{24,8},{32,48},{40,24},{48,64},{56,40},{64,... | collective-permute-start | bytes 983048 | tf_op jit(solution)/shard_map/ppermute | solution.py:310
  22.0 10.2 %collective-permute-start.6 = (bf16[10,128,128]{2,1,0:T(8,128)(2,1)}, bf16[10,128,128]{2,1,0:T(8,128)(2,1)}, u32[]{:S(2)}, u32[]{:S(2)}) collective-permute-start(bf16[10,128,128]{2,1,0:T(8,128)(2,1)} %collective-permute-done.1.rest_5_), channel_id=1, source_target_pairs={{0,16},{8,120},{16,32},{24,8},{32,48},{40,24},{48,64},{56,40},{64,... | collective-permute-start | bytes 983048 | tf_op jit(solution)/shard_map/ppermute | solution.py:310
  24.6 16.2 %all-to-all-start.1 = ((bf16[32,20,128]{2,1,0:T(8,128)(2,1)}), bf16[32,20,128]{2,1,0:T(8,128)(2,1)S(1)}, u32[]{:S(2)}, u32[]{:S(2)}) async-start(bf16[32,20,128]{2,1,0:T(8,128)(2,1)} %shard_map.92), calls=%async_computation.1 | async-start | bytes 393216 | tf_op jit(solution)/shard_map/all_to_all | solution.py:299
  28.9 6.0 %collective-permute-start.3 = (bf16[16,16,128]{2,1,0:T(8,128)(2,1)S(1)}, bf16[16,16,128]{2,1,0:T(8,128)(2,1)S(1)}, u32[]{:S(2)}, u32[]{:S(2)}) collective-permute-start(bf16[16,16,128]{2,1,0:T(8,128)(2,1)S(1)} %shard_map.94), channel_id=1, source_target_pairs={{0,128},{128,0},{1,129},{129,1},{2,130},{130,2},{3,131},{131,3},{4... | collective-permute-start | bytes 196616 | tf_op jit(solution)/shard_map/ppermute | solution.py:302
  30.8 16.3 %collective-permute-start.8 = (bf16[10,128,128]{2,1,0:T(8,128)(2,1)S(1)}, bf16[10,128,128]{2,1,0:T(8,128)(2,1)}, u32[]{:S(2)}, u32[]{:S(2)}) collective-permute-start(bf16[10,128,128]{2,1,0:T(8,128)(2,1)S(1)} %collective-permute-done.2.rest_2_), channel_id=1, source_target_pairs={{0,8},{8,0},{1,9},{9,1},{2,10},{10,2},{3,11},{11,3},{4,12},{12,4},... | collective-permute-start | bytes 983048 | tf_op jit(solution)/shard_map/ppermute | solution.py:302
  30.8 16.5 %collective-permute-start.5 = (bf16[10,128,128]{2,1,0:T(8,128)(2,1)}, bf16[10,128,128]{2,1,0:T(8,128)(2,1)}, u32[]{:S(2)}, u32[]{:S(2)}) collective-permute-start(bf16[10,128,128]{2,1,0:T(8,128)(2,1)} %collective-permute-done.4.rest_3_), channel_id=1, source_target_pairs={{0,16},{8,120},{16,32},{24,8},{32,48},{40,24},{48,64},{56,40},{64,... | collective-permute-start | bytes 983048 | tf_op jit(solution)/shard_map/ppermute | solution.py:310
  32.3 15.4 %collective-permute-start.7 = (bf16[10,128,128]{2,1,0:T(8,128)(2,1)}, bf16[10,128,128]{2,1,0:T(8,128)(2,1)}, u32[]{:S(2)}, u32[]{:S(2)}) collective-permute-start(bf16[10,128,128]{2,1,0:T(8,128)(2,1)} %collective-permute-done.6.rest_6_), channel_id=1, source_target_pairs={{0,16},{8,120},{16,32},{24,8},{32,48},{40,24},{48,64},{56,40},{64,... | collective-permute-start | bytes 983048 | tf_op jit(solution)/shard_map/ppermute | solution.py:310
  33.7 14.1 %collective-permute-start.11 = (bf16[10,128,128]{2,1,0:T(8,128)(2,1)}, bf16[10,128,128]{2,1,0:T(8,128)(2,1)}, u32[]{:S(2)}, u32[]{:S(2)}) collective-permute-start(bf16[10,128,128]{2,1,0:T(8,128)(2,1)} %collective-permute-done.1.rest_5_), channel_id=1, source_target_pairs={{0,8},{8,0},{1,9},{9,1},{2,10},{10,2},{3,11},{11,3},{4,12},{12,4},... | collective-permute-start | bytes 983048 | tf_op jit(solution)/shard_map/ppermute | solution.py:302
  34.9 14.7 %collective-permute-start.9 = (bf16[10,128,128]{2,1,0:T(8,128)(2,1)}, bf16[10,128,128]{2,1,0:T(8,128)(2,1)}, u32[]{:S(2)}, u32[]{:S(2)}) collective-permute-start(bf16[10,128,128]{2,1,0:T(8,128)(2,1)} %collective-permute-done.4.rest_3_), channel_id=1, source_target_pairs={{0,8},{8,0},{1,9},{9,1},{2,10},{10,2},{3,11},{11,3},{4,12},{12,4},... | collective-permute-start | bytes 983048 | tf_op jit(solution)/shard_map/ppermute | solution.py:302
  43.2 17.1 %all-to-all-start.2 = ((bf16[32,32,128]{2,1,0:T(8,128)(2,1)}), bf16[32,32,128]{2,1,0:T(8,128)(2,1)S(1)}, u32[]{:S(2)}, u32[]{:S(2)}) async-start(bf16[32,32,128]{2,1,0:T(8,128)(2,1)} %get-tuple-element.22), calls=%async_computation.2 | async-start | bytes 524288 | tf_op jit(solution)/shard_map/all_to_all | solution.py:299
  47.1 4.0 %collective-permute-start.12 = (bf16[10,128,128]{2,1,0:T(8,128)(2,1)}, bf16[10,128,128]{2,1,0:T(8,128)(2,1)S(1)}, u32[]{:S(2)}, u32[]{:S(2)}) collective-permute-start(bf16[10,128,128]{2,1,0:T(8,128)(2,1)} %collective-permute-done.6.rest_6_), channel_id=1, source_target_pairs={{0,8},{8,0},{1,9},{9,1},{2,10},{10,2},{3,11},{11,3},{4,12},{12,4},... | collective-permute-start | bytes 983048 | tf_op jit(solution)/shard_map/ppermute | solution.py:302
  47.3 3.8 %collective-permute-start.10 = (bf16[10,128,128]{2,1,0:T(8,128)(2,1)}, bf16[10,128,128]{2,1,0:T(8,128)(2,1)S(1)}, u32[]{:S(2)}, u32[]{:S(2)}) collective-permute-start(bf16[10,128,128]{2,1,0:T(8,128)(2,1)} %collective-permute-done.5.rest_4_), channel_id=1, source_target_pairs={{0,8},{8,0},{1,9},{9,1},{2,10},{10,2},{3,11},{11,3},{4,12},{12,4},... | collective-permute-start | bytes 983048 | tf_op jit(solution)/shard_map/ppermute | solution.py:302
  47.7 12.6 %collective-permute-start.13 = (bf16[10,128,128]{2,1,0:T(8,128)(2,1)}, bf16[10,128,128]{2,1,0:T(8,128)(2,1)S(1)}, u32[]{:S(2)}, u32[]{:S(2)}) collective-permute-start(bf16[10,128,128]{2,1,0:T(8,128)(2,1)} %collective-permute-done.7.rest_7_), channel_id=1, source_target_pairs={{0,8},{8,0},{1,9},{9,1},{2,10},{10,2},{3,11},{11,3},{4,12},{12,4},... | collective-permute-start | bytes 983048 | tf_op jit(solution)/shard_map/ppermute | solution.py:302
  47.9 16.1 %collective-permute-start.14 = (bf16[10,128,128]{2,1,0:T(8,128)(2,1)}, bf16[10,128,128]{2,1,0:T(8,128)(2,1)S(1)}, u32[]{:S(2)}, u32[]{:S(2)}) collective-permute-start(bf16[10,128,128]{2,1,0:T(8,128)(2,1)} %collective-permute-done.5.rest_4_), channel_id=1, source_target_pairs={{0,16},{8,120},{16,32},{24,8},{32,48},{40,24},{48,64},{56,40},{64,... | collective-permute-start | bytes 983048 | tf_op jit(solution)/shard_map/ppermute | solution.py:310
  49.6 14.3 %collective-permute-start.15 = (bf16[10,128,128]{2,1,0:T(8,128)(2,1)}, bf16[10,128,128]{2,1,0:T(8,128)(2,1)S(1)}, u32[]{:S(2)}, u32[]{:S(2)}) collective-permute-start(bf16[10,128,128]{2,1,0:T(8,128)(2,1)} %collective-permute-done.7.rest_7_), channel_id=1, source_target_pairs={{0,16},{8,120},{16,32},{24,8},{32,48},{40,24},{48,64},{56,40},{64,... | collective-permute-start | bytes 983048 | tf_op jit(solution)/shard_map/ppermute | solution.py:310

commit v9 on v8

--- a/solution.py
+++ b/solution.py
@@ -42,17 +42,13 @@
     return pl.BlockSpec(memory_space=pltpu.HBM)
 
 
-def spec(shape):
-    return vmem() if isinstance(shape, jax.ShapeDtypeStruct) else hbm()
-
-
-def call(body, out_shape, in_specs, scratch=(), **kw):
+def call(body, out_shape, in_specs, scratch=(), out_specs=None, **kw):
     single = not isinstance(out_shape, (list, tuple))
     return pl.pallas_call(
         body,
         out_shape=out_shape,
         in_specs=in_specs,
-        out_specs=spec(out_shape) if single else [spec(o) for o in out_shape],
+        out_specs=out_specs or (vmem() if single else [vmem()] * len(out_shape)),
         scratch_shapes=list(scratch),
         compiler_params=pltpu.CompilerParams(vmem_limit_bytes=VMEM_LIMIT),
         **kw,
@@ -68,9 +64,9 @@
 
 
 def notice_body(place, *refs):
-    given, (notice, packs), held, sems = refs[:7], refs[7:9], refs[9:16], refs[16]
+    given, notice, held, sems = refs[:5], refs[5], refs[6:11], refs[11]
     copy_in(zip(given, held), sems)
-    dep, dest, lengths, ids, scales, queries, fresh = held
+    dep, dest, lengths, ids, scales = held
     row = lax.broadcasted_iota(I32, (REP, HD), 0)
     lane = lax.broadcasted_iota(I32, (REP, HD), 1)
     base = place[0]
@@ -90,35 +86,21 @@
     for s in range(SLOTS):
         out = jnp.where(lane == LEN + s, lengths[s].astype(F32), out)
     notice[:, 0, :] = out
-    for s in range(SLOTS):
-        packs[s] = jnp.concatenate(
-            [queries[t, s] for t in range(STEPS)]
-            + [fresh[t, s : s + 1, j * HD : (j + 1) * HD] for t in range(STEPS) for j in range(2)],
-            axis=0,
-        )
 
 
 def at(notices, rep, lane):
     return notices[rep, 0, lane].astype(I32)
 
 
-def pull_body(notices, packs, out, sems):
-    me = at(notices, 0, ME)
-
-    def copy(peer):
-        slot = at(notices, me, DEP + jnp.maximum(at(notices, peer, ROUND), 0))
-        return pltpu.make_async_copy(packs.at[slot], out.at[peer], sems.at[peer])
-
-    def start(peer, carry):
-        copy(peer).start()
+def pull_body(notices, packs, out):
+    me = at(notices, 0, ME)
+
+    def one(peer, carry):
+        turn = at(notices, peer, ROUND)
+        out[peer] = packs[at(notices, me, DEP + jnp.maximum(turn, 0))]
         return carry
 
-    def wait(peer, carry):
-        pltpu.make_async_copy(packs.at[0], out.at[peer], sems.at[peer]).wait()
-        return carry
-
-    lax.fori_loop(0, REP, start, 0, unroll=8)
-    lax.fori_loop(0, REP, wait, 0, unroll=8)
+    lax.fori_loop(0, REP, one, 0, unroll=4)
 
 
 def score(pack, keys, length):
@@ -156,8 +138,12 @@
     return (numer / denom).astype(BF16)
 
 
-def stay_body(dep_in, lengths_in, packs, cache, out, dep, lengths, held, leaves, sems):
-    copy_in([(dep_in, dep), (lengths_in, lengths)], sems.at[SLOTS:])
+def stay_body(dep_in, lengths_in, q_in, fresh_in, cache, out, packs, *scratch):
+    dep, lengths, queries, fresh, held, leaves, sems = scratch
+    copy_in(
+        [(dep_in, dep), (lengths_in, lengths), (q_in, queries), (fresh_in, fresh)],
+        sems.at[SLOTS:],
+    )
     for s in range(SLOTS):
         leaves[s] = 0
     for k in range(MOVE):
@@ -184,10 +170,16 @@
         return carry
 
     lax.fori_loop(0, SLOTS, start, 0)
+    for s in range(SLOTS):
+        packs[s] = jnp.concatenate(
+            [queries[t, s] for t in range(STEPS)]
+            + [fresh[t, s : s + 1, j * HD : (j + 1) * HD] for t in range(STEPS) for j in range(2)],
+            axis=0,
+        )
     lax.fori_loop(0, SLOTS, one, 0)
 
 
-def attend_body(notices, pulled, packs, cache, send, out, scores, held, sems):
+def attend_body(notices, pulled, packs, cache, send, out, scores, held):
     per = STEPS * HEADS
     me = at(notices, 0, ME)
     for s in range(SLOTS):
@@ -198,16 +190,11 @@
         scores[s] = score(held[s], cache[s, 0, :, :HD], at(notices, me, LEN + s))
     for s in range(SLOTS):
         out[s] = blend(held[s], scores[s], cache[s, 0, :, HD:])
-    copies = []
     for k in range(MOVE):
         goal = at(notices, me, DEST + k)
-        rows = out.at[at(notices, me, DEP + k)]
-        for side, to in enumerate((goal, lax.rem(goal + REP // XL, REP))):
-            where = send.at[to, side * per : (side + 1) * per, :]
-            copies.append(pltpu.make_async_copy(rows, where, sems.at[k, side]))
-            copies[-1].start()
-    for c in copies:
-        c.wait()
+        rows = out[at(notices, me, DEP + k)]
+        send[goal, :per, :] = rows
+        send[lax.rem(goal + REP // XL, REP), per:, :] = rows
 
 
 def add_blocks(notices, rows, total, blocks, line, step, origin):
@@ -228,28 +215,31 @@
             total[at(notices, src, COL + n)] += products[n - lo]
 
 
-def project_body(notices, came, mine, other, *rest):
+def source_body(notices, out):
+    me = at(notices, 0, ME)
+    pair = lax.rem(me + REP // XL, REP)
+    for side, owner, lane in ((0, me, ROUND), (1, pair, PAIR_ROUND)):
+        for k in range(SLOTS):
+            out[side, k] = 0
+        for k in range(MOVE):
+            out[XL + side, k] = at(notices, owner, DEP + k)
+        for peer in range(REP):
+            turn = at(notices, peer, lane)
+            out[side, jnp.where(turn >= 0, turn, SLOTS - 1)] = peer
+
+
+def project_body(notices, sources, came, mine, other, *rest):
     arrays, rows, total, slots = rest[:-3], rest[-3], rest[-2], rest[-1]
     per = STEPS * HEADS
     me = at(notices, 0, ME)
-    pair = lax.rem(me + REP // XL, REP)
     xl, core = lax.div(me, Z * CORE), lax.rem(me, CORE)
-    first, second = xl * SLOTS, (1 - xl) * SLOTS
-    for s in range(SLOTS):
-        slots[pl.ds(pl.multiple_of((first + s) * per, per), per), :] = mine[s].astype(F32)
-        slots[pl.ds(pl.multiple_of((second + s) * per, per), per), :] = other[s].astype(F32)
-
-    def place_rows(peer, carry):
-        for lane, owner, start, lo in ((ROUND, me, first, 0), (PAIR_ROUND, pair, second, per)):
-            turn = at(notices, peer, lane)
-            slot = start + at(notices, owner, DEP + jnp.maximum(turn, 0))
-            goal = jnp.where(turn >= 0, slot, XL * SLOTS)
-            slots[pl.ds(pl.multiple_of(goal * per, per), per), :] = came[
-                peer, lo : lo + per, :
-            ].astype(F32)
-        return carry
-
-    lax.fori_loop(0, REP, place_rows, 0, unroll=4)
+    for side, here, start in ((0, mine, xl * SLOTS), (1, other, (1 - xl) * SLOTS)):
+        for s in range(SLOTS):
+            slots[pl.ds(pl.multiple_of((start + s) * per, per), per), :] = here[s].astype(F32)
+        for k in range(MOVE):
+            rows_k = came[sources[side, k], side * per : (side + 1) * per, :]
+            goal = start + sources[XL + side, k]
+            slots[pl.ds(pl.multiple_of(goal * per, per), per), :] = rows_k.astype(F32)
     for h in range(HEADS):
         for side in range(XL):
             for t in range(STEPS):
@@ -301,88 +291,77 @@
     def swap(x, axis):
         return lax.ppermute(x, axis, [(0, 1), (1, 0)])
 
-    def around(x, hops):
-        pairs = [
-            (i * CORE + c, ((i + hops * (1 - 2 * c)) % Z) * CORE + c)
-            for i in range(Z)
-            for c in range(CORE)
-        ]
+    def around(x, cross=0):
+        pairs = []
+        for i in range(Z):
+            for c in range(CORE):
+                line = (c + cross) % CORE
+                pairs.append((i * CORE + c, ((i + 1 - 2 * line) % Z) * CORE + line))
         return lax.ppermute(x, ("z", "core"), pairs)
 
     sib = swap(codes, "core")
-    given = [
-        departing,
-        destination,
-        lengths,
-        block_slot,
-        scales,
-        queries,
-        new_kv.reshape(STEPS, SLOTS, 2 * HD),
-    ]
-    notice, packs = call(
+    given = [departing, destination, lengths, block_slot, scales]
+    notice = call(
         notice_body,
-        [
-            jax.ShapeDtypeStruct((REP, 1, HD), F32),
-            jax.ShapeDtypeStruct((SLOTS, PACK, HD), BF16),
-        ],
+        jax.ShapeDtypeStruct((REP, 1, HD), F32),
         [smem()] + [hbm()] * len(given),
-        [pltpu.SMEM(a.shape, a.dtype) for a in given[:5]]
-        + [pltpu.VMEM(a.shape, a.dtype) for a in given[5:]]
-        + [pltpu.SemaphoreType.DMA((len(given),))],
+        [pltpu.SMEM(a.shape, a.dtype) for a in given] + [pltpu.SemaphoreType.DMA((len(given),))],
     )(base.astype(I32)[None], *(in_hbm(a) for a in given))
     cache = in_hbm(kv_cache)
     sib, notice = lax.optimization_barrier((sib, notice))
-    near, near_x = around(codes, 1), around(sib, 1)
+    near, near_x = around(codes), around(sib)
     notices = exchange(notice, rep_axes)
-    stays = call(
+    fresh = new_kv.reshape(STEPS, SLOTS, 2 * HD)
+    stays, packs = call(
         stay_body,
-        jax.ShapeDtypeStruct((SLOTS, per, HD), BF16),
-        [hbm()] * 2 + [vmem(), hbm()],
+        [
+            jax.ShapeDtypeStruct((SLOTS, per, HD), BF16),
+            jax.ShapeDtypeStruct((SLOTS, PACK, HD), BF16),
+        ],
+        [hbm()] * 5,
         [
             pltpu.SMEM(departing.shape, I32),
             pltpu.SMEM(lengths.shape, I32),
+            pltpu.VMEM(queries.shape, BF16),
+            pltpu.VMEM(fresh.shape, BF16),
             pltpu.VMEM(kv_cache.shape, BF16),
             pltpu.SMEM((SLOTS,), I32),
-            pltpu.SemaphoreType.DMA((SLOTS + 2,)),
+            pltpu.SemaphoreType.DMA((SLOTS + 4,)),
         ],
-    )(in_hbm(departing), in_hbm(lengths), packs, cache)
+    )(*(in_hbm(a) for a in (departing, lengths, queries, fresh)), cache)
     near, stays = lax.optimization_barrier((near, stays))
     near_x, notices = lax.optimization_barrier((near_x, notices))
-    two, two_x = around(near, 1), around(near_x, 1)
+    two, two_x = around(near), around(near_x)
     other = swap(stays, "xl")
+    sources = call(
+        source_body, jax.ShapeDtypeStruct((2 * XL, SLOTS), I32), [smem()], out_specs=smem()
+    )(notices)
     to_pull = call(
-        pull_body,
-        pltpu.HBM((REP, PACK, HD), BF16),
-        [smem(), vmem()],
-        [pltpu.SemaphoreType.DMA((REP,))],
+        pull_body, jax.ShapeDtypeStruct((REP, PACK, HD), BF16), [smem(), vmem()]
     )(notices, packs)
     pulled = exchange(to_pull, rep_axes)
-    three, three_x = around(two, 1), around(two_x, 1)
+    three, three_x = around(two), around(two_x)
     send, mine = call(
         attend_body,
         [
-            pltpu.HBM((REP, 2 * per, HD), BF16),
+            jax.ShapeDtypeStruct((REP, 2 * per, HD), BF16),
             jax.ShapeDtypeStruct((SLOTS, per, HD), BF16),
         ],
         [smem()] + [vmem()] * 3,
-        [
-            pltpu.VMEM((SLOTS, per, CTX), F32),
-            pltpu.VMEM((SLOTS, PACK, HD), BF16),
-            pltpu.SemaphoreType.DMA((MOVE, 2)),
-        ],
+        [pltpu.VMEM((SLOTS, per, CTX), F32), pltpu.VMEM((SLOTS, PACK, HD), BF16)],
     )(notices, pulled, packs, kv_cache)
     came = exchange(send, rep_axes)
-    four, four_x = around(three, 1), around(three_x, 1)
+    four, four_x = around(three), around(three_x)
     rows, total = call(
         project_body,
         [
             jax.ShapeDtypeStruct((HEADS, XL * ROWS, HD), BF16),
             jax.ShapeDtypeStruct((COLS, XL * ROWS, HD), F32),
         ],
-        [smem()] + [vmem()] * 17,
-        [pltpu.VMEM(((XL * SLOTS + 1) * per, HD), F32)],
+        [smem()] * 2 + [vmem()] * 17,
+        [pltpu.VMEM((XL * SLOTS * per, HD), F32)],
     )(
-        *(notices, came, mine, other),
+        *(notices, sources, came, mine, other),
         *(codes, sib, near, two, three, near_x, two_x, three_x),
         *(swap(x, "core") for x in (near, two, three, near_x, two_x, three_x)),
     )

time: 84 us -> 83.4 us (level)
  waiting for transfers between devices: 18.6 us -> 17 us
    all_to_all x3, waiting for transfers between devices: 18.5 us -> 16.7 us  [exchange(): return lax.all_to_all(x, axes, split_axis=0, concat_axis=0, tiled=True)]
    pallas_call x4 -> x5, Pallas kernels: 8.95 us -> 9.57 us  [the longest x1 3.1 us: shards(): call(stay_body, [jax.ShapeDtypeStruct((SLOTS, per, HD), BF16), jax.ShapeD...]
  transfers between devices with their start and end apart: 19 -> 19, of which waited for: 3 -> 4; matrix products, arithmetic and copies ran while one was open for 0% -> 0% of each run, Pallas kernels for 15% -> 15%
where the time goes in v9:
time: 83.4 us; the launch traced here: 82.7 us
  starting transfers between devices  32.6 us (39%)
  blocking collectives  17.6 us (21%)
  waiting for transfers between devices  17 us (20%)
  Pallas kernels  14.6 us (18%)
    all_to_all x1, blocking collectives, exchange(): return lax.all_to_all(x, axes, split_axis=0, concat_axis=0, tiled=True)  17.6 us
    all_to_all x3, waiting for transfers between devices, exchange(): return lax.all_to_all(x, axes, split_axis=0, concat_axis=0, tiled=True)  16.7 us
    all_to_all x3, starting transfers between devices, exchange(): return lax.all_to_all(x, axes, split_axis=0, concat_axis=0, tiled=True)  16.2 us
    ppermute x8, starting transfers between devices, around(): return lax.ppermute(x, ('z', 'core'), pairs)  12.6 us
    ppermute x8, starting transfers between devices, swap(): return lax.ppermute(x, axis, [(0, 1), (1, 0)])  3.86 us
    pallas_call x1, Pallas kernels, shards(): call(project_body, [jax.ShapeDtypeStruct((HEADS, XL * ROWS, HD), BF16), j...  3.15 us
    pallas_call x1, Pallas kernels, shards(): call(stay_body, [jax.ShapeDtypeStruct((SLOTS, per, HD), BF16), jax.ShapeD...  3.1 us
    pallas_call x1, Pallas kernels, shards(): call(pull_body, jax.ShapeDtypeStruct((REP, PACK, HD), BF16), [smem(), vme...  1.76 us
  transfers between devices with their start and end apart: 19, of which 4 were waited for; matrix products, arithmetic and copies ran while one was open for 0% of the time, Pallas kernels for 15%

profile of v9, /device:TPU:8, one launch (start us, length us, event | category | flops | bytes accessed | tf_op | source)
XLA Modules:
  0.0 82.7 jit_solution(7558561502887167739)
XLA Ops:
  0.0 2.0 %collective-permute-start.2 = (bf16[10,128,128]{2,1,0:T(8,128)(2,1)}, bf16[10,128,128]{2,1,0:T(8,128)(2,1)S(1)}, u32[]{:S(2)}, u32[]{:S(2)}) collective-permute-start(bf16[10,128,128]{2,1,0:T(8,128)(2,1)} %rest_0_.1), channel_id=1, source_target_pairs={{0,16},{8,120},{16,32},{24,8},{32,48},{40,24},{48,64},{56,40},{64,... | collective-permute-start | bytes 983048 | tf_op jit(solution)/shard_map/ppermute | solution.py:300
  2.0 1.5 %shard_map.91 = f32[32,1,128]{2,1,0:T(1,128)} custom-call(s32[1]{0:T(128)} %bitcast.place, s32[1,13]{1,0:T(1,128)} %dep_in.1, s32[1,13]{1,0:T(1,128)} %refs_1_.1, s32[16]{0:T(128)} %lengths_in.1, s32[10]{0:T(128)} %refs_3_.1, f32[10]{0:T(128)} %refs_4_.1), custom_call_target="tpu_custom_call" | custom-call | tf_op jit(solution)/shard_map/pallas_call | solution.py:304
  3.5 2.0 %collective-permute-start.1 = (bf16[10,128,128]{2,1,0:T(8,128)(2,1)S(1)}, bf16[10,128,128]{2,1,0:T(8,128)(2,1)}, u32[]{:S(2)}, u32[]{:S(2)}) collective-permute-start(bf16[10,128,128]{2,1,0:T(8,128)(2,1)S(1)} %collective-permute-done.rest_1_), channel_id=1, source_target_pairs={{0,16},{8,120},{16,32},{24,8},{32,48},{40,24},{48,64},{56,40},{64,... | collective-permute-start | bytes 983048 | tf_op jit(solution)/shard_map/ppermute | solution.py:300
  5.5 8.0 %all-to-all-start = ((f32[32,1,128]{2,1,0:T(1,128)}), f32[32,1,128]{2,1,0:T(1,128)S(1)}, u32[]{:S(2)}, u32[]{:S(2)}) async-start(f32[32,1,128]{2,1,0:T(1,128)} %shard_map.91), calls=%async_computation | async-start | bytes 32768 | tf_op jit(solution)/shard_map/all_to_all | solution.py:289
  13.5 3.1 %shard_map.93 = (bf16[16,16,128]{2,1,0:T(8,128)(2,1)S(1)}, bf16[16,20,128]{2,1,0:T(8,128)(2,1)S(1)}) custom-call(s32[1,13]{1,0:T(1,128)} %dep_in.1, s32[16]{0:T(128)} %lengths_in.1, bf16[2,16,8,128]{3,2,1,0:T(8,128)(2,1)} %q_in.1, bf16[2,16,256]{2,1,0:T(8,128)(2,1)} %bitcast.4, bf16[16,1,256,256]{3,2,1,0:T(8,128)(2,1)} %cache.3), custom_call_target="tpu_custom_call" | custom-call | tf_op jit(solution)/shard_map/pallas_call | solution.py:315
  16.6 0.0 copy-start.1
  16.6 1.8 %collective-permute-start.4 = (bf16[10,128,128]{2,1,0:T(8,128)(2,1)S(1)}, bf16[10,128,128]{2,1,0:T(8,128)(2,1)}, u32[]{:S(2)}, u32[]{:S(2)}) collective-permute-start(bf16[10,128,128]{2,1,0:T(8,128)(2,1)S(1)} %collective-permute-done.2.rest_2_), channel_id=1, source_target_pairs={{0,16},{8,120},{16,32},{24,8},{32,48},{40,24},{48,64},{56,40},{64,... | collective-permute-start | bytes 983048 | tf_op jit(solution)/shard_map/ppermute | solution.py:300
  18.4 3.4 %all-to-all-done.notices = f32[32,1,128]{2,1,0:T(1,128)S(1)} async-done(((f32[32,1,128]{2,1,0:T(1,128)}), f32[32,1,128]{2,1,0:T(1,128)S(1)}, u32[]{:S(2)}, u32[]{:S(2)}) %all-to-all-start) | async-done | bytes 16416 | tf_op jit(solution)/shard_map/all_to_all | solution.py:289
  21.8 0.6 collective-permute-start.6
  22.4 1.8 %shard_map.94 = bf16[32,20,128]{2,1,0:T(8,128)(2,1)} custom-call(f32[32,1,128]{2,1,0:T(1,128)S(1)} %all-to-all-done.notices, bf16[16,20,128]{2,1,0:T(8,128)(2,1)S(1)} %get-tuple-element.20.packs), custom_call_target="tpu_custom_call" | custom-call | tf_op jit(solution)/shard_map/pallas_call | solution.py:339
  24.2 4.3 %all-to-all-start.1 = ((bf16[32,20,128]{2,1,0:T(8,128)(2,1)}), bf16[32,20,128]{2,1,0:T(8,128)(2,1)S(1)}, u32[]{:S(2)}, u32[]{:S(2)}) async-start(bf16[32,20,128]{2,1,0:T(8,128)(2,1)} %shard_map.94), calls=%async_computation.1 | async-start | bytes 393216 | tf_op jit(solution)/shard_map/all_to_all | solution.py:289
  28.5 1.9 %collective-permute-start.3 = (bf16[16,16,128]{2,1,0:T(8,128)(2,1)S(1)}, bf16[16,16,128]{2,1,0:T(8,128)(2,1)S(1)}, u32[]{:S(2)}, u32[]{:S(2)}) collective-permute-start(bf16[16,16,128]{2,1,0:T(8,128)(2,1)S(1)} %get-tuple-element.24), channel_id=1, source_target_pairs={{0,128},{128,0},{1,129},{129,1},{2,130},{130,2},{3,131},{131,3},{4... | collective-permute-start | bytes 196616 | tf_op jit(solution)/shard_map/ppermute | solution.py:292
  30.4 1.5 %collective-permute-start.5 = (bf16[10,128,128]{2,1,0:T(8,128)(2,1)}, bf16[10,128,128]{2,1,0:T(8,128)(2,1)}, u32[]{:S(2)}, u32[]{:S(2)}) collective-permute-start(bf16[10,128,128]{2,1,0:T(8,128)(2,1)} %collective-permute-done.4.rest_3_), channel_id=1, source_target_pairs={{0,16},{8,120},{16,32},{24,8},{32,48},{40,24},{48,64},{56,40},{64,... | collective-permute-start | bytes 983048 | tf_op jit(solution)/shard_map/ppermute | solution.py:300
  31.9 1.5 %collective-permute-start.7 = (bf16[10,128,128]{2,1,0:T(8,128)(2,1)}, bf16[10,128,128]{2,1,0:T(8,128)(2,1)}, u32[]{:S(2)}, u32[]{:S(2)}) collective-permute-start(bf16[10,128,128]{2,1,0:T(8,128)(2,1)} %collective-permute-done.6.rest_6_), channel_id=1, source_target_pairs={{0,16},{8,120},{16,32},{24,8},{32,48},{40,24},{48,64},{56,40},{64,... | collective-permute-start | bytes 983048 | tf_op jit(solution)/shard_map/ppermute | solution.py:300
  33.3 1.2 %collective-permute-start.11 = (bf16[10,128,128]{2,1,0:T(8,128)(2,1)}, bf16[10,128,128]{2,1,0:T(8,128)(2,1)}, u32[]{:S(2)}, u32[]{:S(2)}) collective-permute-start(bf16[10,128,128]{2,1,0:T(8,128)(2,1)} %collective-permute-done.1.rest_5_), channel_id=1, source_target_pairs={{0,8},{8,0},{1,9},{9,1},{2,10},{10,2},{3,11},{11,3},{4,12},{12,4},... | collective-permute-start | bytes 983048 | tf_op jit(solution)/shard_map/ppermute | solution.py:292
  34.6 0.0 collective-permute-start.9
  34.6 5.8 %all-to-all-done.1.pulled = bf16[32,20,128]{2,1,0:T(8,128)(2,1)S(1)} async-done(((bf16[32,20,128]{2,1,0:T(8,128)(2,1)}), bf16[32,20,128]{2,1,0:T(8,128)(2,1)S(1)}, u32[]{:S(2)}, u32[]{:S(2)}) %all-to-all-start.1) | async-done | bytes 163872 | tf_op jit(solution)/shard_map/all_to_all | solution.py:289
  40.4 1.5 %shard_map.95 = (bf16[32,32,128]{2,1,0:T(8,128)(2,1)S(1)}, bf16[16,16,128]{2,1,0:T(8,128)(2,1)S(1)}) custom-call(f32[32,1,128]{2,1,0:T(1,128)S(1)} %all-to-all-done.notices, bf16[32,20,128]{2,1,0:T(8,128)(2,1)S(1)} %all-to-all-done.1.pulled, bf16[16,20,128]{2,1,0:T(8,128)(2,1)S(1)} %get-tuple-element.20.packs, bf16[16,1,256,256]{3,2,1,0:T(8,128)(2,1)S(1)} %copy-done), custom_call_target="tpu_custom_call" | custom-call | tf_op jit(solution)/shard_map/pallas_call | solution.py:344
  41.9 0.7 copy-done.2
  42.6 3.9 %all-to-all-start.2 = ((bf16[32,32,128]{2,1,0:T(8,128)(2,1)}), bf16[32,32,128]{2,1,0:T(8,128)(2,1)S(1)}, u32[]{:S(2)}, u32[]{:S(2)}) async-start(bf16[32,32,128]{2,1,0:T(8,128)(2,1)} %copy-done.2), calls=%async_computation.2 | async-start | bytes 524288 | tf_op jit(solution)/shard_map/all_to_all | solution.py:289
  46.5 0.2 collective-permute-start.12
  46.8 0.3 collective-permute-start.10
  47.1 0.2 collective-permute-start.13
  47.3 1.8 %collective-permute-start.14 = (bf16[10,128,128]{2,1,0:T(8,128)(2,1)}, bf16[10,128,128]{2,1,0:T(8,128)(2,1)S(1)}, u32[]{:S(2)}, u32[]{:S(2)}) collective-permute-start(bf16[10,128,128]{2,1,0:T(8,128)(2,1)} %collective-permute-done.5.rest_4_), channel_id=1, source_target_pairs={{0,16},{8,120},{16,32},{24,8},{32,48},{40,24},{48,64},{56,40},{64,... | collective-permute-start | bytes 983048 | tf_op jit(solution)/shard_map/ppermute | solution.py:300
  49.1 1.5 %collective-permute-start.15 = (bf16[10,128,128]{2,1,0:T(8,128)(2,1)}, bf16[10,128,128]{2,1,0:T(8,128)(2,1)S(1)}, u32[]{:S(2)}, u32[]{:S(2)}) collective-permute-start(bf16[10,128,128]{2,1,0:T(8,128)(2,1)} %collective-permute-done.7.rest_7_), channel_id=1, source_target_pairs={{0,16},{8,120},{16,32},{24,8},{32,48},{40,24},{48,64},{56,40},{64,... | collective-permute-start | bytes 983048 | tf_op jit(solution)/shard_map/ppermute | solution.py:300
  50.5 1.7 %shard_map.92.sources = s32[4,16]{1,0:T(4,128)S(1)} custom-call(f32[32,1,128]{2,1,0:T(1,128)S(1)} %all-to-all-done.notices), custom_call_target="tpu_custom_call" | custom-call | tf_op jit(solution)/shard_map/pallas_call | solution.py:336
  52.3 7.4 %all-to-all-done.2.came = bf16[32,32,128]{2,1,0:T(8,128)(2,1)S(1)} async-done(((bf16[32,32,128]{2,1,0:T(8,128)(2,1)}), bf16[32,32,128]{2,1,0:T(8,128)(2,1)S(1)}, u32[]{:S(2)}, u32[]{:S(2)}) %all-to-all-start.2) | async-done | bytes 262176 | tf_op jit(solution)/shard_map/all_to_all | solution.py:289
  59.7 3.1 %shard_map.96 = (bf16[8,64,128]{2,1,0:T(8,128)(2,1)S(1)}, f32[40,64,128]{2,1,0:T(8,128)S(1)}) custom-call(f32[32,1,128]{2,1,0:T(1,128)S(1)} %all-to-all-done.notices, s32[4,16]{1,0:T(4,128)S(1)} %shard_map.92.sources, bf16[32,32,128]{2,1,0:T(8,128)(2,1)S(1)} %all-to-all-done.2.came, bf16[16,16,128]{2,1,0:T(8,128)(2,1)S(1)} %get-tuple-element.22.mine, ...), custom_call_target="tpu_custom_call" | custom-call | tf_op jit(solution)/shard_map/pallas_call | solution.py:355
  62.9 0.3 collective-permute-done.15.four_x
  63.2 1.2 %shard_map.97 = bf16[80,32,128]{2,1,0:T(8,128)(2,1)S(1)} custom-call(f32[32,1,128]{2,1,0:T(1,128)S(1)} %all-to-all-done.notices, bf16[8,64,128]{2,1,0:T(8,128)(2,1)S(1)} %get-tuple-element.27.rows, f32[40,64,128]{2,1,0:T(8,128)S(1)} %get-tuple-element.28.so_far, bf16[10,128,128]{2,1,0:T(8,128)(2,1)S(1)} %collective-permute-done.14.four, ...), custom_call_target="tpu_custom_call" | custom-call | tf_op jit(solution)/shard_map/pallas_call | solution.py:368
  64.4 17.6 %all_to_all.20 = bf16[80,32,128]{2,1,0:T(8,128)(2,1)S(1)} all-to-all(bf16[80,32,128]{2,1,0:T(8,128)(2,1)S(1)} %shard_map.97), channel_id=1, replica_groups=mesh['xl'=2,'z'=8,'core'=2,'y'=4,'xh'=2] {'xl','y','xh'}, dimensions={0} | all-to-all | bytes 1310720 | tf_op jit(solution)/shard_map/all_to_all | solution.py:289
  82.0 0.7 shard_map.98
  (21 shorter events, 0.1 us)
Async XLA Ops:
  0.0 40.4 %copy-start = (bf16[16,1,256,256]{3,2,1,0:T(8,128)(2,1)S(1)}, bf16[16,1,256,256]{3,2,1,0:T(8,128)(2,1)}, u32[]{:S(2)}) copy-start(bf16[16,1,256,256]{3,2,1,0:T(8,128)(2,1)} %cache.3) | copy-start | bytes 6291460
  0.0 3.5 %collective-permute-start = (bf16[10,128,128]{2,1,0:T(8,128)(2,1)}, bf16[10,128,128]{2,1,0:T(8,128)(2,1)S(1)}, u32[]{:S(2)}, u32[]{:S(2)}) collective-permute-start(bf16[10,128,128]{2,1,0:T(8,128)(2,1)} %rest_0_.1), channel_id=1, source_target_pairs={{0,8},{8,0},{1,9},{9,1},{2,10},{10,2},{3,11},{11,3},{4,12},{12,4},... | collective-permute-start | bytes 983048 | tf_op jit(solution)/shard_map/ppermute | solution.py:292
  0.0 16.6 %collective-permute-start.2 = (bf16[10,128,128]{2,1,0:T(8,128)(2,1)}, bf16[10,128,128]{2,1,0:T(8,128)(2,1)S(1)}, u32[]{:S(2)}, u32[]{:S(2)}) collective-permute-start(bf16[10,128,128]{2,1,0:T(8,128)(2,1)} %rest_0_.1), channel_id=1, source_target_pairs={{0,16},{8,120},{16,32},{24,8},{32,48},{40,24},{48,64},{56,40},{64,... | collective-permute-start | bytes 983048 | tf_op jit(solution)/shard_map/ppermute | solution.py:300
  3.5 18.3 %collective-permute-start.1 = (bf16[10,128,128]{2,1,0:T(8,128)(2,1)S(1)}, bf16[10,128,128]{2,1,0:T(8,128)(2,1)}, u32[]{:S(2)}, u32[]{:S(2)}) collective-permute-start(bf16[10,128,128]{2,1,0:T(8,128)(2,1)S(1)} %collective-permute-done.rest_1_), channel_id=1, source_target_pairs={{0,16},{8,120},{16,32},{24,8},{32,48},{40,24},{48,64},{56,40},{64,... | collective-permute-start | bytes 983048 | tf_op jit(solution)/shard_map/ppermute | solution.py:300
  5.5 16.3 %all-to-all-start = ((f32[32,1,128]{2,1,0:T(1,128)}), f32[32,1,128]{2,1,0:T(1,128)S(1)}, u32[]{:S(2)}, u32[]{:S(2)}) async-start(f32[32,1,128]{2,1,0:T(1,128)} %shard_map.91), calls=%async_computation | async-start | bytes 32768 | tf_op jit(solution)/shard_map/all_to_all | solution.py:289
  16.6 43.1 %copy-start.1 = (bf16[10,128,128]{2,1,0:T(8,128)(2,1)S(1)}, bf16[10,128,128]{2,1,0:T(8,128)(2,1)}, u32[]{:S(2)}) copy-start(bf16[10,128,128]{2,1,0:T(8,128)(2,1)} %rest_0_.1) | copy-start | bytes 983044
  16.6 13.8 %collective-permute-start.4 = (bf16[10,128,128]{2,1,0:T(8,128)(2,1)S(1)}, bf16[10,128,128]{2,1,0:T(8,128)(2,1)}, u32[]{:S(2)}, u32[]{:S(2)}) collective-permute-start(bf16[10,128,128]{2,1,0:T(8,128)(2,1)S(1)} %collective-permute-done.2.rest_2_), channel_id=1, source_target_pairs={{0,16},{8,120},{16,32},{24,8},{32,48},{40,24},{48,64},{56,40},{64,... | collective-permute-start | bytes 983048 | tf_op jit(solution)/shard_map/ppermute | solution.py:300
  21.8 10.0 %collective-permute-start.6 = (bf16[10,128,128]{2,1,0:T(8,128)(2,1)}, bf16[10,128,128]{2,1,0:T(8,128)(2,1)}, u32[]{:S(2)}, u32[]{:S(2)}) collective-permute-start(bf16[10,128,128]{2,1,0:T(8,128)(2,1)} %collective-permute-done.1.rest_5_), channel_id=1, source_target_pairs={{0,16},{8,120},{16,32},{24,8},{32,48},{40,24},{48,64},{56,40},{64,... | collective-permute-start | bytes 983048 | tf_op jit(solution)/shard_map/ppermute | solution.py:300
  24.2 16.2 %all-to-all-start.1 = ((bf16[32,20,128]{2,1,0:T(8,128)(2,1)}), bf16[32,20,128]{2,1,0:T(8,128)(2,1)S(1)}, u32[]{:S(2)}, u32[]{:S(2)}) async-start(bf16[32,20,128]{2,1,0:T(8,128)(2,1)} %shard_map.94), calls=%async_computation.1 | async-start | bytes 393216 | tf_op jit(solution)/shard_map/all_to_all | solution.py:289
  28.5 6.0 %collective-permute-start.3 = (bf16[16,16,128]{2,1,0:T(8,128)(2,1)S(1)}, bf16[16,16,128]{2,1,0:T(8,128)(2,1)S(1)}, u32[]{:S(2)}, u32[]{:S(2)}) collective-permute-start(bf16[16,16,128]{2,1,0:T(8,128)(2,1)S(1)} %get-tuple-element.24), channel_id=1, source_target_pairs={{0,128},{128,0},{1,129},{129,1},{2,130},{130,2},{3,131},{131,3},{4... | collective-permute-start | bytes 196616 | tf_op jit(solution)/shard_map/ppermute | solution.py:292
  30.4 16.1 %collective-permute-start.8 = (bf16[10,128,128]{2,1,0:T(8,128)(2,1)S(1)}, bf16[10,128,128]{2,1,0:T(8,128)(2,1)}, u32[]{:S(2)}, u32[]{:S(2)}) collective-permute-start(bf16[10,128,128]{2,1,0:T(8,128)(2,1)S(1)} %collective-permute-done.2.rest_2_), channel_id=1, source_target_pairs={{0,8},{8,0},{1,9},{9,1},{2,10},{10,2},{3,11},{11,3},{4,12},{12,4},... | collective-permute-start | bytes 983048 | tf_op jit(solution)/shard_map/ppermute | solution.py:292
  30.4 16.3 %collective-permute-start.5 = (bf16[10,128,128]{2,1,0:T(8,128)(2,1)}, bf16[10,128,128]{2,1,0:T(8,128)(2,1)}, u32[]{:S(2)}, u32[]{:S(2)}) collective-permute-start(bf16[10,128,128]{2,1,0:T(8,128)(2,1)} %collective-permute-done.4.rest_3_), channel_id=1, source_target_pairs={{0,16},{8,120},{16,32},{24,8},{32,48},{40,24},{48,64},{56,40},{64,... | collective-permute-start | bytes 983048 | tf_op jit(solution)/shard_map/ppermute | solution.py:300
  31.9 15.2 %collective-permute-start.7 = (bf16[10,128,128]{2,1,0:T(8,128)(2,1)}, bf16[10,128,128]{2,1,0:T(8,128)(2,1)}, u32[]{:S(2)}, u32[]{:S(2)}) collective-permute-start(bf16[10,128,128]{2,1,0:T(8,128)(2,1)} %collective-permute-done.6.rest_6_), channel_id=1, source_target_pairs={{0,16},{8,120},{16,32},{24,8},{32,48},{40,24},{48,64},{56,40},{64,... | collective-permute-start | bytes 983048 | tf_op jit(solution)/shard_map/ppermute | solution.py:300
  33.3 13.9 %collective-permute-start.11 = (bf16[10,128,128]{2,1,0:T(8,128)(2,1)}, bf16[10,128,128]{2,1,0:T(8,128)(2,1)}, u32[]{:S(2)}, u32[]{:S(2)}) collective-permute-start(bf16[10,128,128]{2,1,0:T(8,128)(2,1)} %collective-permute-done.1.rest_5_), channel_id=1, source_target_pairs={{0,8},{8,0},{1,9},{9,1},{2,10},{10,2},{3,11},{11,3},{4,12},{12,4},... | collective-permute-start | bytes 983048 | tf_op jit(solution)/shard_map/ppermute | solution.py:292
  34.6 14.5 %collective-permute-start.9 = (bf16[10,128,128]{2,1,0:T(8,128)(2,1)}, bf16[10,128,128]{2,1,0:T(8,128)(2,1)}, u32[]{:S(2)}, u32[]{:S(2)}) collective-permute-start(bf16[10,128,128]{2,1,0:T(8,128)(2,1)} %collective-permute-done.4.rest_3_), channel_id=1, source_target_pairs={{0,8},{8,0},{1,9},{9,1},{2,10},{10,2},{3,11},{11,3},{4,12},{12,4},... | collective-permute-start | bytes 983048 | tf_op jit(solution)/shard_map/ppermute | solution.py:292
  41.9 0.7 copy-start.2
  42.6 17.1 %all-to-all-start.2 = ((bf16[32,32,128]{2,1,0:T(8,128)(2,1)}), bf16[32,32,128]{2,1,0:T(8,128)(2,1)S(1)}, u32[]{:S(2)}, u32[]{:S(2)}) async-start(bf16[32,32,128]{2,1,0:T(8,128)(2,1)} %copy-done.2), calls=%async_computation.2 | async-start | bytes 524288 | tf_op jit(solution)/shard_map/all_to_all | solution.py:289
  46.5 5.8 %collective-permute-start.12 = (bf16[10,128,128]{2,1,0:T(8,128)(2,1)}, bf16[10,128,128]{2,1,0:T(8,128)(2,1)S(1)}, u32[]{:S(2)}, u32[]{:S(2)}) collective-permute-start(bf16[10,128,128]{2,1,0:T(8,128)(2,1)} %collective-permute-done.6.rest_6_), channel_id=1, source_target_pairs={{0,8},{8,0},{1,9},{9,1},{2,10},{10,2},{3,11},{11,3},{4,12},{12,4},... | collective-permute-start | bytes 983048 | tf_op jit(solution)/shard_map/ppermute | solution.py:292
  46.8 5.5 %collective-permute-start.10 = (bf16[10,128,128]{2,1,0:T(8,128)(2,1)}, bf16[10,128,128]{2,1,0:T(8,128)(2,1)S(1)}, u32[]{:S(2)}, u32[]{:S(2)}) collective-permute-start(bf16[10,128,128]{2,1,0:T(8,128)(2,1)} %collective-permute-done.5.rest_4_), channel_id=1, source_target_pairs={{0,8},{8,0},{1,9},{9,1},{2,10},{10,2},{3,11},{11,3},{4,12},{12,4},... | collective-permute-start | bytes 983048 | tf_op jit(solution)/shard_map/ppermute | solution.py:292
  47.1 12.6 %collective-permute-start.13 = (bf16[10,128,128]{2,1,0:T(8,128)(2,1)}, bf16[10,128,128]{2,1,0:T(8,128)(2,1)S(1)}, u32[]{:S(2)}, u32[]{:S(2)}) collective-permute-start(bf16[10,128,128]{2,1,0:T(8,128)(2,1)} %collective-permute-done.7.rest_7_), channel_id=1, source_target_pairs={{0,8},{8,0},{1,9},{9,1},{2,10},{10,2},{3,11},{11,3},{4,12},{12,4},... | collective-permute-start | bytes 983048 | tf_op jit(solution)/shard_map/ppermute | solution.py:292
  47.3 15.6 %collective-permute-start.14 = (bf16[10,128,128]{2,1,0:T(8,128)(2,1)}, bf16[10,128,128]{2,1,0:T(8,128)(2,1)S(1)}, u32[]{:S(2)}, u32[]{:S(2)}) collective-permute-start(bf16[10,128,128]{2,1,0:T(8,128)(2,1)} %collective-permute-done.5.rest_4_), channel_id=1, source_target_pairs={{0,16},{8,120},{16,32},{24,8},{32,48},{40,24},{48,64},{56,40},{64,... | collective-permute-start | bytes 983048 | tf_op jit(solution)/shard_map/ppermute | solution.py:300
  49.1 14.1 %collective-permute-start.15 = (bf16[10,128,128]{2,1,0:T(8,128)(2,1)}, bf16[10,128,128]{2,1,0:T(8,128)(2,1)S(1)}, u32[]{:S(2)}, u32[]{:S(2)}) collective-permute-start(bf16[10,128,128]{2,1,0:T(8,128)(2,1)} %collective-permute-done.7.rest_7_), channel_id=1, source_target_pairs={{0,16},{8,120},{16,32},{24,8},{32,48},{40,24},{48,64},{56,40},{64,... | collective-permute-start | bytes 983048 | tf_op jit(solution)/shard_map/ppermute | solution.py:300

commit v10 on v9

--- a/solution.py
+++ b/solution.py
@@ -26,6 +26,10 @@
 PACK = STEPS * HEADS + 2 * STEPS
 
 ROUND, PAIR_ROUND, ME, HEAD, COL, SCALE, DEP, DEST, LEN = 0, 1, 2, 3, 13, 23, 33, 46, 59
+
+SLOT_OF, PEER_OF, HEAD_OF = 0, 2 * SLOTS, 4 * SLOTS
+COL_OF = HEAD_OF + 2 * Z * OWN
+TABLE = COL_OF + 2 * Z * OWN
 
 VMEM_LIMIT = 16 * 1024 * 1024
 
@@ -93,14 +97,8 @@
 
 
 def pull_body(notices, packs, out):
-    me = at(notices, 0, ME)
-
-    def one(peer, carry):
-        turn = at(notices, peer, ROUND)
-        out[peer] = packs[at(notices, me, DEP + jnp.maximum(turn, 0))]
-        return carry
-
-    lax.fori_loop(0, REP, one, 0, unroll=4)
+    for peer in range(REP):
+        out[peer] = packs[jnp.maximum(at(notices, peer, ROUND), 0)]
 
 
 def score(pack, keys, length):
@@ -139,7 +137,7 @@
 
 
 def stay_body(dep_in, lengths_in, q_in, fresh_in, cache, out, packs, *scratch):
-    dep, lengths, queries, fresh, held, leaves, sems = scratch
+    dep, lengths, queries, fresh, held, leaves, mine, sems = scratch
     copy_in(
         [(dep_in, dep), (lengths_in, lengths), (q_in, queries), (fresh_in, fresh)],
         sems.at[SLOTS:],
@@ -163,7 +161,7 @@
         @pl.when(leaves[s] == 0)
         def _():
             copy(s).wait()
-            pack = packs[s]
+            pack = mine[s]
             sc = score(pack, held[s, 0, :, :HD], lengths[s])
             out[s] = blend(pack, sc, held[s, 0, :, HD:])
 
@@ -171,74 +169,78 @@
 
     lax.fori_loop(0, SLOTS, start, 0)
     for s in range(SLOTS):
-        packs[s] = jnp.concatenate(
+        mine[s] = jnp.concatenate(
             [queries[t, s] for t in range(STEPS)]
             + [fresh[t, s : s + 1, j * HD : (j + 1) * HD] for t in range(STEPS) for j in range(2)],
             axis=0,
         )
+    for k in range(MOVE):
+        packs[k] = mine[dep[0, k]]
     lax.fori_loop(0, SLOTS, one, 0)
 
 
-def attend_body(notices, pulled, packs, cache, send, out, scores, held):
+def attend_body(notices, pulled, cache, send, scores):
     per = STEPS * HEADS
     me = at(notices, 0, ME)
-    for s in range(SLOTS):
-        held[s] = packs[s]
-    for k in range(MOVE):
-        held[at(notices, me, DEP + k)] = pulled[at(notices, me, DEST + k)]
-    for s in range(SLOTS):
-        scores[s] = score(held[s], cache[s, 0, :, :HD], at(notices, me, LEN + s))
-    for s in range(SLOTS):
-        out[s] = blend(held[s], scores[s], cache[s, 0, :, HD:])
-    for k in range(MOVE):
-        goal = at(notices, me, DEST + k)
-        rows = out[at(notices, me, DEP + k)]
-        send[goal, :per, :] = rows
-        send[lax.rem(goal + REP // XL, REP), per:, :] = rows
-
-
-def add_blocks(notices, rows, total, blocks, line, step, origin):
-    me = at(notices, 0, ME)
-    xl, z = lax.div(me, Z * CORE), lax.rem(lax.div(me, CORE), Z)
-    far = lax.rem(z - (1 - 2 * line) * step + Z, Z)
-    src = (xl * Z + far) * CORE + origin
-    for lo in range(0, OWN, 5):
-        products = []
+    slots = [at(notices, me, DEP + k) for k in range(MOVE)]
+    goals = [at(notices, me, DEST + k) for k in range(MOVE)]
+    for k in range(MOVE):
+        length = at(notices, me, LEN + slots[k])
+        scores[k] = score(pulled[goals[k]], cache[slots[k], 0, :, :HD], length)
+    for k in range(MOVE):
+        rows = blend(pulled[goals[k]], scores[k], cache[slots[k], 0, :, HD:])
+        send[goals[k], :per, :] = rows
+        send[lax.rem(goals[k] + REP // XL, REP), per:, :] = rows
+
+
+def add_blocks(table, scales, rows, total, blocks, first):
+    for lo in range(first, first + OWN, 5):
+        products = [
+            jnp.dot(rows[table[HEAD_OF + n]], blocks[n - first], preferred_element_type=F32)
+            * scales[n]
+            for n in range(lo, lo + 5)
+        ]
         for n in range(lo, lo + 5):
-            products.append(
-                jnp.dot(
-                    rows[at(notices, src, HEAD + n)], blocks[n], preferred_element_type=F32
-                )
-                * notices[src, 0, SCALE + n]
-            )
-        for n in range(lo, lo + 5):
-            total[at(notices, src, COL + n)] += products[n - lo]
-
-
-def source_body(notices, out):
+            total[table[COL_OF + n]] += products[n - lo]
+
+
+def table_body(notices, table, scales):
     me = at(notices, 0, ME)
     pair = lax.rem(me + REP // XL, REP)
     for side, owner, lane in ((0, me, ROUND), (1, pair, PAIR_ROUND)):
-        for k in range(SLOTS):
-            out[side, k] = 0
         for k in range(MOVE):
-            out[XL + side, k] = at(notices, owner, DEP + k)
+            table[SLOT_OF + side * SLOTS + k] = at(notices, owner, DEP + k)
         for peer in range(REP):
             turn = at(notices, peer, lane)
-            out[side, jnp.where(turn >= 0, turn, SLOTS - 1)] = peer
-
-
-def project_body(notices, sources, came, mine, other, *rest):
+            table[PEER_OF + side * SLOTS + jnp.where(turn >= 0, turn, SLOTS - 1)] = peer
+    xl, z, core = lax.div(me, Z * CORE), lax.rem(lax.div(me, CORE), Z), lax.rem(me, CORE)
+    half = Z // 2
+    for i, (step, line, cross) in enumerate(
+        [(0, 0, 0), (0, 0, 1)]
+        + [(j, 0, cross) for cross in (0, 1) for j in range(1, half)]
+        + [(j, 1, cross) for cross in (0, 1) for j in range(1, half)]
+        + [(half, 0, 0), (half, 0, 1)]
+    ):
+        on = core if line == 0 else 1 - core
+        origin = on if cross == 0 else 1 - on
+        far = lax.rem(z - (1 - 2 * on) * step + Z, Z)
+        src = (xl * Z + far) * CORE + origin
+        for n in range(OWN):
+            table[HEAD_OF + i * OWN + n] = at(notices, src, HEAD + n)
+            table[COL_OF + i * OWN + n] = at(notices, src, COL + n)
+            scales[i * OWN + n] = notices[src, 0, SCALE + n]
+
+
+def project_body(where, table, scales, came, mine, other, *rest):
     arrays, rows, total, slots = rest[:-3], rest[-3], rest[-2], rest[-1]
     per = STEPS * HEADS
-    me = at(notices, 0, ME)
-    xl, core = lax.div(me, Z * CORE), lax.rem(me, CORE)
+    xl = where[0]
     for side, here, start in ((0, mine, xl * SLOTS), (1, other, (1 - xl) * SLOTS)):
         for s in range(SLOTS):
             slots[pl.ds(pl.multiple_of((start + s) * per, per), per), :] = here[s].astype(F32)
         for k in range(MOVE):
-            rows_k = came[sources[side, k], side * per : (side + 1) * per, :]
-            goal = start + sources[XL + side, k]
+            rows_k = came[table[PEER_OF + side * SLOTS + k], side * per : (side + 1) * per, :]
+            goal = start + table[SLOT_OF + side * SLOTS + k]
             slots[pl.ds(pl.multiple_of(goal * per, per), per), :] = rows_k.astype(F32)
     for h in range(HEADS):
         for side in range(XL):
@@ -248,21 +250,14 @@
                     pl.ds(side * SLOTS * per + t * HEADS + h, SLOTS, stride=per), :
                 ].astype(BF16)
     total[...] = jnp.zeros_like(total)
-    half = Z // 2
-    steps = [(0, core, core), (0, core, 1 - core)]
-    steps += [(i, core, core) for i in range(1, half)]
-    steps += [(i, core, 1 - core) for i in range(1, half)]
-    steps += [(i, 1 - core, 1 - core) for i in range(1, half)]
-    steps += [(i, 1 - core, core) for i in range(1, half)]
-    for blocks, (step, line, origin) in zip(arrays, steps):
-        add_blocks(notices, rows, total, blocks, line, step, origin)
-
-
-def last_body(notices, rows, so_far, four, four_x, out, total):
-    core = lax.rem(at(notices, 0, ME), CORE)
+    for i, blocks in enumerate(arrays):
+        add_blocks(table, scales, rows, total, blocks, i * OWN)
+
+
+def last_body(table, scales, rows, so_far, four, four_x, out, total):
     total[...] = so_far[...]
-    add_blocks(notices, rows, total, four, core, Z // 2, core)
-    add_blocks(notices, rows, total, four_x, core, Z // 2, 1 - core)
+    add_blocks(table, scales, rows, total, four, (2 * Z - 2) * OWN)
+    add_blocks(table, scales, rows, total, four_x, (2 * Z - 1) * OWN)
     out[:COLS] = total[:, :ROWS, :].astype(BF16)
     out[COLS:] = total[:, ROWS:, :].astype(BF16)
 
@@ -280,6 +275,7 @@
 def shards(kv_cache, lengths, departing, destination, queries, new_kv, codes, scales, block_slot):
     rep_axes, tp_axes = ("xl", "z", "core"), ("y", "xh")
     base = lax.axis_index(tp_axes) * (HEADS * COLS)
+    xl = lax.axis_index("xl").astype(I32)
     per = STEPS * HEADS
 
     def in_hbm(x):
@@ -316,7 +312,7 @@
         stay_body,
         [
             jax.ShapeDtypeStruct((SLOTS, per, HD), BF16),
-            jax.ShapeDtypeStruct((SLOTS, PACK, HD), BF16),
+            jax.ShapeDtypeStruct((MOVE, PACK, HD), BF16),
         ],
         [hbm()] * 5,
         [
@@ -326,6 +322,7 @@
             pltpu.VMEM(fresh.shape, BF16),
             pltpu.VMEM(kv_cache.shape, BF16),
             pltpu.SMEM((SLOTS,), I32),
+            pltpu.VMEM((SLOTS, PACK, HD), BF16),
             pltpu.SemaphoreType.DMA((SLOTS + 4,)),
         ],
     )(*(in_hbm(a) for a in (departing, lengths, queries, fresh)), cache)
@@ -333,23 +330,23 @@
     near_x, notices = lax.optimization_barrier((near_x, notices))
     two, two_x = around(near), around(near_x)
     other = swap(stays, "xl")
-    sources = call(
-        source_body, jax.ShapeDtypeStruct((2 * XL, SLOTS), I32), [smem()], out_specs=smem()
+    table, factors = call(
+        table_body,
+        [jax.ShapeDtypeStruct((TABLE,), I32), jax.ShapeDtypeStruct((2 * Z * OWN,), F32)],
+        [smem()],
+        out_specs=[smem(), smem()],
     )(notices)
     to_pull = call(
         pull_body, jax.ShapeDtypeStruct((REP, PACK, HD), BF16), [smem(), vmem()]
     )(notices, packs)
     pulled = exchange(to_pull, rep_axes)
     three, three_x = around(two), around(two_x)
-    send, mine = call(
+    send = call(
         attend_body,
-        [
-            jax.ShapeDtypeStruct((REP, 2 * per, HD), BF16),
-            jax.ShapeDtypeStruct((SLOTS, per, HD), BF16),
-        ],
-        [smem()] + [vmem()] * 3,
-        [pltpu.VMEM((SLOTS, per, CTX), F32), pltpu.VMEM((SLOTS, PACK, HD), BF16)],
-    )(notices, pulled, packs, kv_cache)
+        jax.ShapeDtypeStruct((REP, 2 * per, HD), BF16),
+        [smem()] + [vmem()] * 2,
+        [pltpu.VMEM((MOVE, per, CTX), F32)],
+    )(notices, pulled, kv_cache)
     came = exchange(send, rep_axes)
     four, four_x = around(three), around(three_x)
     rows, total = call(
@@ -358,19 +355,19 @@
             jax.ShapeDtypeStruct((HEADS, XL * ROWS, HD), BF16),
             jax.ShapeDtypeStruct((COLS, XL * ROWS, HD), F32),
         ],
-        [smem()] * 2 + [vmem()] * 17,
+        [smem()] * 3 + [vmem()] * 17,
         [pltpu.VMEM((XL * SLOTS * per, HD), F32)],
     )(
-        *(notices, sources, came, mine, other),
+        *(xl[None], table, factors, came, stays, other),
         *(codes, sib, near, two, three, near_x, two_x, three_x),
         *(swap(x, "core") for x in (near, two, three, near_x, two_x, three_x)),
     )
     parts = call(
         last_body,
         jax.ShapeDtypeStruct((XL * COLS, ROWS, HD), BF16),
-        [smem()] + [vmem()] * 4,
+        [smem()] * 2 + [vmem()] * 4,
         [pltpu.VMEM((COLS, XL * ROWS, HD), F32)],
-    )(notices, rows, total, four, four_x)
+    )(table, factors, rows, total, four, four_x)
     parts = exchange(parts, ("xl",) + tp_axes).reshape(XL * TP, OUT_COLS, ROWS, HD)
     return call(
         sum_body, jax.ShapeDtypeStruct((STEPS, SLOTS, OUT_COLS * HD), BF16), [vmem()]

time: 83.4 us -> 82.9 us (level)
  Pallas kernels: 14.6 us -> 15.7 us
  waiting for transfers between devices: 17 us -> 16.1 us
    pallas_call x2, Pallas kernels: 3.19 us -> 4.64 us  [the longest x1 2.55 us: shards(): call(table_body, [jax.ShapeDtypeStruct((TABLE,), I32), jax.ShapeDtypeStru...]
    all_to_all x3, waiting for transfers between devices: 16.7 us -> 15.8 us  [exchange(): return lax.all_to_all(x, axes, split_axis=0, concat_axis=0, tiled=True)]
  transfers between devices with their start and end apart: 19 -> 19, of which waited for: 4 -> 4; matrix products, arithmetic and copies ran while one was open for 0% -> 0% of each run, Pallas kernels for 15% -> 17%
where the time goes in v10:
time: 82.9 us; the launch traced here: 82.2 us
  starting transfers between devices  32.6 us (39%)
  blocking collectives  17.6 us (21%)
  waiting for transfers between devices  16.1 us (19%)
  Pallas kernels  15.7 us (19%)
    all_to_all x1, blocking collectives, exchange(): return lax.all_to_all(x, axes, split_axis=0, concat_axis=0, tiled=True)  17.6 us
    all_to_all x3, starting transfers between devices, exchange(): return lax.all_to_all(x, axes, split_axis=0, concat_axis=0, tiled=True)  16.2 us
    all_to_all x3, waiting for transfers between devices, exchange(): return lax.all_to_all(x, axes, split_axis=0, concat_axis=0, tiled=True)  15.8 us
    ppermute x8, starting transfers between devices, around(): return lax.ppermute(x, ('z', 'core'), pairs)  12.6 us
    ppermute x8, starting transfers between devices, swap(): return lax.ppermute(x, axis, [(0, 1), (1, 0)])  3.86 us
    pallas_call x1, Pallas kernels, shards(): call(project_body, [jax.ShapeDtypeStruct((HEADS, XL * ROWS, HD), BF16), j...  3.2 us
    pallas_call x1, Pallas kernels, shards(): call(stay_body, [jax.ShapeDtypeStruct((SLOTS, per, HD), BF16), jax.ShapeD...  3.06 us
    pallas_call x1, Pallas kernels, shards(): call(table_body, [jax.ShapeDtypeStruct((TABLE,), I32), jax.ShapeDtypeStru...  2.55 us
  transfers between devices with their start and end apart: 19, of which 4 were waited for; matrix products, arithmetic and copies ran while one was open for 0% of the time, Pallas kernels for 17%

profile of v10, /device:TPU:8, one launch (start us, length us, event | category | flops | bytes accessed | tf_op | source)
XLA Modules:
  0.0 82.2 jit_solution(13124079555175072125)
XLA Ops:
  0.0 2.0 %collective-permute-start.2 = (bf16[10,128,128]{2,1,0:T(8,128)(2,1)}, bf16[10,128,128]{2,1,0:T(8,128)(2,1)S(1)}, u32[]{:S(2)}, u32[]{:S(2)}) collective-permute-start(bf16[10,128,128]{2,1,0:T(8,128)(2,1)} %rest_0_.1), channel_id=1, source_target_pairs={{0,16},{8,120},{16,32},{24,8},{32,48},{40,24},{48,64},{56,40},{64,... | collective-permute-start | bytes 983048 | tf_op jit(solution)/shard_map/ppermute | solution.py:296
  2.0 1.5 %shard_map.91 = f32[32,1,128]{2,1,0:T(1,128)} custom-call(s32[1]{0:T(128)} %bitcast.place, s32[1,13]{1,0:T(1,128)} %dep_in.1, s32[1,13]{1,0:T(1,128)} %refs_1_.1, s32[16]{0:T(128)} %lengths_in.1, s32[10]{0:T(128)} %refs_3_.1, f32[10]{0:T(128)} %refs_4_.1), custom_call_target="tpu_custom_call" | custom-call | tf_op jit(solution)/shard_map/pallas_call | solution.py:300
  3.5 0.0 collective-permute-done.rest_1_
  3.5 2.0 %collective-permute-start.1 = (bf16[10,128,128]{2,1,0:T(8,128)(2,1)S(1)}, bf16[10,128,128]{2,1,0:T(8,128)(2,1)}, u32[]{:S(2)}, u32[]{:S(2)}) collective-permute-start(bf16[10,128,128]{2,1,0:T(8,128)(2,1)S(1)} %collective-permute-done.rest_1_), channel_id=1, source_target_pairs={{0,16},{8,120},{16,32},{24,8},{32,48},{40,24},{48,64},{56,40},{64,... | collective-permute-start | bytes 983048 | tf_op jit(solution)/shard_map/ppermute | solution.py:296
  5.5 8.0 %all-to-all-start = ((f32[32,1,128]{2,1,0:T(1,128)}), f32[32,1,128]{2,1,0:T(1,128)S(1)}, u32[]{:S(2)}, u32[]{:S(2)}) async-start(f32[32,1,128]{2,1,0:T(1,128)} %shard_map.91), calls=%async_computation | async-start | bytes 32768 | tf_op jit(solution)/shard_map/all_to_all | solution.py:285
  13.5 3.1 %shard_map.93 = (bf16[16,16,128]{2,1,0:T(8,128)(2,1)S(1)}, bf16[13,20,128]{2,1,0:T(8,128)(2,1)S(1)}) custom-call(s32[1,13]{1,0:T(1,128)} %dep_in.1, s32[16]{0:T(128)} %lengths_in.1, bf16[2,16,8,128]{3,2,1,0:T(8,128)(2,1)} %q_in.1, bf16[2,16,256]{2,1,0:T(8,128)(2,1)} %bitcast.5, bf16[16,1,256,256]{3,2,1,0:T(8,128)(2,1)} %cache.3), custom_call_target="tpu_custom_call" | custom-call | tf_op jit(solution)/shard_map/pallas_call | solution.py:311
  16.6 0.0 copy-start.1
  16.6 1.8 %collective-permute-start.4 = (bf16[10,128,128]{2,1,0:T(8,128)(2,1)S(1)}, bf16[10,128,128]{2,1,0:T(8,128)(2,1)}, u32[]{:S(2)}, u32[]{:S(2)}) collective-permute-start(bf16[10,128,128]{2,1,0:T(8,128)(2,1)S(1)} %collective-permute-done.2.rest_2_), channel_id=1, source_target_pairs={{0,16},{8,120},{16,32},{24,8},{32,48},{40,24},{48,64},{56,40},{64,... | collective-permute-start | bytes 983048 | tf_op jit(solution)/shard_map/ppermute | solution.py:296
  18.4 3.4 %all-to-all-done.notices = f32[32,1,128]{2,1,0:T(1,128)S(1)} async-done(((f32[32,1,128]{2,1,0:T(1,128)}), f32[32,1,128]{2,1,0:T(1,128)S(1)}, u32[]{:S(2)}, u32[]{:S(2)}) %all-to-all-start) | async-done | bytes 16416 | tf_op jit(solution)/shard_map/all_to_all | solution.py:285
  21.8 0.6 collective-permute-start.6
  22.4 1.6 %shard_map.94 = bf16[32,20,128]{2,1,0:T(8,128)(2,1)} custom-call(f32[32,1,128]{2,1,0:T(1,128)S(1)} %all-to-all-done.notices, bf16[13,20,128]{2,1,0:T(8,128)(2,1)S(1)} %get-tuple-element.22.packs), custom_call_target="tpu_custom_call" | custom-call | tf_op jit(solution)/shard_map/pallas_call | solution.py:339
  24.0 4.3 %all-to-all-start.1 = ((bf16[32,20,128]{2,1,0:T(8,128)(2,1)}), bf16[32,20,128]{2,1,0:T(8,128)(2,1)S(1)}, u32[]{:S(2)}, u32[]{:S(2)}) async-start(bf16[32,20,128]{2,1,0:T(8,128)(2,1)} %shard_map.94), calls=%async_computation.1 | async-start | bytes 393216 | tf_op jit(solution)/shard_map/all_to_all | solution.py:285
  28.3 1.9 %collective-permute-start.3 = (bf16[16,16,128]{2,1,0:T(8,128)(2,1)S(1)}, bf16[16,16,128]{2,1,0:T(8,128)(2,1)S(1)}, u32[]{:S(2)}, u32[]{:S(2)}) collective-permute-start(bf16[16,16,128]{2,1,0:T(8,128)(2,1)S(1)} %get-tuple-element.24.mine), channel_id=1, source_target_pairs={{0,128},{128,0},{1,129},{129,1},{2,130},{130,2},{3,131},{131,3},{4... | collective-permute-start | bytes 196616 | tf_op jit(solution)/shard_map/ppermute | solution.py:288
  30.2 1.5 %collective-permute-start.5 = (bf16[10,128,128]{2,1,0:T(8,128)(2,1)}, bf16[10,128,128]{2,1,0:T(8,128)(2,1)}, u32[]{:S(2)}, u32[]{:S(2)}) collective-permute-start(bf16[10,128,128]{2,1,0:T(8,128)(2,1)} %collective-permute-done.4.rest_3_), channel_id=1, source_target_pairs={{0,16},{8,120},{16,32},{24,8},{32,48},{40,24},{48,64},{56,40},{64,... | collective-permute-start | bytes 983048 | tf_op jit(solution)/shard_map/ppermute | solution.py:296
  31.7 1.5 %collective-permute-start.7 = (bf16[10,128,128]{2,1,0:T(8,128)(2,1)}, bf16[10,128,128]{2,1,0:T(8,128)(2,1)}, u32[]{:S(2)}, u32[]{:S(2)}) collective-permute-start(bf16[10,128,128]{2,1,0:T(8,128)(2,1)} %collective-permute-done.6.rest_6_), channel_id=1, source_target_pairs={{0,16},{8,120},{16,32},{24,8},{32,48},{40,24},{48,64},{56,40},{64,... | collective-permute-start | bytes 983048 | tf_op jit(solution)/shard_map/ppermute | solution.py:296
  33.2 1.2 %collective-permute-start.11 = (bf16[10,128,128]{2,1,0:T(8,128)(2,1)}, bf16[10,128,128]{2,1,0:T(8,128)(2,1)}, u32[]{:S(2)}, u32[]{:S(2)}) collective-permute-start(bf16[10,128,128]{2,1,0:T(8,128)(2,1)} %collective-permute-done.1.rest_5_), channel_id=1, source_target_pairs={{0,8},{8,0},{1,9},{9,1},{2,10},{10,2},{3,11},{11,3},{4,12},{12,4},... | collective-permute-start | bytes 983048 | tf_op jit(solution)/shard_map/ppermute | solution.py:288
  34.4 0.0 collective-permute-start.9
  34.4 5.8 %all-to-all-done.1.pulled = bf16[32,20,128]{2,1,0:T(8,128)(2,1)S(1)} async-done(((bf16[32,20,128]{2,1,0:T(8,128)(2,1)}), bf16[32,20,128]{2,1,0:T(8,128)(2,1)S(1)}, u32[]{:S(2)}, u32[]{:S(2)}) %all-to-all-start.1) | async-done | bytes 163872 | tf_op jit(solution)/shard_map/all_to_all | solution.py:285
  40.2 2.1 %shard_map.95 = bf16[32,32,128]{2,1,0:T(8,128)(2,1)} custom-call(f32[32,1,128]{2,1,0:T(1,128)S(1)} %all-to-all-done.notices, bf16[32,20,128]{2,1,0:T(8,128)(2,1)S(1)} %all-to-all-done.1.pulled, bf16[16,1,256,256]{3,2,1,0:T(8,128)(2,1)S(1)} %copy-done), custom_call_target="tpu_custom_call" | custom-call | tf_op jit(solution)/shard_map/pallas_call | solution.py:344
  42.3 3.9 %all-to-all-start.2 = ((bf16[32,32,128]{2,1,0:T(8,128)(2,1)}), bf16[32,32,128]{2,1,0:T(8,128)(2,1)S(1)}, u32[]{:S(2)}, u32[]{:S(2)}) async-start(bf16[32,32,128]{2,1,0:T(8,128)(2,1)} %shard_map.95), calls=%async_computation.2 | async-start | bytes 524288 | tf_op jit(solution)/shard_map/all_to_all | solution.py:285
  46.2 0.2 collective-permute-start.12
  46.4 0.3 collective-permute-start.10
  46.8 0.2 collective-permute-start.13
  47.0 1.8 %collective-permute-start.14 = (bf16[10,128,128]{2,1,0:T(8,128)(2,1)}, bf16[10,128,128]{2,1,0:T(8,128)(2,1)S(1)}, u32[]{:S(2)}, u32[]{:S(2)}) collective-permute-start(bf16[10,128,128]{2,1,0:T(8,128)(2,1)} %collective-permute-done.5.rest_4_), channel_id=1, source_target_pairs={{0,16},{8,120},{16,32},{24,8},{32,48},{40,24},{48,64},{56,40},{64,... | collective-permute-start | bytes 983048 | tf_op jit(solution)/shard_map/ppermute | solution.py:296
  48.8 1.5 %collective-permute-start.15 = (bf16[10,128,128]{2,1,0:T(8,128)(2,1)}, bf16[10,128,128]{2,1,0:T(8,128)(2,1)S(1)}, u32[]{:S(2)}, u32[]{:S(2)}) collective-permute-start(bf16[10,128,128]{2,1,0:T(8,128)(2,1)} %collective-permute-done.7.rest_7_), channel_id=1, source_target_pairs={{0,16},{8,120},{16,32},{24,8},{32,48},{40,24},{48,64},{56,40},{64,... | collective-permute-start | bytes 983048 | tf_op jit(solution)/shard_map/ppermute | solution.py:296
  50.2 2.5 %shard_map.92 = (s32[384]{0:T(512)S(1)}, f32[160]{0:T(256)S(1)}) custom-call(f32[32,1,128]{2,1,0:T(1,128)S(1)} %all-to-all-done.notices), custom_call_target="tpu_custom_call" | custom-call | tf_op jit(solution)/shard_map/pallas_call | solution.py:333
  52.8 6.6 %all-to-all-done.2.came = bf16[32,32,128]{2,1,0:T(8,128)(2,1)S(1)} async-done(((bf16[32,32,128]{2,1,0:T(8,128)(2,1)}), bf16[32,32,128]{2,1,0:T(8,128)(2,1)S(1)}, u32[]{:S(2)}, u32[]{:S(2)}) %all-to-all-start.2) | async-done | bytes 262176 | tf_op jit(solution)/shard_map/all_to_all | solution.py:285
  59.4 3.2 %shard_map.96 = (bf16[8,64,128]{2,1,0:T(8,128)(2,1)S(1)}, f32[40,64,128]{2,1,0:T(8,128)S(1)}) custom-call(s32[1]{0:T(128)} %bitcast.1.where, s32[384]{0:T(512)S(1)} %get-tuple-element.20.table, f32[160]{0:T(256)S(1)} %get-tuple-element.21.scales, bf16[32,32,128]{2,1,0:T(8,128)(2,1)S(1)} %all-to-all-done.2.came, ...), custom_call_target="tpu_custom_call" | custom-call | tf_op jit(solution)/shard_map/pallas_call | solution.py:352
  62.6 0.3 collective-permute-done.15.four_x
  62.9 1.0 %shard_map.97 = bf16[80,32,128]{2,1,0:T(8,128)(2,1)S(1)} custom-call(s32[384]{0:T(512)S(1)} %get-tuple-element.20.table, f32[160]{0:T(256)S(1)} %get-tuple-element.21.scales, bf16[8,64,128]{2,1,0:T(8,128)(2,1)S(1)} %get-tuple-element.27.rows, f32[40,64,128]{2,1,0:T(8,128)S(1)} %get-tuple-element.28.so_far, ...), custom_call_target="tpu_custom_call" | custom-call | tf_op jit(solution)/shard_map/pallas_call | solution.py:365
  63.9 17.6 %all_to_all.20 = bf16[80,32,128]{2,1,0:T(8,128)(2,1)S(1)} all-to-all(bf16[80,32,128]{2,1,0:T(8,128)(2,1)S(1)} %shard_map.97), channel_id=1, replica_groups=mesh['xl'=2,'z'=8,'core'=2,'y'=4,'xh'=2] {'xl','y','xh'}, dimensions={0} | all-to-all | bytes 1310720 | tf_op jit(solution)/shard_map/all_to_all | solution.py:285
  81.5 0.7 shard_map.98
  (19 shorter events, 0.0 us)
Async XLA Ops:
  0.0 40.2 %copy-start = (bf16[16,1,256,256]{3,2,1,0:T(8,128)(2,1)S(1)}, bf16[16,1,256,256]{3,2,1,0:T(8,128)(2,1)}, u32[]{:S(2)}) copy-start(bf16[16,1,256,256]{3,2,1,0:T(8,128)(2,1)} %cache.3) | copy-start | bytes 6291460
  0.0 3.5 %collective-permute-start = (bf16[10,128,128]{2,1,0:T(8,128)(2,1)}, bf16[10,128,128]{2,1,0:T(8,128)(2,1)S(1)}, u32[]{:S(2)}, u32[]{:S(2)}) collective-permute-start(bf16[10,128,128]{2,1,0:T(8,128)(2,1)} %rest_0_.1), channel_id=1, source_target_pairs={{0,8},{8,0},{1,9},{9,1},{2,10},{10,2},{3,11},{11,3},{4,12},{12,4},... | collective-permute-start | bytes 983048 | tf_op jit(solution)/shard_map/ppermute | solution.py:288
  0.0 16.6 %collective-permute-start.2 = (bf16[10,128,128]{2,1,0:T(8,128)(2,1)}, bf16[10,128,128]{2,1,0:T(8,128)(2,1)S(1)}, u32[]{:S(2)}, u32[]{:S(2)}) collective-permute-start(bf16[10,128,128]{2,1,0:T(8,128)(2,1)} %rest_0_.1), channel_id=1, source_target_pairs={{0,16},{8,120},{16,32},{24,8},{32,48},{40,24},{48,64},{56,40},{64,... | collective-permute-start | bytes 983048 | tf_op jit(solution)/shard_map/ppermute | solution.py:296
  3.5 18.3 %collective-permute-start.1 = (bf16[10,128,128]{2,1,0:T(8,128)(2,1)S(1)}, bf16[10,128,128]{2,1,0:T(8,128)(2,1)}, u32[]{:S(2)}, u32[]{:S(2)}) collective-permute-start(bf16[10,128,128]{2,1,0:T(8,128)(2,1)S(1)} %collective-permute-done.rest_1_), channel_id=1, source_target_pairs={{0,16},{8,120},{16,32},{24,8},{32,48},{40,24},{48,64},{56,40},{64,... | collective-permute-start | bytes 983048 | tf_op jit(solution)/shard_map/ppermute | solution.py:296
  5.5 16.3 %all-to-all-start = ((f32[32,1,128]{2,1,0:T(1,128)}), f32[32,1,128]{2,1,0:T(1,128)S(1)}, u32[]{:S(2)}, u32[]{:S(2)}) async-start(f32[32,1,128]{2,1,0:T(1,128)} %shard_map.91), calls=%async_computation | async-start | bytes 32768 | tf_op jit(solution)/shard_map/all_to_all | solution.py:285
  16.6 42.8 %copy-start.1 = (bf16[10,128,128]{2,1,0:T(8,128)(2,1)S(1)}, bf16[10,128,128]{2,1,0:T(8,128)(2,1)}, u32[]{:S(2)}) copy-start(bf16[10,128,128]{2,1,0:T(8,128)(2,1)} %rest_0_.1) | copy-start | bytes 983044
  16.6 13.6 %collective-permute-start.4 = (bf16[10,128,128]{2,1,0:T(8,128)(2,1)S(1)}, bf16[10,128,128]{2,1,0:T(8,128)(2,1)}, u32[]{:S(2)}, u32[]{:S(2)}) collective-permute-start(bf16[10,128,128]{2,1,0:T(8,128)(2,1)S(1)} %collective-permute-done.2.rest_2_), channel_id=1, source_target_pairs={{0,16},{8,120},{16,32},{24,8},{32,48},{40,24},{48,64},{56,40},{64,... | collective-permute-start | bytes 983048 | tf_op jit(solution)/shard_map/ppermute | solution.py:296
  21.8 9.8 %collective-permute-start.6 = (bf16[10,128,128]{2,1,0:T(8,128)(2,1)}, bf16[10,128,128]{2,1,0:T(8,128)(2,1)}, u32[]{:S(2)}, u32[]{:S(2)}) collective-permute-start(bf16[10,128,128]{2,1,0:T(8,128)(2,1)} %collective-permute-done.1.rest_5_), channel_id=1, source_target_pairs={{0,16},{8,120},{16,32},{24,8},{32,48},{40,24},{48,64},{56,40},{64,... | collective-permute-start | bytes 983048 | tf_op jit(solution)/shard_map/ppermute | solution.py:296
  24.0 16.2 %all-to-all-start.1 = ((bf16[32,20,128]{2,1,0:T(8,128)(2,1)}), bf16[32,20,128]{2,1,0:T(8,128)(2,1)S(1)}, u32[]{:S(2)}, u32[]{:S(2)}) async-start(bf16[32,20,128]{2,1,0:T(8,128)(2,1)} %shard_map.94), calls=%async_computation.1 | async-start | bytes 393216 | tf_op jit(solution)/shard_map/all_to_all | solution.py:285
  28.3 6.0 %collective-permute-start.3 = (bf16[16,16,128]{2,1,0:T(8,128)(2,1)S(1)}, bf16[16,16,128]{2,1,0:T(8,128)(2,1)S(1)}, u32[]{:S(2)}, u32[]{:S(2)}) collective-permute-start(bf16[16,16,128]{2,1,0:T(8,128)(2,1)S(1)} %get-tuple-element.24.mine), channel_id=1, source_target_pairs={{0,128},{128,0},{1,129},{129,1},{2,130},{130,2},{3,131},{131,3},{4... | collective-permute-start | bytes 196616 | tf_op jit(solution)/shard_map/ppermute | solution.py:288
  30.2 16.0 %collective-permute-start.8 = (bf16[10,128,128]{2,1,0:T(8,128)(2,1)S(1)}, bf16[10,128,128]{2,1,0:T(8,128)(2,1)}, u32[]{:S(2)}, u32[]{:S(2)}) collective-permute-start(bf16[10,128,128]{2,1,0:T(8,128)(2,1)S(1)} %collective-permute-done.2.rest_2_), channel_id=1, source_target_pairs={{0,8},{8,0},{1,9},{9,1},{2,10},{10,2},{3,11},{11,3},{4,12},{12,4},... | collective-permute-start | bytes 983048 | tf_op jit(solution)/shard_map/ppermute | solution.py:288
  30.2 16.2 %collective-permute-start.5 = (bf16[10,128,128]{2,1,0:T(8,128)(2,1)}, bf16[10,128,128]{2,1,0:T(8,128)(2,1)}, u32[]{:S(2)}, u32[]{:S(2)}) collective-permute-start(bf16[10,128,128]{2,1,0:T(8,128)(2,1)} %collective-permute-done.4.rest_3_), channel_id=1, source_target_pairs={{0,16},{8,120},{16,32},{24,8},{32,48},{40,24},{48,64},{56,40},{64,... | collective-permute-start | bytes 983048 | tf_op jit(solution)/shard_map/ppermute | solution.py:296
  31.7 15.1 %collective-permute-start.7 = (bf16[10,128,128]{2,1,0:T(8,128)(2,1)}, bf16[10,128,128]{2,1,0:T(8,128)(2,1)}, u32[]{:S(2)}, u32[]{:S(2)}) collective-permute-start(bf16[10,128,128]{2,1,0:T(8,128)(2,1)} %collective-permute-done.6.rest_6_), channel_id=1, source_target_pairs={{0,16},{8,120},{16,32},{24,8},{32,48},{40,24},{48,64},{56,40},{64,... | collective-permute-start | bytes 983048 | tf_op jit(solution)/shard_map/ppermute | solution.py:296
  33.2 13.8 %collective-permute-start.11 = (bf16[10,128,128]{2,1,0:T(8,128)(2,1)}, bf16[10,128,128]{2,1,0:T(8,128)(2,1)}, u32[]{:S(2)}, u32[]{:S(2)}) collective-permute-start(bf16[10,128,128]{2,1,0:T(8,128)(2,1)} %collective-permute-done.1.rest_5_), channel_id=1, source_target_pairs={{0,8},{8,0},{1,9},{9,1},{2,10},{10,2},{3,11},{11,3},{4,12},{12,4},... | collective-permute-start | bytes 983048 | tf_op jit(solution)/shard_map/ppermute | solution.py:288
  34.4 14.4 %collective-permute-start.9 = (bf16[10,128,128]{2,1,0:T(8,128)(2,1)}, bf16[10,128,128]{2,1,0:T(8,128)(2,1)}, u32[]{:S(2)}, u32[]{:S(2)}) collective-permute-start(bf16[10,128,128]{2,1,0:T(8,128)(2,1)} %collective-permute-done.4.rest_3_), channel_id=1, source_target_pairs={{0,8},{8,0},{1,9},{9,1},{2,10},{10,2},{3,11},{11,3},{4,12},{12,4},... | collective-permute-start | bytes 983048 | tf_op jit(solution)/shard_map/ppermute | solution.py:288
  42.3 17.1 %all-to-all-start.2 = ((bf16[32,32,128]{2,1,0:T(8,128)(2,1)}), bf16[32,32,128]{2,1,0:T(8,128)(2,1)S(1)}, u32[]{:S(2)}, u32[]{:S(2)}) async-start(bf16[32,32,128]{2,1,0:T(8,128)(2,1)} %shard_map.95), calls=%async_computation.2 | async-start | bytes 524288 | tf_op jit(solution)/shard_map/all_to_all | solution.py:285
  46.2 6.6 %collective-permute-start.12 = (bf16[10,128,128]{2,1,0:T(8,128)(2,1)}, bf16[10,128,128]{2,1,0:T(8,128)(2,1)S(1)}, u32[]{:S(2)}, u32[]{:S(2)}) collective-permute-start(bf16[10,128,128]{2,1,0:T(8,128)(2,1)} %collective-permute-done.6.rest_6_), channel_id=1, source_target_pairs={{0,8},{8,0},{1,9},{9,1},{2,10},{10,2},{3,11},{11,3},{4,12},{12,4},... | collective-permute-start | bytes 983048 | tf_op jit(solution)/shard_map/ppermute | solution.py:288
  46.4 6.4 %collective-permute-start.10 = (bf16[10,128,128]{2,1,0:T(8,128)(2,1)}, bf16[10,128,128]{2,1,0:T(8,128)(2,1)S(1)}, u32[]{:S(2)}, u32[]{:S(2)}) collective-permute-start(bf16[10,128,128]{2,1,0:T(8,128)(2,1)} %collective-permute-done.5.rest_4_), channel_id=1, source_target_pairs={{0,8},{8,0},{1,9},{9,1},{2,10},{10,2},{3,11},{11,3},{4,12},{12,4},... | collective-permute-start | bytes 983048 | tf_op jit(solution)/shard_map/ppermute | solution.py:288
  46.8 12.6 %collective-permute-start.13 = (bf16[10,128,128]{2,1,0:T(8,128)(2,1)}, bf16[10,128,128]{2,1,0:T(8,128)(2,1)S(1)}, u32[]{:S(2)}, u32[]{:S(2)}) collective-permute-start(bf16[10,128,128]{2,1,0:T(8,128)(2,1)} %collective-permute-done.7.rest_7_), channel_id=1, source_target_pairs={{0,8},{8,0},{1,9},{9,1},{2,10},{10,2},{3,11},{11,3},{4,12},{12,4},... | collective-permute-start | bytes 983048 | tf_op jit(solution)/shard_map/ppermute | solution.py:288
  47.0 15.6 %collective-permute-start.14 = (bf16[10,128,128]{2,1,0:T(8,128)(2,1)}, bf16[10,128,128]{2,1,0:T(8,128)(2,1)S(1)}, u32[]{:S(2)}, u32[]{:S(2)}) collective-permute-start(bf16[10,128,128]{2,1,0:T(8,128)(2,1)} %collective-permute-done.5.rest_4_), channel_id=1, source_target_pairs={{0,16},{8,120},{16,32},{24,8},{32,48},{40,24},{48,64},{56,40},{64,... | collective-permute-start | bytes 983048 | tf_op jit(solution)/shard_map/ppermute | solution.py:296
  48.8 14.1 %collective-permute-start.15 = (bf16[10,128,128]{2,1,0:T(8,128)(2,1)}, bf16[10,128,128]{2,1,0:T(8,128)(2,1)S(1)}, u32[]{:S(2)}, u32[]{:S(2)}) collective-permute-start(bf16[10,128,128]{2,1,0:T(8,128)(2,1)} %collective-permute-done.7.rest_7_), channel_id=1, source_target_pairs={{0,16},{8,120},{16,32},{24,8},{32,48},{40,24},{48,64},{56,40},{64,... | collective-permute-start | bytes 983048 | tf_op jit(solution)/shard_map/ppermute | solution.py:296

commit v11 on v10

--- a/solution.py
+++ b/solution.py
@@ -304,8 +304,7 @@
         [pltpu.SMEM(a.shape, a.dtype) for a in given] + [pltpu.SemaphoreType.DMA((len(given),))],
     )(base.astype(I32)[None], *(in_hbm(a) for a in given))
     cache = in_hbm(kv_cache)
-    sib, notice = lax.optimization_barrier((sib, notice))
-    near, near_x = around(codes), around(sib)
+    near, near_x = around(codes), around(codes, 1)
     notices = exchange(notice, rep_axes)
     fresh = new_kv.reshape(STEPS, SLOTS, 2 * HD)
     stays, packs = call(
@@ -327,7 +326,7 @@
         ],
     )(*(in_hbm(a) for a in (departing, lengths, queries, fresh)), cache)
     near, stays = lax.optimization_barrier((near, stays))
-    near_x, notices = lax.optimization_barrier((near_x, notices))
+    near_x, notices, stays = lax.optimization_barrier((near_x, notices, stays))
     two, two_x = around(near), around(near_x)
     other = swap(stays, "xl")
     table, factors = call(

time: 82.9 us -> 84.1 us (1.014)
  waiting for transfers between devices: 16.1 us -> 18.5 us
  starting transfers between devices: 32.6 us -> 31.5 us
    all_to_all x3, waiting for transfers between devices: 15.8 us -> 17.7 us  [exchange(): return lax.all_to_all(x, axes, split_axis=0, concat_axis=0, tiled=True)]
    all_to_all x3, starting transfers between devices: 16.2 us -> 14.7 us  [exchange(): return lax.all_to_all(x, axes, split_axis=0, concat_axis=0, tiled=True)]
  transfers between devices with their start and end apart: 19 -> 19, of which waited for: 4 -> 5; matrix products, arithmetic and copies ran while one was open for 0% -> 0% of each run, Pallas kernels for 17% -> 17%
where the time goes in v11:
time: 84.1 us; the launch traced here: 83.4 us
  starting transfers between devices  31.5 us (37%)
  waiting for transfers between devices  18.5 us (22%)
  blocking collectives  17.6 us (21%)
  Pallas kernels  15.7 us (19%)
    all_to_all x3, waiting for transfers between devices, exchange(): return lax.all_to_all(x, axes, split_axis=0, concat_axis=0, tiled=True)  17.7 us
    all_to_all x1, blocking collectives, exchange(): return lax.all_to_all(x, axes, split_axis=0, concat_axis=0, tiled=True)  17.6 us
    all_to_all x3, starting transfers between devices, exchange(): return lax.all_to_all(x, axes, split_axis=0, concat_axis=0, tiled=True)  14.7 us
    ppermute x8, starting transfers between devices, around(): return lax.ppermute(x, ('z', 'core'), pairs)  12.8 us
    ppermute x8, starting transfers between devices, swap(): return lax.ppermute(x, axis, [(0, 1), (1, 0)])  3.95 us
    pallas_call x1, Pallas kernels, shards(): call(project_body, [jax.ShapeDtypeStruct((HEADS, XL * ROWS, HD), BF16), j...  3.2 us
    pallas_call x1, Pallas kernels, shards(): call(stay_body, [jax.ShapeDtypeStruct((SLOTS, per, HD), BF16), jax.ShapeD...  3.09 us
    pallas_call x1, Pallas kernels, shards(): call(table_body, [jax.ShapeDtypeStruct((TABLE,), I32), jax.ShapeDtypeStru...  2.55 us
  transfers between devices with their start and end apart: 19, of which 5 were waited for; matrix products, arithmetic and copies ran while one was open for 0% of the time, Pallas kernels for 17%

profile of v11, /device:TPU:8, one launch (start us, length us, event | category | flops | bytes accessed | tf_op | source)
XLA Modules:
  0.0 83.4 jit_solution(3539782752936171862)
XLA Ops:
  0.0 1.9 %collective-permute-start.1 = (bf16[10,128,128]{2,1,0:T(8,128)(2,1)}, bf16[10,128,128]{2,1,0:T(8,128)(2,1)S(1)}, u32[]{:S(2)}, u32[]{:S(2)}) collective-permute-start(bf16[10,128,128]{2,1,0:T(8,128)(2,1)} %rest_0_.1), channel_id=1, source_target_pairs={{0,16},{8,120},{16,32},{24,8},{32,48},{40,24},{48,64},{56,40},{64,... | collective-permute-start | bytes 983048 | tf_op jit(solution)/shard_map/ppermute | solution.py:296
  1.9 4.1 %collective-permute-start = (bf16[10,128,128]{2,1,0:T(8,128)(2,1)}, bf16[10,128,128]{2,1,0:T(8,128)(2,1)S(1)}, u32[]{:S(2)}, u32[]{:S(2)}) collective-permute-start(bf16[10,128,128]{2,1,0:T(8,128)(2,1)} %rest_0_.1), channel_id=1, source_target_pairs={{0,120},{8,16},{16,8},{24,32},{32,24},{40,48},{48,40},{56,64},{64,... | collective-permute-start | bytes 983048 | tf_op jit(solution)/shard_map/ppermute | solution.py:296
  6.0 1.5 %shard_map.91 = f32[32,1,128]{2,1,0:T(1,128)} custom-call(s32[1]{0:T(128)} %bitcast.place, s32[1,13]{1,0:T(1,128)} %dep_in.1, s32[1,13]{1,0:T(1,128)} %refs_1_.1, s32[16]{0:T(128)} %lengths_in.1, s32[10]{0:T(128)} %refs_3_.1, f32[10]{0:T(128)} %refs_4_.1), custom_call_target="tpu_custom_call" | custom-call | tf_op jit(solution)/shard_map/pallas_call | solution.py:300
  7.6 5.5 %all-to-all-start = ((f32[32,1,128]{2,1,0:T(1,128)}), f32[32,1,128]{2,1,0:T(1,128)S(1)}, u32[]{:S(2)}, u32[]{:S(2)}) async-start(f32[32,1,128]{2,1,0:T(1,128)} %shard_map.91), calls=%async_computation | async-start | bytes 32768 | tf_op jit(solution)/shard_map/all_to_all | solution.py:285
  13.1 3.1 %shard_map.92 = (bf16[16,16,128]{2,1,0:T(8,128)(2,1)S(1)}, bf16[13,20,128]{2,1,0:T(8,128)(2,1)S(1)}) custom-call(s32[1,13]{1,0:T(1,128)} %dep_in.1, s32[16]{0:T(128)} %lengths_in.1, bf16[2,16,8,128]{3,2,1,0:T(8,128)(2,1)} %q_in.1, bf16[2,16,256]{2,1,0:T(8,128)(2,1)} %bitcast.5, bf16[16,1,256,256]{3,2,1,0:T(8,128)(2,1)} %cache.3), custom_call_target="tpu_custom_call" | custom-call | tf_op jit(solution)/shard_map/pallas_call | solution.py:310
  16.2 5.2 %all-to-all-done.notices = f32[32,1,128]{2,1,0:T(1,128)S(1)} async-done(((f32[32,1,128]{2,1,0:T(1,128)}), f32[32,1,128]{2,1,0:T(1,128)S(1)}, u32[]{:S(2)}, u32[]{:S(2)}) %all-to-all-start) | async-done | bytes 16416 | tf_op jit(solution)/shard_map/all_to_all | solution.py:285
  21.4 0.0 collective-permute-done.rest_5_
  21.4 0.6 collective-permute-start.6
  22.0 0.5 collective-permute-start.4
  22.6 1.6 %shard_map.94 = bf16[32,20,128]{2,1,0:T(8,128)(2,1)} custom-call(f32[32,1,128]{2,1,0:T(1,128)S(1)} %all-to-all-done.notices, bf16[13,20,128]{2,1,0:T(8,128)(2,1)S(1)} %get-tuple-element.21.packs), custom_call_target="tpu_custom_call" | custom-call | tf_op jit(solution)/shard_map/pallas_call | solution.py:338
  24.1 5.3 %all-to-all-start.1 = ((bf16[32,20,128]{2,1,0:T(8,128)(2,1)}), bf16[32,20,128]{2,1,0:T(8,128)(2,1)S(1)}, u32[]{:S(2)}, u32[]{:S(2)}) async-start(bf16[32,20,128]{2,1,0:T(8,128)(2,1)} %shard_map.94), calls=%async_computation.1 | async-start | bytes 393216 | tf_op jit(solution)/shard_map/all_to_all | solution.py:285
  29.5 1.9 %collective-permute-start.2 = (bf16[16,16,128]{2,1,0:T(8,128)(2,1)S(1)}, bf16[16,16,128]{2,1,0:T(8,128)(2,1)S(1)}, u32[]{:S(2)}, u32[]{:S(2)}) collective-permute-start(bf16[16,16,128]{2,1,0:T(8,128)(2,1)S(1)} %get-tuple-element.22.mine), channel_id=1, source_target_pairs={{0,128},{128,0},{1,129},{129,1},{2,130},{130,2},{3,131},{131,3},{4... | collective-permute-start | bytes 196616 | tf_op jit(solution)/shard_map/ppermute | solution.py:288
  31.4 1.5 %collective-permute-start.7 = (bf16[10,128,128]{2,1,0:T(8,128)(2,1)}, bf16[10,128,128]{2,1,0:T(8,128)(2,1)}, u32[]{:S(2)}, u32[]{:S(2)}) collective-permute-start(bf16[10,128,128]{2,1,0:T(8,128)(2,1)} %collective-permute-done.6.rest_6_), channel_id=1, source_target_pairs={{0,16},{8,120},{16,32},{24,8},{32,48},{40,24},{48,64},{56,40},{64,... | collective-permute-start | bytes 983048 | tf_op jit(solution)/shard_map/ppermute | solution.py:296
  32.8 0.5 collective-permute-done.4.rest_3_
  33.3 1.0 %collective-permute-start.5 = (bf16[10,128,128]{2,1,0:T(8,128)(2,1)}, bf16[10,128,128]{2,1,0:T(8,128)(2,1)}, u32[]{:S(2)}, u32[]{:S(2)}) collective-permute-start(bf16[10,128,128]{2,1,0:T(8,128)(2,1)} %collective-permute-done.4.rest_3_), channel_id=1, source_target_pairs={{0,16},{8,120},{16,32},{24,8},{32,48},{40,24},{48,64},{56,40},{64,... | collective-permute-start | bytes 983048 | tf_op jit(solution)/shard_map/ppermute | solution.py:296
  34.3 1.2 %collective-permute-start.8 = (bf16[10,128,128]{2,1,0:T(8,128)(2,1)S(1)}, bf16[10,128,128]{2,1,0:T(8,128)(2,1)}, u32[]{:S(2)}, u32[]{:S(2)}) collective-permute-start(bf16[10,128,128]{2,1,0:T(8,128)(2,1)S(1)} %collective-permute-done.1.rest_2_), channel_id=1, source_target_pairs={{0,8},{8,0},{1,9},{9,1},{2,10},{10,2},{3,11},{11,3},{4,12},{12,4},... | collective-permute-start | bytes 983048 | tf_op jit(solution)/shard_map/ppermute | solution.py:288
  35.5 0.1 collective-permute-start.12
  35.6 5.7 %all-to-all-done.1.pulled = bf16[32,20,128]{2,1,0:T(8,128)(2,1)S(1)} async-done(((bf16[32,20,128]{2,1,0:T(8,128)(2,1)}), bf16[32,20,128]{2,1,0:T(8,128)(2,1)S(1)}, u32[]{:S(2)}, u32[]{:S(2)}) %all-to-all-start.1) | async-done | bytes 163872 | tf_op jit(solution)/shard_map/all_to_all | solution.py:285
  41.4 2.1 %shard_map.95 = bf16[32,32,128]{2,1,0:T(8,128)(2,1)} custom-call(f32[32,1,128]{2,1,0:T(1,128)S(1)} %all-to-all-done.notices, bf16[32,20,128]{2,1,0:T(8,128)(2,1)S(1)} %all-to-all-done.1.pulled, bf16[16,1,256,256]{3,2,1,0:T(8,128)(2,1)S(1)} %copy-done), custom_call_target="tpu_custom_call" | custom-call | tf_op jit(solution)/shard_map/pallas_call | solution.py:343
  43.5 3.9 %all-to-all-start.2 = ((bf16[32,32,128]{2,1,0:T(8,128)(2,1)}), bf16[32,32,128]{2,1,0:T(8,128)(2,1)S(1)}, u32[]{:S(2)}, u32[]{:S(2)}) async-start(bf16[32,32,128]{2,1,0:T(8,128)(2,1)} %shard_map.95), calls=%async_computation.2 | async-start | bytes 524288 | tf_op jit(solution)/shard_map/all_to_all | solution.py:285
  47.3 0.2 collective-permute-start.9
  47.6 0.3 collective-permute-start.13
  48.0 0.2 collective-permute-start.10
  48.1 1.7 %collective-permute-start.15 = (bf16[10,128,128]{2,1,0:T(8,128)(2,1)}, bf16[10,128,128]{2,1,0:T(8,128)(2,1)S(1)}, u32[]{:S(2)}, u32[]{:S(2)}) collective-permute-start(bf16[10,128,128]{2,1,0:T(8,128)(2,1)} %collective-permute-done.7.rest_7_), channel_id=1, source_target_pairs={{0,16},{8,120},{16,32},{24,8},{32,48},{40,24},{48,64},{56,40},{64,... | collective-permute-start | bytes 983048 | tf_op jit(solution)/shard_map/ppermute | solution.py:296
  49.8 1.5 %collective-permute-start.14 = (bf16[10,128,128]{2,1,0:T(8,128)(2,1)}, bf16[10,128,128]{2,1,0:T(8,128)(2,1)S(1)}, u32[]{:S(2)}, u32[]{:S(2)}) collective-permute-start(bf16[10,128,128]{2,1,0:T(8,128)(2,1)} %collective-permute-done.5.rest_4_), channel_id=1, source_target_pairs={{0,16},{8,120},{16,32},{24,8},{32,48},{40,24},{48,64},{56,40},{64,... | collective-permute-start | bytes 983048 | tf_op jit(solution)/shard_map/ppermute | solution.py:296
  51.3 2.5 %shard_map.93 = (s32[384]{0:T(512)S(1)}, f32[160]{0:T(256)S(1)}) custom-call(f32[32,1,128]{2,1,0:T(1,128)S(1)} %all-to-all-done.notices), custom_call_target="tpu_custom_call" | custom-call | tf_op jit(solution)/shard_map/pallas_call | solution.py:332
  53.8 6.7 %all-to-all-done.2.came = bf16[32,32,128]{2,1,0:T(8,128)(2,1)S(1)} async-done(((bf16[32,32,128]{2,1,0:T(8,128)(2,1)}), bf16[32,32,128]{2,1,0:T(8,128)(2,1)S(1)}, u32[]{:S(2)}, u32[]{:S(2)}) %all-to-all-start.2) | async-done | bytes 262176 | tf_op jit(solution)/shard_map/all_to_all | solution.py:285
  60.6 3.2 %shard_map.96 = (bf16[8,64,128]{2,1,0:T(8,128)(2,1)S(1)}, f32[40,64,128]{2,1,0:T(8,128)S(1)}) custom-call(s32[1]{0:T(128)} %bitcast.2.where, s32[384]{0:T(512)S(1)} %get-tuple-element.19.table, f32[160]{0:T(256)S(1)} %get-tuple-element.20.scales, bf16[32,32,128]{2,1,0:T(8,128)(2,1)S(1)} %all-to-all-done.2.came, ...), custom_call_target="tpu_custom_call" | custom-call | tf_op jit(solution)/shard_map/pallas_call | solution.py:351
  63.8 0.3 collective-permute-done.14.four
  64.0 1.0 %shard_map.97 = bf16[80,32,128]{2,1,0:T(8,128)(2,1)S(1)} custom-call(s32[384]{0:T(512)S(1)} %get-tuple-element.19.table, f32[160]{0:T(256)S(1)} %get-tuple-element.20.scales, bf16[8,64,128]{2,1,0:T(8,128)(2,1)S(1)} %get-tuple-element.25.rows, f32[40,64,128]{2,1,0:T(8,128)S(1)} %get-tuple-element.26.so_far, ...), custom_call_target="tpu_custom_call" | custom-call | tf_op jit(solution)/shard_map/pallas_call | solution.py:364
  65.0 17.6 %all_to_all.20 = bf16[80,32,128]{2,1,0:T(8,128)(2,1)S(1)} all-to-all(bf16[80,32,128]{2,1,0:T(8,128)(2,1)S(1)} %shard_map.97), channel_id=1, replica_groups=mesh['xl'=2,'z'=8,'core'=2,'y'=4,'xh'=2] {'xl','y','xh'}, dimensions={0} | all-to-all | bytes 1310720 | tf_op jit(solution)/shard_map/all_to_all | solution.py:285
  82.7 0.7 shard_map.98
  (19 shorter events, 0.0 us)
Async XLA Ops:
  0.0 22.6 %copy-start.1 = (bf16[10,128,128]{2,1,0:T(8,128)(2,1)S(1)}, bf16[10,128,128]{2,1,0:T(8,128)(2,1)}, u32[]{:S(2)}) copy-start(bf16[10,128,128]{2,1,0:T(8,128)(2,1)} %rest_0_.1) | copy-start | bytes 983044
  0.0 41.4 %copy-start = (bf16[16,1,256,256]{3,2,1,0:T(8,128)(2,1)S(1)}, bf16[16,1,256,256]{3,2,1,0:T(8,128)(2,1)}, u32[]{:S(2)}) copy-start(bf16[16,1,256,256]{3,2,1,0:T(8,128)(2,1)} %cache.3) | copy-start | bytes 6291460
  0.0 16.2 %collective-permute-start.1 = (bf16[10,128,128]{2,1,0:T(8,128)(2,1)}, bf16[10,128,128]{2,1,0:T(8,128)(2,1)S(1)}, u32[]{:S(2)}, u32[]{:S(2)}) collective-permute-start(bf16[10,128,128]{2,1,0:T(8,128)(2,1)} %rest_0_.1), channel_id=1, source_target_pairs={{0,16},{8,120},{16,32},{24,8},{32,48},{40,24},{48,64},{56,40},{64,... | collective-permute-start | bytes 983048 | tf_op jit(solution)/shard_map/ppermute | solution.py:296
  1.9 19.5 %collective-permute-start = (bf16[10,128,128]{2,1,0:T(8,128)(2,1)}, bf16[10,128,128]{2,1,0:T(8,128)(2,1)S(1)}, u32[]{:S(2)}, u32[]{:S(2)}) collective-permute-start(bf16[10,128,128]{2,1,0:T(8,128)(2,1)} %rest_0_.1), channel_id=1, source_target_pairs={{0,120},{8,16},{16,8},{24,32},{32,24},{40,48},{48,40},{56,64},{64,... | collective-permute-start | bytes 983048 | tf_op jit(solution)/shard_map/ppermute | solution.py:296
  7.6 13.9 %all-to-all-start = ((f32[32,1,128]{2,1,0:T(1,128)}), f32[32,1,128]{2,1,0:T(1,128)S(1)}, u32[]{:S(2)}, u32[]{:S(2)}) async-start(f32[32,1,128]{2,1,0:T(1,128)} %shard_map.91), calls=%async_computation | async-start | bytes 32768 | tf_op jit(solution)/shard_map/all_to_all | solution.py:285
  21.4 10.0 %collective-permute-start.6 = (bf16[10,128,128]{2,1,0:T(8,128)(2,1)S(1)}, bf16[10,128,128]{2,1,0:T(8,128)(2,1)}, u32[]{:S(2)}, u32[]{:S(2)}) collective-permute-start(bf16[10,128,128]{2,1,0:T(8,128)(2,1)S(1)} %collective-permute-done.rest_5_), channel_id=1, source_target_pairs={{0,16},{8,120},{16,32},{24,8},{32,48},{40,24},{48,64},{56,40},{64,... | collective-permute-start | bytes 983048 | tf_op jit(solution)/shard_map/ppermute | solution.py:296
  22.0 11.3 %collective-permute-start.4 = (bf16[10,128,128]{2,1,0:T(8,128)(2,1)S(1)}, bf16[10,128,128]{2,1,0:T(8,128)(2,1)}, u32[]{:S(2)}, u32[]{:S(2)}) collective-permute-start(bf16[10,128,128]{2,1,0:T(8,128)(2,1)S(1)} %collective-permute-done.1.rest_2_), channel_id=1, source_target_pairs={{0,16},{8,120},{16,32},{24,8},{32,48},{40,24},{48,64},{56,40},{64,... | collective-permute-start | bytes 983048 | tf_op jit(solution)/shard_map/ppermute | solution.py:296
  22.6 11.8 %collective-permute-start.3 = (bf16[10,128,128]{2,1,0:T(8,128)(2,1)S(1)}, bf16[10,128,128]{2,1,0:T(8,128)(2,1)}, u32[]{:S(2)}, u32[]{:S(2)}) collective-permute-start(bf16[10,128,128]{2,1,0:T(8,128)(2,1)S(1)} %copy-done.1), channel_id=1, source_target_pairs={{0,8},{8,0},{1,9},{9,1},{2,10},{10,2},{3,11},{11,3},{4,12},{12,4},... | collective-permute-start | bytes 983048 | tf_op jit(solution)/shard_map/ppermute | solution.py:288
  24.1 17.2 %all-to-all-start.1 = ((bf16[32,20,128]{2,1,0:T(8,128)(2,1)}), bf16[32,20,128]{2,1,0:T(8,128)(2,1)S(1)}, u32[]{:S(2)}, u32[]{:S(2)}) async-start(bf16[32,20,128]{2,1,0:T(8,128)(2,1)} %shard_map.94), calls=%async_computation.1 | async-start | bytes 393216 | tf_op jit(solution)/shard_map/all_to_all | solution.py:285
  29.5 6.1 %collective-permute-start.2 = (bf16[16,16,128]{2,1,0:T(8,128)(2,1)S(1)}, bf16[16,16,128]{2,1,0:T(8,128)(2,1)S(1)}, u32[]{:S(2)}, u32[]{:S(2)}) collective-permute-start(bf16[16,16,128]{2,1,0:T(8,128)(2,1)S(1)} %get-tuple-element.22.mine), channel_id=1, source_target_pairs={{0,128},{128,0},{1,129},{129,1},{2,130},{130,2},{3,131},{131,3},{4... | collective-permute-start | bytes 196616 | tf_op jit(solution)/shard_map/ppermute | solution.py:288
  31.4 16.0 %collective-permute-start.11 = (bf16[10,128,128]{2,1,0:T(8,128)(2,1)S(1)}, bf16[10,128,128]{2,1,0:T(8,128)(2,1)}, u32[]{:S(2)}, u32[]{:S(2)}) collective-permute-start(bf16[10,128,128]{2,1,0:T(8,128)(2,1)S(1)} %collective-permute-done.rest_5_), channel_id=1, source_target_pairs={{0,8},{8,0},{1,9},{9,1},{2,10},{10,2},{3,11},{11,3},{4,12},{12,4},... | collective-permute-start | bytes 983048 | tf_op jit(solution)/shard_map/ppermute | solution.py:288
  31.4 16.2 %collective-permute-start.7 = (bf16[10,128,128]{2,1,0:T(8,128)(2,1)}, bf16[10,128,128]{2,1,0:T(8,128)(2,1)}, u32[]{:S(2)}, u32[]{:S(2)}) collective-permute-start(bf16[10,128,128]{2,1,0:T(8,128)(2,1)} %collective-permute-done.6.rest_6_), channel_id=1, source_target_pairs={{0,16},{8,120},{16,32},{24,8},{32,48},{40,24},{48,64},{56,40},{64,... | collective-permute-start | bytes 983048 | tf_op jit(solution)/shard_map/ppermute | solution.py:296
  33.3 14.6 %collective-permute-start.5 = (bf16[10,128,128]{2,1,0:T(8,128)(2,1)}, bf16[10,128,128]{2,1,0:T(8,128)(2,1)}, u32[]{:S(2)}, u32[]{:S(2)}) collective-permute-start(bf16[10,128,128]{2,1,0:T(8,128)(2,1)} %collective-permute-done.4.rest_3_), channel_id=1, source_target_pairs={{0,16},{8,120},{16,32},{24,8},{32,48},{40,24},{48,64},{56,40},{64,... | collective-permute-start | bytes 983048 | tf_op jit(solution)/shard_map/ppermute | solution.py:296
  34.3 13.8 %collective-permute-start.8 = (bf16[10,128,128]{2,1,0:T(8,128)(2,1)S(1)}, bf16[10,128,128]{2,1,0:T(8,128)(2,1)}, u32[]{:S(2)}, u32[]{:S(2)}) collective-permute-start(bf16[10,128,128]{2,1,0:T(8,128)(2,1)S(1)} %collective-permute-done.1.rest_2_), channel_id=1, source_target_pairs={{0,8},{8,0},{1,9},{9,1},{2,10},{10,2},{3,11},{11,3},{4,12},{12,4},... | collective-permute-start | bytes 983048 | tf_op jit(solution)/shard_map/ppermute | solution.py:288
  35.5 14.3 %collective-permute-start.12 = (bf16[10,128,128]{2,1,0:T(8,128)(2,1)}, bf16[10,128,128]{2,1,0:T(8,128)(2,1)}, u32[]{:S(2)}, u32[]{:S(2)}) collective-permute-start(bf16[10,128,128]{2,1,0:T(8,128)(2,1)} %collective-permute-done.6.rest_6_), channel_id=1, source_target_pairs={{0,8},{8,0},{1,9},{9,1},{2,10},{10,2},{3,11},{11,3},{4,12},{12,4},... | collective-permute-start | bytes 983048 | tf_op jit(solution)/shard_map/ppermute | solution.py:288
  43.5 17.1 %all-to-all-start.2 = ((bf16[32,32,128]{2,1,0:T(8,128)(2,1)}), bf16[32,32,128]{2,1,0:T(8,128)(2,1)S(1)}, u32[]{:S(2)}, u32[]{:S(2)}) async-start(bf16[32,32,128]{2,1,0:T(8,128)(2,1)} %shard_map.95), calls=%async_computation.2 | async-start | bytes 524288 | tf_op jit(solution)/shard_map/all_to_all | solution.py:285
  47.3 6.5 %collective-permute-start.9 = (bf16[10,128,128]{2,1,0:T(8,128)(2,1)}, bf16[10,128,128]{2,1,0:T(8,128)(2,1)S(1)}, u32[]{:S(2)}, u32[]{:S(2)}) collective-permute-start(bf16[10,128,128]{2,1,0:T(8,128)(2,1)} %collective-permute-done.4.rest_3_), channel_id=1, source_target_pairs={{0,8},{8,0},{1,9},{9,1},{2,10},{10,2},{3,11},{11,3},{4,12},{12,4},... | collective-permute-start | bytes 983048 | tf_op jit(solution)/shard_map/ppermute | solution.py:288
  47.6 12.9 %collective-permute-start.13 = (bf16[10,128,128]{2,1,0:T(8,128)(2,1)}, bf16[10,128,128]{2,1,0:T(8,128)(2,1)S(1)}, u32[]{:S(2)}, u32[]{:S(2)}) collective-permute-start(bf16[10,128,128]{2,1,0:T(8,128)(2,1)} %collective-permute-done.7.rest_7_), channel_id=1, source_target_pairs={{0,8},{8,0},{1,9},{9,1},{2,10},{10,2},{3,11},{11,3},{4,12},{12,4},... | collective-permute-start | bytes 983048 | tf_op jit(solution)/shard_map/ppermute | solution.py:288
  48.0 12.6 %collective-permute-start.10 = (bf16[10,128,128]{2,1,0:T(8,128)(2,1)}, bf16[10,128,128]{2,1,0:T(8,128)(2,1)S(1)}, u32[]{:S(2)}, u32[]{:S(2)}) collective-permute-start(bf16[10,128,128]{2,1,0:T(8,128)(2,1)} %collective-permute-done.5.rest_4_), channel_id=1, source_target_pairs={{0,8},{8,0},{1,9},{9,1},{2,10},{10,2},{3,11},{11,3},{4,12},{12,4},... | collective-permute-start | bytes 983048 | tf_op jit(solution)/shard_map/ppermute | solution.py:288
  48.1 15.6 %collective-permute-start.15 = (bf16[10,128,128]{2,1,0:T(8,128)(2,1)}, bf16[10,128,128]{2,1,0:T(8,128)(2,1)S(1)}, u32[]{:S(2)}, u32[]{:S(2)}) collective-permute-start(bf16[10,128,128]{2,1,0:T(8,128)(2,1)} %collective-permute-done.7.rest_7_), channel_id=1, source_target_pairs={{0,16},{8,120},{16,32},{24,8},{32,48},{40,24},{48,64},{56,40},{64,... | collective-permute-start | bytes 983048 | tf_op jit(solution)/shard_map/ppermute | solution.py:296
  49.8 14.3 %collective-permute-start.14 = (bf16[10,128,128]{2,1,0:T(8,128)(2,1)}, bf16[10,128,128]{2,1,0:T(8,128)(2,1)S(1)}, u32[]{:S(2)}, u32[]{:S(2)}) collective-permute-start(bf16[10,128,128]{2,1,0:T(8,128)(2,1)} %collective-permute-done.5.rest_4_), channel_id=1, source_target_pairs={{0,16},{8,120},{16,32},{24,8},{32,48},{40,24},{48,64},{56,40},{64,... | collective-permute-start | bytes 983048 | tf_op jit(solution)/shard_map/ppermute | solution.py:296

commit v12 on v10

--- a/solution.py
+++ b/solution.py
@@ -340,6 +340,7 @@
         pull_body, jax.ShapeDtypeStruct((REP, PACK, HD), BF16), [smem(), vmem()]
     )(notices, packs)
     pulled = exchange(to_pull, rep_axes)
+    other, pulled = lax.optimization_barrier((other, pulled))
     three, three_x = around(two), around(two_x)
     send = call(
         attend_body,
@@ -348,7 +349,8 @@
         [pltpu.VMEM((MOVE, per, CTX), F32)],
     )(notices, pulled, kv_cache)
     came = exchange(send, rep_axes)
-    four, four_x = around(three), around(three_x)
+    four = around(three)
+    four_x = swap(four, "core")
     rows, total = call(
         project_body,
         [
@@ -357,6 +359,7 @@
         ],
         [smem()] * 3 + [vmem()] * 17,
         [pltpu.VMEM((XL * SLOTS * per, HD), F32)],
+        cost_estimate=pl.CostEstimate(flops=5000000000, bytes_accessed=15000000, transcendentals=0),
     )(
         *(xl[None], table, factors, came, stays, other),
         *(codes, sib, near, two, three, near_x, two_x, three_x),

time: 82.9 us -> 85 us (1.025)
  blocking collectives: 17.6 us -> 19.3 us
    all_to_all x3, waiting for transfers between devices: 15.8 us -> 5.82 us  [exchange(): return lax.all_to_all(x, axes, split_axis=0, concat_axis=0, tiled=True)]
    ppermute x8 -> x7, waiting for transfers between devices: 0.29 us -> 6.84 us  [around(): return lax.ppermute(x, ('z', 'core'), pairs)]
    ppermute x8 -> x9, waiting for transfers between devices: 0.02 us -> 4.07 us  [swap(): return lax.ppermute(x, axis, [(0, 1), (1, 0)])]
    ppermute x8 -> x7, starting transfers between devices: 12.6 us -> 10.9 us  [around(): return lax.ppermute(x, ('z', 'core'), pairs)]
    all_to_all x1, blocking collectives: 17.6 us -> 19.3 us  [exchange(): return lax.all_to_all(x, axes, split_axis=0, concat_axis=0, tiled=True)]
    ppermute x8 -> x9, starting transfers between devices: 3.86 us -> 4.71 us  [swap(): return lax.ppermute(x, axis, [(0, 1), (1, 0)])]
where the time goes in v12:
time: 85 us; the launch traced here: 83.5 us
  starting transfers between devices  31.8 us (37%)
  blocking collectives  19.3 us (23%)
  waiting for transfers between devices  16.7 us (20%)
  Pallas kernels  15.6 us (18%)
    all_to_all x1, blocking collectives, exchange(): return lax.all_to_all(x, axes, split_axis=0, concat_axis=0, tiled=True)  19.3 us
    all_to_all x3, starting transfers between devices, exchange(): return lax.all_to_all(x, axes, split_axis=0, concat_axis=0, tiled=True)  16.2 us
    ppermute x7, starting transfers between devices, around(): return lax.ppermute(x, ('z', 'core'), pairs)  10.9 us
    ppermute x7, waiting for transfers between devices, around(): return lax.ppermute(x, ('z', 'core'), pairs)  6.84 us
    all_to_all x3, waiting for transfers between devices, exchange(): return lax.all_to_all(x, axes, split_axis=0, concat_axis=0, tiled=True)  5.82 us
    ppermute x9, starting transfers between devices, swap(): return lax.ppermute(x, axis, [(0, 1), (1, 0)])  4.71 us
    ppermute x9, waiting for transfers between devices, swap(): return lax.ppermute(x, axis, [(0, 1), (1, 0)])  4.07 us
    pallas_call x1, Pallas kernels, shards(): call(project_body, [jax.ShapeDtypeStruct((HEADS, XL * ROWS, HD), BF16), j...  3.1 us
  transfers between devices with their start and end apart: 19, of which 4 were waited for; matrix products, arithmetic and copies ran while one was open for 0% of the time, Pallas kernels for 17%

profile of v12, /device:TPU:8, one launch (start us, length us, event | category | flops | bytes accessed | tf_op | source)
XLA Modules:
  0.0 83.5 jit_solution(11040854949866026114)
XLA Ops:
  0.0 0.0 collective-permute-start
  0.0 2.0 %collective-permute-start.2 = (bf16[10,128,128]{2,1,0:T(8,128)(2,1)}, bf16[10,128,128]{2,1,0:T(8,128)(2,1)S(1)}, u32[]{:S(2)}, u32[]{:S(2)}) collective-permute-start(bf16[10,128,128]{2,1,0:T(8,128)(2,1)} %rest_0_.1), channel_id=1, source_target_pairs={{0,16},{8,120},{16,32},{24,8},{32,48},{40,24},{48,64},{56,40},{64,... | collective-permute-start | bytes 983048 | tf_op jit(solution)/shard_map/ppermute | solution.py:296
  2.0 1.5 %shard_map.91 = f32[32,1,128]{2,1,0:T(1,128)} custom-call(s32[1]{0:T(128)} %bitcast.place, s32[1,13]{1,0:T(1,128)} %dep_in.1, s32[1,13]{1,0:T(1,128)} %refs_1_.1, s32[16]{0:T(128)} %lengths_in.1, s32[10]{0:T(128)} %refs_3_.1, f32[10]{0:T(128)} %refs_4_.1), custom_call_target="tpu_custom_call" | custom-call | tf_op jit(solution)/shard_map/pallas_call | solution.py:300
  3.5 0.0 collective-permute-done.rest_1_
  3.5 2.0 %collective-permute-start.1 = (bf16[10,128,128]{2,1,0:T(8,128)(2,1)S(1)}, bf16[10,128,128]{2,1,0:T(8,128)(2,1)}, u32[]{:S(2)}, u32[]{:S(2)}) collective-permute-start(bf16[10,128,128]{2,1,0:T(8,128)(2,1)S(1)} %collective-permute-done.rest_1_), channel_id=1, source_target_pairs={{0,16},{8,120},{16,32},{24,8},{32,48},{40,24},{48,64},{56,40},{64,... | collective-permute-start | bytes 983048 | tf_op jit(solution)/shard_map/ppermute | solution.py:296
  5.5 8.0 %all-to-all-start = ((f32[32,1,128]{2,1,0:T(1,128)}), f32[32,1,128]{2,1,0:T(1,128)S(1)}, u32[]{:S(2)}, u32[]{:S(2)}) async-start(f32[32,1,128]{2,1,0:T(1,128)} %shard_map.91), calls=%async_computation | async-start | bytes 32768 | tf_op jit(solution)/shard_map/all_to_all | solution.py:285
  13.5 3.1 %shard_map.93 = (bf16[16,16,128]{2,1,0:T(8,128)(2,1)S(1)}, bf16[13,20,128]{2,1,0:T(8,128)(2,1)S(1)}) custom-call(s32[1,13]{1,0:T(1,128)} %dep_in.1, s32[16]{0:T(128)} %lengths_in.1, bf16[2,16,8,128]{3,2,1,0:T(8,128)(2,1)} %q_in.1, bf16[2,16,256]{2,1,0:T(8,128)(2,1)} %bitcast.5, bf16[16,1,256,256]{3,2,1,0:T(8,128)(2,1)} %cache.3), custom_call_target="tpu_custom_call" | custom-call | tf_op jit(solution)/shard_map/pallas_call | solution.py:311
  16.6 0.0 copy-start.1
  16.6 1.9 %collective-permute-start.4 = (bf16[10,128,128]{2,1,0:T(8,128)(2,1)S(1)}, bf16[10,128,128]{2,1,0:T(8,128)(2,1)}, u32[]{:S(2)}, u32[]{:S(2)}) collective-permute-start(bf16[10,128,128]{2,1,0:T(8,128)(2,1)S(1)} %collective-permute-done.2.rest_2_), channel_id=1, source_target_pairs={{0,16},{8,120},{16,32},{24,8},{32,48},{40,24},{48,64},{56,40},{64,... | collective-permute-start | bytes 983048 | tf_op jit(solution)/shard_map/ppermute | solution.py:296
  18.5 3.3 %all-to-all-done.notices = f32[32,1,128]{2,1,0:T(1,128)S(1)} async-done(((f32[32,1,128]{2,1,0:T(1,128)}), f32[32,1,128]{2,1,0:T(1,128)S(1)}, u32[]{:S(2)}, u32[]{:S(2)}) %all-to-all-start) | async-done | bytes 16416 | tf_op jit(solution)/shard_map/all_to_all | solution.py:285
  21.8 0.6 collective-permute-start.6
  22.4 1.6 %shard_map.94 = bf16[32,20,128]{2,1,0:T(8,128)(2,1)} custom-call(f32[32,1,128]{2,1,0:T(1,128)S(1)} %all-to-all-done.notices, bf16[13,20,128]{2,1,0:T(8,128)(2,1)S(1)} %get-tuple-element.26.packs), custom_call_target="tpu_custom_call" | custom-call | tf_op jit(solution)/shard_map/pallas_call | solution.py:339
  24.0 4.3 %all-to-all-start.1 = ((bf16[32,20,128]{2,1,0:T(8,128)(2,1)}), bf16[32,20,128]{2,1,0:T(8,128)(2,1)S(1)}, u32[]{:S(2)}, u32[]{:S(2)}) async-start(bf16[32,20,128]{2,1,0:T(8,128)(2,1)} %shard_map.94), calls=%async_computation.1 | async-start | bytes 393216 | tf_op jit(solution)/shard_map/all_to_all | solution.py:285
  28.3 1.9 %collective-permute-start.5 = (bf16[10,128,128]{2,1,0:T(8,128)(2,1)}, bf16[10,128,128]{2,1,0:T(8,128)(2,1)}, u32[]{:S(2)}, u32[]{:S(2)}) collective-permute-start(bf16[10,128,128]{2,1,0:T(8,128)(2,1)} %collective-permute-done.4.rest_3_), channel_id=1, source_target_pairs={{0,16},{8,120},{16,32},{24,8},{32,48},{40,24},{48,64},{56,40},{64,... | collective-permute-start | bytes 983048 | tf_op jit(solution)/shard_map/ppermute | solution.py:296
  30.2 1.1 %collective-permute-start.8 = (bf16[10,128,128]{2,1,0:T(8,128)(2,1)S(1)}, bf16[10,128,128]{2,1,0:T(8,128)(2,1)}, u32[]{:S(2)}, u32[]{:S(2)}) collective-permute-start(bf16[10,128,128]{2,1,0:T(8,128)(2,1)S(1)} %collective-permute-done.2.rest_2_), channel_id=1, source_target_pairs={{0,8},{8,0},{1,9},{9,1},{2,10},{10,2},{3,11},{11,3},{4,12},{12,4},... | collective-permute-start | bytes 983048 | tf_op jit(solution)/shard_map/ppermute | solution.py:288
  31.3 0.9 %collective-permute-start.7 = (bf16[10,128,128]{2,1,0:T(8,128)(2,1)}, bf16[10,128,128]{2,1,0:T(8,128)(2,1)}, u32[]{:S(2)}, u32[]{:S(2)}) collective-permute-start(bf16[10,128,128]{2,1,0:T(8,128)(2,1)} %collective-permute-done.6.rest_6_), channel_id=1, source_target_pairs={{0,16},{8,120},{16,32},{24,8},{32,48},{40,24},{48,64},{56,40},{64,... | collective-permute-start | bytes 983048 | tf_op jit(solution)/shard_map/ppermute | solution.py:296
  32.2 1.5 %collective-permute-start.3 = (bf16[16,16,128]{2,1,0:T(8,128)(2,1)S(1)}, bf16[16,16,128]{2,1,0:T(8,128)(2,1)S(1)}, u32[]{:S(2)}, u32[]{:S(2)}) collective-permute-start(bf16[16,16,128]{2,1,0:T(8,128)(2,1)S(1)} %get-tuple-element.25.mine), channel_id=1, source_target_pairs={{0,128},{128,0},{1,129},{129,1},{2,130},{130,2},{3,131},{131,3},{4... | collective-permute-start | bytes 196616 | tf_op jit(solution)/shard_map/ppermute | solution.py:288
  33.7 4.0 %collective-permute-done.3.other = bf16[16,16,128]{2,1,0:T(8,128)(2,1)S(1)} collective-permute-done((bf16[16,16,128]{2,1,0:T(8,128)(2,1)S(1)}, bf16[16,16,128]{2,1,0:T(8,128)(2,1)S(1)}, u32[]{:S(2)}, u32[]{:S(2)}) %collective-permute-start.3) | collective-permute-done | bytes 65568 | tf_op jit(solution)/shard_map/ppermute | solution.py:288
  37.7 2.5 %all-to-all-done.1.pulled = bf16[32,20,128]{2,1,0:T(8,128)(2,1)S(1)} async-done(((bf16[32,20,128]{2,1,0:T(8,128)(2,1)}), bf16[32,20,128]{2,1,0:T(8,128)(2,1)S(1)}, u32[]{:S(2)}, u32[]{:S(2)}) %all-to-all-start.1) | async-done | bytes 163872 | tf_op jit(solution)/shard_map/all_to_all | solution.py:285
  40.2 2.1 %shard_map.95 = bf16[32,32,128]{2,1,0:T(8,128)(2,1)} custom-call(f32[32,1,128]{2,1,0:T(1,128)S(1)} %all-to-all-done.notices, bf16[32,20,128]{2,1,0:T(8,128)(2,1)S(1)} %all-to-all-done.1.pulled, bf16[16,1,256,256]{3,2,1,0:T(8,128)(2,1)S(1)} %copy-done), custom_call_target="tpu_custom_call" | custom-call | tf_op jit(solution)/shard_map/pallas_call | solution.py:345
  42.3 3.9 %all-to-all-start.2 = ((bf16[32,32,128]{2,1,0:T(8,128)(2,1)}), bf16[32,32,128]{2,1,0:T(8,128)(2,1)S(1)}, u32[]{:S(2)}, u32[]{:S(2)}) async-start(bf16[32,32,128]{2,1,0:T(8,128)(2,1)} %shard_map.95), calls=%async_computation.2 | async-start | bytes 524288 | tf_op jit(solution)/shard_map/all_to_all | solution.py:285
  46.2 0.2 collective-permute-start.9
  46.4 1.7 %collective-permute-start.14 = (bf16[10,128,128]{2,1,0:T(8,128)(2,1)}, bf16[10,128,128]{2,1,0:T(8,128)(2,1)S(1)}, u32[]{:S(2)}, u32[]{:S(2)}) collective-permute-start(bf16[10,128,128]{2,1,0:T(8,128)(2,1)} %collective-permute-done.5.rest_4_), channel_id=1, source_target_pairs={{0,16},{8,120},{16,32},{24,8},{32,48},{40,24},{48,64},{56,40},{64,... | collective-permute-start | bytes 983048 | tf_op jit(solution)/shard_map/ppermute | solution.py:296
  48.1 1.4 %collective-permute-start.12 = (bf16[10,128,128]{2,1,0:T(8,128)(2,1)}, bf16[10,128,128]{2,1,0:T(8,128)(2,1)S(1)}, u32[]{:S(2)}, u32[]{:S(2)}) collective-permute-start(bf16[10,128,128]{2,1,0:T(8,128)(2,1)} %collective-permute-done.6.rest_6_), channel_id=1, source_target_pairs={{0,8},{8,0},{1,9},{9,1},{2,10},{10,2},{3,11},{11,3},{4,12},{12,4},... | collective-permute-start | bytes 983048 | tf_op jit(solution)/shard_map/ppermute | solution.py:288
  49.5 0.1 collective-permute-start.10
  49.6 0.4 collective-permute-start.13
  50.0 2.5 %shard_map.92 = (s32[384]{0:T(512)S(1)}, f32[160]{0:T(256)S(1)}) custom-call(f32[32,1,128]{2,1,0:T(1,128)S(1)} %all-to-all-done.notices), custom_call_target="tpu_custom_call" | custom-call | tf_op jit(solution)/shard_map/pallas_call | solution.py:333
  52.6 6.8 %collective-permute-done.14.four = bf16[10,128,128]{2,1,0:T(8,128)(2,1)S(1)} collective-permute-done((bf16[10,128,128]{2,1,0:T(8,128)(2,1)}, bf16[10,128,128]{2,1,0:T(8,128)(2,1)S(1)}, u32[]{:S(2)}, u32[]{:S(2)}) %collective-permute-start.14) | collective-permute-done | bytes 327712 | tf_op jit(solution)/shard_map/ppermute | solution.py:296
  59.4 3.1 %shard_map.96 = (bf16[8,64,128]{2,1,0:T(8,128)(2,1)S(1)}, f32[40,64,128]{2,1,0:T(8,128)S(1)}) custom-call(s32[1]{0:T(128)} %bitcast.1.where, s32[384]{0:T(512)S(1)} %get-tuple-element.22.table, f32[160]{0:T(256)S(1)} %get-tuple-element.23.scales, bf16[32,32,128]{2,1,0:T(8,128)(2,1)S(1)} %all-to-all-done.2.came, ...), custom_call_target="tpu_custom_call" | custom-call | flops 5000000000 | bytes 15000000 | tf_op jit(solution)/shard_map/pallas_call | solution.py:354
  62.5 1.0 %shard_map.97 = bf16[80,32,128]{2,1,0:T(8,128)(2,1)S(1)} custom-call(s32[384]{0:T(512)S(1)} %get-tuple-element.22.table, f32[160]{0:T(256)S(1)} %get-tuple-element.23.scales, bf16[8,64,128]{2,1,0:T(8,128)(2,1)S(1)} %get-tuple-element.31.rows, f32[40,64,128]{2,1,0:T(8,128)S(1)} %get-tuple-element.32.so_far, ...), custom_call_target="tpu_custom_call" | custom-call | tf_op jit(solution)/shard_map/pallas_call | solution.py:368
  63.5 19.3 %all_to_all.20 = bf16[80,32,128]{2,1,0:T(8,128)(2,1)S(1)} all-to-all(bf16[80,32,128]{2,1,0:T(8,128)(2,1)S(1)} %shard_map.97), channel_id=1, replica_groups=mesh['xl'=2,'z'=8,'core'=2,'y'=4,'xh'=2] {'xl','y','xh'}, dimensions={0} | all-to-all | bytes 1310720 | tf_op jit(solution)/shard_map/all_to_all | solution.py:285
  82.8 0.7 shard_map.98
  (19 shorter events, 0.0 us)
Async XLA Ops:
  0.0 40.2 %copy-start = (bf16[16,1,256,256]{3,2,1,0:T(8,128)(2,1)S(1)}, bf16[16,1,256,256]{3,2,1,0:T(8,128)(2,1)}, u32[]{:S(2)}) copy-start(bf16[16,1,256,256]{3,2,1,0:T(8,128)(2,1)} %cache.3) | copy-start | bytes 6291460
  0.0 3.5 %collective-permute-start = (bf16[10,128,128]{2,1,0:T(8,128)(2,1)}, bf16[10,128,128]{2,1,0:T(8,128)(2,1)S(1)}, u32[]{:S(2)}, u32[]{:S(2)}) collective-permute-start(bf16[10,128,128]{2,1,0:T(8,128)(2,1)} %rest_0_.1), channel_id=1, source_target_pairs={{0,8},{8,0},{1,9},{9,1},{2,10},{10,2},{3,11},{11,3},{4,12},{12,4},... | collective-permute-start | bytes 983048 | tf_op jit(solution)/shard_map/ppermute | solution.py:288
  0.0 16.6 %collective-permute-start.2 = (bf16[10,128,128]{2,1,0:T(8,128)(2,1)}, bf16[10,128,128]{2,1,0:T(8,128)(2,1)S(1)}, u32[]{:S(2)}, u32[]{:S(2)}) collective-permute-start(bf16[10,128,128]{2,1,0:T(8,128)(2,1)} %rest_0_.1), channel_id=1, source_target_pairs={{0,16},{8,120},{16,32},{24,8},{32,48},{40,24},{48,64},{56,40},{64,... | collective-permute-start | bytes 983048 | tf_op jit(solution)/shard_map/ppermute | solution.py:296
  3.5 18.3 %collective-permute-start.1 = (bf16[10,128,128]{2,1,0:T(8,128)(2,1)S(1)}, bf16[10,128,128]{2,1,0:T(8,128)(2,1)}, u32[]{:S(2)}, u32[]{:S(2)}) collective-permute-start(bf16[10,128,128]{2,1,0:T(8,128)(2,1)S(1)} %collective-permute-done.rest_1_), channel_id=1, source_target_pairs={{0,16},{8,120},{16,32},{24,8},{32,48},{40,24},{48,64},{56,40},{64,... | collective-permute-start | bytes 983048 | tf_op jit(solution)/shard_map/ppermute | solution.py:296
  5.5 16.3 %all-to-all-start = ((f32[32,1,128]{2,1,0:T(1,128)}), f32[32,1,128]{2,1,0:T(1,128)S(1)}, u32[]{:S(2)}, u32[]{:S(2)}) async-start(f32[32,1,128]{2,1,0:T(1,128)} %shard_map.91), calls=%async_computation | async-start | bytes 32768 | tf_op jit(solution)/shard_map/all_to_all | solution.py:285
  16.6 42.8 %copy-start.1 = (bf16[10,128,128]{2,1,0:T(8,128)(2,1)S(1)}, bf16[10,128,128]{2,1,0:T(8,128)(2,1)}, u32[]{:S(2)}) copy-start(bf16[10,128,128]{2,1,0:T(8,128)(2,1)} %rest_0_.1) | copy-start | bytes 983044
  16.6 11.7 %collective-permute-start.4 = (bf16[10,128,128]{2,1,0:T(8,128)(2,1)S(1)}, bf16[10,128,128]{2,1,0:T(8,128)(2,1)}, u32[]{:S(2)}, u32[]{:S(2)}) collective-permute-start(bf16[10,128,128]{2,1,0:T(8,128)(2,1)S(1)} %collective-permute-done.2.rest_2_), channel_id=1, source_target_pairs={{0,16},{8,120},{16,32},{24,8},{32,48},{40,24},{48,64},{56,40},{64,... | collective-permute-start | bytes 983048 | tf_op jit(solution)/shard_map/ppermute | solution.py:296
  21.8 9.5 %collective-permute-start.6 = (bf16[10,128,128]{2,1,0:T(8,128)(2,1)}, bf16[10,128,128]{2,1,0:T(8,128)(2,1)}, u32[]{:S(2)}, u32[]{:S(2)}) collective-permute-start(bf16[10,128,128]{2,1,0:T(8,128)(2,1)} %collective-permute-done.1.rest_5_), channel_id=1, source_target_pairs={{0,16},{8,120},{16,32},{24,8},{32,48},{40,24},{48,64},{56,40},{64,... | collective-permute-start | bytes 983048 | tf_op jit(solution)/shard_map/ppermute | solution.py:296
  24.0 16.2 %all-to-all-start.1 = ((bf16[32,20,128]{2,1,0:T(8,128)(2,1)}), bf16[32,20,128]{2,1,0:T(8,128)(2,1)S(1)}, u32[]{:S(2)}, u32[]{:S(2)}) async-start(bf16[32,20,128]{2,1,0:T(8,128)(2,1)} %shard_map.94), calls=%async_computation.1 | async-start | bytes 393216 | tf_op jit(solution)/shard_map/all_to_all | solution.py:285
  28.3 18.1 %collective-permute-start.5 = (bf16[10,128,128]{2,1,0:T(8,128)(2,1)}, bf16[10,128,128]{2,1,0:T(8,128)(2,1)}, u32[]{:S(2)}, u32[]{:S(2)}) collective-permute-start(bf16[10,128,128]{2,1,0:T(8,128)(2,1)} %collective-permute-done.4.rest_3_), channel_id=1, source_target_pairs={{0,16},{8,120},{16,32},{24,8},{32,48},{40,24},{48,64},{56,40},{64,... | collective-permute-start | bytes 983048 | tf_op jit(solution)/shard_map/ppermute | solution.py:296
  30.2 17.9 %collective-permute-start.8 = (bf16[10,128,128]{2,1,0:T(8,128)(2,1)S(1)}, bf16[10,128,128]{2,1,0:T(8,128)(2,1)}, u32[]{:S(2)}, u32[]{:S(2)}) collective-permute-start(bf16[10,128,128]{2,1,0:T(8,128)(2,1)S(1)} %collective-permute-done.2.rest_2_), channel_id=1, source_target_pairs={{0,8},{8,0},{1,9},{9,1},{2,10},{10,2},{3,11},{11,3},{4,12},{12,4},... | collective-permute-start | bytes 983048 | tf_op jit(solution)/shard_map/ppermute | solution.py:288
  31.3 18.2 %collective-permute-start.11 = (bf16[10,128,128]{2,1,0:T(8,128)(2,1)}, bf16[10,128,128]{2,1,0:T(8,128)(2,1)}, u32[]{:S(2)}, u32[]{:S(2)}) collective-permute-start(bf16[10,128,128]{2,1,0:T(8,128)(2,1)} %collective-permute-done.1.rest_5_), channel_id=1, source_target_pairs={{0,8},{8,0},{1,9},{9,1},{2,10},{10,2},{3,11},{11,3},{4,12},{12,4},... | collective-permute-start | bytes 983048 | tf_op jit(solution)/shard_map/ppermute | solution.py:288
  31.3 18.3 %collective-permute-start.7 = (bf16[10,128,128]{2,1,0:T(8,128)(2,1)}, bf16[10,128,128]{2,1,0:T(8,128)(2,1)}, u32[]{:S(2)}, u32[]{:S(2)}) collective-permute-start(bf16[10,128,128]{2,1,0:T(8,128)(2,1)} %collective-permute-done.6.rest_6_), channel_id=1, source_target_pairs={{0,16},{8,120},{16,32},{24,8},{32,48},{40,24},{48,64},{56,40},{64,... | collective-permute-start | bytes 983048 | tf_op jit(solution)/shard_map/ppermute | solution.py:296
  32.2 5.5 %collective-permute-start.3 = (bf16[16,16,128]{2,1,0:T(8,128)(2,1)S(1)}, bf16[16,16,128]{2,1,0:T(8,128)(2,1)S(1)}, u32[]{:S(2)}, u32[]{:S(2)}) collective-permute-start(bf16[16,16,128]{2,1,0:T(8,128)(2,1)S(1)} %get-tuple-element.25.mine), channel_id=1, source_target_pairs={{0,128},{128,0},{1,129},{129,1},{2,130},{130,2},{3,131},{131,3},{4... | collective-permute-start | bytes 196616 | tf_op jit(solution)/shard_map/ppermute | solution.py:288
  42.3 17.1 %all-to-all-start.2 = ((bf16[32,32,128]{2,1,0:T(8,128)(2,1)}), bf16[32,32,128]{2,1,0:T(8,128)(2,1)S(1)}, u32[]{:S(2)}, u32[]{:S(2)}) async-start(bf16[32,32,128]{2,1,0:T(8,128)(2,1)} %shard_map.95), calls=%async_computation.2 | async-start | bytes 524288 | tf_op jit(solution)/shard_map/all_to_all | solution.py:285
  46.2 13.2 %collective-permute-start.9 = (bf16[10,128,128]{2,1,0:T(8,128)(2,1)}, bf16[10,128,128]{2,1,0:T(8,128)(2,1)S(1)}, u32[]{:S(2)}, u32[]{:S(2)}) collective-permute-start(bf16[10,128,128]{2,1,0:T(8,128)(2,1)} %collective-permute-done.4.rest_3_), channel_id=1, source_target_pairs={{0,8},{8,0},{1,9},{9,1},{2,10},{10,2},{3,11},{11,3},{4,12},{12,4},... | collective-permute-start | bytes 983048 | tf_op jit(solution)/shard_map/ppermute | solution.py:288
  46.4 12.9 %collective-permute-start.14 = (bf16[10,128,128]{2,1,0:T(8,128)(2,1)}, bf16[10,128,128]{2,1,0:T(8,128)(2,1)S(1)}, u32[]{:S(2)}, u32[]{:S(2)}) collective-permute-start(bf16[10,128,128]{2,1,0:T(8,128)(2,1)} %collective-permute-done.5.rest_4_), channel_id=1, source_target_pairs={{0,16},{8,120},{16,32},{24,8},{32,48},{40,24},{48,64},{56,40},{64,... | collective-permute-start | bytes 983048 | tf_op jit(solution)/shard_map/ppermute | solution.py:296
  48.1 11.3 %collective-permute-start.12 = (bf16[10,128,128]{2,1,0:T(8,128)(2,1)}, bf16[10,128,128]{2,1,0:T(8,128)(2,1)S(1)}, u32[]{:S(2)}, u32[]{:S(2)}) collective-permute-start(bf16[10,128,128]{2,1,0:T(8,128)(2,1)} %collective-permute-done.6.rest_6_), channel_id=1, source_target_pairs={{0,8},{8,0},{1,9},{9,1},{2,10},{10,2},{3,11},{11,3},{4,12},{12,4},... | collective-permute-start | bytes 983048 | tf_op jit(solution)/shard_map/ppermute | solution.py:288
  49.5 9.9 %collective-permute-start.10 = (bf16[10,128,128]{2,1,0:T(8,128)(2,1)}, bf16[10,128,128]{2,1,0:T(8,128)(2,1)S(1)}, u32[]{:S(2)}, u32[]{:S(2)}) collective-permute-start(bf16[10,128,128]{2,1,0:T(8,128)(2,1)} %collective-permute-done.5.rest_4_), channel_id=1, source_target_pairs={{0,8},{8,0},{1,9},{9,1},{2,10},{10,2},{3,11},{11,3},{4,12},{12,4},... | collective-permute-start | bytes 983048 | tf_op jit(solution)/shard_map/ppermute | solution.py:288
  49.6 9.8 %collective-permute-start.13 = (bf16[10,128,128]{2,1,0:T(8,128)(2,1)}, bf16[10,128,128]{2,1,0:T(8,128)(2,1)S(1)}, u32[]{:S(2)}, u32[]{:S(2)}) collective-permute-start(bf16[10,128,128]{2,1,0:T(8,128)(2,1)} %collective-permute-done.7.rest_7_), channel_id=1, source_target_pairs={{0,8},{8,0},{1,9},{9,1},{2,10},{10,2},{3,11},{11,3},{4,12},{12,4},... | collective-permute-start | bytes 983048 | tf_op jit(solution)/shard_map/ppermute | solution.py:288
  59.4 3.2 %collective-permute-start.15 = (bf16[10,128,128]{2,1,0:T(8,128)(2,1)S(1)}, bf16[10,128,128]{2,1,0:T(8,128)(2,1)S(1)}, u32[]{:S(2)}, u32[]{:S(2)}) collective-permute-start(bf16[10,128,128]{2,1,0:T(8,128)(2,1)S(1)} %collective-permute-done.14.four), channel_id=1, source_target_pairs={{0,8},{8,0},{1,9},{9,1},{2,10},{10,2},{3,11},{11,3},{4,12},{12,4},... | collective-permute-start | bytes 983048 | tf_op jit(solution)/shard_map/ppermute | solution.py:288

commit v13 on v10

--- a/solution.py
+++ b/solution.py
@@ -25,7 +25,7 @@
 ROWS = SLOTS * STEPS
 PACK = STEPS * HEADS + 2 * STEPS
 
-ROUND, PAIR_ROUND, ME, HEAD, COL, SCALE, DEP, DEST, LEN = 0, 1, 2, 3, 13, 23, 33, 46, 59
+ROUND, PAIR_ROUND, ME, HEAD, COL, SCALE, DEP = 0, 1, 2, 3, 13, 23, 33
 
 SLOT_OF, PEER_OF, HEAD_OF = 0, 2 * SLOTS, 4 * SLOTS
 COL_OF = HEAD_OF + 2 * Z * OWN
@@ -68,9 +68,9 @@
 
 
 def notice_body(place, *refs):
-    given, notice, held, sems = refs[:5], refs[5], refs[6:11], refs[11]
+    given, notice, held, sems = refs[:4], refs[4], refs[5:9], refs[9]
     copy_in(zip(given, held), sems)
-    dep, dest, lengths, ids, scales = held
+    dep, dest, ids, scales = held
     row = lax.broadcasted_iota(I32, (REP, HD), 0)
     lane = lax.broadcasted_iota(I32, (REP, HD), 1)
     base = place[0]
@@ -80,15 +80,12 @@
         out = jnp.where((lane == ROUND) & (row == dest[0, k]), float(k), out)
         out = jnp.where((lane == PAIR_ROUND) & (pair_row == dest[0, k]), float(k), out)
         out = jnp.where(lane == DEP + k, dep[0, k].astype(F32), out)
-        out = jnp.where(lane == DEST + k, dest[0, k].astype(F32), out)
     for n in range(OWN):
         place_n = ids[n] - base
         head = lax.div(place_n, COLS)
         out = jnp.where(lane == HEAD + n, head.astype(F32), out)
         out = jnp.where(lane == COL + n, (place_n - head * COLS).astype(F32), out)
         out = jnp.where(lane == SCALE + n, scales[n], out)
-    for s in range(SLOTS):
-        out = jnp.where(lane == LEN + s, lengths[s].astype(F32), out)
     notice[:, 0, :] = out
 
 
@@ -136,12 +133,14 @@
     return (numer / denom).astype(BF16)
 
 
-def stay_body(dep_in, lengths_in, q_in, fresh_in, cache, out, packs, *scratch):
-    dep, lengths, queries, fresh, held, leaves, mine, sems = scratch
-    copy_in(
-        [(dep_in, dep), (lengths_in, lengths), (q_in, queries), (fresh_in, fresh)],
-        sems.at[SLOTS:],
-    )
+def stay_body(dep_in, dest_in, lengths_in, q_in, fresh_in, cache, out, packs, lists, *scratch):
+    dep, dest, lengths, queries, fresh, held, leaves, mine, sems = scratch
+    given = zip((dep_in, dest_in, lengths_in, q_in, fresh_in), (dep, dest, lengths, queries, fresh))
+    copy_in(given, sems.at[SLOTS:])
+    for k in range(MOVE):
+        lists[k] = dep[0, k]
+        lists[SLOTS + k] = dest[0, k]
+        lists[2 * SLOTS + k] = lengths[dep[0, k]]
     for s in range(SLOTS):
         leaves[s] = 0
     for k in range(MOVE):
@@ -179,13 +178,12 @@
     lax.fori_loop(0, SLOTS, one, 0)
 
 
-def attend_body(notices, pulled, cache, send, scores):
-    per = STEPS * HEADS
-    me = at(notices, 0, ME)
-    slots = [at(notices, me, DEP + k) for k in range(MOVE)]
-    goals = [at(notices, me, DEST + k) for k in range(MOVE)]
-    for k in range(MOVE):
-        length = at(notices, me, LEN + slots[k])
+def attend_body(lists, pulled, cache, send, scores):
+    per = STEPS * HEADS
+    slots = [lists[k] for k in range(MOVE)]
+    goals = [lists[SLOTS + k] for k in range(MOVE)]
+    for k in range(MOVE):
+        length = lists[2 * SLOTS + k]
         scores[k] = score(pulled[goals[k]], cache[slots[k], 0, :, :HD], length)
     for k in range(MOVE):
         rows = blend(pulled[goals[k]], scores[k], cache[slots[k], 0, :, HD:])
@@ -296,7 +294,7 @@
         return lax.ppermute(x, ("z", "core"), pairs)
 
     sib = swap(codes, "core")
-    given = [departing, destination, lengths, block_slot, scales]
+    given = [departing, destination, block_slot, scales]
     notice = call(
         notice_body,
         jax.ShapeDtypeStruct((REP, 1, HD), F32),
@@ -308,24 +306,27 @@
     near, near_x = around(codes), around(sib)
     notices = exchange(notice, rep_axes)
     fresh = new_kv.reshape(STEPS, SLOTS, 2 * HD)
-    stays, packs = call(
+    stays, packs, lists = call(
         stay_body,
         [
             jax.ShapeDtypeStruct((SLOTS, per, HD), BF16),
             jax.ShapeDtypeStruct((MOVE, PACK, HD), BF16),
+            jax.ShapeDtypeStruct((3 * SLOTS,), I32),
         ],
-        [hbm()] * 5,
+        [hbm()] * 6,
         [
             pltpu.SMEM(departing.shape, I32),
+            pltpu.SMEM(destination.shape, I32),
             pltpu.SMEM(lengths.shape, I32),
             pltpu.VMEM(queries.shape, BF16),
             pltpu.VMEM(fresh.shape, BF16),
             pltpu.VMEM(kv_cache.shape, BF16),
             pltpu.SMEM((SLOTS,), I32),
             pltpu.VMEM((SLOTS, PACK, HD), BF16),
-            pltpu.SemaphoreType.DMA((SLOTS + 4,)),
+            pltpu.SemaphoreType.DMA((SLOTS + 5,)),
         ],
-    )(*(in_hbm(a) for a in (departing, lengths, queries, fresh)), cache)
+        out_specs=[vmem(), vmem(), smem()],
+    )(*(in_hbm(a) for a in (departing, destination, lengths, queries, fresh)), cache)
     near, stays = lax.optimization_barrier((near, stays))
     near_x, notices = lax.optimization_barrier((near_x, notices))
     two, two_x = around(near), around(near_x)
@@ -346,7 +347,7 @@
         jax.ShapeDtypeStruct((REP, 2 * per, HD), BF16),
         [smem()] + [vmem()] * 2,
         [pltpu.VMEM((MOVE, per, CTX), F32)],
-    )(notices, pulled, kv_cache)
+    )(lists, pulled, kv_cache)
     came = exchange(send, rep_axes)
     four, four_x = around(three), around(three_x)
     rows, total = call(

time: 82.9 us -> 82.6 us (level)
  no operation moved by 1% of the time
where the time goes in v13:
time: 82.6 us; the launch traced here: 81.9 us
  starting transfers between devices  32.8 us (40%)
  blocking collectives  17.6 us (21%)
  Pallas kernels  15.9 us (19%)
  waiting for transfers between devices  15.4 us (19%)
    all_to_all x1, blocking collectives, exchange(): return lax.all_to_all(x, axes, split_axis=0, concat_axis=0, tiled=True)  17.6 us
    all_to_all x3, starting transfers between devices, exchange(): return lax.all_to_all(x, axes, split_axis=0, concat_axis=0, tiled=True)  16.2 us
    all_to_all x3, waiting for transfers between devices, exchange(): return lax.all_to_all(x, axes, split_axis=0, concat_axis=0, tiled=True)  15.1 us
    ppermute x8, starting transfers between devices, around(): return lax.ppermute(x, ('z', 'core'), pairs)  12.7 us
    ppermute x8, starting transfers between devices, swap(): return lax.ppermute(x, axis, [(0, 1), (1, 0)])  3.86 us
    pallas_call x1, Pallas kernels, shards(): call(stay_body, [jax.ShapeDtypeStruct((SLOTS, per, HD), BF16), jax.ShapeD...  3.63 us
    pallas_call x1, Pallas kernels, shards(): call(project_body, [jax.ShapeDtypeStruct((HEADS, XL * ROWS, HD), BF16), j...  3.2 us
    pallas_call x1, Pallas kernels, shards(): call(table_body, [jax.ShapeDtypeStruct((TABLE,), I32), jax.ShapeDtypeStru...  2.55 us
  transfers between devices with their start and end apart: 19, of which 4 were waited for; matrix products, arithmetic and copies ran while one was open for 0% of the time, Pallas kernels for 17%

profile of v13, /device:TPU:8, one launch (start us, length us, event | category | flops | bytes accessed | tf_op | source)
XLA Modules:
  0.0 81.9 jit_solution(5446882107659050310)
XLA Ops:
  0.0 2.0 %collective-permute-start.2 = (bf16[10,128,128]{2,1,0:T(8,128)(2,1)}, bf16[10,128,128]{2,1,0:T(8,128)(2,1)S(1)}, u32[]{:S(2)}, u32[]{:S(2)}) collective-permute-start(bf16[10,128,128]{2,1,0:T(8,128)(2,1)} %rest_0_.1), channel_id=1, source_target_pairs={{0,16},{8,120},{16,32},{24,8},{32,48},{40,24},{48,64},{56,40},{64,... | collective-permute-start | bytes 983048 | tf_op jit(solution)/shard_map/ppermute | solution.py:294
  2.0 1.5 %shard_map.91 = f32[32,1,128]{2,1,0:T(1,128)} custom-call(s32[1]{0:T(128)} %bitcast.place, s32[1,13]{1,0:T(1,128)} %dep_in.1, s32[1,13]{1,0:T(1,128)} %dest_in.1, s32[10]{0:T(128)} %refs_2_.1, f32[10]{0:T(128)} %refs_3_.1), custom_call_target="tpu_custom_call" | custom-call | tf_op jit(solution)/shard_map/pallas_call | solution.py:298
  3.5 2.0 %collective-permute-start.1 = (bf16[10,128,128]{2,1,0:T(8,128)(2,1)S(1)}, bf16[10,128,128]{2,1,0:T(8,128)(2,1)}, u32[]{:S(2)}, u32[]{:S(2)}) collective-permute-start(bf16[10,128,128]{2,1,0:T(8,128)(2,1)S(1)} %collective-permute-done.rest_1_), channel_id=1, source_target_pairs={{0,16},{8,120},{16,32},{24,8},{32,48},{40,24},{48,64},{56,40},{64,... | collective-permute-start | bytes 983048 | tf_op jit(solution)/shard_map/ppermute | solution.py:294
  5.5 8.0 %all-to-all-start = ((f32[32,1,128]{2,1,0:T(1,128)}), f32[32,1,128]{2,1,0:T(1,128)S(1)}, u32[]{:S(2)}, u32[]{:S(2)}) async-start(f32[32,1,128]{2,1,0:T(1,128)} %shard_map.91), calls=%async_computation | async-start | bytes 32768 | tf_op jit(solution)/shard_map/all_to_all | solution.py:283
  13.5 3.6 %shard_map.93 = (bf16[16,16,128]{2,1,0:T(8,128)(2,1)S(1)}, bf16[13,20,128]{2,1,0:T(8,128)(2,1)S(1)}, s32[48]{0:T(128)S(1)}) custom-call(s32[1,13]{1,0:T(1,128)} %dep_in.1, s32[1,13]{1,0:T(1,128)} %dest_in.1, s32[16]{0:T(128)} %lengths_in.1, bf16[2,16,8,128]{3,2,1,0:T(8,128)(2,1)} %q_in.1, bf16[2,16,256]{2,1,0:T(8,128)(2,1)} %bitcast.5, ...), custom_call_target="tpu_custom_call" | custom-call | tf_op jit(solution)/shard_map/pallas_call | solution.py:309
  17.1 0.0 copy-start.1
  17.1 0.0 collective-permute-done.2.rest_2_
  17.1 1.9 %collective-permute-start.4 = (bf16[10,128,128]{2,1,0:T(8,128)(2,1)S(1)}, bf16[10,128,128]{2,1,0:T(8,128)(2,1)}, u32[]{:S(2)}, u32[]{:S(2)}) collective-permute-start(bf16[10,128,128]{2,1,0:T(8,128)(2,1)S(1)} %collective-permute-done.2.rest_2_), channel_id=1, source_target_pairs={{0,16},{8,120},{16,32},{24,8},{32,48},{40,24},{48,64},{56,40},{64,... | collective-permute-start | bytes 983048 | tf_op jit(solution)/shard_map/ppermute | solution.py:294
  19.1 2.7 %all-to-all-done.notices = f32[32,1,128]{2,1,0:T(1,128)S(1)} async-done(((f32[32,1,128]{2,1,0:T(1,128)}), f32[32,1,128]{2,1,0:T(1,128)S(1)}, u32[]{:S(2)}, u32[]{:S(2)}) %all-to-all-start) | async-done | bytes 16416 | tf_op jit(solution)/shard_map/all_to_all | solution.py:283
  21.8 0.6 collective-permute-start.6
  22.4 1.6 %shard_map.94 = bf16[32,20,128]{2,1,0:T(8,128)(2,1)} custom-call(f32[32,1,128]{2,1,0:T(1,128)S(1)} %all-to-all-done.notices, bf16[13,20,128]{2,1,0:T(8,128)(2,1)S(1)} %get-tuple-element.24.packs), custom_call_target="tpu_custom_call" | custom-call | tf_op jit(solution)/shard_map/pallas_call | solution.py:340
  24.0 4.3 %all-to-all-start.1 = ((bf16[32,20,128]{2,1,0:T(8,128)(2,1)}), bf16[32,20,128]{2,1,0:T(8,128)(2,1)S(1)}, u32[]{:S(2)}, u32[]{:S(2)}) async-start(bf16[32,20,128]{2,1,0:T(8,128)(2,1)} %shard_map.94), calls=%async_computation.1 | async-start | bytes 393216 | tf_op jit(solution)/shard_map/all_to_all | solution.py:283
  28.3 1.9 %collective-permute-start.3 = (bf16[16,16,128]{2,1,0:T(8,128)(2,1)S(1)}, bf16[16,16,128]{2,1,0:T(8,128)(2,1)S(1)}, u32[]{:S(2)}, u32[]{:S(2)}) collective-permute-start(bf16[16,16,128]{2,1,0:T(8,128)(2,1)S(1)} %get-tuple-element.26.mine), channel_id=1, source_target_pairs={{0,128},{128,0},{1,129},{129,1},{2,130},{130,2},{3,131},{131,3},{4... | collective-permute-start | bytes 196616 | tf_op jit(solution)/shard_map/ppermute | solution.py:286
  30.2 1.5 %collective-permute-start.5 = (bf16[10,128,128]{2,1,0:T(8,128)(2,1)}, bf16[10,128,128]{2,1,0:T(8,128)(2,1)}, u32[]{:S(2)}, u32[]{:S(2)}) collective-permute-start(bf16[10,128,128]{2,1,0:T(8,128)(2,1)} %collective-permute-done.4.rest_3_), channel_id=1, source_target_pairs={{0,16},{8,120},{16,32},{24,8},{32,48},{40,24},{48,64},{56,40},{64,... | collective-permute-start | bytes 983048 | tf_op jit(solution)/shard_map/ppermute | solution.py:294
  31.7 1.5 %collective-permute-start.7 = (bf16[10,128,128]{2,1,0:T(8,128)(2,1)}, bf16[10,128,128]{2,1,0:T(8,128)(2,1)}, u32[]{:S(2)}, u32[]{:S(2)}) collective-permute-start(bf16[10,128,128]{2,1,0:T(8,128)(2,1)} %collective-permute-done.6.rest_6_), channel_id=1, source_target_pairs={{0,16},{8,120},{16,32},{24,8},{32,48},{40,24},{48,64},{56,40},{64,... | collective-permute-start | bytes 983048 | tf_op jit(solution)/shard_map/ppermute | solution.py:294
  33.1 1.2 %collective-permute-start.11 = (bf16[10,128,128]{2,1,0:T(8,128)(2,1)}, bf16[10,128,128]{2,1,0:T(8,128)(2,1)}, u32[]{:S(2)}, u32[]{:S(2)}) collective-permute-start(bf16[10,128,128]{2,1,0:T(8,128)(2,1)} %collective-permute-done.1.rest_5_), channel_id=1, source_target_pairs={{0,8},{8,0},{1,9},{9,1},{2,10},{10,2},{3,11},{11,3},{4,12},{12,4},... | collective-permute-start | bytes 983048 | tf_op jit(solution)/shard_map/ppermute | solution.py:286
  34.3 0.0 collective-permute-start.9
  34.4 5.8 %all-to-all-done.1.pulled = bf16[32,20,128]{2,1,0:T(8,128)(2,1)S(1)} async-done(((bf16[32,20,128]{2,1,0:T(8,128)(2,1)}), bf16[32,20,128]{2,1,0:T(8,128)(2,1)S(1)}, u32[]{:S(2)}, u32[]{:S(2)}) %all-to-all-start.1) | async-done | bytes 163872 | tf_op jit(solution)/shard_map/all_to_all | solution.py:283
  40.2 1.8 %shard_map.95 = bf16[32,32,128]{2,1,0:T(8,128)(2,1)} custom-call(s32[48]{0:T(128)S(1)} %get-tuple-element.23.lists, bf16[32,20,128]{2,1,0:T(8,128)(2,1)S(1)} %all-to-all-done.1.pulled, bf16[16,1,256,256]{3,2,1,0:T(8,128)(2,1)S(1)} %copy-done), custom_call_target="tpu_custom_call" | custom-call | tf_op jit(solution)/shard_map/pallas_call | solution.py:345
  42.0 3.9 %all-to-all-start.2 = ((bf16[32,32,128]{2,1,0:T(8,128)(2,1)}), bf16[32,32,128]{2,1,0:T(8,128)(2,1)S(1)}, u32[]{:S(2)}, u32[]{:S(2)}) async-start(bf16[32,32,128]{2,1,0:T(8,128)(2,1)} %shard_map.95), calls=%async_computation.2 | async-start | bytes 524288 | tf_op jit(solution)/shard_map/all_to_all | solution.py:283
  45.9 0.2 collective-permute-start.12
  46.1 0.3 collective-permute-start.10
  46.5 0.2 collective-permute-start.13
  46.7 1.8 %collective-permute-start.14 = (bf16[10,128,128]{2,1,0:T(8,128)(2,1)}, bf16[10,128,128]{2,1,0:T(8,128)(2,1)S(1)}, u32[]{:S(2)}, u32[]{:S(2)}) collective-permute-start(bf16[10,128,128]{2,1,0:T(8,128)(2,1)} %collective-permute-done.5.rest_4_), channel_id=1, source_target_pairs={{0,16},{8,120},{16,32},{24,8},{32,48},{40,24},{48,64},{56,40},{64,... | collective-permute-start | bytes 983048 | tf_op jit(solution)/shard_map/ppermute | solution.py:294
  48.5 1.5 %collective-permute-start.15 = (bf16[10,128,128]{2,1,0:T(8,128)(2,1)}, bf16[10,128,128]{2,1,0:T(8,128)(2,1)S(1)}, u32[]{:S(2)}, u32[]{:S(2)}) collective-permute-start(bf16[10,128,128]{2,1,0:T(8,128)(2,1)} %collective-permute-done.7.rest_7_), channel_id=1, source_target_pairs={{0,16},{8,120},{16,32},{24,8},{32,48},{40,24},{48,64},{56,40},{64,... | collective-permute-start | bytes 983048 | tf_op jit(solution)/shard_map/ppermute | solution.py:294
  49.9 2.5 %shard_map.92 = (s32[384]{0:T(512)S(1)}, f32[160]{0:T(256)S(1)}) custom-call(f32[32,1,128]{2,1,0:T(1,128)S(1)} %all-to-all-done.notices), custom_call_target="tpu_custom_call" | custom-call | tf_op jit(solution)/shard_map/pallas_call | solution.py:334
  52.5 6.6 %all-to-all-done.2.came = bf16[32,32,128]{2,1,0:T(8,128)(2,1)S(1)} async-done(((bf16[32,32,128]{2,1,0:T(8,128)(2,1)}), bf16[32,32,128]{2,1,0:T(8,128)(2,1)S(1)}, u32[]{:S(2)}, u32[]{:S(2)}) %all-to-all-start.2) | async-done | bytes 262176 | tf_op jit(solution)/shard_map/all_to_all | solution.py:283
  59.1 3.2 %shard_map.96 = (bf16[8,64,128]{2,1,0:T(8,128)(2,1)S(1)}, f32[40,64,128]{2,1,0:T(8,128)S(1)}) custom-call(s32[1]{0:T(128)} %bitcast.1.where, s32[384]{0:T(512)S(1)} %get-tuple-element.21.table, f32[160]{0:T(256)S(1)} %get-tuple-element.22.scales, bf16[32,32,128]{2,1,0:T(8,128)(2,1)S(1)} %all-to-all-done.2.came, ...), custom_call_target="tpu_custom_call" | custom-call | tf_op jit(solution)/shard_map/pallas_call | solution.py:353
  62.3 0.3 collective-permute-done.15.four_x
  62.6 1.0 %shard_map.97 = bf16[80,32,128]{2,1,0:T(8,128)(2,1)S(1)} custom-call(s32[384]{0:T(512)S(1)} %get-tuple-element.21.table, f32[160]{0:T(256)S(1)} %get-tuple-element.22.scales, bf16[8,64,128]{2,1,0:T(8,128)(2,1)S(1)} %get-tuple-element.29.rows, f32[40,64,128]{2,1,0:T(8,128)S(1)} %get-tuple-element.30.so_far, ...), custom_call_target="tpu_custom_call" | custom-call | tf_op jit(solution)/shard_map/pallas_call | solution.py:366
  63.6 17.6 %all_to_all.20 = bf16[80,32,128]{2,1,0:T(8,128)(2,1)S(1)} all-to-all(bf16[80,32,128]{2,1,0:T(8,128)(2,1)S(1)} %shard_map.97), channel_id=1, replica_groups=mesh['xl'=2,'z'=8,'core'=2,'y'=4,'xh'=2] {'xl','y','xh'}, dimensions={0} | all-to-all | bytes 1310720 | tf_op jit(solution)/shard_map/all_to_all | solution.py:283
  81.2 0.7 shard_map.98
  (19 shorter events, 0.0 us)
Async XLA Ops:
  0.0 40.2 %copy-start = (bf16[16,1,256,256]{3,2,1,0:T(8,128)(2,1)S(1)}, bf16[16,1,256,256]{3,2,1,0:T(8,128)(2,1)}, u32[]{:S(2)}) copy-start(bf16[16,1,256,256]{3,2,1,0:T(8,128)(2,1)} %cache.3) | copy-start | bytes 6291460
  0.0 3.5 %collective-permute-start = (bf16[10,128,128]{2,1,0:T(8,128)(2,1)}, bf16[10,128,128]{2,1,0:T(8,128)(2,1)S(1)}, u32[]{:S(2)}, u32[]{:S(2)}) collective-permute-start(bf16[10,128,128]{2,1,0:T(8,128)(2,1)} %rest_0_.1), channel_id=1, source_target_pairs={{0,8},{8,0},{1,9},{9,1},{2,10},{10,2},{3,11},{11,3},{4,12},{12,4},... | collective-permute-start | bytes 983048 | tf_op jit(solution)/shard_map/ppermute | solution.py:286
  0.0 17.1 %collective-permute-start.2 = (bf16[10,128,128]{2,1,0:T(8,128)(2,1)}, bf16[10,128,128]{2,1,0:T(8,128)(2,1)S(1)}, u32[]{:S(2)}, u32[]{:S(2)}) collective-permute-start(bf16[10,128,128]{2,1,0:T(8,128)(2,1)} %rest_0_.1), channel_id=1, source_target_pairs={{0,16},{8,120},{16,32},{24,8},{32,48},{40,24},{48,64},{56,40},{64,... | collective-permute-start | bytes 983048 | tf_op jit(solution)/shard_map/ppermute | solution.py:294
  3.5 18.3 %collective-permute-start.1 = (bf16[10,128,128]{2,1,0:T(8,128)(2,1)S(1)}, bf16[10,128,128]{2,1,0:T(8,128)(2,1)}, u32[]{:S(2)}, u32[]{:S(2)}) collective-permute-start(bf16[10,128,128]{2,1,0:T(8,128)(2,1)S(1)} %collective-permute-done.rest_1_), channel_id=1, source_target_pairs={{0,16},{8,120},{16,32},{24,8},{32,48},{40,24},{48,64},{56,40},{64,... | collective-permute-start | bytes 983048 | tf_op jit(solution)/shard_map/ppermute | solution.py:294
  5.5 16.3 %all-to-all-start = ((f32[32,1,128]{2,1,0:T(1,128)}), f32[32,1,128]{2,1,0:T(1,128)S(1)}, u32[]{:S(2)}, u32[]{:S(2)}) async-start(f32[32,1,128]{2,1,0:T(1,128)} %shard_map.91), calls=%async_computation | async-start | bytes 32768 | tf_op jit(solution)/shard_map/all_to_all | solution.py:283
  17.1 42.0 %copy-start.1 = (bf16[10,128,128]{2,1,0:T(8,128)(2,1)S(1)}, bf16[10,128,128]{2,1,0:T(8,128)(2,1)}, u32[]{:S(2)}) copy-start(bf16[10,128,128]{2,1,0:T(8,128)(2,1)} %rest_0_.1) | copy-start | bytes 983044
  17.1 13.1 %collective-permute-start.4 = (bf16[10,128,128]{2,1,0:T(8,128)(2,1)S(1)}, bf16[10,128,128]{2,1,0:T(8,128)(2,1)}, u32[]{:S(2)}, u32[]{:S(2)}) collective-permute-start(bf16[10,128,128]{2,1,0:T(8,128)(2,1)S(1)} %collective-permute-done.2.rest_2_), channel_id=1, source_target_pairs={{0,16},{8,120},{16,32},{24,8},{32,48},{40,24},{48,64},{56,40},{64,... | collective-permute-start | bytes 983048 | tf_op jit(solution)/shard_map/ppermute | solution.py:294
  21.8 9.9 %collective-permute-start.6 = (bf16[10,128,128]{2,1,0:T(8,128)(2,1)}, bf16[10,128,128]{2,1,0:T(8,128)(2,1)}, u32[]{:S(2)}, u32[]{:S(2)}) collective-permute-start(bf16[10,128,128]{2,1,0:T(8,128)(2,1)} %collective-permute-done.1.rest_5_), channel_id=1, source_target_pairs={{0,16},{8,120},{16,32},{24,8},{32,48},{40,24},{48,64},{56,40},{64,... | collective-permute-start | bytes 983048 | tf_op jit(solution)/shard_map/ppermute | solution.py:294
  24.0 16.2 %all-to-all-start.1 = ((bf16[32,20,128]{2,1,0:T(8,128)(2,1)}), bf16[32,20,128]{2,1,0:T(8,128)(2,1)S(1)}, u32[]{:S(2)}, u32[]{:S(2)}) async-start(bf16[32,20,128]{2,1,0:T(8,128)(2,1)} %shard_map.94), calls=%async_computation.1 | async-start | bytes 393216 | tf_op jit(solution)/shard_map/all_to_all | solution.py:283
  28.3 6.0 %collective-permute-start.3 = (bf16[16,16,128]{2,1,0:T(8,128)(2,1)S(1)}, bf16[16,16,128]{2,1,0:T(8,128)(2,1)S(1)}, u32[]{:S(2)}, u32[]{:S(2)}) collective-permute-start(bf16[16,16,128]{2,1,0:T(8,128)(2,1)S(1)} %get-tuple-element.26.mine), channel_id=1, source_target_pairs={{0,128},{128,0},{1,129},{129,1},{2,130},{130,2},{3,131},{131,3},{4... | collective-permute-start | bytes 196616 | tf_op jit(solution)/shard_map/ppermute | solution.py:286
  30.2 15.7 %collective-permute-start.8 = (bf16[10,128,128]{2,1,0:T(8,128)(2,1)S(1)}, bf16[10,128,128]{2,1,0:T(8,128)(2,1)}, u32[]{:S(2)}, u32[]{:S(2)}) collective-permute-start(bf16[10,128,128]{2,1,0:T(8,128)(2,1)S(1)} %collective-permute-done.2.rest_2_), channel_id=1, source_target_pairs={{0,8},{8,0},{1,9},{9,1},{2,10},{10,2},{3,11},{11,3},{4,12},{12,4},... | collective-permute-start | bytes 983048 | tf_op jit(solution)/shard_map/ppermute | solution.py:286
  30.2 16.0 %collective-permute-start.5 = (bf16[10,128,128]{2,1,0:T(8,128)(2,1)}, bf16[10,128,128]{2,1,0:T(8,128)(2,1)}, u32[]{:S(2)}, u32[]{:S(2)}) collective-permute-start(bf16[10,128,128]{2,1,0:T(8,128)(2,1)} %collective-permute-done.4.rest_3_), channel_id=1, source_target_pairs={{0,16},{8,120},{16,32},{24,8},{32,48},{40,24},{48,64},{56,40},{64,... | collective-permute-start | bytes 983048 | tf_op jit(solution)/shard_map/ppermute | solution.py:294
  31.7 14.8 %collective-permute-start.7 = (bf16[10,128,128]{2,1,0:T(8,128)(2,1)}, bf16[10,128,128]{2,1,0:T(8,128)(2,1)}, u32[]{:S(2)}, u32[]{:S(2)}) collective-permute-start(bf16[10,128,128]{2,1,0:T(8,128)(2,1)} %collective-permute-done.6.rest_6_), channel_id=1, source_target_pairs={{0,16},{8,120},{16,32},{24,8},{32,48},{40,24},{48,64},{56,40},{64,... | collective-permute-start | bytes 983048 | tf_op jit(solution)/shard_map/ppermute | solution.py:294
  33.1 13.5 %collective-permute-start.11 = (bf16[10,128,128]{2,1,0:T(8,128)(2,1)}, bf16[10,128,128]{2,1,0:T(8,128)(2,1)}, u32[]{:S(2)}, u32[]{:S(2)}) collective-permute-start(bf16[10,128,128]{2,1,0:T(8,128)(2,1)} %collective-permute-done.1.rest_5_), channel_id=1, source_target_pairs={{0,8},{8,0},{1,9},{9,1},{2,10},{10,2},{3,11},{11,3},{4,12},{12,4},... | collective-permute-start | bytes 983048 | tf_op jit(solution)/shard_map/ppermute | solution.py:286
  34.3 14.1 %collective-permute-start.9 = (bf16[10,128,128]{2,1,0:T(8,128)(2,1)}, bf16[10,128,128]{2,1,0:T(8,128)(2,1)}, u32[]{:S(2)}, u32[]{:S(2)}) collective-permute-start(bf16[10,128,128]{2,1,0:T(8,128)(2,1)} %collective-permute-done.4.rest_3_), channel_id=1, source_target_pairs={{0,8},{8,0},{1,9},{9,1},{2,10},{10,2},{3,11},{11,3},{4,12},{12,4},... | collective-permute-start | bytes 983048 | tf_op jit(solution)/shard_map/ppermute | solution.py:286
  42.0 17.1 %all-to-all-start.2 = ((bf16[32,32,128]{2,1,0:T(8,128)(2,1)}), bf16[32,32,128]{2,1,0:T(8,128)(2,1)S(1)}, u32[]{:S(2)}, u32[]{:S(2)}) async-start(bf16[32,32,128]{2,1,0:T(8,128)(2,1)} %shard_map.95), calls=%async_computation.2 | async-start | bytes 524288 | tf_op jit(solution)/shard_map/all_to_all | solution.py:283
  45.9 6.6 %collective-permute-start.12 = (bf16[10,128,128]{2,1,0:T(8,128)(2,1)}, bf16[10,128,128]{2,1,0:T(8,128)(2,1)S(1)}, u32[]{:S(2)}, u32[]{:S(2)}) collective-permute-start(bf16[10,128,128]{2,1,0:T(8,128)(2,1)} %collective-permute-done.6.rest_6_), channel_id=1, source_target_pairs={{0,8},{8,0},{1,9},{9,1},{2,10},{10,2},{3,11},{11,3},{4,12},{12,4},... | collective-permute-start | bytes 983048 | tf_op jit(solution)/shard_map/ppermute | solution.py:286
  46.1 6.4 %collective-permute-start.10 = (bf16[10,128,128]{2,1,0:T(8,128)(2,1)}, bf16[10,128,128]{2,1,0:T(8,128)(2,1)S(1)}, u32[]{:S(2)}, u32[]{:S(2)}) collective-permute-start(bf16[10,128,128]{2,1,0:T(8,128)(2,1)} %collective-permute-done.5.rest_4_), channel_id=1, source_target_pairs={{0,8},{8,0},{1,9},{9,1},{2,10},{10,2},{3,11},{11,3},{4,12},{12,4},... | collective-permute-start | bytes 983048 | tf_op jit(solution)/shard_map/ppermute | solution.py:286
  46.5 12.6 %collective-permute-start.13 = (bf16[10,128,128]{2,1,0:T(8,128)(2,1)}, bf16[10,128,128]{2,1,0:T(8,128)(2,1)S(1)}, u32[]{:S(2)}, u32[]{:S(2)}) collective-permute-start(bf16[10,128,128]{2,1,0:T(8,128)(2,1)} %collective-permute-done.7.rest_7_), channel_id=1, source_target_pairs={{0,8},{8,0},{1,9},{9,1},{2,10},{10,2},{3,11},{11,3},{4,12},{12,4},... | collective-permute-start | bytes 983048 | tf_op jit(solution)/shard_map/ppermute | solution.py:286
  46.7 15.6 %collective-permute-start.14 = (bf16[10,128,128]{2,1,0:T(8,128)(2,1)}, bf16[10,128,128]{2,1,0:T(8,128)(2,1)S(1)}, u32[]{:S(2)}, u32[]{:S(2)}) collective-permute-start(bf16[10,128,128]{2,1,0:T(8,128)(2,1)} %collective-permute-done.5.rest_4_), channel_id=1, source_target_pairs={{0,16},{8,120},{16,32},{24,8},{32,48},{40,24},{48,64},{56,40},{64,... | collective-permute-start | bytes 983048 | tf_op jit(solution)/shard_map/ppermute | solution.py:294
  48.5 14.1 %collective-permute-start.15 = (bf16[10,128,128]{2,1,0:T(8,128)(2,1)}, bf16[10,128,128]{2,1,0:T(8,128)(2,1)S(1)}, u32[]{:S(2)}, u32[]{:S(2)}) collective-permute-start(bf16[10,128,128]{2,1,0:T(8,128)(2,1)} %collective-permute-done.7.rest_7_), channel_id=1, source_target_pairs={{0,16},{8,120},{16,32},{24,8},{32,48},{40,24},{48,64},{56,40},{64,... | collective-permute-start | bytes 983048 | tf_op jit(solution)/shard_map/ppermute | solution.py:294

commit v14 on v13

--- a/solution.py
+++ b/solution.py
@@ -341,6 +341,7 @@
         pull_body, jax.ShapeDtypeStruct((REP, PACK, HD), BF16), [smem(), vmem()]
     )(notices, packs)
     pulled = exchange(to_pull, rep_axes)
+    other, pulled = lax.optimization_barrier((other, pulled))
     three, three_x = around(two), around(two_x)
     send = call(
         attend_body,
@@ -349,7 +350,7 @@
         [pltpu.VMEM((MOVE, per, CTX), F32)],
     )(lists, pulled, kv_cache)
     came = exchange(send, rep_axes)
-    four, four_x = around(three), around(three_x)
+    four = around(three)
     rows, total = call(
         project_body,
         [
@@ -363,6 +364,8 @@
         *(codes, sib, near, two, three, near_x, two_x, three_x),
         *(swap(x, "core") for x in (near, two, three, near_x, two_x, three_x)),
     )
+    four, rows = lax.optimization_barrier((four, rows))
+    four_x = swap(four, "core")
     parts = call(
         last_body,
         jax.ShapeDtypeStruct((XL * COLS, ROWS, HD), BF16),

time: 82.6 us -> 85.5 us (1.035)
  waiting for transfers between devices: 15.4 us -> 18.1 us
  starting transfers between devices: 32.8 us -> 31.5 us
  blocking collectives: 17.6 us -> 18.8 us
    ppermute x8 -> x9, waiting for transfers between devices: 0.02 us -> 4.86 us  [swap(): return lax.ppermute(x, axis, [(0, 1), (1, 0)])]
    all_to_all x3, waiting for transfers between devices: 15.1 us -> 13.2 us  [exchange(): return lax.all_to_all(x, axes, split_axis=0, concat_axis=0, tiled=True)]
    ppermute x8 -> x7, starting transfers between devices: 12.7 us -> 11.2 us  [around(): return lax.ppermute(x, ('z', 'core'), pairs)]
    all_to_all x1, blocking collectives: 17.6 us -> 18.8 us  [exchange(): return lax.all_to_all(x, axes, split_axis=0, concat_axis=0, tiled=True)]
    ppermute x8 -> x9, starting transfers between devices: 3.86 us -> 4.11 us  [swap(): return lax.ppermute(x, axis, [(0, 1), (1, 0)])]
  transfers between devices with their start and end apart: 19 -> 19, of which waited for: 4 -> 5; matrix products, arithmetic and copies ran while one was open for 0% -> 0% of each run, Pallas kernels for 17% -> 17%
where the time goes in v14:
time: 85.5 us; the launch traced here: 84.4 us
  starting transfers between devices  31.5 us (37%)
  blocking collectives  18.8 us (22%)
  waiting for transfers between devices  18.1 us (21%)
  Pallas kernels  15.8 us (18%)
    all_to_all x1, blocking collectives, exchange(): return lax.all_to_all(x, axes, split_axis=0, concat_axis=0, tiled=True)  18.8 us
    all_to_all x3, starting transfers between devices, exchange(): return lax.all_to_all(x, axes, split_axis=0, concat_axis=0, tiled=True)  16.2 us
    all_to_all x3, waiting for transfers between devices, exchange(): return lax.all_to_all(x, axes, split_axis=0, concat_axis=0, tiled=True)  13.2 us
    ppermute x7, starting transfers between devices, around(): return lax.ppermute(x, ('z', 'core'), pairs)  11.2 us
    ppermute x9, waiting for transfers between devices, swap(): return lax.ppermute(x, axis, [(0, 1), (1, 0)])  4.86 us
    ppermute x9, starting transfers between devices, swap(): return lax.ppermute(x, axis, [(0, 1), (1, 0)])  4.11 us
    pallas_call x1, Pallas kernels, shards(): call(stay_body, [jax.ShapeDtypeStruct((SLOTS, per, HD), BF16), jax.ShapeD...  3.7 us
    pallas_call x1, Pallas kernels, shards(): call(project_body, [jax.ShapeDtypeStruct((HEADS, XL * ROWS, HD), BF16), j...  3.08 us
  transfers between devices with their start and end apart: 19, of which 5 were waited for; matrix products, arithmetic and copies ran while one was open for 0% of the time, Pallas kernels for 17%

profile of v14, /device:TPU:8, one launch (start us, length us, event | category | flops | bytes accessed | tf_op | source)
XLA Modules:
  0.0 84.4 jit_solution(16992332551875895758)
XLA Ops:
  0.0 2.0 %collective-permute-start.2 = (bf16[10,128,128]{2,1,0:T(8,128)(2,1)}, bf16[10,128,128]{2,1,0:T(8,128)(2,1)S(1)}, u32[]{:S(2)}, u32[]{:S(2)}) collective-permute-start(bf16[10,128,128]{2,1,0:T(8,128)(2,1)} %rest_0_.1), channel_id=1, source_target_pairs={{0,16},{8,120},{16,32},{24,8},{32,48},{40,24},{48,64},{56,40},{64,... | collective-permute-start | bytes 983048 | tf_op jit(solution)/shard_map/ppermute | solution.py:294
  2.0 1.5 %shard_map.91 = f32[32,1,128]{2,1,0:T(1,128)} custom-call(s32[1]{0:T(128)} %bitcast.place, s32[1,13]{1,0:T(1,128)} %dep_in.1, s32[1,13]{1,0:T(1,128)} %dest_in.1, s32[10]{0:T(128)} %refs_2_.1, f32[10]{0:T(128)} %refs_3_.1), custom_call_target="tpu_custom_call" | custom-call | tf_op jit(solution)/shard_map/pallas_call | solution.py:298
  3.5 2.0 %collective-permute-start.1 = (bf16[10,128,128]{2,1,0:T(8,128)(2,1)S(1)}, bf16[10,128,128]{2,1,0:T(8,128)(2,1)}, u32[]{:S(2)}, u32[]{:S(2)}) collective-permute-start(bf16[10,128,128]{2,1,0:T(8,128)(2,1)S(1)} %collective-permute-done.rest_1_), channel_id=1, source_target_pairs={{0,16},{8,120},{16,32},{24,8},{32,48},{40,24},{48,64},{56,40},{64,... | collective-permute-start | bytes 983048 | tf_op jit(solution)/shard_map/ppermute | solution.py:294
  5.5 8.0 %all-to-all-start = ((f32[32,1,128]{2,1,0:T(1,128)}), f32[32,1,128]{2,1,0:T(1,128)S(1)}, u32[]{:S(2)}, u32[]{:S(2)}) async-start(f32[32,1,128]{2,1,0:T(1,128)} %shard_map.91), calls=%async_computation | async-start | bytes 32768 | tf_op jit(solution)/shard_map/all_to_all | solution.py:283
  13.5 3.7 %shard_map.93 = (bf16[16,16,128]{2,1,0:T(8,128)(2,1)S(1)}, bf16[13,20,128]{2,1,0:T(8,128)(2,1)S(1)}, s32[48]{0:T(128)S(1)}) custom-call(s32[1,13]{1,0:T(1,128)} %dep_in.1, s32[1,13]{1,0:T(1,128)} %dest_in.1, s32[16]{0:T(128)} %lengths_in.1, bf16[2,16,8,128]{3,2,1,0:T(8,128)(2,1)} %q_in.1, bf16[2,16,256]{2,1,0:T(8,128)(2,1)} %bitcast.5, ...), custom_call_target="tpu_custom_call" | custom-call | tf_op jit(solution)/shard_map/pallas_call | solution.py:309
  17.2 1.9 %collective-permute-start.3 = (bf16[10,128,128]{2,1,0:T(8,128)(2,1)S(1)}, bf16[10,128,128]{2,1,0:T(8,128)(2,1)}, u32[]{:S(2)}, u32[]{:S(2)}) collective-permute-start(bf16[10,128,128]{2,1,0:T(8,128)(2,1)S(1)} %collective-permute-done.2.rest_2_), channel_id=1, source_target_pairs={{0,16},{8,120},{16,32},{24,8},{32,48},{40,24},{48,64},{56,40},{64,... | collective-permute-start | bytes 983048 | tf_op jit(solution)/shard_map/ppermute | solution.py:294
  19.1 2.7 %all-to-all-done.notices = f32[32,1,128]{2,1,0:T(1,128)S(1)} async-done(((f32[32,1,128]{2,1,0:T(1,128)}), f32[32,1,128]{2,1,0:T(1,128)S(1)}, u32[]{:S(2)}, u32[]{:S(2)}) %all-to-all-start) | async-done | bytes 16416 | tf_op jit(solution)/shard_map/all_to_all | solution.py:283
  21.8 0.6 collective-permute-start.7
  22.4 1.6 %shard_map.94 = bf16[32,20,128]{2,1,0:T(8,128)(2,1)} custom-call(f32[32,1,128]{2,1,0:T(1,128)S(1)} %all-to-all-done.notices, bf16[13,20,128]{2,1,0:T(8,128)(2,1)S(1)} %get-tuple-element.31.packs), custom_call_target="tpu_custom_call" | custom-call | tf_op jit(solution)/shard_map/pallas_call | solution.py:340
  24.0 4.3 %all-to-all-start.1 = ((bf16[32,20,128]{2,1,0:T(8,128)(2,1)}), bf16[32,20,128]{2,1,0:T(8,128)(2,1)S(1)}, u32[]{:S(2)}, u32[]{:S(2)}) async-start(bf16[32,20,128]{2,1,0:T(8,128)(2,1)} %shard_map.94), calls=%async_computation.1 | async-start | bytes 393216 | tf_op jit(solution)/shard_map/all_to_all | solution.py:283
  28.3 0.4 collective-permute-start.9
  28.7 1.7 %collective-permute-start.4 = (bf16[10,128,128]{2,1,0:T(8,128)(2,1)}, bf16[10,128,128]{2,1,0:T(8,128)(2,1)}, u32[]{:S(2)}, u32[]{:S(2)}) collective-permute-start(bf16[10,128,128]{2,1,0:T(8,128)(2,1)} %collective-permute-done.3.rest_3_), channel_id=1, source_target_pairs={{0,16},{8,120},{16,32},{24,8},{32,48},{40,24},{48,64},{56,40},{64,... | collective-permute-start | bytes 983048 | tf_op jit(solution)/shard_map/ppermute | solution.py:294
  30.4 1.4 %collective-permute-start.8 = (bf16[10,128,128]{2,1,0:T(8,128)(2,1)}, bf16[10,128,128]{2,1,0:T(8,128)(2,1)}, u32[]{:S(2)}, u32[]{:S(2)}) collective-permute-start(bf16[10,128,128]{2,1,0:T(8,128)(2,1)} %collective-permute-done.7.rest_6_), channel_id=1, source_target_pairs={{0,16},{8,120},{16,32},{24,8},{32,48},{40,24},{48,64},{56,40},{64,... | collective-permute-start | bytes 983048 | tf_op jit(solution)/shard_map/ppermute | solution.py:294
  31.8 1.0 %collective-permute-start.12 = (bf16[10,128,128]{2,1,0:T(8,128)(2,1)}, bf16[10,128,128]{2,1,0:T(8,128)(2,1)}, u32[]{:S(2)}, u32[]{:S(2)}) collective-permute-start(bf16[10,128,128]{2,1,0:T(8,128)(2,1)} %collective-permute-done.1.rest_5_), channel_id=1, source_target_pairs={{0,8},{8,0},{1,9},{9,1},{2,10},{10,2},{3,11},{11,3},{4,12},{12,4},... | collective-permute-start | bytes 983048 | tf_op jit(solution)/shard_map/ppermute | solution.py:286
  32.8 1.5 %collective-permute-start.6 = (bf16[16,16,128]{2,1,0:T(8,128)(2,1)S(1)}, bf16[16,16,128]{2,1,0:T(8,128)(2,1)S(1)}, u32[]{:S(2)}, u32[]{:S(2)}) collective-permute-start(bf16[16,16,128]{2,1,0:T(8,128)(2,1)S(1)} %get-tuple-element.30.mine), channel_id=1, source_target_pairs={{0,128},{128,0},{1,129},{129,1},{2,130},{130,2},{3,131},{131,3},{4... | collective-permute-start | bytes 196616 | tf_op jit(solution)/shard_map/ppermute | solution.py:286
  34.4 3.2 %collective-permute-done.6.other = bf16[16,16,128]{2,1,0:T(8,128)(2,1)S(1)} collective-permute-done((bf16[16,16,128]{2,1,0:T(8,128)(2,1)S(1)}, bf16[16,16,128]{2,1,0:T(8,128)(2,1)S(1)}, u32[]{:S(2)}, u32[]{:S(2)}) %collective-permute-start.6) | collective-permute-done | bytes 65568 | tf_op jit(solution)/shard_map/ppermute | solution.py:286
  37.6 2.6 %all-to-all-done.1.pulled = bf16[32,20,128]{2,1,0:T(8,128)(2,1)S(1)} async-done(((bf16[32,20,128]{2,1,0:T(8,128)(2,1)}), bf16[32,20,128]{2,1,0:T(8,128)(2,1)S(1)}, u32[]{:S(2)}, u32[]{:S(2)}) %all-to-all-start.1) | async-done | bytes 163872 | tf_op jit(solution)/shard_map/all_to_all | solution.py:283
  40.2 1.8 %shard_map.95 = bf16[32,32,128]{2,1,0:T(8,128)(2,1)} custom-call(s32[48]{0:T(128)S(1)} %get-tuple-element.29.lists, bf16[32,20,128]{2,1,0:T(8,128)(2,1)S(1)} %all-to-all-done.1.pulled, bf16[16,1,256,256]{3,2,1,0:T(8,128)(2,1)S(1)} %copy-done), custom_call_target="tpu_custom_call" | custom-call | tf_op jit(solution)/shard_map/pallas_call | solution.py:346
  42.0 3.9 %all-to-all-start.2 = ((bf16[32,32,128]{2,1,0:T(8,128)(2,1)}), bf16[32,32,128]{2,1,0:T(8,128)(2,1)S(1)}, u32[]{:S(2)}, u32[]{:S(2)}) async-start(bf16[32,32,128]{2,1,0:T(8,128)(2,1)} %shard_map.95), calls=%async_computation.2 | async-start | bytes 524288 | tf_op jit(solution)/shard_map/all_to_all | solution.py:283
  45.9 0.2 collective-permute-start.10
  46.1 0.3 collective-permute-start.13
  46.5 0.2 collective-permute-start.11
  46.7 0.3 collective-permute-start.14
  47.0 1.7 %collective-permute-start.5 = (bf16[10,128,128]{2,1,0:T(8,128)(2,1)}, bf16[10,128,128]{2,1,0:T(8,128)(2,1)S(1)}, u32[]{:S(2)}, u32[]{:S(2)}) collective-permute-start(bf16[10,128,128]{2,1,0:T(8,128)(2,1)} %collective-permute-done.4.rest_4_), channel_id=1, source_target_pairs={{0,16},{8,120},{16,32},{24,8},{32,48},{40,24},{48,64},{56,40},{64,... | collective-permute-start | bytes 983048 | tf_op jit(solution)/shard_map/ppermute | solution.py:294
  48.7 2.5 %shard_map.92 = (s32[384]{0:T(512)S(1)}, f32[160]{0:T(256)S(1)}) custom-call(f32[32,1,128]{2,1,0:T(1,128)S(1)} %all-to-all-done.notices), custom_call_target="tpu_custom_call" | custom-call | tf_op jit(solution)/shard_map/pallas_call | solution.py:334
  51.3 7.8 %all-to-all-done.2.came = bf16[32,32,128]{2,1,0:T(8,128)(2,1)S(1)} async-done(((bf16[32,32,128]{2,1,0:T(8,128)(2,1)}), bf16[32,32,128]{2,1,0:T(8,128)(2,1)S(1)}, u32[]{:S(2)}, u32[]{:S(2)}) %all-to-all-start.2) | async-done | bytes 262176 | tf_op jit(solution)/shard_map/all_to_all | solution.py:283
  59.1 3.1 %shard_map.96 = (bf16[8,64,128]{2,1,0:T(8,128)(2,1)S(1)}, f32[40,64,128]{2,1,0:T(8,128)S(1)}) custom-call(s32[1]{0:T(128)} %bitcast.2.where, s32[384]{0:T(512)S(1)} %get-tuple-element.25.table, f32[160]{0:T(256)S(1)} %get-tuple-element.26.scales, bf16[32,32,128]{2,1,0:T(8,128)(2,1)S(1)} %all-to-all-done.2.came, ...), custom_call_target="tpu_custom_call" | custom-call | tf_op jit(solution)/shard_map/pallas_call | solution.py:354
  62.2 0.1 collective-permute-start.15
  62.3 1.6 %collective-permute-done.15.four_x = bf16[10,128,128]{2,1,0:T(8,128)(2,1)S(1)} collective-permute-done((bf16[10,128,128]{2,1,0:T(8,128)(2,1)S(1)}, bf16[10,128,128]{2,1,0:T(8,128)(2,1)S(1)}, u32[]{:S(2)}, u32[]{:S(2)}) %collective-permute-start.15) | collective-permute-done | bytes 327712 | tf_op jit(solution)/shard_map/ppermute | solution.py:286
  63.9 1.0 %shard_map.97 = bf16[80,32,128]{2,1,0:T(8,128)(2,1)S(1)} custom-call(s32[384]{0:T(512)S(1)} %get-tuple-element.25.table, f32[160]{0:T(256)S(1)} %get-tuple-element.26.scales, bf16[8,64,128]{2,1,0:T(8,128)(2,1)S(1)} %get-tuple-element.36.rows, f32[40,64,128]{2,1,0:T(8,128)S(1)} %get-tuple-element.37.so_far, ...), custom_call_target="tpu_custom_call" | custom-call | tf_op jit(solution)/shard_map/pallas_call | solution.py:369
  64.9 18.8 %all_to_all.20 = bf16[80,32,128]{2,1,0:T(8,128)(2,1)S(1)} all-to-all(bf16[80,32,128]{2,1,0:T(8,128)(2,1)S(1)} %shard_map.97), channel_id=1, replica_groups=mesh['xl'=2,'z'=8,'core'=2,'y'=4,'xh'=2] {'xl','y','xh'}, dimensions={0} | all-to-all | bytes 1310720 | tf_op jit(solution)/shard_map/all_to_all | solution.py:283
  83.7 0.7 shard_map.98
  (19 shorter events, 0.1 us)
Async XLA Ops:
  0.0 40.2 %copy-start = (bf16[16,1,256,256]{3,2,1,0:T(8,128)(2,1)S(1)}, bf16[16,1,256,256]{3,2,1,0:T(8,128)(2,1)}, u32[]{:S(2)}) copy-start(bf16[16,1,256,256]{3,2,1,0:T(8,128)(2,1)} %cache.3) | copy-start | bytes 6291460
  0.0 3.5 %collective-permute-start = (bf16[10,128,128]{2,1,0:T(8,128)(2,1)}, bf16[10,128,128]{2,1,0:T(8,128)(2,1)S(1)}, u32[]{:S(2)}, u32[]{:S(2)}) collective-permute-start(bf16[10,128,128]{2,1,0:T(8,128)(2,1)} %rest_0_.1), channel_id=1, source_target_pairs={{0,8},{8,0},{1,9},{9,1},{2,10},{10,2},{3,11},{11,3},{4,12},{12,4},... | collective-permute-start | bytes 983048 | tf_op jit(solution)/shard_map/ppermute | solution.py:286
  0.0 17.2 %collective-permute-start.2 = (bf16[10,128,128]{2,1,0:T(8,128)(2,1)}, bf16[10,128,128]{2,1,0:T(8,128)(2,1)S(1)}, u32[]{:S(2)}, u32[]{:S(2)}) collective-permute-start(bf16[10,128,128]{2,1,0:T(8,128)(2,1)} %rest_0_.1), channel_id=1, source_target_pairs={{0,16},{8,120},{16,32},{24,8},{32,48},{40,24},{48,64},{56,40},{64,... | collective-permute-start | bytes 983048 | tf_op jit(solution)/shard_map/ppermute | solution.py:294
  3.5 18.3 %collective-permute-start.1 = (bf16[10,128,128]{2,1,0:T(8,128)(2,1)S(1)}, bf16[10,128,128]{2,1,0:T(8,128)(2,1)}, u32[]{:S(2)}, u32[]{:S(2)}) collective-permute-start(bf16[10,128,128]{2,1,0:T(8,128)(2,1)S(1)} %collective-permute-done.rest_1_), channel_id=1, source_target_pairs={{0,16},{8,120},{16,32},{24,8},{32,48},{40,24},{48,64},{56,40},{64,... | collective-permute-start | bytes 983048 | tf_op jit(solution)/shard_map/ppermute | solution.py:294
  5.5 16.3 %all-to-all-start = ((f32[32,1,128]{2,1,0:T(1,128)}), f32[32,1,128]{2,1,0:T(1,128)S(1)}, u32[]{:S(2)}, u32[]{:S(2)}) async-start(f32[32,1,128]{2,1,0:T(1,128)} %shard_map.91), calls=%async_computation | async-start | bytes 32768 | tf_op jit(solution)/shard_map/all_to_all | solution.py:283
  17.2 41.9 %copy-start.1 = (bf16[10,128,128]{2,1,0:T(8,128)(2,1)S(1)}, bf16[10,128,128]{2,1,0:T(8,128)(2,1)}, u32[]{:S(2)}) copy-start(bf16[10,128,128]{2,1,0:T(8,128)(2,1)} %rest_0_.1) | copy-start | bytes 983044
  17.2 11.5 %collective-permute-start.3 = (bf16[10,128,128]{2,1,0:T(8,128)(2,1)S(1)}, bf16[10,128,128]{2,1,0:T(8,128)(2,1)}, u32[]{:S(2)}, u32[]{:S(2)}) collective-permute-start(bf16[10,128,128]{2,1,0:T(8,128)(2,1)S(1)} %collective-permute-done.2.rest_2_), channel_id=1, source_target_pairs={{0,16},{8,120},{16,32},{24,8},{32,48},{40,24},{48,64},{56,40},{64,... | collective-permute-start | bytes 983048 | tf_op jit(solution)/shard_map/ppermute | solution.py:294
  21.8 8.6 %collective-permute-start.7 = (bf16[10,128,128]{2,1,0:T(8,128)(2,1)}, bf16[10,128,128]{2,1,0:T(8,128)(2,1)}, u32[]{:S(2)}, u32[]{:S(2)}) collective-permute-start(bf16[10,128,128]{2,1,0:T(8,128)(2,1)} %collective-permute-done.1.rest_5_), channel_id=1, source_target_pairs={{0,16},{8,120},{16,32},{24,8},{32,48},{40,24},{48,64},{56,40},{64,... | collective-permute-start | bytes 983048 | tf_op jit(solution)/shard_map/ppermute | solution.py:294
  24.0 16.2 %all-to-all-start.1 = ((bf16[32,20,128]{2,1,0:T(8,128)(2,1)}), bf16[32,20,128]{2,1,0:T(8,128)(2,1)S(1)}, u32[]{:S(2)}, u32[]{:S(2)}) async-start(bf16[32,20,128]{2,1,0:T(8,128)(2,1)} %shard_map.94), calls=%async_computation.1 | async-start | bytes 393216 | tf_op jit(solution)/shard_map/all_to_all | solution.py:283
  28.3 17.8 %collective-permute-start.9 = (bf16[10,128,128]{2,1,0:T(8,128)(2,1)S(1)}, bf16[10,128,128]{2,1,0:T(8,128)(2,1)}, u32[]{:S(2)}, u32[]{:S(2)}) collective-permute-start(bf16[10,128,128]{2,1,0:T(8,128)(2,1)S(1)} %collective-permute-done.2.rest_2_), channel_id=1, source_target_pairs={{0,8},{8,0},{1,9},{9,1},{2,10},{10,2},{3,11},{11,3},{4,12},{12,4},... | collective-permute-start | bytes 983048 | tf_op jit(solution)/shard_map/ppermute | solution.py:286
  28.7 17.8 %collective-permute-start.4 = (bf16[10,128,128]{2,1,0:T(8,128)(2,1)}, bf16[10,128,128]{2,1,0:T(8,128)(2,1)}, u32[]{:S(2)}, u32[]{:S(2)}) collective-permute-start(bf16[10,128,128]{2,1,0:T(8,128)(2,1)} %collective-permute-done.3.rest_3_), channel_id=1, source_target_pairs={{0,16},{8,120},{16,32},{24,8},{32,48},{40,24},{48,64},{56,40},{64,... | collective-permute-start | bytes 983048 | tf_op jit(solution)/shard_map/ppermute | solution.py:294
  30.4 16.3 %collective-permute-start.8 = (bf16[10,128,128]{2,1,0:T(8,128)(2,1)}, bf16[10,128,128]{2,1,0:T(8,128)(2,1)}, u32[]{:S(2)}, u32[]{:S(2)}) collective-permute-start(bf16[10,128,128]{2,1,0:T(8,128)(2,1)} %collective-permute-done.7.rest_6_), channel_id=1, source_target_pairs={{0,16},{8,120},{16,32},{24,8},{32,48},{40,24},{48,64},{56,40},{64,... | collective-permute-start | bytes 983048 | tf_op jit(solution)/shard_map/ppermute | solution.py:294
  31.8 15.2 %collective-permute-start.12 = (bf16[10,128,128]{2,1,0:T(8,128)(2,1)}, bf16[10,128,128]{2,1,0:T(8,128)(2,1)}, u32[]{:S(2)}, u32[]{:S(2)}) collective-permute-start(bf16[10,128,128]{2,1,0:T(8,128)(2,1)} %collective-permute-done.1.rest_5_), channel_id=1, source_target_pairs={{0,8},{8,0},{1,9},{9,1},{2,10},{10,2},{3,11},{11,3},{4,12},{12,4},... | collective-permute-start | bytes 983048 | tf_op jit(solution)/shard_map/ppermute | solution.py:286
  32.8 4.8 %collective-permute-start.6 = (bf16[16,16,128]{2,1,0:T(8,128)(2,1)S(1)}, bf16[16,16,128]{2,1,0:T(8,128)(2,1)S(1)}, u32[]{:S(2)}, u32[]{:S(2)}) collective-permute-start(bf16[16,16,128]{2,1,0:T(8,128)(2,1)S(1)} %get-tuple-element.30.mine), channel_id=1, source_target_pairs={{0,128},{128,0},{1,129},{129,1},{2,130},{130,2},{3,131},{131,3},{4... | collective-permute-start | bytes 196616 | tf_op jit(solution)/shard_map/ppermute | solution.py:286
  42.0 17.1 %all-to-all-start.2 = ((bf16[32,32,128]{2,1,0:T(8,128)(2,1)}), bf16[32,32,128]{2,1,0:T(8,128)(2,1)S(1)}, u32[]{:S(2)}, u32[]{:S(2)}) async-start(bf16[32,32,128]{2,1,0:T(8,128)(2,1)} %shard_map.95), calls=%async_computation.2 | async-start | bytes 524288 | tf_op jit(solution)/shard_map/all_to_all | solution.py:283
  45.9 5.4 %collective-permute-start.10 = (bf16[10,128,128]{2,1,0:T(8,128)(2,1)}, bf16[10,128,128]{2,1,0:T(8,128)(2,1)S(1)}, u32[]{:S(2)}, u32[]{:S(2)}) collective-permute-start(bf16[10,128,128]{2,1,0:T(8,128)(2,1)} %collective-permute-done.3.rest_3_), channel_id=1, source_target_pairs={{0,8},{8,0},{1,9},{9,1},{2,10},{10,2},{3,11},{11,3},{4,12},{12,4},... | collective-permute-start | bytes 983048 | tf_op jit(solution)/shard_map/ppermute | solution.py:286
  46.1 5.1 %collective-permute-start.13 = (bf16[10,128,128]{2,1,0:T(8,128)(2,1)}, bf16[10,128,128]{2,1,0:T(8,128)(2,1)S(1)}, u32[]{:S(2)}, u32[]{:S(2)}) collective-permute-start(bf16[10,128,128]{2,1,0:T(8,128)(2,1)} %collective-permute-done.7.rest_6_), channel_id=1, source_target_pairs={{0,8},{8,0},{1,9},{9,1},{2,10},{10,2},{3,11},{11,3},{4,12},{12,4},... | collective-permute-start | bytes 983048 | tf_op jit(solution)/shard_map/ppermute | solution.py:286
  46.5 4.8 %collective-permute-start.11 = (bf16[10,128,128]{2,1,0:T(8,128)(2,1)}, bf16[10,128,128]{2,1,0:T(8,128)(2,1)S(1)}, u32[]{:S(2)}, u32[]{:S(2)}) collective-permute-start(bf16[10,128,128]{2,1,0:T(8,128)(2,1)} %collective-permute-done.4.rest_4_), channel_id=1, source_target_pairs={{0,8},{8,0},{1,9},{9,1},{2,10},{10,2},{3,11},{11,3},{4,12},{12,4},... | collective-permute-start | bytes 983048 | tf_op jit(solution)/shard_map/ppermute | solution.py:286
  46.7 12.4 %collective-permute-start.14 = (bf16[10,128,128]{2,1,0:T(8,128)(2,1)}, bf16[10,128,128]{2,1,0:T(8,128)(2,1)S(1)}, u32[]{:S(2)}, u32[]{:S(2)}) collective-permute-start(bf16[10,128,128]{2,1,0:T(8,128)(2,1)} %collective-permute-done.8.rest_7_), channel_id=1, source_target_pairs={{0,8},{8,0},{1,9},{9,1},{2,10},{10,2},{3,11},{11,3},{4,12},{12,4},... | collective-permute-start | bytes 983048 | tf_op jit(solution)/shard_map/ppermute | solution.py:286
  47.0 15.2 %collective-permute-start.5 = (bf16[10,128,128]{2,1,0:T(8,128)(2,1)}, bf16[10,128,128]{2,1,0:T(8,128)(2,1)S(1)}, u32[]{:S(2)}, u32[]{:S(2)}) collective-permute-start(bf16[10,128,128]{2,1,0:T(8,128)(2,1)} %collective-permute-done.4.rest_4_), channel_id=1, source_target_pairs={{0,16},{8,120},{16,32},{24,8},{32,48},{40,24},{48,64},{56,40},{64,... | collective-permute-start | bytes 983048 | tf_op jit(solution)/shard_map/ppermute | solution.py:294
  62.2 1.7 %collective-permute-start.15 = (bf16[10,128,128]{2,1,0:T(8,128)(2,1)S(1)}, bf16[10,128,128]{2,1,0:T(8,128)(2,1)S(1)}, u32[]{:S(2)}, u32[]{:S(2)}) collective-permute-start(bf16[10,128,128]{2,1,0:T(8,128)(2,1)S(1)} %collective-permute-done.5.four), channel_id=1, source_target_pairs={{0,8},{8,0},{1,9},{9,1},{2,10},{10,2},{3,11},{11,3},{4,12},{12,4},... | collective-permute-start | bytes 983048 | tf_op jit(solution)/shard_map/ppermute | solution.py:286

commit v15 on v13

--- a/solution.py
+++ b/solution.py
@@ -31,7 +31,7 @@
 COL_OF = HEAD_OF + 2 * Z * OWN
 TABLE = COL_OF + 2 * Z * OWN
 
-VMEM_LIMIT = 16 * 1024 * 1024
+VMEM_LIMIT = 10 * 1024 * 1024
 
 
 def smem():

time: 82.6 us -> 82.7 us (level)
  no operation moved by 1% of the time
where the time goes in v15:
time: 82.7 us; the launch traced here: 82 us
  starting transfers between devices  32.8 us (40%)
  blocking collectives  17.6 us (21%)
  Pallas kernels  15.9 us (19%)
  waiting for transfers between devices  15.5 us (19%)
    all_to_all x1, blocking collectives, exchange(): return lax.all_to_all(x, axes, split_axis=0, concat_axis=0, tiled=True)  17.6 us
    all_to_all x3, starting transfers between devices, exchange(): return lax.all_to_all(x, axes, split_axis=0, concat_axis=0, tiled=True)  16.2 us
    all_to_all x3, waiting for transfers between devices, exchange(): return lax.all_to_all(x, axes, split_axis=0, concat_axis=0, tiled=True)  15.2 us
    ppermute x8, starting transfers between devices, around(): return lax.ppermute(x, ('z', 'core'), pairs)  12.7 us
    ppermute x8, starting transfers between devices, swap(): return lax.ppermute(x, axis, [(0, 1), (1, 0)])  3.86 us
    pallas_call x1, Pallas kernels, shards(): call(stay_body, [jax.ShapeDtypeStruct((SLOTS, per, HD), BF16), jax.ShapeD...  3.65 us
    pallas_call x1, Pallas kernels, shards(): call(project_body, [jax.ShapeDtypeStruct((HEADS, XL * ROWS, HD), BF16), j...  3.2 us
    pallas_call x1, Pallas kernels, shards(): call(table_body, [jax.ShapeDtypeStruct((TABLE,), I32), jax.ShapeDtypeStru...  2.55 us
  transfers between devices with their start and end apart: 19, of which 4 were waited for; matrix products, arithmetic and copies ran while one was open for 0% of the time, Pallas kernels for 17%

profile of v15, /device:TPU:8, one launch (start us, length us, event | category | flops | bytes accessed | tf_op | source)
XLA Modules:
  0.0 82.0 jit_solution(14779530781919630182)
XLA Ops:
  0.0 2.0 %collective-permute-start.2 = (bf16[10,128,128]{2,1,0:T(8,128)(2,1)}, bf16[10,128,128]{2,1,0:T(8,128)(2,1)S(1)}, u32[]{:S(2)}, u32[]{:S(2)}) collective-permute-start(bf16[10,128,128]{2,1,0:T(8,128)(2,1)} %rest_0_.1), channel_id=1, source_target_pairs={{0,16},{8,120},{16,32},{24,8},{32,48},{40,24},{48,64},{56,40},{64,... | collective-permute-start | bytes 983048 | tf_op jit(solution)/shard_map/ppermute | solution.py:294
  2.0 1.5 %shard_map.91 = f32[32,1,128]{2,1,0:T(1,128)} custom-call(s32[1]{0:T(128)} %bitcast.place, s32[1,13]{1,0:T(1,128)} %dep_in.1, s32[1,13]{1,0:T(1,128)} %dest_in.1, s32[10]{0:T(128)} %refs_2_.1, f32[10]{0:T(128)} %refs_3_.1), custom_call_target="tpu_custom_call" | custom-call | tf_op jit(solution)/shard_map/pallas_call | solution.py:298
  3.5 2.0 %collective-permute-start.1 = (bf16[10,128,128]{2,1,0:T(8,128)(2,1)S(1)}, bf16[10,128,128]{2,1,0:T(8,128)(2,1)}, u32[]{:S(2)}, u32[]{:S(2)}) collective-permute-start(bf16[10,128,128]{2,1,0:T(8,128)(2,1)S(1)} %collective-permute-done.rest_1_), channel_id=1, source_target_pairs={{0,16},{8,120},{16,32},{24,8},{32,48},{40,24},{48,64},{56,40},{64,... | collective-permute-start | bytes 983048 | tf_op jit(solution)/shard_map/ppermute | solution.py:294
  5.5 8.0 %all-to-all-start = ((f32[32,1,128]{2,1,0:T(1,128)}), f32[32,1,128]{2,1,0:T(1,128)S(1)}, u32[]{:S(2)}, u32[]{:S(2)}) async-start(f32[32,1,128]{2,1,0:T(1,128)} %shard_map.91), calls=%async_computation | async-start | bytes 32768 | tf_op jit(solution)/shard_map/all_to_all | solution.py:283
  13.5 3.6 %shard_map.93 = (bf16[16,16,128]{2,1,0:T(8,128)(2,1)S(1)}, bf16[13,20,128]{2,1,0:T(8,128)(2,1)S(1)}, s32[48]{0:T(128)S(1)}) custom-call(s32[1,13]{1,0:T(1,128)} %dep_in.1, s32[1,13]{1,0:T(1,128)} %dest_in.1, s32[16]{0:T(128)} %lengths_in.1, bf16[2,16,8,128]{3,2,1,0:T(8,128)(2,1)} %q_in.1, bf16[2,16,256]{2,1,0:T(8,128)(2,1)} %bitcast.5, ...), custom_call_target="tpu_custom_call" | custom-call | tf_op jit(solution)/shard_map/pallas_call | solution.py:309
  17.1 0.0 copy-start.1
  17.1 1.9 %collective-permute-start.4 = (bf16[10,128,128]{2,1,0:T(8,128)(2,1)S(1)}, bf16[10,128,128]{2,1,0:T(8,128)(2,1)}, u32[]{:S(2)}, u32[]{:S(2)}) collective-permute-start(bf16[10,128,128]{2,1,0:T(8,128)(2,1)S(1)} %collective-permute-done.2.rest_2_), channel_id=1, source_target_pairs={{0,16},{8,120},{16,32},{24,8},{32,48},{40,24},{48,64},{56,40},{64,... | collective-permute-start | bytes 983048 | tf_op jit(solution)/shard_map/ppermute | solution.py:294
  19.0 2.8 %all-to-all-done.notices = f32[32,1,128]{2,1,0:T(1,128)S(1)} async-done(((f32[32,1,128]{2,1,0:T(1,128)}), f32[32,1,128]{2,1,0:T(1,128)S(1)}, u32[]{:S(2)}, u32[]{:S(2)}) %all-to-all-start) | async-done | bytes 16416 | tf_op jit(solution)/shard_map/all_to_all | solution.py:283
  21.8 0.6 collective-permute-start.6
  22.4 1.6 %shard_map.94 = bf16[32,20,128]{2,1,0:T(8,128)(2,1)} custom-call(f32[32,1,128]{2,1,0:T(1,128)S(1)} %all-to-all-done.notices, bf16[13,20,128]{2,1,0:T(8,128)(2,1)S(1)} %get-tuple-element.24.packs), custom_call_target="tpu_custom_call" | custom-call | tf_op jit(solution)/shard_map/pallas_call | solution.py:340
  24.0 4.4 %all-to-all-start.1 = ((bf16[32,20,128]{2,1,0:T(8,128)(2,1)}), bf16[32,20,128]{2,1,0:T(8,128)(2,1)S(1)}, u32[]{:S(2)}, u32[]{:S(2)}) async-start(bf16[32,20,128]{2,1,0:T(8,128)(2,1)} %shard_map.94), calls=%async_computation.1 | async-start | bytes 393216 | tf_op jit(solution)/shard_map/all_to_all | solution.py:283
  28.4 1.9 %collective-permute-start.3 = (bf16[16,16,128]{2,1,0:T(8,128)(2,1)S(1)}, bf16[16,16,128]{2,1,0:T(8,128)(2,1)S(1)}, u32[]{:S(2)}, u32[]{:S(2)}) collective-permute-start(bf16[16,16,128]{2,1,0:T(8,128)(2,1)S(1)} %get-tuple-element.26.mine), channel_id=1, source_target_pairs={{0,128},{128,0},{1,129},{129,1},{2,130},{130,2},{3,131},{131,3},{4... | collective-permute-start | bytes 196616 | tf_op jit(solution)/shard_map/ppermute | solution.py:286
  30.2 0.0 collective-permute-start.8
  30.2 1.5 %collective-permute-start.5 = (bf16[10,128,128]{2,1,0:T(8,128)(2,1)}, bf16[10,128,128]{2,1,0:T(8,128)(2,1)}, u32[]{:S(2)}, u32[]{:S(2)}) collective-permute-start(bf16[10,128,128]{2,1,0:T(8,128)(2,1)} %collective-permute-done.4.rest_3_), channel_id=1, source_target_pairs={{0,16},{8,120},{16,32},{24,8},{32,48},{40,24},{48,64},{56,40},{64,... | collective-permute-start | bytes 983048 | tf_op jit(solution)/shard_map/ppermute | solution.py:294
  31.7 1.5 %collective-permute-start.7 = (bf16[10,128,128]{2,1,0:T(8,128)(2,1)}, bf16[10,128,128]{2,1,0:T(8,128)(2,1)}, u32[]{:S(2)}, u32[]{:S(2)}) collective-permute-start(bf16[10,128,128]{2,1,0:T(8,128)(2,1)} %collective-permute-done.6.rest_6_), channel_id=1, source_target_pairs={{0,16},{8,120},{16,32},{24,8},{32,48},{40,24},{48,64},{56,40},{64,... | collective-permute-start | bytes 983048 | tf_op jit(solution)/shard_map/ppermute | solution.py:294
  33.2 1.2 %collective-permute-start.11 = (bf16[10,128,128]{2,1,0:T(8,128)(2,1)}, bf16[10,128,128]{2,1,0:T(8,128)(2,1)}, u32[]{:S(2)}, u32[]{:S(2)}) collective-permute-start(bf16[10,128,128]{2,1,0:T(8,128)(2,1)} %collective-permute-done.1.rest_5_), channel_id=1, source_target_pairs={{0,8},{8,0},{1,9},{9,1},{2,10},{10,2},{3,11},{11,3},{4,12},{12,4},... | collective-permute-start | bytes 983048 | tf_op jit(solution)/shard_map/ppermute | solution.py:286
  34.4 0.0 collective-permute-start.9
  34.4 5.8 %all-to-all-done.1.pulled = bf16[32,20,128]{2,1,0:T(8,128)(2,1)S(1)} async-done(((bf16[32,20,128]{2,1,0:T(8,128)(2,1)}), bf16[32,20,128]{2,1,0:T(8,128)(2,1)S(1)}, u32[]{:S(2)}, u32[]{:S(2)}) %all-to-all-start.1) | async-done | bytes 163872 | tf_op jit(solution)/shard_map/all_to_all | solution.py:283
  40.2 1.8 %shard_map.95 = bf16[32,32,128]{2,1,0:T(8,128)(2,1)} custom-call(s32[48]{0:T(128)S(1)} %get-tuple-element.23.lists, bf16[32,20,128]{2,1,0:T(8,128)(2,1)S(1)} %all-to-all-done.1.pulled, bf16[16,1,256,256]{3,2,1,0:T(8,128)(2,1)S(1)} %copy-done), custom_call_target="tpu_custom_call" | custom-call | tf_op jit(solution)/shard_map/pallas_call | solution.py:345
  42.1 3.9 %all-to-all-start.2 = ((bf16[32,32,128]{2,1,0:T(8,128)(2,1)}), bf16[32,32,128]{2,1,0:T(8,128)(2,1)S(1)}, u32[]{:S(2)}, u32[]{:S(2)}) async-start(bf16[32,32,128]{2,1,0:T(8,128)(2,1)} %shard_map.95), calls=%async_computation.2 | async-start | bytes 524288 | tf_op jit(solution)/shard_map/all_to_all | solution.py:283
  45.9 0.2 collective-permute-start.12
  46.2 0.3 collective-permute-start.10
  46.6 0.2 collective-permute-start.13
  46.7 1.8 %collective-permute-start.14 = (bf16[10,128,128]{2,1,0:T(8,128)(2,1)}, bf16[10,128,128]{2,1,0:T(8,128)(2,1)S(1)}, u32[]{:S(2)}, u32[]{:S(2)}) collective-permute-start(bf16[10,128,128]{2,1,0:T(8,128)(2,1)} %collective-permute-done.5.rest_4_), channel_id=1, source_target_pairs={{0,16},{8,120},{16,32},{24,8},{32,48},{40,24},{48,64},{56,40},{64,... | collective-permute-start | bytes 983048 | tf_op jit(solution)/shard_map/ppermute | solution.py:294
  48.5 1.5 %collective-permute-start.15 = (bf16[10,128,128]{2,1,0:T(8,128)(2,1)}, bf16[10,128,128]{2,1,0:T(8,128)(2,1)S(1)}, u32[]{:S(2)}, u32[]{:S(2)}) collective-permute-start(bf16[10,128,128]{2,1,0:T(8,128)(2,1)} %collective-permute-done.7.rest_7_), channel_id=1, source_target_pairs={{0,16},{8,120},{16,32},{24,8},{32,48},{40,24},{48,64},{56,40},{64,... | collective-permute-start | bytes 983048 | tf_op jit(solution)/shard_map/ppermute | solution.py:294
  50.0 2.5 %shard_map.92 = (s32[384]{0:T(512)S(1)}, f32[160]{0:T(256)S(1)}) custom-call(f32[32,1,128]{2,1,0:T(1,128)S(1)} %all-to-all-done.notices), custom_call_target="tpu_custom_call" | custom-call | tf_op jit(solution)/shard_map/pallas_call | solution.py:334
  52.6 6.6 %all-to-all-done.2.came = bf16[32,32,128]{2,1,0:T(8,128)(2,1)S(1)} async-done(((bf16[32,32,128]{2,1,0:T(8,128)(2,1)}), bf16[32,32,128]{2,1,0:T(8,128)(2,1)S(1)}, u32[]{:S(2)}, u32[]{:S(2)}) %all-to-all-start.2) | async-done | bytes 262176 | tf_op jit(solution)/shard_map/all_to_all | solution.py:283
  59.2 3.2 %shard_map.96 = (bf16[8,64,128]{2,1,0:T(8,128)(2,1)S(1)}, f32[40,64,128]{2,1,0:T(8,128)S(1)}) custom-call(s32[1]{0:T(128)} %bitcast.1.where, s32[384]{0:T(512)S(1)} %get-tuple-element.21.table, f32[160]{0:T(256)S(1)} %get-tuple-element.22.scales, bf16[32,32,128]{2,1,0:T(8,128)(2,1)S(1)} %all-to-all-done.2.came, ...), custom_call_target="tpu_custom_call" | custom-call | tf_op jit(solution)/shard_map/pallas_call | solution.py:353
  62.4 0.3 collective-permute-done.15.four_x
  62.6 1.0 %shard_map.97 = bf16[80,32,128]{2,1,0:T(8,128)(2,1)S(1)} custom-call(s32[384]{0:T(512)S(1)} %get-tuple-element.21.table, f32[160]{0:T(256)S(1)} %get-tuple-element.22.scales, bf16[8,64,128]{2,1,0:T(8,128)(2,1)S(1)} %get-tuple-element.29.rows, f32[40,64,128]{2,1,0:T(8,128)S(1)} %get-tuple-element.30.so_far, ...), custom_call_target="tpu_custom_call" | custom-call | tf_op jit(solution)/shard_map/pallas_call | solution.py:366
  63.6 17.6 %all_to_all.20 = bf16[80,32,128]{2,1,0:T(8,128)(2,1)S(1)} all-to-all(bf16[80,32,128]{2,1,0:T(8,128)(2,1)S(1)} %shard_map.97), channel_id=1, replica_groups=mesh['xl'=2,'z'=8,'core'=2,'y'=4,'xh'=2] {'xl','y','xh'}, dimensions={0} | all-to-all | bytes 1310720 | tf_op jit(solution)/shard_map/all_to_all | solution.py:283
  81.3 0.7 shard_map.98
  (19 shorter events, 0.0 us)
Async XLA Ops:
  0.0 40.2 %copy-start = (bf16[16,1,256,256]{3,2,1,0:T(8,128)(2,1)S(1)}, bf16[16,1,256,256]{3,2,1,0:T(8,128)(2,1)}, u32[]{:S(2)}) copy-start(bf16[16,1,256,256]{3,2,1,0:T(8,128)(2,1)} %cache.3) | copy-start | bytes 6291460
  0.0 3.5 %collective-permute-start = (bf16[10,128,128]{2,1,0:T(8,128)(2,1)}, bf16[10,128,128]{2,1,0:T(8,128)(2,1)S(1)}, u32[]{:S(2)}, u32[]{:S(2)}) collective-permute-start(bf16[10,128,128]{2,1,0:T(8,128)(2,1)} %rest_0_.1), channel_id=1, source_target_pairs={{0,8},{8,0},{1,9},{9,1},{2,10},{10,2},{3,11},{11,3},{4,12},{12,4},... | collective-permute-start | bytes 983048 | tf_op jit(solution)/shard_map/ppermute | solution.py:286
  0.0 17.1 %collective-permute-start.2 = (bf16[10,128,128]{2,1,0:T(8,128)(2,1)}, bf16[10,128,128]{2,1,0:T(8,128)(2,1)S(1)}, u32[]{:S(2)}, u32[]{:S(2)}) collective-permute-start(bf16[10,128,128]{2,1,0:T(8,128)(2,1)} %rest_0_.1), channel_id=1, source_target_pairs={{0,16},{8,120},{16,32},{24,8},{32,48},{40,24},{48,64},{56,40},{64,... | collective-permute-start | bytes 983048 | tf_op jit(solution)/shard_map/ppermute | solution.py:294
  3.5 18.3 %collective-permute-start.1 = (bf16[10,128,128]{2,1,0:T(8,128)(2,1)S(1)}, bf16[10,128,128]{2,1,0:T(8,128)(2,1)}, u32[]{:S(2)}, u32[]{:S(2)}) collective-permute-start(bf16[10,128,128]{2,1,0:T(8,128)(2,1)S(1)} %collective-permute-done.rest_1_), channel_id=1, source_target_pairs={{0,16},{8,120},{16,32},{24,8},{32,48},{40,24},{48,64},{56,40},{64,... | collective-permute-start | bytes 983048 | tf_op jit(solution)/shard_map/ppermute | solution.py:294
  5.5 16.3 %all-to-all-start = ((f32[32,1,128]{2,1,0:T(1,128)}), f32[32,1,128]{2,1,0:T(1,128)S(1)}, u32[]{:S(2)}, u32[]{:S(2)}) async-start(f32[32,1,128]{2,1,0:T(1,128)} %shard_map.91), calls=%async_computation | async-start | bytes 32768 | tf_op jit(solution)/shard_map/all_to_all | solution.py:283
  17.1 42.0 %copy-start.1 = (bf16[10,128,128]{2,1,0:T(8,128)(2,1)S(1)}, bf16[10,128,128]{2,1,0:T(8,128)(2,1)}, u32[]{:S(2)}) copy-start(bf16[10,128,128]{2,1,0:T(8,128)(2,1)} %rest_0_.1) | copy-start | bytes 983044
  17.1 13.1 %collective-permute-start.4 = (bf16[10,128,128]{2,1,0:T(8,128)(2,1)S(1)}, bf16[10,128,128]{2,1,0:T(8,128)(2,1)}, u32[]{:S(2)}, u32[]{:S(2)}) collective-permute-start(bf16[10,128,128]{2,1,0:T(8,128)(2,1)S(1)} %collective-permute-done.2.rest_2_), channel_id=1, source_target_pairs={{0,16},{8,120},{16,32},{24,8},{32,48},{40,24},{48,64},{56,40},{64,... | collective-permute-start | bytes 983048 | tf_op jit(solution)/shard_map/ppermute | solution.py:294
  21.8 9.9 %collective-permute-start.6 = (bf16[10,128,128]{2,1,0:T(8,128)(2,1)}, bf16[10,128,128]{2,1,0:T(8,128)(2,1)}, u32[]{:S(2)}, u32[]{:S(2)}) collective-permute-start(bf16[10,128,128]{2,1,0:T(8,128)(2,1)} %collective-permute-done.1.rest_5_), channel_id=1, source_target_pairs={{0,16},{8,120},{16,32},{24,8},{32,48},{40,24},{48,64},{56,40},{64,... | collective-permute-start | bytes 983048 | tf_op jit(solution)/shard_map/ppermute | solution.py:294
  24.0 16.3 %all-to-all-start.1 = ((bf16[32,20,128]{2,1,0:T(8,128)(2,1)}), bf16[32,20,128]{2,1,0:T(8,128)(2,1)S(1)}, u32[]{:S(2)}, u32[]{:S(2)}) async-start(bf16[32,20,128]{2,1,0:T(8,128)(2,1)} %shard_map.94), calls=%async_computation.1 | async-start | bytes 393216 | tf_op jit(solution)/shard_map/all_to_all | solution.py:283
  28.4 6.0 %collective-permute-start.3 = (bf16[16,16,128]{2,1,0:T(8,128)(2,1)S(1)}, bf16[16,16,128]{2,1,0:T(8,128)(2,1)S(1)}, u32[]{:S(2)}, u32[]{:S(2)}) collective-permute-start(bf16[16,16,128]{2,1,0:T(8,128)(2,1)S(1)} %get-tuple-element.26.mine), channel_id=1, source_target_pairs={{0,128},{128,0},{1,129},{129,1},{2,130},{130,2},{3,131},{131,3},{4... | collective-permute-start | bytes 196616 | tf_op jit(solution)/shard_map/ppermute | solution.py:286
  30.2 15.7 %collective-permute-start.8 = (bf16[10,128,128]{2,1,0:T(8,128)(2,1)S(1)}, bf16[10,128,128]{2,1,0:T(8,128)(2,1)}, u32[]{:S(2)}, u32[]{:S(2)}) collective-permute-start(bf16[10,128,128]{2,1,0:T(8,128)(2,1)S(1)} %collective-permute-done.2.rest_2_), channel_id=1, source_target_pairs={{0,8},{8,0},{1,9},{9,1},{2,10},{10,2},{3,11},{11,3},{4,12},{12,4},... | collective-permute-start | bytes 983048 | tf_op jit(solution)/shard_map/ppermute | solution.py:286
  30.2 16.0 %collective-permute-start.5 = (bf16[10,128,128]{2,1,0:T(8,128)(2,1)}, bf16[10,128,128]{2,1,0:T(8,128)(2,1)}, u32[]{:S(2)}, u32[]{:S(2)}) collective-permute-start(bf16[10,128,128]{2,1,0:T(8,128)(2,1)} %collective-permute-done.4.rest_3_), channel_id=1, source_target_pairs={{0,16},{8,120},{16,32},{24,8},{32,48},{40,24},{48,64},{56,40},{64,... | collective-permute-start | bytes 983048 | tf_op jit(solution)/shard_map/ppermute | solution.py:294
  31.7 14.8 %collective-permute-start.7 = (bf16[10,128,128]{2,1,0:T(8,128)(2,1)}, bf16[10,128,128]{2,1,0:T(8,128)(2,1)}, u32[]{:S(2)}, u32[]{:S(2)}) collective-permute-start(bf16[10,128,128]{2,1,0:T(8,128)(2,1)} %collective-permute-done.6.rest_6_), channel_id=1, source_target_pairs={{0,16},{8,120},{16,32},{24,8},{32,48},{40,24},{48,64},{56,40},{64,... | collective-permute-start | bytes 983048 | tf_op jit(solution)/shard_map/ppermute | solution.py:294
  33.2 13.5 %collective-permute-start.11 = (bf16[10,128,128]{2,1,0:T(8,128)(2,1)}, bf16[10,128,128]{2,1,0:T(8,128)(2,1)}, u32[]{:S(2)}, u32[]{:S(2)}) collective-permute-start(bf16[10,128,128]{2,1,0:T(8,128)(2,1)} %collective-permute-done.1.rest_5_), channel_id=1, source_target_pairs={{0,8},{8,0},{1,9},{9,1},{2,10},{10,2},{3,11},{11,3},{4,12},{12,4},... | collective-permute-start | bytes 983048 | tf_op jit(solution)/shard_map/ppermute | solution.py:286
  34.4 14.1 %collective-permute-start.9 = (bf16[10,128,128]{2,1,0:T(8,128)(2,1)}, bf16[10,128,128]{2,1,0:T(8,128)(2,1)}, u32[]{:S(2)}, u32[]{:S(2)}) collective-permute-start(bf16[10,128,128]{2,1,0:T(8,128)(2,1)} %collective-permute-done.4.rest_3_), channel_id=1, source_target_pairs={{0,8},{8,0},{1,9},{9,1},{2,10},{10,2},{3,11},{11,3},{4,12},{12,4},... | collective-permute-start | bytes 983048 | tf_op jit(solution)/shard_map/ppermute | solution.py:286
  42.1 17.1 %all-to-all-start.2 = ((bf16[32,32,128]{2,1,0:T(8,128)(2,1)}), bf16[32,32,128]{2,1,0:T(8,128)(2,1)S(1)}, u32[]{:S(2)}, u32[]{:S(2)}) async-start(bf16[32,32,128]{2,1,0:T(8,128)(2,1)} %shard_map.95), calls=%async_computation.2 | async-start | bytes 524288 | tf_op jit(solution)/shard_map/all_to_all | solution.py:283
  45.9 6.6 %collective-permute-start.12 = (bf16[10,128,128]{2,1,0:T(8,128)(2,1)}, bf16[10,128,128]{2,1,0:T(8,128)(2,1)S(1)}, u32[]{:S(2)}, u32[]{:S(2)}) collective-permute-start(bf16[10,128,128]{2,1,0:T(8,128)(2,1)} %collective-permute-done.6.rest_6_), channel_id=1, source_target_pairs={{0,8},{8,0},{1,9},{9,1},{2,10},{10,2},{3,11},{11,3},{4,12},{12,4},... | collective-permute-start | bytes 983048 | tf_op jit(solution)/shard_map/ppermute | solution.py:286
  46.2 6.4 %collective-permute-start.10 = (bf16[10,128,128]{2,1,0:T(8,128)(2,1)}, bf16[10,128,128]{2,1,0:T(8,128)(2,1)S(1)}, u32[]{:S(2)}, u32[]{:S(2)}) collective-permute-start(bf16[10,128,128]{2,1,0:T(8,128)(2,1)} %collective-permute-done.5.rest_4_), channel_id=1, source_target_pairs={{0,8},{8,0},{1,9},{9,1},{2,10},{10,2},{3,11},{11,3},{4,12},{12,4},... | collective-permute-start | bytes 983048 | tf_op jit(solution)/shard_map/ppermute | solution.py:286
  46.6 12.6 %collective-permute-start.13 = (bf16[10,128,128]{2,1,0:T(8,128)(2,1)}, bf16[10,128,128]{2,1,0:T(8,128)(2,1)S(1)}, u32[]{:S(2)}, u32[]{:S(2)}) collective-permute-start(bf16[10,128,128]{2,1,0:T(8,128)(2,1)} %collective-permute-done.7.rest_7_), channel_id=1, source_target_pairs={{0,8},{8,0},{1,9},{9,1},{2,10},{10,2},{3,11},{11,3},{4,12},{12,4},... | collective-permute-start | bytes 983048 | tf_op jit(solution)/shard_map/ppermute | solution.py:286
  46.7 15.6 %collective-permute-start.14 = (bf16[10,128,128]{2,1,0:T(8,128)(2,1)}, bf16[10,128,128]{2,1,0:T(8,128)(2,1)S(1)}, u32[]{:S(2)}, u32[]{:S(2)}) collective-permute-start(bf16[10,128,128]{2,1,0:T(8,128)(2,1)} %collective-permute-done.5.rest_4_), channel_id=1, source_target_pairs={{0,16},{8,120},{16,32},{24,8},{32,48},{40,24},{48,64},{56,40},{64,... | collective-permute-start | bytes 983048 | tf_op jit(solution)/shard_map/ppermute | solution.py:294
  48.5 14.1 %collective-permute-start.15 = (bf16[10,128,128]{2,1,0:T(8,128)(2,1)}, bf16[10,128,128]{2,1,0:T(8,128)(2,1)S(1)}, u32[]{:S(2)}, u32[]{:S(2)}) collective-permute-start(bf16[10,128,128]{2,1,0:T(8,128)(2,1)} %collective-permute-done.7.rest_7_), channel_id=1, source_target_pairs={{0,16},{8,120},{16,32},{24,8},{32,48},{40,24},{48,64},{56,40},{64,... | collective-permute-start | bytes 983048 | tf_op jit(solution)/shard_map/ppermute | solution.py:294
